TPU v7x, 32 devices: a whole 2x2x4 slice. The times are simulated.
32 devices in a mesh: dp: 8 (over z, y), seq: 4 (over x, core).
Axes of the slice: x: 2, y: 2, z: 4, core: 2. Of those that a mesh axis runs over, the one named last changes fastest.
Arguments:
- tokens: bfloat16 [32, 8, 196, 768], P('dp', 'seq'), may hold values from -6 to 6
- temporal_gain: bfloat16 [768], P(('dp', 'seq')), may hold values from 0.5 to 1.5
- temporal_biases: bfloat16 [3, 768], P(None, ('dp', 'seq')), may hold values from -1.1953125 to 1.1953125
- temporal_inproj: bfloat16 [768, 2304], P(('dp', 'seq')), may hold values from -0.21875 to 0.21875
- temporal_outproj: bfloat16 [768, 768], P(('dp', 'seq')), may hold values from -0.4375 to 0.4375
- temporal_linear: bfloat16 [768, 768], P(('dp', 'seq')), may hold values from -0.21875 to 0.21875
- spatial_gain: bfloat16 [768], P(('dp', 'seq')), may hold values from 0.5 to 1.5
- spatial_biases: bfloat16 [2, 768], P(None, ('dp', 'seq')), may hold values from -1.1953125 to 1.1953125
- spatial_inproj: bfloat16 [768, 2304], P(('dp', 'seq')), may hold values from -0.21875 to 0.21875
- spatial_outproj: bfloat16 [768, 768], P(('dp', 'seq')), may hold values from -1.75 to 1.75
- feed_gain: bfloat16 [768], P(('dp', 'seq')), may hold values from 0.5 to 1.5
- feed_biases: bfloat16 [2, 768], P(None, ('dp', 'seq')), may hold values from -1.1953125 to 1.1953125
- widen_weight: bfloat16 [768, 3072], P(('dp', 'seq')), may hold values from -0.21875 to 0.21875
- widen_bias: bfloat16 [3072], P(('dp', 'seq')), may hold values from -1.1953125 to 1.1953125
- narrow_weight: bfloat16 [3072, 768], P(('dp', 'seq')), may hold values from -0.109375 to 0.109375
- cotangent: bfloat16 [32, 8, 196, 768], P('dp', 'seq'), may hold values from -6 to 6
Outputs:
- output: bfloat16 [32, 8, 196, 768], P('dp', 'seq')
- grad_tokens: bfloat16 [32, 8, 196, 768], P('dp', 'seq')
- grad_temporal_gain: float32 [768], P(('dp', 'seq'))
- grad_temporal_biases: float32 [3, 768], P(None, ('dp', 'seq'))
- grad_temporal_inproj: float32 [768, 2304], P(('dp', 'seq'))
- grad_temporal_outproj: float32 [768, 768], P(('dp', 'seq'))
- grad_temporal_linear: float32 [768, 768], P(('dp', 'seq'))
- grad_spatial_gain: float32 [768], P(('dp', 'seq'))
- grad_spatial_biases: float32 [2, 768], P(None, ('dp', 'seq'))
- grad_spatial_inproj: float32 [768, 2304], P(('dp', 'seq'))
- grad_spatial_outproj: float32 [768, 768], P(('dp', 'seq'))
- grad_feed_gain: float32 [768], P(('dp', 'seq'))
- grad_feed_biases: float32 [2, 768], P(None, ('dp', 'seq'))
- grad_widen_weight: float32 [768, 3072], P(('dp', 'seq'))
- grad_widen_bias: float32 [3072], P(('dp', 'seq'))
- grad_narrow_weight: float32 [3072, 768], P(('dp', 'seq'))
All inputs are finite; a program needn't handle non-finite values.
Results may differ from a plain program's by a relative error of at most 0.02.
Values may be sent and summed in bfloat16 or wider, within the bound.
No kernel may reach another device: no remote copies, remote signals or barrier semaphores. Data moves between devices by JAX's collectives and lax.ppermute only.
A program may use at most 320 MiB of HBM per device.

v0:
```python
import jax
import jax.numpy as jnp
from jax import lax
from jax.sharding import PartitionSpec as P

HEADS = 12
HEAD_DIM = 64


def norm_rows(values, gain_row, bias_row):
    center = values - jnp.mean(values, axis=-1, keepdims=True)
    spread = jnp.mean(center * center, axis=-1, keepdims=True)
    return center * lax.rsqrt(spread + 1e-05) * gain_row + bias_row


def gelu_exact(values):
    return jax.nn.gelu(values, approximate=False)


def matmul(left_side, right_side):
    flattened = left_side.reshape(-1, left_side.shape[-1])
    result = jnp.dot(flattened, right_side, preferred_element_type=jnp.float32)
    return result.reshape(left_side.shape[:-1] + (right_side.shape[1],))


def times_transpose(left_side, right_side):
    flattened = left_side.reshape(-1, left_side.shape[-1])
    result = lax.dot_general(
        flattened, right_side, (((1,), (1,)), ((), ())), preferred_element_type=jnp.float32
    )
    return result.reshape(left_side.shape[:-1] + (right_side.shape[0],))


def outer_sum(left_side, right_side):
    return lax.dot_general(
        left_side.reshape(-1, left_side.shape[-1]),
        right_side.reshape(-1, right_side.shape[-1]),
        (((0,), (0,)), ((), ())),
        preferred_element_type=jnp.float32,
    )


def token_sum(values):
    return jnp.sum(values.astype(jnp.float32).reshape(-1, values.shape[-1]), axis=0)


def to_sequences(grid_array):
    clip_count, frame_count, place_count, width = grid_array.shape
    return jnp.transpose(grid_array, (0, 2, 1, 3)).reshape(
        clip_count * place_count, frame_count, width
    )


def to_grid(seq_array, clip_count):
    seq_count, frame_count, width = seq_array.shape
    return jnp.transpose(
        seq_array.reshape(clip_count, seq_count // clip_count, frame_count, width), (0, 2, 1, 3)
    )


def split_heads(joined):
    parted = joined.reshape(joined.shape[0], joined.shape[1], 3, HEADS, HEAD_DIM)
    return (parted[:, :, 0], parted[:, :, 1], parted[:, :, 2])


def score_rows(query_heads, key_heads):
    raw_scores = jnp.einsum(
        "blhd,bmhd->bhlm", query_heads, key_heads, preferred_element_type=jnp.float32
    )
    return raw_scores * HEAD_DIM ** (-0.5)


def attend_forward(joined):
    query_heads, key_heads, value_heads = split_heads(joined)
    scores = score_rows(query_heads, key_heads)
    row_max = jnp.max(scores, axis=-1, keepdims=True)
    log_total = jnp.log(jnp.sum(jnp.exp(scores - row_max), axis=-1, keepdims=True)) + row_max
    shares = jnp.exp(scores - log_total).astype(jnp.bfloat16)
    mixture = jnp.einsum("bhlm,bmhd->blhd", shares, value_heads, preferred_element_type=jnp.float32)
    return (
        mixture.reshape(joined.shape[0], joined.shape[1], HEADS * HEAD_DIM).astype(jnp.bfloat16),
        log_total,
    )


def attend_backward(joined, log_total, grad_mixture):
    query_heads, key_heads, value_heads = split_heads(joined)
    exact_shares = jnp.exp(score_rows(query_heads, key_heads) - log_total)
    shares = exact_shares.astype(jnp.bfloat16)
    grad_heads = grad_mixture.reshape(query_heads.shape)
    grad_values = jnp.einsum(
        "bhlm,blhd->bmhd", shares, grad_heads, preferred_element_type=jnp.float32
    )
    grad_shares = jnp.einsum(
        "blhd,bmhd->bhlm", grad_heads, value_heads, preferred_element_type=jnp.float32
    )
    row_terms = jnp.sum(grad_shares * exact_shares, axis=-1, keepdims=True)
    grad_scores = (exact_shares * (grad_shares - row_terms)).astype(jnp.bfloat16)
    scaling = HEAD_DIM ** (-0.5)
    grad_queries = (
        jnp.einsum("bhlm,bmhd->blhd", grad_scores, key_heads, preferred_element_type=jnp.float32)
        * scaling
    )
    grad_keys = (
        jnp.einsum("bhlm,blhd->bmhd", grad_scores, query_heads, preferred_element_type=jnp.float32)
        * scaling
    )
    stacked = jnp.stack([grad_queries, grad_keys, grad_values], axis=2)
    return stacked.reshape(joined.shape).astype(jnp.bfloat16)


def on_device(
    tokens,
    temporal_gain,
    temporal_biases,
    temporal_inproj,
    temporal_outproj,
    temporal_linear,
    spatial_gain,
    spatial_biases,
    spatial_inproj,
    spatial_outproj,
    feed_gain,
    feed_biases,
    widen_weight,
    widen_bias,
    narrow_weight,
    cotangent,
):
    temporal = (
        lax.all_gather(temporal_gain, ("dp", "seq"), axis=0, tiled=True),
        lax.all_gather(temporal_biases, ("dp", "seq"), axis=1, tiled=True),
        lax.all_gather(temporal_inproj, ("dp", "seq"), axis=0, tiled=True),
        lax.all_gather(temporal_outproj, ("dp", "seq"), axis=0, tiled=True),
        lax.all_gather(temporal_linear, ("dp", "seq"), axis=0, tiled=True),
    )
    inputs = tokens.astype(jnp.float32)
    clip_count = inputs.shape[0]
    temporal_shift = temporal[1].astype(jnp.float32)
    temporal_norm = norm_rows(inputs, temporal[0].astype(jnp.float32), temporal_shift[0]).astype(
        jnp.bfloat16
    )
    placed = lax.all_to_all(temporal_norm, "seq", split_axis=2, concat_axis=1, tiled=True)
    temporal_joined = to_sequences(matmul(placed, temporal[2]).astype(jnp.bfloat16))
    temporal_mixed, temporal_total = attend_forward(temporal_joined)
    temporal_grid = to_grid(temporal_mixed, clip_count)
    temporal_proj = (matmul(temporal_grid, temporal[3]) + temporal_shift[1]).astype(jnp.bfloat16)
    temporal_branch = (matmul(temporal_proj, temporal[4]) + temporal_shift[2]).astype(jnp.bfloat16)
    after_time = inputs + lax.all_to_all(
        temporal_branch, "seq", split_axis=1, concat_axis=2, tiled=True
    ).astype(jnp.float32)
    spatial = (
        lax.all_gather(spatial_gain, ("dp", "seq"), axis=0, tiled=True),
        lax.all_gather(spatial_biases, ("dp", "seq"), axis=1, tiled=True),
        lax.all_gather(spatial_inproj, ("dp", "seq"), axis=0, tiled=True),
        lax.all_gather(spatial_outproj, ("dp", "seq"), axis=0, tiled=True),
    )
    spatial_shift = spatial[1].astype(jnp.float32)
    spatial_norm = norm_rows(after_time, spatial[0].astype(jnp.float32), spatial_shift[0]).astype(
        jnp.bfloat16
    )
    frames_here, place_count = (after_time.shape[1], after_time.shape[2])
    spatial_joined = (
        matmul(spatial_norm, spatial[2])
        .astype(jnp.bfloat16)
        .reshape(clip_count * frames_here, place_count, -1)
    )
    spatial_mixed, spatial_total = attend_forward(spatial_joined)
    spatial_grid = spatial_mixed.reshape(after_time.shape)
    after_space = after_time + matmul(spatial_grid, spatial[3]) + spatial_shift[1]
    feed = (
        lax.all_gather(feed_gain, ("dp", "seq"), axis=0, tiled=True),
        lax.all_gather(feed_biases, ("dp", "seq"), axis=1, tiled=True),
        lax.all_gather(widen_weight, ("dp", "seq"), axis=0, tiled=True),
        lax.all_gather(widen_bias, ("dp", "seq"), axis=0, tiled=True),
        lax.all_gather(narrow_weight, ("dp", "seq"), axis=0, tiled=True),
    )
    feed_shift = feed[1].astype(jnp.float32)
    feed_norm = norm_rows(after_space, feed[0].astype(jnp.float32), feed_shift[0]).astype(
        jnp.bfloat16
    )
    hidden = matmul(feed_norm, feed[2]) + feed[3].astype(jnp.float32)
    active = gelu_exact(hidden).astype(jnp.bfloat16)
    output = after_space + matmul(active, feed[4]) + feed_shift[1]
    feed_back = (
        lax.all_gather(feed_gain, ("dp", "seq"), axis=0, tiled=True),
        lax.all_gather(feed_biases, ("dp", "seq"), axis=1, tiled=True),
        lax.all_gather(widen_weight, ("dp", "seq"), axis=0, tiled=True),
        lax.all_gather(widen_bias, ("dp", "seq"), axis=0, tiled=True),
        lax.all_gather(narrow_weight, ("dp", "seq"), axis=0, tiled=True),
    )
    grad_output = cotangent.astype(jnp.float32)
    grad_narrow = outer_sum(active, cotangent)
    grad_narrow_bias = token_sum(cotangent)
    unused_value, gelu_pull = jax.vjp(gelu_exact, hidden)
    grad_hidden = gelu_pull(times_transpose(cotangent, feed_back[4]))[0].astype(jnp.bfloat16)
    grad_widen = outer_sum(feed_norm, grad_hidden)
    grad_widen_bias = token_sum(grad_hidden)
    unused_value, feed_pull = jax.vjp(
        norm_rows,
        after_space,
        feed_back[0].astype(jnp.float32),
        feed_back[1].astype(jnp.float32)[0],
    )
    grad_space_norm, grad_feed_gain, grad_feed_shift = feed_pull(
        times_transpose(grad_hidden, feed_back[2])
    )
    grad_after_space = grad_output + grad_space_norm
    feed_pair = jnp.stack([grad_feed_shift, grad_narrow_bias])
    feed_grads = (
        lax.psum_scatter(grad_feed_gain, ("dp", "seq"), scatter_dimension=0, tiled=True),
        lax.psum_scatter(feed_pair, ("dp", "seq"), scatter_dimension=1, tiled=True),
        lax.psum_scatter(grad_widen, ("dp", "seq"), scatter_dimension=0, tiled=True),
        lax.psum_scatter(grad_widen_bias, ("dp", "seq"), scatter_dimension=0, tiled=True),
        lax.psum_scatter(grad_narrow, ("dp", "seq"), scatter_dimension=0, tiled=True),
    )
    spatial_back = (
        lax.all_gather(spatial_gain, ("dp", "seq"), axis=0, tiled=True),
        lax.all_gather(spatial_biases, ("dp", "seq"), axis=1, tiled=True),
        lax.all_gather(spatial_inproj, ("dp", "seq"), axis=0, tiled=True),
        lax.all_gather(spatial_outproj, ("dp", "seq"), axis=0, tiled=True),
    )
    grad_space = grad_after_space.astype(jnp.bfloat16)
    grad_spatial_out = outer_sum(spatial_grid, grad_space)
    grad_spatial_bias = token_sum(grad_space)
    grad_spatial_mixed = (
        times_transpose(grad_space, spatial_back[3])
        .astype(jnp.bfloat16)
        .reshape(spatial_mixed.shape)
    )
    grad_spatial_joined = attend_backward(spatial_joined, spatial_total, grad_spatial_mixed)
    grad_spatial_in = outer_sum(spatial_norm, grad_spatial_joined)
    unused_value, spatial_pull = jax.vjp(
        norm_rows,
        after_time,
        spatial_back[0].astype(jnp.float32),
        spatial_back[1].astype(jnp.float32)[0],
    )
    grad_time_norm, grad_spatial_gain, grad_spatial_shift = spatial_pull(
        times_transpose(grad_spatial_joined, spatial_back[2]).reshape(after_time.shape)
    )
    grad_after_time = grad_after_space + grad_time_norm
    spatial_pair = jnp.stack([grad_spatial_shift, grad_spatial_bias])
    spatial_grads = (
        lax.psum_scatter(grad_spatial_gain, ("dp", "seq"), scatter_dimension=0, tiled=True),
        lax.psum_scatter(spatial_pair, ("dp", "seq"), scatter_dimension=1, tiled=True),
        lax.psum_scatter(grad_spatial_in, ("dp", "seq"), scatter_dimension=0, tiled=True),
        lax.psum_scatter(grad_spatial_out, ("dp", "seq"), scatter_dimension=0, tiled=True),
    )
    temporal_back = (
        lax.all_gather(temporal_gain, ("dp", "seq"), axis=0, tiled=True),
        lax.all_gather(temporal_biases, ("dp", "seq"), axis=1, tiled=True),
        lax.all_gather(temporal_inproj, ("dp", "seq"), axis=0, tiled=True),
        lax.all_gather(temporal_outproj, ("dp", "seq"), axis=0, tiled=True),
        lax.all_gather(temporal_linear, ("dp", "seq"), axis=0, tiled=True),
    )
    grad_placed = lax.all_to_all(
        grad_after_time.astype(jnp.bfloat16), "seq", split_axis=2, concat_axis=1, tiled=True
    )
    grad_linear = outer_sum(temporal_proj, grad_placed)
    grad_linear_bias = token_sum(grad_placed)
    grad_proj = times_transpose(grad_placed, temporal_back[4]).astype(jnp.bfloat16)
    grad_outproj = outer_sum(temporal_grid, grad_proj)
    grad_proj_bias = token_sum(grad_proj)
    grad_temporal_mixed = to_sequences(
        times_transpose(grad_proj, temporal_back[3]).astype(jnp.bfloat16)
    )
    grad_temporal_joined = to_grid(
        attend_backward(temporal_joined, temporal_total, grad_temporal_mixed), clip_count
    )
    grad_inproj = outer_sum(placed, grad_temporal_joined)
    grad_norm_placed = times_transpose(grad_temporal_joined, temporal_back[2]).astype(jnp.bfloat16)
    grad_norm_frames = lax.all_to_all(
        grad_norm_placed, "seq", split_axis=1, concat_axis=2, tiled=True
    ).astype(jnp.float32)
    unused_value, temporal_pull = jax.vjp(
        norm_rows,
        inputs,
        temporal_back[0].astype(jnp.float32),
        temporal_back[1].astype(jnp.float32)[0],
    )
    grad_input_norm, grad_temporal_gain, grad_temporal_shift = temporal_pull(grad_norm_frames)
    grad_inputs = grad_after_time + grad_input_norm
    temporal_triple = jnp.stack([grad_temporal_shift, grad_proj_bias, grad_linear_bias])
    temporal_grads = (
        lax.psum_scatter(grad_temporal_gain, ("dp", "seq"), scatter_dimension=0, tiled=True),
        lax.psum_scatter(temporal_triple, ("dp", "seq"), scatter_dimension=1, tiled=True),
        lax.psum_scatter(grad_inproj, ("dp", "seq"), scatter_dimension=0, tiled=True),
        lax.psum_scatter(grad_outproj, ("dp", "seq"), scatter_dimension=0, tiled=True),
        lax.psum_scatter(grad_linear, ("dp", "seq"), scatter_dimension=0, tiled=True),
    )
    return (
        output.astype(jnp.bfloat16),
        grad_inputs.astype(jnp.bfloat16),
        temporal_grads[0],
        temporal_grads[1],
        temporal_grads[2],
        temporal_grads[3],
        temporal_grads[4],
        spatial_grads[0],
        spatial_grads[1],
        spatial_grads[2],
        spatial_grads[3],
        feed_grads[0],
        feed_grads[1],
        feed_grads[2],
        feed_grads[3],
        feed_grads[4],
    )


def solution(mesh):
    in_specs = (
        P("dp", "seq", None, None),
        P(("dp", "seq")),
        P(None, ("dp", "seq")),
        P(("dp", "seq"), None),
        P(("dp", "seq"), None),
        P(("dp", "seq"), None),
        P(("dp", "seq")),
        P(None, ("dp", "seq")),
        P(("dp", "seq"), None),
        P(("dp", "seq"), None),
        P(("dp", "seq")),
        P(None, ("dp", "seq")),
        P(("dp", "seq"), None),
        P(("dp", "seq")),
        P(("dp", "seq"), None),
        P("dp", "seq", None, None),
    )
    out_specs = (
        P("dp", "seq", None, None),
        P("dp", "seq", None, None),
        P(("dp", "seq")),
        P(None, ("dp", "seq")),
        P(("dp", "seq"), None),
        P(("dp", "seq"), None),
        P(("dp", "seq"), None),
        P(("dp", "seq")),
        P(None, ("dp", "seq")),
        P(("dp", "seq"), None),
        P(("dp", "seq"), None),
        P(("dp", "seq")),
        P(None, ("dp", "seq")),
        P(("dp", "seq"), None),
        P(("dp", "seq")),
        P(("dp", "seq"), None),
    )
    return jax.shard_map(
        on_device, mesh=mesh, in_specs=in_specs, out_specs=out_specs, check_vma=False
    )
```

profile of v0, /device:TPU:0, one launch (start us, length us, event | category | flops | bytes accessed | tf_op | source)
XLA Modules:
  0.0 1548.4 jit_solution(2813360270132285919)
XLA Ops:
  14.0 42.3 %all-reduce.12 = (bf16[768]{0:T(1024)(128)(2,1)S(1)}, bf16[768]{0:T(1024)(128)(2,1)S(1)}, bf16[768]{0:T(1024)(128)(2,1)S(1)}, bf16[3072]{0:T(1024)(128)(2,1)S(1)}) all-reduce(bf16[768]{0:T(1024)(128)(2,1)S(1)} %dynamic-update-slice, bf16[768]{0:T(1024)(128)(2,1)S(1)} %dynamic-update-slice.1, ...), channel_id=1, replica_groups=mesh['dp'=8,'seq'=4] {'dp','seq'}, use_global_device_ids=true, to_apply=%add | all-reduce | flops 5376 | bytes 21504
  58.4 40.7 %all-gather = bf16[32,24,3]{1,2,0:T(4,128)(2,1)S(1)} all-gather(bf16[1,24,3]{1,2,0:T(4,128)(2,1)} %bitcast.278), channel_id=1, replica_groups=mesh['dp'=8,'seq'=4] {'dp','seq'}, dimensions={0}, use_global_device_ids=true | all-gather | bytes 4752 | tf_op jit(solution)/shard_map/all_gather | solution.py:132
  111.4 30.6 %all-to-all-done = bf16[4,2,196,768]{3,0,1,2:T(4,128)(2,1)} async-done(((bf16[4,2,196,768]{3,0,1,2:T(4,128)(2,1)}), bf16[4,2,196,768]{3,0,1,2:T(4,128)(2,1)}, u32[]{:S(2)}, u32[]{:S(2)}) %all-to-all-start) | async-done | bytes 2408480 | tf_op jit(solution)/shard_map/all_to_all | solution.py:143
  147.5 11.1 convert_bitcast_fusion
  158.7 7.7 copy.160
  166.4 22.5 %reshape_reshape.8 = bf16[196,8,3,12,64]{4,3,2,1,0:T(8,128)(2,1)} reshape(bf16[4,49,8,2304]{3,2,1,0:T(8,128)(2,1)} %copy.160) | data formatting | bytes 14450688 | tf_op jit(solution)/shard_map/reshape;reshape | solution.py:62
  188.9 19.1 %fusion.91 = (bf16[196,8,1,12,64]{4,3,2,1,0:T(8,128)(2,1)}, bf16[196,8,1,12,64]{4,3,2,1,0:T(8,128)(2,1)}, bf16[196,8,1,12,64]{4,3,2,1,0:T(8,128)(2,1)}) fusion(bf16[196,8,3,12,64]{4,3,2,1,0:T(8,128)(2,1)} %reshape_reshape.8), kind=kLoop, calls=%fused_computation.178 | loop fusion | bytes 14450688 | tf_op jit(solution)/shard_map/slice | solution.py:63
  208.0 13.5 multiply_reduce_fusion.3
  221.5 9.4 exponential_reduce_fusion.1
  234.5 7.7 convert_bitcast_fusion.2
  242.3 4.9 copy.165
  247.1 9.0 convert_element_type.203
  256.2 5.9 add_convert_fusion.2
  275.2 59.8 %all-gather.1 = bf16[32,24,2]{1,2,0:T(2,128)(2,1)S(1)} all-gather(bf16[1,24,2]{1,2,0:T(2,128)(2,1)S(1)} %bitcast.279), channel_id=1, replica_groups=mesh['dp'=8,'seq'=4] {'dp','seq'}, dimensions={0}, use_global_device_ids=true | all-gather | bytes 3168 | tf_op jit(solution)/shard_map/all_gather | solution.py:154
  335.1 37.8 %all-gather.2 = bf16[32,24,2]{1,2,0:T(2,128)(2,1)S(1)} all-gather(bf16[1,24,2]{1,2,0:T(2,128)(2,1)S(1)} %bitcast.280), channel_id=1, replica_groups=mesh['dp'=8,'seq'=4] {'dp','seq'}, dimensions={0}, use_global_device_ids=true | all-gather | bytes 3168 | tf_op jit(solution)/shard_map/all_gather | solution.py:173
  382.0 10.8 convolution_convert_fusion
  392.8 11.9 copy.172
  404.7 12.4 multiply_reduce_fusion.1
  417.1 12.5 exponential_reduce_fusion
  429.7 11.8 fusion.54
  441.5 6.4 fusion.92
  450.9 21.1 %fusion.20 = (u8[2,196,3072]{2,1,0:T(8,128)(4,1)S(1)}, u8[2,196,3072]{2,1,0:T(8,128)(4,1)S(1)}, f32[4,2,196,3072]{3,2,1,0:T(8,128)}) fusion(f32[3072]{0:T(1024)S(1)} %convert_element_type.221, bf16[768,3072]{1,0:T(8,128)(2,1)} %all-gather.21.cloned.1.call-done, f32[4,2,196,768]{3,2,1,0:T(8,128)} %copy-done.10, f32[768]{0:T(1024)S(1)} %get-tuple-element.94, ...), kind=kOutput, calls=%fused_computation.81 | convolution fusion | flops 7469801472 | bytes 31242496 | tf_op jit(solution)/shard_map/dot_general | solution.py:22
  472.0 47.6 %multiply_convert_fusion.1 = (bf16[4,2,196,3072]{3,2,1,0:T(8,128)(2,1)}, f32[4,2,196,3072]{3,2,1,0:T(8,128)}) fusion(f32[4,2,196,3072]{3,2,1,0:T(8,128)} %get-tuple-element.129, f32[3072]{0:T(1024)S(1)} %convert_element_type.221, u8[2,196,3072]{2,1,0:T(8,128)(4,1)S(1)} %get-tuple-element.81, u8[2,196,3072]{2,1,0:T(8,128)(4,1)S(1)} %get-tuple-element.80), kind=kLoop, calls=%fused_computation.11 | loop fusion | flops 341999616 | bytes 50589696 | tf_op jit(solution)/shard_map/convert_element_type | solution.py:183
  519.6 26.0 %convert_reduce_fusion = (f32[3072]{0:T(1024)}, bf16[4,2,196,3072]{3,2,1,0:T(8,128)(2,1)}) fusion(f32[4,2,196,3072]{3,2,1,0:T(8,128)} %get-tuple-element.116, bf16[3072,768]{1,0:T(8,128)(2,1)} %all-gather.23.cloned.1.call-done, bf16[4,2,196,768]{3,1,2,0:T(2,128)(2,1)} %param.31, f32[4,2,196,3072]{3,2,1,0:T(8,128)} %get-tuple-element.129, ...), kind=kOutput, calls=%fused_computation.7 | convolution fusion | flops 7480636416 | bytes 55320576 | tf_op jit(solution)/shard_map/dot_general | solution.py:28
  545.6 13.7 multiply_reduce_fusion.4
  573.2 11.9 convolution_bitcast_fusion.2
  585.1 15.1 multiply_reduce_fusion
  600.2 18.0 %multiply_convert_fusion = bf16[8,12,196,196]{2,3,1,0:T(8,128)(2,1)} fusion(f32[8,12,196,196]{2,3,1,0:T(8,128)} %get-tuple-element.132, f32[8,12,196,196]{2,3,1,0:T(8,128)} %get-tuple-element.126, f32[8,12,196]{2,1,0:T(8,128)S(1)} %get-tuple-element.131, f32[8,12,196]{2,1,0:T(8,128)S(1)} %log_add_fusion.1), kind=kLoop, calls=%fused_computation.8 | loop fusion | flops 18439680 | bytes 37029888 | tf_op jit(solution)/shard_map/convert_element_type | solution.py:98
  618.2 9.6 multiply_bitcast_fusion
  627.9 8.6 multiply_bitcast_fusion.1
  636.4 7.7 maximum_convert_fusion
  644.1 9.3 copy.186
  653.5 13.8 fusion.85
  670.3 6.9 fusion.87
  688.2 6.6 convert_element_type.248
  697.0 6.1 fusion.96
  703.2 10.3 all-to-all-done.2
  734.1 6.4 fusion.94
  743.2 18.5 %copy.204 = bf16[8,196,3,12,64]{1,0,4,3,2:T(8,128)(2,1)} copy(bf16[8,196,3,12,64]{1,4,3,0,2:T(8,128)(2,1)} %maximum_convert_fusion) | data formatting | bytes 14450688 | tf_op jit(solution)/shard_map/convert_element_type | solution.py:109
  761.6 16.8 %convert_element_type.247 = bf16[1568,2304]{0,1:T(8,128)(2,1)} reshape(bf16[8,196,3,12,64]{1,0,4,3,2:T(8,128)(2,1)} %copy.204) | data formatting | bytes 14450688 | tf_op jit(solution)/shard_map/convert_element_type | solution.py:109
  778.4 11.5 fusion.95
  800.3 8.4 reshape_reshape.20
  808.7 14.0 multiply_reduce_fusion.2
  822.7 9.7 multiply_convert_fusion.4
  832.4 7.8 fusion.22
  840.2 7.3 fusion.21
  847.5 7.9 convert_bitcast_fusion.1
  855.5 6.4 pad_maximum_fusion
  861.9 7.1 copy.195
  869.0 23.9 %convert_element_type.236 = bf16[4,49,8,2304]{3,2,1,0:T(8,128)(2,1)} reshape(bf16[196,8,3,12,64]{4,3,2,1,0:T(8,128)(2,1)} %copy.195) | data formatting | bytes 14450688 | tf_op jit(solution)/shard_map/convert_element_type | solution.py:109
  892.9 7.7 copy.306
  900.6 7.6 reshape.275
  908.2 11.3 fusion.93
  921.3 13.7 convolution_bitcast_fusion
  935.7 16.3 %convolution_bitcast_fusion.1 = f32[768,3072]{1,0:T(8,128)} fusion(bf16[4,2,196,3072]{3,2,1,0:T(8,128)(2,1)} %get-tuple-element.139, f32[4,2,196,768]{3,2,1,0:T(8,128)} %copy-done.10, f32[768]{0:T(1024)S(1)} %copy-done.55, f32[768]{0:T(1024)S(1)} %copy-done.50, f32[4,2,196]{2,1,0:T(2,128)S(1)} %copy-done.45, f32[4,2,196]{2,1,0:T(2,128)S(1)} %copy-done.37), kind=kOutput, calls=%fused_computation.56 | convolution fusion | flops 7404773376 | bytes 23906560 | tf_op jit(solution)/shard_map/dot_general | solution.py:35
  954.0 9.8 fusion.57
  971.9 12.6 add_convert_fusion.4
  989.9 12.6 all-to-all-done.3
  1012.8 37.8 %all-reduce.11 = (f32[768]{0:T(1024)S(1)}, f32[3,768]{1,0:T(4,128)S(1)}, f32[768]{0:T(1024)S(1)}, f32[2,768]{1,0:T(2,128)S(1)}, f32[768]{0:T(1024)S(1)}, /*index=5*/f32[2,768]{1,0:T(2,128)S(1)}, f32[3072]{0:T(1024)S(1)}) all-reduce(f32[768]{0:T(1024)S(1)} %get-tuple-element.86, ...), channel_id=2, replica_groups=mesh['dp'=8,'seq'=4] {'dp','seq'}, use_global_device_ids=true, to_apply=%region_19.0.clone | all-reduce | flops 10752 | bytes 86016
  1052.3 5.1 add_convert_fusion.3
  1062.6 71.1 %reduce-scatter.17.cloned.1.call-done = f32[24,2304]{1,0:T(8,128)} async-done(((f32[768,2304]{1,0:T(8,128)}), f32[24,2304]{1,0:T(8,128)}) %reduce-scatter.17.cloned.1.call-update) | async-done | bytes 221200 | tf_op jit(solution)/shard_map/reduce_scatter | solution.py:247
  1133.7 124.6 %reduce-scatter.11.cloned.1.call-done = f32[24,2304]{1,0:T(8,128)} async-done(((f32[768,2304]{1,0:T(8,128)}), f32[24,2304]{1,0:T(8,128)}) %reduce-scatter.11.cloned.1.call-update) | async-done | bytes 221200 | tf_op jit(solution)/shard_map/reduce_scatter | solution.py:288
  1258.3 142.3 %reduce-scatter.23.cloned.1.call-done = f32[96,768]{1,0:T(8,128)} async-done(((f32[3072,768]{1,0:T(8,128)}), f32[96,768]{1,0:T(8,128)}) %reduce-scatter.23.cloned.1.call-update) | async-done | bytes 294928 | tf_op jit(solution)/shard_map/reduce_scatter | solution.py:215
  1400.6 141.0 %reduce-scatter.21.cloned.1.call-done = f32[24,3072]{1,0:T(8,128)} async-done(((f32[768,3072]{1,0:T(8,128)}), f32[24,3072]{1,0:T(8,128)}) %reduce-scatter.21.cloned.1.call-update) | async-done | bytes 294928 | tf_op jit(solution)/shard_map/reduce_scatter | solution.py:213
  (274 shorter events, 153.7 us)
Async XLA Ops:
  7.2 95.4 %copy-start.1 = (bf16[4,2,196,768]{3,1,2,0:T(2,128)(2,1)S(1)}, bf16[4,2,196,768]{3,1,2,0:T(2,128)(2,1)}, u32[]{:S(2)}) copy-start(bf16[4,2,196,768]{3,1,2,0:T(2,128)(2,1)} %param.16) | copy-start | bytes 7225348
  7.2 140.3 %all-gather.11.cloned.1.call-start = ((), (), s32[]{:S(2)}) async-start(), calls=%async_computation.11 | async-start | bytes 3649536 | tf_op jit(solution)/shard_map/all_gather | solution.py:133
  7.9 248.3 %all-gather.13.cloned.1.call-start = ((), (), s32[]{:S(2)}) async-start(), calls=%async_computation.12 | async-start | bytes 1216512 | tf_op jit(solution)/shard_map/all_gather | solution.py:134
  8.7 253.4 %all-gather.15.cloned.1.call-start = ((), (), s32[]{:S(2)}) async-start(), calls=%async_computation.13 | async-start | bytes 1216512 | tf_op jit(solution)/shard_map/all_gather | solution.py:135
  9.4 372.6 %all-gather.17.cloned.1.call-start = ((), (), s32[]{:S(2)}) async-start(), calls=%async_computation.14 | async-start | bytes 3649536 | tf_op jit(solution)/shard_map/all_gather | solution.py:155
  10.0 431.5 %all-gather.19.cloned.1.call-start = ((), (), s32[]{:S(2)}) async-start(), calls=%async_computation.15 | async-start | bytes 1216512 | tf_op jit(solution)/shard_map/all_gather | solution.py:156
  56.3 47.4 %copy-start.34 = (f32[768]{0:T(1024)}, f32[768]{0:T(1024)S(1)}, u32[]{:S(2)}) copy-start(f32[768]{0:T(1024)S(1)} %convert_element_type.195) | copy-start | bytes 9220
  102.0 4.3 copy-start.38
  106.3 35.7 %all-to-all-start = ((bf16[4,2,196,768]{3,0,1,2:T(4,128)(2,1)}), bf16[4,2,196,768]{3,0,1,2:T(4,128)(2,1)}, u32[]{:S(2)}, u32[]{:S(2)}) async-start(bf16[4,2,196,768]{3,0,1,2:T(4,128)(2,1)} %copy.157), calls=%async_computation | async-start | bytes 4816896 | tf_op jit(solution)/shard_map/all_to_all | solution.py:143
  110.8 340.0 %all-gather.21.cloned.1.call-start = ((), (), s32[]{:S(2)}) async-start(), calls=%async_computation.16 | async-start | bytes 4866048 | tf_op jit(solution)/shard_map/all_gather | solution.py:174
  266.5 8.7 copy-start.59
  266.6 68.5 %copy-start.60 = (bf16[2,24]{1,0:T(2,128)(2,1)S(1)}, bf16[2,24]{1,0:T(2,128)(2,1)}, u32[]{:S(2)}) copy-start(bf16[2,24]{1,0:T(2,128)(2,1)} %param.27) | copy-start | bytes 292
  269.9 104.1 %all-to-all-start.1 = ((bf16[4,8,49,768]{3,0,2,1:T(4,128)(2,1)}), bf16[4,8,49,768]{3,0,2,1:T(4,128)(2,1)}, u32[]{:S(2)}, u32[]{:S(2)}) async-start(bf16[4,8,49,768]{3,0,2,1:T(4,128)(2,1)} %copy.167), calls=%async_computation.1 | async-start | bytes 4816896 | tf_op jit(solution)/shard_map/all_to_all | solution.py:149
  274.4 245.2 %all-gather.23.cloned.1.call-start = ((), (), s32[]{:S(2)}) async-start(), calls=%async_computation.17 | async-start | bytes 4866048 | tf_op jit(solution)/shard_map/all_gather | solution.py:176
  275.2 105.3 %copy-start.42 = (f32[768]{0:T(1024)}, f32[768]{0:T(1024)S(1)}, u32[]{:S(2)}) copy-start(f32[768]{0:T(1024)S(1)} %convert_element_type.210) | copy-start | bytes 9220
  275.2 284.1 %copy-start.49 = (f32[768]{0:T(1024)}, f32[768]{0:T(1024)S(1)}, u32[]{:S(2)}) copy-start(f32[768]{0:T(1024)S(1)} %convert_element_type.218) | copy-start | bytes 9220
  374.0 76.9 %copy-start.54 = (f32[768]{0:T(1024)}, f32[768]{0:T(1024)S(1)}, u32[]{:S(2)}) copy-start(f32[768]{0:T(1024)S(1)} %get-tuple-element.94) | copy-start | bytes 9220
  382.0 10.8 copy-start.18
  441.4 6.5 copy-start.13
  447.9 111.4 %copy-start.36 = (f32[4,2,196]{2,1,0:T(2,128)}, f32[4,2,196]{2,1,0:T(2,128)S(1)}, u32[]{:S(2)}) copy-start(f32[4,2,196]{2,1,0:T(2,128)S(1)} %broadcast_multiply_fusion) | copy-start | bytes 18820
  450.8 108.5 %copy-start.44 = (f32[4,2,196]{2,1,0:T(2,128)}, f32[4,2,196]{2,1,0:T(2,128)S(1)}, u32[]{:S(2)}) copy-start(f32[4,2,196]{2,1,0:T(2,128)S(1)} %fusion.79) | copy-start | bytes 18820
  472.0 73.6 %slice-start.2 = ((s8[4915200]{0:T(1024)(128)(4,1)}), s8[720896]{0:T(1024)(128)(4,1)S(1)}, s32[]{:S(2)}) async-start(s8[4915200]{0:T(1024)(128)(4,1)} %bitcast.265), calls=%async_computation.27 | async-start | bytes 1441792
  519.6 26.0 %slice-start.3 = ((s8[4915200]{0:T(1024)(128)(4,1)}), s8[4194304]{0:T(1024)(128)(4,1)S(1)}, s32[]{:S(2)}) async-start(s8[4915200]{0:T(1024)(128)(4,1)} %bitcast.265), calls=%async_computation.28 | async-start | bytes 8388608
  559.3 4.1 copy-start.20
  561.2 5.0 copy-start.62
  627.9 8.6 copy-start.12
  644.1 9.4 copy-start.29
  644.1 9.4 copy-start.43
  644.1 23.1 %slice-start = ((s8[4915200]{0:T(1024)(128)(4,1)}), s8[720896]{0:T(1024)(128)(4,1)S(1)}, s32[]{:S(2)}) async-start(s8[4915200]{0:T(1024)(128)(4,1)} %bitcast.250), calls=%async_computation.25 | async-start | bytes 1441792
  653.5 13.8 copy-start.41
  653.5 13.8 slice-start.1
  653.5 13.8 copy-start.33
  667.3 3.0 copy-start.21
  677.2 7.3 copy-start.14
  679.9 33.6 %all-to-all-start.2 = ((bf16[4,2,196,768]{3,0,1,2:T(4,128)(2,1)}), bf16[4,2,196,768]{3,0,1,2:T(4,128)(2,1)}, u32[]{:S(2)}, u32[]{:S(2)}) async-start(bf16[4,2,196,768]{3,0,1,2:T(4,128)(2,1)} %copy.188), calls=%async_computation.2 | async-start | bytes 4816896 | tf_op jit(solution)/shard_map/all_to_all | solution.py:257
  684.4 378.2 %reduce-scatter.19.cloned.1.call-start = ((), (), s32[]{:S(2)}) async-start(), calls=%async_computation.22 | async-start | bytes 2433024 | tf_op jit(solution)/shard_map/reduce_scatter | solution.py:248
  688.2 6.6 copy-start.17
  703.1 359.5 %reduce-scatter.13.cloned.1.call-start = ((), (), s32[]{:S(2)}) async-start(), calls=%async_computation.19 | async-start | bytes 2433024 | tf_op jit(solution)/shard_map/reduce_scatter | solution.py:289
  717.1 5.2 copy-start.8
  717.5 6.3 copy-start.25
  727.5 335.1 %reduce-scatter.15.cloned.1.call-start = ((), (), s32[]{:S(2)}) async-start(), calls=%async_computation.20 | async-start | bytes 2433024 | tf_op jit(solution)/shard_map/reduce_scatter | solution.py:290
  734.1 6.5 copy-start.19
  740.5 393.2 %reduce-scatter.17.cloned.1.call-start = ((), (), s32[]{:S(2)}) async-start(), calls=%async_computation.21 | async-start | bytes 7299072 | tf_op jit(solution)/shard_map/reduce_scatter | solution.py:247
  761.6 16.8 %copy-start.24 = (bf16[1568,768]{1,0:T(8,128)(2,1)S(1)}, bf16[1568,768]{1,0:T(8,128)(2,1)}, u32[]{:S(2)}) copy-start(bf16[1568,768]{1,0:T(8,128)(2,1)} %reshape.278) | copy-start | bytes 7225348
  790.0 468.3 %reduce-scatter.11.cloned.1.call-start = ((), (), s32[]{:S(2)}) async-start(), calls=%async_computation.18 | async-start | bytes 7299072 | tf_op jit(solution)/shard_map/reduce_scatter | solution.py:288
  800.3 8.4 copy-start.6
  840.2 7.4 copy-start.7
  847.5 7.9 copy-start.11
  900.6 7.7 copy-start.23
  919.6 481.0 %reduce-scatter.23.cloned.1.call-start = ((), (), s32[]{:S(2)}) async-start(), calls=%async_computation.24 | async-start | bytes 9732096 | tf_op jit(solution)/shard_map/reduce_scatter | solution.py:215
  935.0 606.6 %reduce-scatter.21.cloned.1.call-start = ((), (), s32[]{:S(2)}) async-start(), calls=%async_computation.23 | async-start | bytes 9732096 | tf_op jit(solution)/shard_map/reduce_scatter | solution.py:213
  963.8 8.0 copy-start.52
  967.1 35.4 %all-to-all-start.3 = ((bf16[4,8,49,768]{3,0,2,1:T(4,128)(2,1)}), bf16[4,8,49,768]{3,0,2,1:T(4,128)(2,1)}, u32[]{:S(2)}, u32[]{:S(2)}) async-start(bf16[4,8,49,768]{3,0,2,1:T(4,128)(2,1)} %copy.197), calls=%async_computation.3 | async-start | bytes 4816896 | tf_op jit(solution)/shard_map/all_to_all | solution.py:273
  971.8 15.9 %copy-start.56 = (f32[768]{0:T(1024)S(1)}, f32[768]{0:T(1024)}, u32[]{:S(2)}) copy-start(f32[768]{0:T(1024)} %get-tuple-element.88) | copy-start | bytes 9220
  971.9 15.9 %copy-start.46 = (f32[768]{0:T(1024)S(1)}, f32[768]{0:T(1024)}, u32[]{:S(2)}) copy-start(f32[768]{0:T(1024)} %get-tuple-element.109) | copy-start | bytes 9220
  971.9 15.9 %copy-start.57 = (f32[768]{0:T(1024)S(1)}, f32[768]{0:T(1024)}, u32[]{:S(2)}) copy-start(f32[768]{0:T(1024)} %get-tuple-element.89) | copy-start | bytes 9220
  971.9 15.9 %copy-start.48 = (f32[768]{0:T(1024)S(1)}, f32[768]{0:T(1024)}, u32[]{:S(2)}) copy-start(f32[768]{0:T(1024)} %get-tuple-element.122) | copy-start | bytes 9220
  984.4 3.4 copy-start.9
  984.5 5.4 copy-start.58
  989.8 19.0 %copy-start.2 = (bf16[4,2,196,768]{3,1,2,0:T(2,128)(2,1)S(1)}, bf16[4,2,196,768]{3,1,2,0:T(2,128)(2,1)}, u32[]{:S(2)}) copy-start(bf16[4,2,196,768]{3,1,2,0:T(2,128)(2,1)} %param.16) | copy-start | bytes 7225348
  989.8 19.0 %copy-start.27 = (f32[4,2,196]{2,1,0:T(2,128)S(1)}, f32[4,2,196]{2,1,0:T(2,128)}, u32[]{:S(2)}) copy-start(f32[4,2,196]{2,1,0:T(2,128)} %copy-done.26) | copy-start | bytes 18820
  989.8 19.0 %copy-start.35 = (f32[768]{0:T(1024)S(1)}, f32[768]{0:T(1024)}, u32[]{:S(2)}) copy-start(f32[768]{0:T(1024)} %copy-done.34) | copy-start | bytes 9220
  1008.8 4.0 copy-start.3
  1010.0 2.7 copy-start.47
  (22 other events, 34.5 us)
Sparse Core Ops, SparseCore 0:
  10.9 63.1 all-gather.10
  77.0 54.1 all-gather.12
  134.1 53.0 all-gather.14
  189.9 58.9 all-gather.16
  251.7 54.9 all-gather.18
  309.4 62.6 all-gather.20
  375.0 62.5 all-gather.22
  703.3 96.7 reduce-scatter.18
  806.8 98.0 reduce-scatter.12
  910.5 97.9 reduce-scatter.14
  1015.8 117.8 reduce-scatter.16
  1139.8 118.4 reduce-scatter.10
  1265.8 134.7 reduce-scatter.22
  1406.9 134.6 reduce-scatter.20
where the time goes:
time: 1560 us; the launch traced here: 1550 us
  waiting for transfers between devices  537 us (34%)
  matrix products  345 us (22%)
  local copies, waits for them, and re-layouts  264 us (17%)
  blocking collectives  218 us (14%)
  other arithmetic  149 us (10%)
  starting transfers between devices  19.1 us (1%)
    reduce_scatter x1, waiting for transfers between devices, on_device(): lax.psum_scatter(grad_narrow, ('dp', 'seq'), scatter_dimension=0, tiled=T...  142 us
    reduce_scatter x1, waiting for transfers between devices, on_device(): lax.psum_scatter(grad_widen, ('dp', 'seq'), scatter_dimension=0, tiled=True)  141 us
    reduce_scatter x1, waiting for transfers between devices, on_device(): lax.psum_scatter(grad_inproj, ('dp', 'seq'), scatter_dimension=0, tiled=T...  125 us
    unnamed x2, blocking collectives  80.1 us
    convert_element_type x5, local copies, waits for them, and re-layouts, attend_backward(): return stacked.reshape(joined.shape).astype(jnp.bfloat16)  76.2 us
    dot_general x7, matrix products, times_transpose(): lax.dot_general(flattened, right_side, (((1,), (1,)), ((), ())), preferre...  76.1 us
    dot_general x7, matrix products, matmul(): result = jnp.dot(flattened, right_side, preferred_element_type=jnp.float32)  72.4 us
    reduce_scatter x1, waiting for transfers between devices, on_device(): lax.psum_scatter(grad_spatial_in, ('dp', 'seq'), scatter_dimension=0, til...  71.1 us
  transfers between devices with their start and end apart: 18, of which 7 were waited for; matrix products, arithmetic and copies ran while one was open for 38% of the time, Pallas kernels for 0%

commit v1 on v0

v1 whole, which is shorter than its diff:
```python
import functools

import jax
import jax.numpy as jnp
from jax import lax
from jax.sharding import PartitionSpec as P

HEADS = 12
HEAD_DIM = 64


def norm_rows(values, gain_row, bias_row):
    center = values - jnp.mean(values, axis=-1, keepdims=True)
    spread = jnp.mean(center * center, axis=-1, keepdims=True)
    return center * lax.rsqrt(spread + 1e-05) * gain_row + bias_row


def gelu_exact(values):
    return jax.nn.gelu(values, approximate=False)


def matmul(left_side, right_side):
    flattened = left_side.reshape(-1, left_side.shape[-1])
    result = jnp.dot(flattened, right_side, preferred_element_type=jnp.float32)
    return result.reshape(left_side.shape[:-1] + (right_side.shape[1],))


def times_transpose(left_side, right_side):
    flattened = left_side.reshape(-1, left_side.shape[-1])
    result = lax.dot_general(
        flattened, right_side, (((1,), (1,)), ((), ())), preferred_element_type=jnp.float32
    )
    return result.reshape(left_side.shape[:-1] + (right_side.shape[0],))


def outer_sum(left_side, right_side):
    return lax.dot_general(
        left_side.reshape(-1, left_side.shape[-1]),
        right_side.reshape(-1, right_side.shape[-1]),
        (((0,), (0,)), ((), ())),
        preferred_element_type=jnp.float32,
    )


def token_sum(values):
    return jnp.sum(values.astype(jnp.float32).reshape(-1, values.shape[-1]), axis=0)


def to_sequences(grid_array):
    clip_count, frame_count, place_count, width = grid_array.shape
    return jnp.transpose(grid_array, (0, 2, 1, 3)).reshape(
        clip_count * place_count, frame_count, width
    )


def to_grid(seq_array, clip_count):
    seq_count, frame_count, width = seq_array.shape
    return jnp.transpose(
        seq_array.reshape(clip_count, seq_count // clip_count, frame_count, width), (0, 2, 1, 3)
    )


def split_heads(joined):
    parted = joined.reshape(joined.shape[0], joined.shape[1], 3, HEADS, HEAD_DIM)
    return (parted[:, :, 0], parted[:, :, 1], parted[:, :, 2])


def score_rows(query_heads, key_heads):
    raw_scores = jnp.einsum(
        "blhd,bmhd->bhlm", query_heads, key_heads, preferred_element_type=jnp.float32
    )
    return raw_scores * HEAD_DIM ** (-0.5)


def attend_forward(joined):
    query_heads, key_heads, value_heads = split_heads(joined)
    scores = score_rows(query_heads, key_heads)
    row_max = jnp.max(scores, axis=-1, keepdims=True)
    log_total = jnp.log(jnp.sum(jnp.exp(scores - row_max), axis=-1, keepdims=True)) + row_max
    shares = jnp.exp(scores - log_total).astype(jnp.bfloat16)
    mixture = jnp.einsum("bhlm,bmhd->blhd", shares, value_heads, preferred_element_type=jnp.float32)
    return (
        mixture.reshape(joined.shape[0], joined.shape[1], HEADS * HEAD_DIM).astype(jnp.bfloat16),
        log_total,
    )


def attend_backward(joined, log_total, grad_mixture):
    query_heads, key_heads, value_heads = split_heads(joined)
    exact_shares = jnp.exp(score_rows(query_heads, key_heads) - log_total)
    shares = exact_shares.astype(jnp.bfloat16)
    grad_heads = grad_mixture.reshape(query_heads.shape)
    grad_values = jnp.einsum(
        "bhlm,blhd->bmhd", shares, grad_heads, preferred_element_type=jnp.float32
    )
    grad_shares = jnp.einsum(
        "blhd,bmhd->bhlm", grad_heads, value_heads, preferred_element_type=jnp.float32
    )
    row_terms = jnp.sum(grad_shares * exact_shares, axis=-1, keepdims=True)
    grad_scores = (exact_shares * (grad_shares - row_terms)).astype(jnp.bfloat16)
    scaling = HEAD_DIM ** (-0.5)
    grad_queries = (
        jnp.einsum("bhlm,bmhd->blhd", grad_scores, key_heads, preferred_element_type=jnp.float32)
        * scaling
    )
    grad_keys = (
        jnp.einsum("bhlm,blhd->bmhd", grad_scores, query_heads, preferred_element_type=jnp.float32)
        * scaling
    )
    stacked = jnp.stack([grad_queries, grad_keys, grad_values], axis=2)
    return stacked.reshape(joined.shape).astype(jnp.bfloat16)


def _vec_rows(vecs):
    return jnp.concatenate([v.reshape(-1, v.shape[-1]) for v in vecs], axis=0)


def on_device(n, tokens, tg, tb, t_in, t_out, t_lin, sg, sb, s_in, s_out, fg, fb, w1, b1, w2, cotangent):
    axes = ("dp", "seq")
    rows, width = t_in.shape[0], t_in.shape[0] * n
    parts = w2.shape[0] // rows
    hidden_units = w1.shape[1]

    def permute_cols(w):
        lead = w.shape[0]
        return w.reshape(lead, n, parts, rows).transpose(0, 2, 1, 3).reshape(lead, hidden_units)

    def unpermute_cols(w):
        lead = w.shape[0]
        return w.reshape(lead, parts, n, rows).transpose(0, 2, 1, 3).reshape(lead, hidden_units)

    w2_packed = w2.reshape(parts, rows, width).transpose(1, 0, 2).reshape(rows, parts * width)
    vecs = _vec_rows([tg[None], tb, sg[None], sb, fg[None], fb, b1.reshape(parts, rows)])
    n_vec = vecs.shape[0]
    vec_cols = jnp.pad(vecs.T, ((0, 0), (0, 128 - n_vec)))
    pack = jnp.concatenate([t_in, t_out, t_lin, s_in, s_out, permute_cols(w1), w2_packed, vec_cols], axis=1)
    full = lax.all_gather(pack, axes, axis=0, tiled=True)
    x = lax.all_to_all(tokens, "seq", split_axis=0, concat_axis=0, tiled=True)
    cot = lax.all_to_all(cotangent, "seq", split_axis=0, concat_axis=0, tiled=True)
    frames, places = x.shape[0] * x.shape[1], x.shape[2]
    x = x.reshape(1, frames, places, width)
    cot = cot.reshape(1, frames, places, width)
    c = [0]

    def take(k):
        c[0] += k
        return full[:, c[0] - k : c[0]]

    T_in, T_out, T_lin, S_in, S_out, W1 = take(3 * width), take(width), take(width), take(3 * width), take(width), take(hidden_units)
    W2 = jnp.concatenate([take(width) for _ in range(parts)], axis=0)
    V = take(128).astype(jnp.float32).T
    Tg, Tb, Sg, Sb, Fg, Fb = V[0], V[1:4], V[4], V[5:7], V[7], V[8:10]
    B1 = V[10 : 10 + parts].reshape(-1)
    bf = jnp.bfloat16

    inputs = x.astype(jnp.float32)
    norm_t = norm_rows(inputs, Tg, Tb[0]).astype(bf)
    joined_t = to_sequences(matmul(norm_t, T_in).astype(bf))
    mixed_t, lse_t = attend_forward(joined_t)
    mixed_g = to_grid(mixed_t, 1)
    proj_t = (matmul(mixed_g, T_out) + Tb[1]).astype(bf)
    branch_t = (matmul(proj_t, T_lin) + Tb[2]).astype(bf)
    after_time = inputs + branch_t.astype(jnp.float32)
    norm_s = norm_rows(after_time, Sg, Sb[0]).astype(bf)
    joined_s = matmul(norm_s, S_in).astype(bf).reshape(frames, places, -1)
    mixed_s, lse_s = attend_forward(joined_s)
    mixed_sg = mixed_s.reshape(after_time.shape)
    after_space = after_time + matmul(mixed_sg, S_out) + Sb[1]
    norm_m = norm_rows(after_space, Fg, Fb[0]).astype(bf)
    hidden = matmul(norm_m, W1) + B1
    active = gelu_exact(hidden).astype(bf)
    output = (after_space + matmul(active, W2) + Fb[1]).astype(bf)
    output = lax.all_to_all(output.reshape(tokens.shape), "seq", split_axis=0, concat_axis=0, tiled=True)

    def scatter(*grads):
        packed = jnp.concatenate([g.astype(bf) for g in grads], axis=1)
        return lax.psum_scatter(packed, axes, scatter_dimension=0, tiled=True).astype(jnp.float32)

    g_w2 = outer_sum(active, cot)
    g_fb1 = token_sum(cot)
    unused, gelu_pull = jax.vjp(gelu_exact, hidden)
    d_hidden = gelu_pull(times_transpose(cot, W2))[0].astype(bf)
    g_w1 = outer_sum(norm_m, d_hidden)
    g_b1 = token_sum(d_hidden)
    unused, pull = jax.vjp(norm_rows, after_space, Fg, Fb[0])
    d_norm, g_fg, g_fb0 = pull(times_transpose(d_hidden, W1))
    d_as = cot.astype(jnp.float32) + d_norm
    f_scat = scatter(g_w1, *[g_w2[j * width : (j + 1) * width] for j in range(parts)])

    d_space = d_as.astype(bf)
    g_sout = outer_sum(mixed_sg, d_space)
    g_sb1 = token_sum(d_space)
    d_mixed = times_transpose(d_space, S_out).astype(bf).reshape(mixed_s.shape)
    d_js = attend_backward(joined_s, lse_s, d_mixed)
    g_sin = outer_sum(norm_s, d_js)
    unused, pull = jax.vjp(norm_rows, after_time, Sg, Sb[0])
    d_norm, g_sg, g_sb0 = pull(times_transpose(d_js, S_in).reshape(after_time.shape))
    d_at = d_as + d_norm

    d_time = d_at.astype(bf)
    g_tlin = outer_sum(proj_t, d_time)
    g_tb2 = token_sum(d_time)
    d_proj = times_transpose(d_time, T_lin).astype(bf)
    g_tout = outer_sum(mixed_g, d_proj)
    g_tb1 = token_sum(d_proj)
    d_mt = to_sequences(times_transpose(d_proj, T_out).astype(bf))
    d_jt = to_grid(attend_backward(joined_t, lse_t, d_mt), 1)
    g_tin = outer_sum(norm_t, d_jt)
    d_nt = times_transpose(d_jt, T_in).astype(bf).astype(jnp.float32)
    unused, pull = jax.vjp(norm_rows, inputs, Tg, Tb[0])
    d_in, g_tg, g_tb0 = pull(d_nt)
    g_x = (d_at + d_in).astype(bf)
    g_x = lax.all_to_all(g_x.reshape(tokens.shape), "seq", split_axis=0, concat_axis=0, tiled=True)
    g_vec = jnp.concatenate(
        [jnp.stack([g_tg, g_tb0, g_tb1, g_tb2, g_sg, g_sb0, g_sb1, g_fg, g_fb0, g_fb1]), g_b1.reshape(parts, width)], axis=0
    )
    ts_scat = scatter(g_sin, g_sout, g_tin, g_tout, g_tlin, jnp.pad(g_vec.T, ((0, 0), (0, 128 - n_vec))))
    k = [0]

    def out(m):
        k[0] += m
        return ts_scat[:, k[0] - m : k[0]]

    o_sin, o_sout, o_tin, o_tout, o_tlin = out(3 * width), out(width), out(3 * width), out(width), out(width)
    v = out(128).T
    o_w1 = unpermute_cols(f_scat[:, :hidden_units])
    o_w2 = f_scat[:, hidden_units:].reshape(rows, parts, width).transpose(1, 0, 2).reshape(parts * rows, width)
    return (
        output, g_x, v[0], v[1:4], o_tin, o_tout, o_tlin, v[4], v[5:7], o_sin, o_sout, v[7], v[8:10],
        o_w1, v[10 : 10 + parts].reshape(-1), o_w2,
    )


def solution(mesh):
    shard = P(("dp", "seq"))
    cols = P(None, ("dp", "seq"))
    mat = P(("dp", "seq"), None)
    tok = P("dp", "seq", None, None)
    in_specs = (tok, shard, cols, mat, mat, mat, shard, cols, mat, mat, shard, cols, mat, shard, mat, tok)
    out_specs = (tok, tok, shard, cols, mat, mat, mat, shard, cols, mat, mat, shard, cols, mat, shard, mat)
    n = mesh.size
    return jax.shard_map(
        functools.partial(on_device, n), mesh=mesh, in_specs=in_specs, out_specs=out_specs, check_vma=False
    )
```

time: 1560 us -> 1090 us (0.70)
  waiting for transfers between devices: 537 us -> 134 us
  blocking collectives: 218 us -> 79.5 us
  other arithmetic: 149 us -> 218 us
  local copies, waits for them, and re-layouts: 264 us -> 298 us
  matrix products: 345 us -> 323 us
    reduce_scatter x7 -> x1, waiting for transfers between devices: 479 us -> 0.01 us  [scatter(): lax.psum_scatter(packed, axes, scatter_dimension=0, tiled=True)]
    all_gather x3 -> x0, blocking collectives: 138 us -> none  [the longest x1 59.8 us: on_device(): lax.all_gather(spatial_biases, ('dp', 'seq'), axis=1, tiled=True)]
    unnamed x2 -> x0, blocking collectives: 80.1 us -> none
    all_to_all x0 -> x2, blocking collectives: none -> 79.5 us  [the longest x1 41.7 us: on_device(): lax.all_to_all(g_x.reshape(tokens.shape), 'seq', split_axis=0, concat_axi...]
    reduce_sum x2 -> x4, other arithmetic: 3.3 us -> 62.3 us  [token_sum(): jnp.sum(values.astype(jnp.float32).reshape(-1, values.shape[-1]), axis=0)]
    reshape x0 -> x14, local copies, waits for them, and re-layouts: none -> 44.2 us  [the longest x2 25.5 us: times_transpose(): return result.reshape(left_side.shape[:-1] + (right_side.shape[0],))]
    all_gather x7 -> x1, waiting for transfers between devices: 0.11 us -> 44 us  [on_device(): full = lax.all_gather(pack, axes, axis=0, tiled=True)]
    unnamed x14 -> x4, waiting for transfers between devices: 4.15 us -> 45.1 us
  transfers between devices with their start and end apart: 18 -> 5, of which waited for: 7 -> 4; matrix products, arithmetic and copies ran while one was open for 38% -> 23% of each run, Pallas kernels for 0% -> 0%
where the time goes in v1:
time: 1090 us; the launch traced here: 1080 us
  matrix products  323 us (30%)
  local copies, waits for them, and re-layouts  298 us (27%)
  other arithmetic  218 us (20%)
  waiting for transfers between devices  134 us (12%)
  blocking collectives  79.5 us (7%)
  between operations  15.1 us (1%)
    dot_general x7, matrix products, matmul(): result = jnp.dot(flattened, right_side, preferred_element_type=jnp.float32)  69.1 us
    dot_general x7, matrix products, times_transpose(): lax.dot_general(flattened, right_side, (((1,), (1,)), ((), ())), preferre...  65.5 us
    reduce_sum x4, other arithmetic, token_sum(): jnp.sum(values.astype(jnp.float32).reshape(-1, values.shape[-1]), axis=0)  62.3 us
    dot_general x7, matrix products, outer_sum(): lax.dot_general(left_side.reshape(-1, left_side.shape[-1]), right_side.re...  60.6 us
    unnamed x178, local copies, waits for them, and re-layouts  52.8 us
    convert_element_type x3, local copies, waits for them, and re-layouts, attend_backward(): return stacked.reshape(joined.shape).astype(jnp.bfloat16)  46.6 us
    unnamed x4, waiting for transfers between devices  45.1 us
    all_gather x1, waiting for transfers between devices, on_device(): full = lax.all_gather(pack, axes, axis=0, tiled=True)  44 us
  transfers between devices with their start and end apart: 5, of which 4 were waited for; matrix products, arithmetic and copies ran while one was open for 23% of the time, Pallas kernels for 0%

profile of v1, /device:TPU:0, one launch (start us, length us, event | category | flops | bytes accessed | tf_op | source)
XLA Modules:
  0.0 1076.4 jit_solution(8545855506031124362)
XLA Ops:
  22.2 37.8 %all_to_all.20 = bf16[4,2,196,768]{3,1,2,0:T(2,128)(2,1)S(1)} all-to-all(bf16[4,2,196,768]{3,1,2,0:T(2,128)(2,1)} %param.16), channel_id=1, replica_groups=mesh['dp'=8,'seq'=4] {'seq'}, dimensions={0} | all-to-all | bytes 4816896 | tf_op jit(solution)/shard_map/all_to_all | solution.py:138
  66.8 11.6 %multiply_reduce_fusion.10 = f32[4,2,196]{1,2,0:T(8,128)S(1)} fusion(bf16[4,2,196,768]{3,1,2,0:T(2,128)(2,1)S(1)} %all_to_all.20, f32[4,2,196]{1,2,0:T(8,128)S(1)} %broadcast_multiply_fusion), kind=kLoop, calls=%fused_computation.97 | loop fusion | flops 4815328 | bytes 2420992 | tf_op jit(solution)/shard_map/reduce_sum | solution.py:14
  79.3 25.9 %all-to-all-done.2 = bf16[4,2,196,768]{3,1,2,0:T(2,128)(2,1)} async-done(((bf16[4,2,196,768]{3,1,2,0:T(2,128)(2,1)}), bf16[4,2,196,768]{3,1,2,0:T(2,128)(2,1)}, u32[]{:S(2)}, u32[]{:S(2)}) %all-to-all-start.2) | async-done | bytes 2408480 | tf_op jit(solution)/shard_map/all_to_all | solution.py:139
  125.5 44.0 %all-gather.2.cloned.1.call-done = bf16[768,13184]{1,0:T(8,128)(2,1)} async-done(((bf16[24,13184]{1,0:T(8,128)(2,1)}), bf16[768,13184]{1,0:T(8,128)(2,1)}) %all-gather.2.cloned.1.call-update) | async-done | bytes 20250640 | tf_op jit(solution)/shard_map/all_gather | solution.py:137
  173.6 10.4 convert_bitcast_fusion
  184.0 11.4 %copy.321 = bf16[1,196,8,2304]{1,3,2,0:T(8,128)(2,1)} copy(bf16[1,196,8,2304]{3,1,2,0:T(8,128)(2,1)} %convert_bitcast_fusion) | data formatting | bytes 14450688 | tf_op jit(solution)/shard_map/transpose | solution.py:51
  195.4 6.0 fusion.94
  201.4 7.6 copy.380
  209.0 7.7 copy.382
  216.7 6.2 copy.381
  222.8 11.2 %multiply_reduce_fusion.3 = (f32[196,12,8]{2,1,0:T(8,128)S(1)}, f32[196,12,8,8]{2,3,1,0:T(8,128)}) fusion(bf16[196,8,1,12,64]{4,1,3,0,2:T(8,128)(2,1)} %copy.382, bf16[196,8,1,12,64]{4,1,3,0,2:T(8,128)(2,1)} %copy.381), kind=kOutput, calls=%fused_computation.37 | convolution fusion | flops 19549824 | bytes 5494272 | tf_op jit(solution)/shard_map/blhd,bmhd->bhlm/dot_general | solution.py:69
  234.0 7.8 exponential_reduce_fusion.1
  243.2 9.0 convert_bitcast_fusion.2
  252.2 7.9 copy.326
  273.8 10.0 convolution_convert_fusion
  283.8 11.5 %copy.328 = bf16[8,196,2304]{1,2,0:T(8,128)(2,1)} copy(bf16[8,196,2304]{2,1,0:T(8,128)(2,1)} %convolution_convert_fusion) | data formatting | bytes 14450688 | tf_op jit(solution)/shard_map/convert_element_type | solution.py:165
  295.3 12.3 %multiply_reduce_fusion.1 = (f32[8,12,196]{2,1,0:T(8,128)S(1)}, f32[8,12,196,196]{2,3,1,0:T(8,128)}) fusion(bf16[8,196,3,12,64]{1,4,3,2,0:T(8,128)(2,1)} %bitcast.245), kind=kOutput, calls=%fused_computation.26 | convolution fusion | flops 479412864 | bytes 21118464 | tf_op jit(solution)/shard_map/blhd,bmhd->bhlm/dot_general | solution.py:69
  307.6 11.8 %exponential_reduce_fusion = f32[8,12,196]{2,1,0:T(8,128)S(1)} fusion(f32[8,12,196,196]{2,3,1,0:T(8,128)} %get-tuple-element.166, f32[8,12,196]{2,1,0:T(8,128)S(1)} %get-tuple-element.165), kind=kLoop, calls=%fused_computation.24 | loop fusion | flops 11044992 | bytes 14902272 | tf_op jit(solution)/shard_map/reduce_sum | solution.py:79
  319.4 11.4 %fusion.64 = bf16[8,12,64,196]{3,2,1,0:T(8,128)(2,1)S(1)} fusion(bf16[8,196,3,12,64]{1,4,3,2,0:T(8,128)(2,1)} %bitcast.246, f32[8,12,196,196]{2,3,1,0:T(8,128)} %get-tuple-element.166, f32[8,12,196]{2,1,0:T(8,128)S(1)} %log_add_fusion.1), kind=kOutput, calls=%fused_computation.128 | convolution fusion | flops 484323840 | bytes 25290240 | tf_op jit(solution)/shard_map/bhlm,bmhd->blhd/dot_general | solution.py:81
  337.0 15.8 %convolution_bitcast_fusion = f32[1568,3072]{1,0:T(8,128)} fusion(bf16[1568,768]{1,0:T(8,128)(2,1)S(1)} %copy-done.20, bf16[768,768]{1,0:T(8,128)(2,1)S(1)} %get-tuple-element.144, bf16[768,768]{1,0:T(8,128)(2,1)S(1)} %get-tuple-element.145, bf16[768,768]{1,0:T(8,128)(2,1)S(1)} %get-tuple-element.146, bf16[768,768]{1,0:T(8,128)(2,1)S(1)} %get-tuple-element.143), kind=kOutput, calls=%fused_computation.28 | convolution fusion | flops 7417626624 | bytes 26394624 | tf_op jit(solution)/shard_map/dot_general | solution.py:30
  352.8 20.2 %reshape.688 = f32[8,196,3072]{2,1,0:T(8,128)} reshape(f32[1568,3072]{1,0:T(8,128)} %convolution_bitcast_fusion) | data formatting | bytes 38535168 | tf_op jit(solution)/shard_map/reshape | solution.py:33
  374.2 5.4 fusion.100
  380.3 21.5 %fusion.24 = (u8[196,3072]{1,0:T(8,128)(4,1)S(1)}, u8[196,3072]{1,0:T(8,128)(4,1)S(1)}, f32[8,196,3072]{2,1,0:T(8,128)}) fusion(f32[3072]{0:T(1024)S(1)} %add.213, bf16[768,13184]{1,0:T(8,128)(2,1)} %all-gather.2.cloned.1.call-done, f32[8,196,768]{2,1,0:T(8,128)S(1)} %get-tuple-element.168, f32[768]{0:T(1024)S(1)} %get-tuple-element.122, ...), kind=kOutput, calls=%fused_computation.80 | convolution fusion | flops 7471005696 | bytes 30038272 | tf_op jit(solution)/shard_map/dot_general | solution.py:24
  401.9 52.5 %fusion.87 = (bf16[3072]{0:T(1024)(128)(2,1)}, bf16[8,196,3072]{2,1,0:T(8,128)(2,1)}, f32[8,196,3072]{2,1,0:T(8,128)}) fusion(f32[8,196,3072]{2,1,0:T(8,128)} %reshape.688, f32[8,196,3072]{2,1,0:T(8,128)} %get-tuple-element.169, f32[3072]{0:T(1024)S(1)} %add.213, u8[196,3072]{1,0:T(8,128)(4,1)S(1)} %get-tuple-element.113, ...), kind=kLoop, calls=%fused_computation.191 | loop fusion | flops 380531712 | bytes 68659200 | tf_op jit(solution)/shard_map/reduce_sum | solution.py:46
  454.4 8.3 reshape.689
  462.7 13.8 %fusion.103 = (bf16[768]{0:T(1024)(128)(2,1)}, f32[1568,768]{1,0:T(8,128)}) fusion(bf16[1568,3072]{1,0:T(8,128)(2,1)} %reshape.689, bf16[768,13184]{1,0:T(8,128)(2,1)} %all-gather.2.cloned.1.call-done), kind=kOutput, calls=%fused_computation.205 | convolution fusion | flops 7399955456 | bytes 19170816 | tf_op jit(solution)/shard_map/dot_general | solution.py:30
  476.5 5.2 reshape.690
  481.7 5.0 multiply_reduce_fusion.7
  505.0 11.9 %convolution_bitcast_fusion.1 = bf16[8,196,1,12,64]{1,4,3,0,2:T(8,128)(2,1)} fusion(bf16[8,196,12,64]{1,3,2,0:T(8,128)(2,1)S(1)} %bitcast.268, f32[8,12,196,196]{2,3,1,0:T(8,128)} %get-tuple-element.166, f32[8,12,196]{2,1,0:T(8,128)S(1)} %log_add_fusion.1), kind=kOutput, calls=%fused_computation.120 | convolution fusion | flops 483119616 | bytes 19643904 | tf_op jit(solution)/shard_map/bhlm,blhd->bmhd/dot_general | solution.py:93
  516.9 15.4 %multiply_reduce_fusion = (f32[8,12,196]{2,1,0:T(8,128)S(1)}, f32[8,12,196,196]{2,3,1,0:T(8,128)}) fusion(f32[8,12,196,196]{2,3,1,0:T(8,128)} %get-tuple-element.166, f32[8,12,196]{2,1,0:T(8,128)S(1)} %log_add_fusion.1, bf16[8,196,12,64]{1,3,2,0:T(8,128)(2,1)S(1)} %bitcast.269, bf16[8,196,3,12,64]{1,4,3,2,0:T(8,128)(2,1)} %bitcast.247), kind=kOutput, calls=%fused_computation.8 | convolution fusion | flops 486788736 | bytes 40117248 | tf_op jit(solution)/shard_map/blhd,bmhd->bhlm/dot_general | solution.py:96
  532.4 18.0 %multiply_convert_fusion = bf16[8,12,196,196]{2,3,1,0:T(8,128)(2,1)} fusion(f32[8,12,196,196]{2,3,1,0:T(8,128)} %get-tuple-element.171, f32[8,12,196,196]{2,3,1,0:T(8,128)} %get-tuple-element.166, f32[8,12,196]{2,1,0:T(8,128)S(1)} %get-tuple-element.170, f32[8,12,196]{2,1,0:T(8,128)S(1)} %log_add_fusion.1), kind=kLoop, calls=%fused_computation.7 | loop fusion | flops 18439680 | bytes 37029888 | tf_op jit(solution)/shard_map/convert_element_type | solution.py:100
  550.4 9.7 multiply_bitcast_fusion
  560.1 8.6 multiply_bitcast_fusion.1
  568.7 14.2 %fusion.20 = bf16[768,6144]{1,0:T(8,128)(2,1)} fusion(bf16[8,196,3072]{2,1,0:T(8,128)(2,1)} %get-tuple-element.134, f32[8,196,768]{2,1,0:T(8,128)S(1)} %bitcast.261, f32[768]{0:T(1024)S(1)} %get-tuple-element.122, f32[768]{0:T(1024)S(1)} %get-tuple-element.120, f32[8,196]{1,0:T(8,128)S(1)} %fusion.79, f32[8,196]{1,0:T(8,128)S(1)} %broadcast_multiply_fusion.1), kind=kOutput, calls=%fused_computation.59 | convolution fusion | flops 7407132672 | bytes 19187968 | tf_op jit(solution)/shard_map/dot_general | solution.py:37
  583.0 17.4 %multiply_convert_fusion.1 = bf16[8,196,3072]{2,1,0:T(8,128)(2,1)} fusion(f32[8,196,3072]{2,1,0:T(8,128)} %get-tuple-element.135, f32[8,196,3072]{2,1,0:T(8,128)} %get-tuple-element.169, f32[3072]{0:T(1024)S(1)} %add.213), kind=kLoop, calls=%fused_computation.10 | loop fusion | flops 19267584 | bytes 48181248 | tf_op jit(solution)/shard_map/convert_element_type | solution.py:171
  600.4 7.6 maximum_convert_fusion
  608.0 18.4 %copy.342 = bf16[8,196,3,12,64]{1,0,4,3,2:T(8,128)(2,1)} copy(bf16[8,196,3,12,64]{1,4,3,0,2:T(8,128)(2,1)} %maximum_convert_fusion) | data formatting | bytes 14450688 | tf_op jit(solution)/shard_map/convert_element_type | solution.py:111
  626.4 16.6 %convert_element_type.273 = bf16[1568,2304]{0,1:T(8,128)(2,1)} reshape(bf16[8,196,3,12,64]{1,0,4,3,2:T(8,128)(2,1)} %copy.342) | data formatting | bytes 14450688 | tf_op jit(solution)/shard_map/convert_element_type | solution.py:111
  643.1 13.2 %fusion.102 = (bf16[768]{0:T(1024)(128)(2,1)}, f32[1568,768]{1,0:T(8,128)}) fusion(bf16[1568,2304]{0,1:T(8,128)(2,1)} %convert_element_type.273, bf16[768,13184]{1,0:T(8,128)(2,1)} %all-gather.2.cloned.1.call-done), kind=kOutput, calls=%fused_computation.204 | convolution fusion | flops 5550267392 | bytes 16025088 | tf_op jit(solution)/shard_map/dot_general | solution.py:30
  656.2 5.3 reshape_reshape.27
  661.6 5.8 multiply_reduce_fusion.5
  686.1 7.7 copy.344
  693.8 12.6 %multiply_reduce_fusion.2 = (f32[196,12,8]{2,1,0:T(8,128)}, f32[196,12,8,8]{2,3,1,0:T(8,128)}) fusion(f32[196,12,8,8]{2,3,1,0:T(8,128)} %get-tuple-element.162, f32[196,12,8]{2,1,0:T(8,128)S(1)} %copy-done.8, bf16[196,8,12,64]{3,1,2,0:T(8,128)(2,1)} %copy.344, bf16[196,8,1,12,64]{4,1,3,0,2:T(8,128)(2,1)} %copy.380), kind=kOutput, calls=%fused_computation.33 | convolution fusion | flops 19850880 | bytes 6171648 | tf_op jit(solution)/shard_map/blhd,bmhd->bhlm/dot_general | solution.py:96
  706.4 8.3 reshape.695
  714.7 12.2 %convolution_convert_fusion.1 = bf16[3072,768]{1,0:T(8,128)(2,1)S(1)} fusion(bf16[1568,3072]{1,0:T(8,128)(2,1)} %reshape.695, bf16[1568,768]{1,0:T(8,128)(2,1)} %reshape_reshape.25), kind=kOutput, calls=%fused_computation.56 | convolution fusion | flops 7401111552 | bytes 16760832 | tf_op jit(solution)/shard_map/dot_general | solution.py:37
  731.6 11.8 %multiply_convert_fusion.4 = bf16[196,12,8,8]{2,3,1,0:T(8,128)(2,1)} fusion(f32[196,12,8,8]{2,3,1,0:T(8,128)} %get-tuple-element.173, f32[196,12,8,8]{2,3,1,0:T(8,128)} %get-tuple-element.162, f32[196,12,8]{2,1,0:T(8,128)} %get-tuple-element.172, f32[196,12,8]{2,1,0:T(8,128)S(1)} %copy-done.8), kind=kLoop, calls=%fused_computation.32 | loop fusion | flops 752640 | bytes 1655808 | tf_op jit(solution)/shard_map/convert_element_type | solution.py:100
  751.7 9.2 fusion.26
  760.9 8.6 fusion.25
  769.5 7.5 convert_bitcast_fusion.1
  777.0 13.3 %pad_maximum_fusion = bf16[196,8,3,12,64]{4,1,3,0,2:T(8,128)(2,1)} fusion(bf16[196,8,1,12,64]{4,1,3,0,2:T(8,128)(2,1)} %convert_bitcast_fusion.1, bf16[196,8,1,12,64]{4,1,3,0,2:T(8,128)(2,1)} %fusion.26, bf16[196,8,1,12,64]{4,1,3,0,2:T(8,128)(2,1)} %fusion.25), kind=kLoop, calls=%fused_computation.27 | loop fusion | flops 7225344 | bytes 14450688 | tf_op jit(solution)/shard_map/stack | solution.py:110
  790.3 20.0 %copy.347 = bf16[196,8,3,12,64]{0,4,3,2,1:T(8,128)(2,1)} copy(bf16[196,8,3,12,64]{4,1,3,0,2:T(8,128)(2,1)} %pad_maximum_fusion) | data formatting | bytes 14450688 | tf_op jit(solution)/shard_map/stack | solution.py:110
  810.3 11.5 %copy.348 = bf16[1,196,8,2304]{3,1,2,0:T(8,128)(2,1)} copy(bf16[1,196,8,2304]{1,3,2,0:T(8,128)(2,1)} %bitcast.267) | data formatting | bytes 14450688 | tf_op jit(solution)/shard_map/convert_element_type | solution.py:111
  821.9 5.7 copy.350
  827.6 6.5 convert_element_type.284
  834.2 17.8 %add_convert_fusion.8 = bf16[4,2,196,768]{3,1,2,0:T(2,128)(2,1)S(1)} fusion(bf16[4,2,196,768]{3,1,2,0:T(2,128)(2,1)S(1)} %copy-done.5, f32[768]{0:T(1024)S(1)} %copy-done.47, f32[768]{0:T(1024)S(1)} %copy-done.42, f32[4,2,196]{1,2,0:T(8,128)} %copy.352, f32[4,2,196]{1,2,0:T(8,128)S(1)} %copy-done.14), kind=kLoop, calls=%fused_computation.94 | loop fusion | flops 7225344 | bytes 4835584 | tf_op jit(solution)/shard_map/convert_element_type | solution.py:157
  853.8 9.6 fusion.21
  864.0 6.8 fusion.22
  871.3 12.3 %fusion.19 = bf16[768,7040]{1,0:T(8,128)(2,1)} fusion(bf16[1568,768]{1,0:T(8,128)(2,1)} %reshape.692, bf16[1568,2304]{0,1:T(8,128)(2,1)} %convert_element_type.273), kind=kOutput, calls=%fused_computation.58 | convolution fusion | flops 5550833664 | bytes 13172736 | tf_op jit(solution)/shard_map/dot_general | solution.py:37
  887.1 11.4 %fusion.16 = bf16[768,7040]{1,0:T(8,128)(2,1)} fusion(bf16[768,7040]{1,0:T(8,128)(2,1)} %fusion.72, bf16[8,196,768]{2,1,0:T(8,128)(2,1)S(1)} %bitcast.280, bf16[1,196,8,2304]{3,1,2,0:T(8,128)(2,1)} %copy.348), kind=kOutput, calls=%fused_computation.55 | convolution fusion | flops 5550833664 | bytes 13320192 | tf_op jit(solution)/shard_map/dot_general | solution.py:37
  907.0 12.9 %add_convert_fusion.2 = bf16[8,196,768]{2,1,0:T(8,128)(2,1)S(1)} fusion(f32[8,196,768]{2,1,0:T(8,128)} %copy-done.1, f32[768]{0:T(1024)S(1)} %copy-done.53, bf16[8,196,3072]{2,1,0:T(8,128)(2,1)} %multiply_convert_fusion.1, bf16[768,768]{1,0:T(8,128)(2,1)} %copy-done.23, bf16[768,768]{1,0:T(8,128)(2,1)} %copy-done.24, bf16[768,768]{1,0:T(8,128)(2,1)} %copy-done.25, ...), kind=kOutput, calls=%fused_computation.69 | convolution fusion | flops 7421239296 | bytes 21580800 | tf_op jit(solution)/shard_map/dot_general | solution.py:24
  927.8 7.0 add_convert_fusion.1
  938.1 18.9 %all-to-all-done.1 = bf16[4,2,196,768]{3,1,2,0:T(2,128)(2,1)} async-done(((bf16[4,2,196,768]{3,1,2,0:T(2,128)(2,1)}), bf16[4,2,196,768]{3,1,2,0:T(2,128)(2,1)}, u32[]{:S(2)}, u32[]{:S(2)}) %all-to-all-start.1) | async-done | bytes 2408480 | tf_op jit(solution)/shard_map/all_to_all | solution.py:173
  956.9 41.7 %all_to_all.21 = bf16[4,2,196,768]{3,1,2,0:T(2,128)(2,1)S(1)} all-to-all(bf16[4,2,196,768]{3,1,2,0:T(2,128)(2,1)} %copy.349), channel_id=1, replica_groups=mesh['dp'=8,'seq'=4] {'seq'}, dimensions={0} | all-to-all | bytes 4816896 | tf_op jit(solution)/shard_map/all_to_all | solution.py:213
  1010.6 45.1 %reduce-scatter.7.cloned.1.call-done = bf16[24,7040]{1,0:T(8,128)(2,1)} async-done(((bf16[768,7040]{1,0:T(8,128)(2,1)}), bf16[24,7040]{1,0:T(8,128)(2,1)}) %reduce-scatter.7.cloned.1.call-update) | async-done | bytes 337936
  (290 shorter events, 171.4 us)
Async XLA Ops:
  7.2 162.3 %all-gather.2.cloned.1.call-start = ((), (), s32[]{:S(2)}) async-start(), calls=%async_computation.6 | async-start | bytes 20883456 | tf_op jit(solution)/shard_map/all_gather | solution.py:137
  60.0 58.5 %copy-start.4 = (bf16[4,2,196,768]{3,1,2,0:T(2,128)(2,1)}, bf16[4,2,196,768]{3,1,2,0:T(2,128)(2,1)S(1)}, u32[]{:S(2)}) copy-start(bf16[4,2,196,768]{3,1,2,0:T(2,128)(2,1)S(1)} %all_to_all.20) | copy-start | bytes 7225348
  60.0 45.2 %all-to-all-start.2 = ((bf16[4,2,196,768]{3,1,2,0:T(2,128)(2,1)}), bf16[4,2,196,768]{3,1,2,0:T(2,128)(2,1)}, u32[]{:S(2)}, u32[]{:S(2)}) async-start(bf16[4,2,196,768]{3,1,2,0:T(2,128)(2,1)} %param.31), calls=%async_computation.2 | async-start | bytes 4816896 | tf_op jit(solution)/shard_map/all_to_all | solution.py:139
  64.6 934.0 %reduce-scatter.5.cloned.1.call-start = ((), (), s32[]{:S(2)}) async-start(), calls=%async_computation.7 | async-start | bytes 9732096 | tf_op jit(solution)/shard_map/reduce_scatter | solution.py:177
  66.7 46.6 %copy-start.13 = (f32[4,2,196]{1,2,0:T(8,128)}, f32[4,2,196]{1,2,0:T(8,128)S(1)}, u32[]{:S(2)}) copy-start(f32[4,2,196]{1,2,0:T(8,128)S(1)} %broadcast_multiply_fusion) | copy-start | bytes 18820
  79.3 94.3 %copy-start.31 = (f32[8,196]{1,0:T(8,128)}, f32[8,196]{1,0:T(8,128)S(1)}, u32[]{:S(2)}) copy-start(f32[8,196]{1,0:T(8,128)S(1)} %rsqrt.39) | copy-start | bytes 18820
  79.3 94.3 %copy-start.33 = (f32[8,196]{1,0:T(8,128)}, f32[8,196]{1,0:T(8,128)S(1)}, u32[]{:S(2)}) copy-start(f32[8,196]{1,0:T(8,128)S(1)} %div.66) | copy-start | bytes 18820
  169.5 4.1 copy-start
  172.7 11.4 %copy-start.41 = (f32[768]{0:T(1024)}, f32[768]{0:T(1024)S(1)}, u32[]{:S(2)}) copy-start(f32[768]{0:T(1024)S(1)} %get-tuple-element.129) | copy-start | bytes 9220
  172.7 11.4 %copy-start.46 = (f32[768]{0:T(1024)}, f32[768]{0:T(1024)S(1)}, u32[]{:S(2)}) copy-start(f32[768]{0:T(1024)S(1)} %get-tuple-element.128) | copy-start | bytes 9220
  172.7 98.3 %copy-start.43 = (f32[768]{0:T(1024)}, f32[768]{0:T(1024)S(1)}, u32[]{:S(2)}) copy-start(f32[768]{0:T(1024)S(1)} %get-tuple-element.125) | copy-start | bytes 9220
  252.2 12.5 %slice-start.3 = ((s8[4915200]{0:T(1024)(128)(4,1)}), s8[720896]{0:T(1024)(128)(4,1)S(1)}, s32[]{:S(2)}) async-start(s8[4915200]{0:T(1024)(128)(4,1)} %bitcast.252), calls=%async_computation.12 | async-start | bytes 1441792
  260.2 4.5 slice-start.4
  264.7 4.5 copy-start.57
  330.8 43.4 %copy-start.10 = (bf16[8,12,64,196]{3,2,1,0:T(8,128)(2,1)}, bf16[8,12,64,196]{3,2,1,0:T(8,128)(2,1)S(1)}, u32[]{:S(2)}) copy-start(bf16[8,12,64,196]{3,2,1,0:T(8,128)(2,1)S(1)} %fusion.64) | copy-start | bytes 7225348
  330.8 6.2 copy-start.20
  379.6 22.3 %copy-start.1 = (f32[8,196,768]{2,1,0:T(8,128)}, f32[8,196,768]{2,1,0:T(8,128)S(1)}, u32[]{:S(2)}) copy-start(f32[8,196,768]{2,1,0:T(8,128)S(1)} %get-tuple-element.168) | copy-start | bytes 14450692
  476.5 10.3 slice-start.7
  481.7 5.1 slice-start.8
  481.7 6.5 copy-start.2
  481.7 9.5 slice-start.15
  550.4 18.4 %slice-start.9 = ((s8[4915200]{0:T(1024)(128)(4,1)}), s8[720896]{0:T(1024)(128)(4,1)S(1)}, s32[]{:S(2)}) async-start(s8[4915200]{0:T(1024)(128)(4,1)} %bitcast.260), calls=%async_computation.18 | async-start | bytes 1441792
  560.1 8.6 slice-start.10
  583.0 17.4 %copy-start.9 = (bf16[8,196,1,12,64]{1,4,3,0,2:T(8,128)(2,1)S(1)}, bf16[8,196,1,12,64]{1,4,3,0,2:T(8,128)(2,1)}, u32[]{:S(2)}) copy-start(bf16[8,196,1,12,64]{1,4,3,0,2:T(8,128)(2,1)} %convolution_bitcast_fusion.1) | copy-start | bytes 7225348
  656.2 5.3 copy-start.28
  656.2 5.3 copy-start.30
  656.2 5.3 copy-start.44
  656.2 11.1 %slice-start.11 = ((s8[4915200]{0:T(1024)(128)(4,1)}), s8[720896]{0:T(1024)(128)(4,1)S(1)}, s32[]{:S(2)}) async-start(s8[4915200]{0:T(1024)(128)(4,1)} %bitcast.262), calls=%async_computation.20 | async-start | bytes 1441792
  661.5 5.8 copy-start.38
  661.5 5.8 slice-start.12
  661.5 9.7 slice-start.13
  667.4 3.9 slice-start.14
  673.5 4.9 copy-start.17
  686.1 7.7 copy-start.8
  731.5 324.1 %reduce-scatter.7.cloned.1.call-start = ((), (), s32[]{:S(2)}) async-start(), calls=%async_computation.8 | async-start | bytes 11151360
  751.7 17.8 %slice-start = ((s8[9633792]{0:T(1024)(128)(4,1)}), s8[4194304]{0:T(1024)(128)(4,1)S(1)}, s32[]{:S(2)}) async-start(s8[9633792]{0:T(1024)(128)(4,1)} %bitcast.243), calls=%async_computation.9 | async-start | bytes 8388608
  751.7 17.8 %slice-start.1 = ((s8[9633792]{0:T(1024)(128)(4,1)}), s8[1245184]{0:T(1024)(128)(4,1)S(1)}, s32[]{:S(2)}) async-start(s8[9633792]{0:T(1024)(128)(4,1)} %bitcast.243), calls=%async_computation.10 | async-start | bytes 2490368
  760.9 8.6 slice-start.2
  821.9 12.3 %copy-start.5 = (bf16[4,2,196,768]{3,1,2,0:T(2,128)(2,1)S(1)}, bf16[4,2,196,768]{3,1,2,0:T(2,128)(2,1)}, u32[]{:S(2)}) copy-start(bf16[4,2,196,768]{3,1,2,0:T(2,128)(2,1)} %copy-done.4) | copy-start | bytes 7225348
  821.9 12.3 %copy-start.14 = (f32[4,2,196]{1,2,0:T(8,128)S(1)}, f32[4,2,196]{1,2,0:T(8,128)}, u32[]{:S(2)}) copy-start(f32[4,2,196]{1,2,0:T(8,128)} %copy-done.13) | copy-start | bytes 18820
  821.9 12.3 %copy-start.42 = (f32[768]{0:T(1024)S(1)}, f32[768]{0:T(1024)}, u32[]{:S(2)}) copy-start(f32[768]{0:T(1024)} %copy-done.41) | copy-start | bytes 9220
  821.9 12.3 %copy-start.47 = (f32[768]{0:T(1024)S(1)}, f32[768]{0:T(1024)}, u32[]{:S(2)}) copy-start(f32[768]{0:T(1024)} %copy-done.46) | copy-start | bytes 9220
  827.6 26.2 %slice-start.5 = ((s8[4915200]{0:T(1024)(128)(4,1)}), s8[720896]{0:T(1024)(128)(4,1)S(1)}, s32[]{:S(2)}) async-start(s8[4915200]{0:T(1024)(128)(4,1)} %bitcast.255), calls=%async_computation.14 | async-start | bytes 1441792
  834.2 19.6 %slice-start.6 = ((s8[4915200]{0:T(1024)(128)(4,1)}), s8[4194304]{0:T(1024)(128)(4,1)S(1)}, s32[]{:S(2)}) async-start(s8[4915200]{0:T(1024)(128)(4,1)} %bitcast.255), calls=%async_computation.15 | async-start | bytes 8388608
  834.2 19.6 %copy-start.34 = (f32[8,196]{1,0:T(8,128)S(1)}, f32[8,196]{1,0:T(8,128)}, u32[]{:S(2)}) copy-start(f32[8,196]{1,0:T(8,128)} %copy-done.33) | copy-start | bytes 18820
  853.8 10.1 copy-start.40
  853.8 10.1 copy-start.32
  863.9 6.9 copy-start.56
  863.9 6.9 copy-start.52
  863.9 6.9 copy-start.51
  863.9 7.0 copy-start.55
  863.9 7.0 copy-start.50
  863.9 7.0 copy-start.49
  864.0 7.0 copy-start.54
  864.0 7.0 copy-start.45
  864.0 7.0 copy-start.48
  871.3 12.4 %copy-start.16 = (bf16[1568,768]{0,1:T(8,128)(2,1)S(1)}, bf16[1568,768]{0,1:T(8,128)(2,1)}, u32[]{:S(2)}) copy-start(bf16[1568,768]{0,1:T(8,128)(2,1)} %convert_element_type.284) | copy-start | bytes 7225348
  871.3 12.4 %copy-start.21 = (bf16[1568,768]{1,0:T(8,128)(2,1)S(1)}, bf16[1568,768]{1,0:T(8,128)(2,1)}, u32[]{:S(2)}) copy-start(bf16[1568,768]{1,0:T(8,128)(2,1)} %reshape.693) | copy-start | bytes 7225348
  887.0 11.4 %copy-start.15 = (bf16[196,8,12,64]{0,3,2,1:T(8,128)(2,1)S(1)}, bf16[196,8,12,64]{0,3,2,1:T(8,128)(2,1)}, u32[]{:S(2)}) copy-start(bf16[196,8,12,64]{0,3,2,1:T(8,128)(2,1)} %copy.326) | copy-start | bytes 7225348
  887.1 11.4 %copy-start.60 = (bf16[8,196,768]{2,1,0:T(8,128)(2,1)S(1)}, bf16[8,196,768]{2,1,0:T(8,128)(2,1)}, u32[]{:S(2)}) copy-start(bf16[8,196,768]{2,1,0:T(8,128)(2,1)} %copy-done.59) | copy-start | bytes 7225348
  898.5 3.5 copy-start.18
  898.5 3.5 copy-start.58
  919.9 7.9 copy-start.36
  923.2 33.8 %all-to-all-start.1 = ((bf16[4,2,196,768]{3,1,2,0:T(2,128)(2,1)}), bf16[4,2,196,768]{3,1,2,0:T(2,128)(2,1)}, u32[]{:S(2)}, u32[]{:S(2)}) async-start(bf16[4,2,196,768]{3,1,2,0:T(2,128)(2,1)} %copy.335), calls=%async_computation.1 | async-start | bytes 4816896 | tf_op jit(solution)/shard_map/all_to_all | solution.py:173
  (19 other events, 31.9 us)
Sparse Core Ops, SparseCore 0:
  22.4 147.1 all-gather.1
  731.7 133.6 reduce-scatter.4
  906.5 149.1 reduce-scatter.6

commit v2 on v1

v2 whole, which is shorter than its diff:
```python
import functools

import jax
import jax.numpy as jnp
from jax import lax
from jax.experimental import pallas as pl
from jax.experimental.pallas import tpu as pltpu
from jax.sharding import PartitionSpec as P

HEADS = 12
HEAD_DIM = 64
PAIR = 2 * HEAD_DIM
PAIRS = HEADS // 2
TILE = 16
GROUP_T = 6
GROUP_S = 2
GROUP_SB = 1
GROUP_TB = 3
LOW = -1e30
BF = jnp.bfloat16
F32 = jnp.float32


def dot_nn(a, b):
    return lax.dot_general(a, b, (((1,), (0,)), ((), ())), preferred_element_type=F32)


def dot_nt(a, b):
    return lax.dot_general(a, b, (((1,), (1,)), ((), ())), preferred_element_type=F32)


def dot_tn(a, b):
    return lax.dot_general(a, b, (((0,), (0,)), ((), ())), preferred_element_type=F32)


def normalize(values):
    center = values - jnp.mean(values, axis=-1, keepdims=True)
    scale = lax.rsqrt(jnp.mean(center * center, axis=-1, keepdims=True) + 1e-05)
    return center * scale, scale


def norm_back(unit, scale, gain, grad):
    graded = grad * gain
    shift = jnp.mean(graded, axis=-1, keepdims=True)
    slope = jnp.mean(graded * unit, axis=-1, keepdims=True)
    return scale * (graded - shift - unit * slope)


def rows_of(block):
    return block.reshape(block.shape[0] * block.shape[1], block.shape[2])


def col_sum(values):
    return jnp.sum(values, axis=0, keepdims=True)


def lane_halves(shape):
    return lax.broadcasted_iota(jnp.int32, shape, len(shape) - 1) < HEAD_DIM


def half_masks():
    low_half = lane_halves((1, PAIR))
    return (
        jnp.where(low_half, 1.0, 0.0).astype(BF),
        jnp.where(low_half, 0.0, 1.0).astype(BF),
    )


def heads_forward(tiles, bias):
    low_mask, high_mask = half_masks()
    scale = HEAD_DIM ** (-0.5)
    scores = []
    for query, key, value in tiles:
        for mask in (low_mask, high_mask):
            scores.append(dot_nt(query * (mask * scale), key) + bias)
    tops = [jnp.max(s, axis=-1, keepdims=True) for s in scores]
    shares = [jnp.exp(s - top).astype(BF) for s, top in zip(scores, tops)]
    outs = []
    for at, share in enumerate(shares):
        value = tiles[at // 2][2]
        outs.append(dot_nn(share, jnp.concatenate([value, jnp.ones_like(value)], axis=1)))
    mixed = []
    for at in range(len(tiles)):
        first, second = outs[2 * at], outs[2 * at + 1]
        low_half = lane_halves((first.shape[0], PAIR))
        top = jnp.where(low_half, first[:, :PAIR], second[:, :PAIR])
        total = jnp.where(low_half, first[:, PAIR:], second[:, PAIR:])
        mixed.append((top / total).astype(BF))
    return mixed


def heads_backward(tiles, bias):
    low_mask, high_mask = half_masks()
    scale = HEAD_DIM ** (-0.5)
    turned = [key.T for query, key, value, grad in tiles]
    queries, grads, scores, grad_shares = [], [], [], []
    for query, key, value, grad in tiles:
        for mask in (low_mask, high_mask):
            queries.append(query * (mask * scale))
            grads.append(grad * mask)
            scores.append(dot_nt(key, queries[-1]) + bias)
            grad_shares.append(dot_nt(value, grads[-1]))
    tops = [jnp.max(s, axis=0, keepdims=True) for s in scores]
    raw = [jnp.exp(s - top) for s, top in zip(scores, tops)]
    inverse = [1.0 / jnp.sum(e, axis=0, keepdims=True) for e in raw]
    shares = [e * i for e, i in zip(raw, inverse)]
    terms = [jnp.sum(g * p, axis=0, keepdims=True) for g, p in zip(grad_shares, shares)]
    grad_scores = [(p * (g - t)).astype(BF) for p, g, t in zip(shares, grad_shares, terms)]
    shares = [p.astype(BF) for p in shares]
    out = []
    for at in range(len(tiles)):
        a, b = 2 * at, 2 * at + 1
        grad_value = dot_nn(shares[a], grads[a]) + dot_nn(shares[b], grads[b])
        grad_key = dot_nn(grad_scores[a], queries[a]) + dot_nn(grad_scores[b], queries[b])
        key_turned = turned[at]
        grad_query = jnp.concatenate(
            [dot_nn(key_turned[:HEAD_DIM], grad_scores[a]), dot_nn(key_turned[HEAD_DIM:], grad_scores[b])], axis=0
        )
        out.append(((grad_query * scale).astype(BF).T, grad_key.astype(BF), grad_value.astype(BF)))
    return out


def place_mask(size):
    row = lax.broadcasted_iota(jnp.int32, (size, size), 0)
    col = lax.broadcasted_iota(jnp.int32, (size, size), 1)
    return jnp.where(((row ^ col) & (TILE - 1)) == 0, 0.0, LOW)


def pair_cols(part, pair, width):
    start = part * width + pair * PAIR
    return slice(start, start + PAIR)


def temporal_forward(chunk, x_ref, qk_ref, v_in_ref, ol_ref, v_ref, norm_ref, joined_ref, mixed_ref, proj_ref, after_ref):
    frames, padded, width = x_ref.shape
    steps = frames // chunk

    def project(c, carry):
        at = pl.ds(c * chunk, chunk)
        unit, scale = normalize(rows_of(x_ref[at]).astype(F32))
        norm = (unit * v_ref[0:1] + v_ref[1:2]).astype(BF)
        norm_ref[at] = norm.reshape(chunk, padded, width)
        for part in range(3):
            cols = slice(part * width, (part + 1) * width)
            weight = qk_ref[:, cols] if part < 2 else v_in_ref[:, :width]
            joined_ref[at, :, cols] = dot_nn(norm, weight).astype(BF).reshape(chunk, padded, width)
        return carry

    lax.fori_loop(0, steps, project, 0)

    def attend(g, carry):
        at = pl.ds(pl.multiple_of(g * TILE, TILE), TILE)
        allowed = place_mask(frames * TILE)
        for first in range(0, PAIRS, GROUP_T):
            group = range(first, first + GROUP_T)
            tiles = [[rows_of(joined_ref[:, at, pair_cols(i, pair, width)]) for i in range(3)] for pair in group]
            for pair, mixed in zip(group, heads_forward(tiles, allowed)):
                mixed_ref[:, at, pair_cols(0, pair, width)] = mixed.reshape(frames, TILE, PAIR)
        return carry

    lax.fori_loop(0, padded // TILE, attend, 0)

    def finish(c, carry):
        at = pl.ds(c * chunk, chunk)
        mixed = rows_of(mixed_ref[at])
        proj = (dot_nn(mixed, ol_ref[:, :width]) + v_ref[2:3]).astype(BF)
        proj_ref[at] = proj.reshape(chunk, padded, width)
        branch = (dot_nn(proj, ol_ref[:, width:]) + v_ref[3:4]).astype(BF)
        after = rows_of(x_ref[at]).astype(F32) + branch.astype(F32)
        after_ref[at] = after.reshape(chunk, padded, width)
        return carry

    lax.fori_loop(0, steps, finish, 0)


def spatial_forward(places, after_ref, qk_ref, vo_ref, v_ref, norm_ref, joined_ref, mixed_ref, space_ref):
    chunk, padded, width = after_ref.shape
    after = rows_of(after_ref[...])
    unit, scale = normalize(after)
    norm = (unit * v_ref[4:5] + v_ref[5:6]).astype(BF)
    norm_ref[...] = norm.reshape(chunk, padded, width)
    for part in range(3):
        cols = slice(part * width, (part + 1) * width)
        weight = qk_ref[:, cols] if part < 2 else vo_ref[:, :width]
        joined_ref[:, :, cols] = dot_nn(norm, weight).astype(BF).reshape(chunk, padded, width)
    allowed = jnp.where(lax.broadcasted_iota(jnp.int32, (1, padded), 1) < places, 0.0, LOW)
    for frame in range(chunk):
        for first in range(0, PAIRS, GROUP_S):
            group = range(first, first + GROUP_S)
            tiles = [[joined_ref[frame, :, pair_cols(i, pair, width)] for i in range(3)] for pair in group]
            for pair, mixed in zip(group, heads_forward(tiles, allowed)):
                mixed_ref[frame, :, pair_cols(0, pair, width)] = mixed
    space = after + dot_nn(rows_of(mixed_ref[...]), vo_ref[:, width:]) + v_ref[6:7]
    space_ref[...] = space.reshape(chunk, padded, width)


def gelu_parts(hidden):
    phi = 0.5 * (1.0 + lax.erf(hidden * 0.7071067811865476))
    density = jnp.exp(-0.5 * hidden * hidden) * 0.3989422804014327
    return phi, density


def feed_both(places, space_ref, cot_ref, w1_ref, w2_ref, v_ref, out_ref, grad_ref, norm_ref, active_ref, dhid_ref, vec_ref):
    chunk, padded, width = space_ref.shape
    blocks = w1_ref.shape[1] // width

    @pl.when(pl.program_id(0) == 0)
    def _():
        vec_ref[...] = jnp.zeros_like(vec_ref)

    space = rows_of(space_ref[...])
    cot = rows_of(cot_ref[...])
    unit, scale = normalize(space)
    norm = (unit * v_ref[7:8] + v_ref[8:9]).astype(BF)
    norm_ref[...] = norm.reshape(chunk, padded, width)
    out = space + v_ref[9:10]
    d_norm = jnp.zeros_like(space)
    for block in range(blocks):
        cols = slice(block * width, (block + 1) * width)
        hidden = dot_nn(norm, w1_ref[:, cols]) + v_ref[10 + block : 11 + block]
        phi, density = gelu_parts(hidden)
        active = (hidden * phi).astype(BF)
        active_ref[:, :, cols] = active.reshape(chunk, padded, width)
        out += dot_nn(active, w2_ref[:, cols])
        d_hidden = dot_nt(cot, w2_ref[:, cols]) * (phi + hidden * density)
        vec_ref[3 + block : 4 + block] += col_sum(d_hidden.astype(BF).astype(F32))
        d_hidden = d_hidden.astype(BF)
        dhid_ref[:, :, cols] = d_hidden.reshape(chunk, padded, width)
        d_norm += dot_nt(d_hidden, w1_ref[:, cols])
    for frame in range(chunk):
        out_ref[frame] = out[frame * padded : frame * padded + places].astype(BF)
    vec_ref[0:1] += col_sum(d_norm * unit)
    vec_ref[1:2] += col_sum(d_norm)
    vec_ref[2:3] += col_sum(cot.astype(F32))
    grad = cot.astype(F32) + norm_back(unit, scale, v_ref[7:8], d_norm)
    grad_ref[...] = grad.reshape(chunk, padded, width)


def feed_grads(norm_ref, dhid_ref, active_ref, cot_ref, out_ref, norm_turned, cot_turned):
    width = norm_ref.shape[1]

    @pl.when(pl.program_id(0) == 0)
    def _():
        norm_turned[...] = norm_ref[...].T
        cot_turned[...] = cot_ref[...].T

    out_ref[:, :width] = dot_nn(norm_turned[...], dhid_ref[...]).astype(BF)
    out_ref[:, width:] = dot_nn(cot_turned[...], active_ref[...]).astype(BF).T


def spatial_back(places, grad_ref, after_ref, joined_ref, qk_ref, vo_ref, v_ref, dspace_ref, djoin_ref, dat_ref, dtime_ref, vec_ref, dmix_ref):
    chunk, padded, width = grad_ref.shape

    @pl.when(pl.program_id(0) == 0)
    def _():
        vec_ref[...] = jnp.zeros_like(vec_ref)

    grad = rows_of(grad_ref[...])
    d_space = grad.astype(BF)
    dspace_ref[...] = d_space.reshape(chunk, padded, width)
    vec_ref[2:3] += col_sum(d_space.astype(F32))
    dmix_ref[...] = dot_nt(d_space, vo_ref[:, width:]).astype(BF).reshape(chunk, padded, width)
    allowed = jnp.where(lax.broadcasted_iota(jnp.int32, (padded, 1), 0) < places, 0.0, LOW)
    for frame in range(chunk):
        for first in range(0, PAIRS, GROUP_SB):
            group = range(first, first + GROUP_SB)
            tiles = [
                [joined_ref[frame, :, pair_cols(i, pair, width)] for i in range(3)]
                + [dmix_ref[frame, :, pair_cols(0, pair, width)]]
                for pair in group
            ]
            for pair, grads in zip(group, heads_backward(tiles, allowed)):
                for i in range(3):
                    djoin_ref[frame, :, pair_cols(i, pair, width)] = grads[i]
    d_joined = rows_of(djoin_ref[...])
    d_norm = dot_nt(d_joined[:, : 2 * width], qk_ref[...]) + dot_nt(d_joined[:, 2 * width :], vo_ref[:, :width])
    unit, scale = normalize(rows_of(after_ref[...]))
    vec_ref[0:1] += col_sum(d_norm * unit)
    vec_ref[1:2] += col_sum(d_norm)
    d_time = grad + norm_back(unit, scale, v_ref[4:5], d_norm)
    dat_ref[...] = d_time.reshape(chunk, padded, width)
    dtime_ref[...] = d_time.astype(BF).reshape(chunk, padded, width)


def join_grads(norm_ref, djoin_ref, mixed_ref, dspace_ref, out_ref, norm_turned):
    i = pl.program_id(0)
    parts = 3

    @pl.when(i == 0)
    def _():
        norm_turned[...] = norm_ref[...].T

    @pl.when(i < parts)
    def _():
        out_ref[...] = dot_nn(norm_turned[...], djoin_ref[...]).astype(BF)

    @pl.when(i == parts)
    def _():
        out_ref[...] = dot_tn(mixed_ref[...], dspace_ref[...]).astype(BF)


def temporal_back(chunk, places, dat_ref, dtime_ref, x_ref, joined_ref, qk_ref, v_in_ref, ol_ref, v_ref, dproj_ref, djoin_ref, gx_ref, vec_ref, dmix_ref):
    frames, padded, width = x_ref.shape
    steps = frames // chunk
    vec_ref[...] = jnp.zeros_like(vec_ref)

    def project(c, carry):
        at = pl.ds(c * chunk, chunk)
        d_time = rows_of(dtime_ref[at])
        vec_ref[3:4] += col_sum(d_time.astype(F32))
        d_proj = dot_nt(d_time, ol_ref[:, width:]).astype(BF)
        vec_ref[2:3] += col_sum(d_proj.astype(F32))
        dproj_ref[at] = d_proj.reshape(chunk, padded, width)
        d_mixed = dot_nt(d_proj, ol_ref[:, :width]).astype(BF)
        dmix_ref[at] = d_mixed.reshape(chunk, padded, width)
        return carry

    lax.fori_loop(0, steps, project, 0)

    def attend(g, carry):
        at = pl.ds(pl.multiple_of(g * TILE, TILE), TILE)
        allowed = place_mask(frames * TILE)
        for first in range(0, PAIRS, GROUP_TB):
            group = range(first, first + GROUP_TB)
            tiles = [
                [rows_of(joined_ref[:, at, pair_cols(i, pair, width)]) for i in range(3)]
                + [rows_of(dmix_ref[:, at, pair_cols(0, pair, width)])]
                for pair in group
            ]
            for pair, grads in zip(group, heads_backward(tiles, allowed)):
                for i in range(3):
                    djoin_ref[:, at, pair_cols(i, pair, width)] = grads[i].reshape(frames, TILE, PAIR)
        return carry

    lax.fori_loop(0, padded // TILE, attend, 0)

    def finish(c, carry):
        at = pl.ds(c * chunk, chunk)
        d_joined = rows_of(djoin_ref[at])
        d_norm = dot_nt(d_joined[:, : 2 * width], qk_ref[...]) + dot_nt(d_joined[:, 2 * width :], v_in_ref[:, :width])
        d_norm = d_norm.astype(BF).astype(F32)
        unit, scale = normalize(rows_of(x_ref[at]).astype(F32))
        vec_ref[0:1] += col_sum(d_norm * unit)
        vec_ref[1:2] += col_sum(d_norm)
        grad = rows_of(dat_ref[at]) + norm_back(unit, scale, v_ref[0:1], d_norm)
        grad = grad.astype(BF).reshape(chunk, padded, width)
        gx_ref[at] = grad[:, :places]
        return carry

    lax.fori_loop(0, steps, finish, 0)


def whole(shape):
    return pl.BlockSpec(shape, lambda *i: (0,) * len(shape))


def params(mib=60):
    return pltpu.CompilerParams(vmem_limit_bytes=mib << 20)


def shape_of(*dims, dtype=BF):
    return jax.ShapeDtypeStruct(dims, dtype)


def run_temporal_forward(x, weights, v, chunk=2):
    frames, padded, width = x.shape
    dims = (frames, padded, width)
    wide = (frames, padded, 3 * width)
    return pl.pallas_call(
        functools.partial(temporal_forward, chunk),
        out_shape=(shape_of(*dims), shape_of(*wide), shape_of(*dims), shape_of(*dims), shape_of(*dims, dtype=F32)),
        compiler_params=params(),
    )(x, *weights, v)


def frame_block(chunk, padded, width):
    return pl.BlockSpec((chunk, padded, width), lambda i: (i, 0, 0))


def run_spatial_forward(places, after, weights, v, chunk=2):
    frames, padded, width = after.shape
    block = frame_block(chunk, padded, width)
    wide = frame_block(chunk, padded, 3 * width)
    dims = (frames, padded, width)
    return pl.pallas_call(
        functools.partial(spatial_forward, places),
        grid=(frames // chunk,),
        in_specs=[block] + [whole(w.shape) for w in weights] + [whole(v.shape)],
        out_specs=[block, wide, block, block],
        out_shape=(shape_of(*dims), shape_of(frames, padded, 3 * width), shape_of(*dims), shape_of(*dims, dtype=F32)),
        compiler_params=params(),
    )(after, *weights, v)


def run_feed(places, space, cot, pack, v, chunk=2):
    frames, padded, width = space.shape
    hidden = 4 * width
    block = frame_block(chunk, padded, width)
    wide = frame_block(chunk, padded, hidden)
    dims = (frames, padded, width)
    return pl.pallas_call(
        functools.partial(feed_both, places),
        grid=(frames // chunk,),
        in_specs=[
            block, block,
            pl.BlockSpec((width, hidden), lambda i: (0, 0)),
            pl.BlockSpec((width, hidden), lambda i: (0, 1)),
            whole(v.shape),
        ],
        out_specs=[frame_block(chunk, places, width), block, block, wide, wide, whole((8, width))],
        out_shape=(
            shape_of(frames, places, width), shape_of(*dims, dtype=F32), shape_of(*dims),
            shape_of(frames, padded, hidden), shape_of(frames, padded, hidden), shape_of(8, width, dtype=F32),
        ),
        compiler_params=params(),
    )(space, cot, pack, pack, v)


def flat(a):
    return a.reshape(-1, a.shape[-1])


def run_feed_grads(norm, d_hidden, active, cot):
    norm, d_hidden, active, cot = flat(norm), flat(d_hidden), flat(active), flat(cot)
    rows, width = norm.shape
    blocks = d_hidden.shape[1] // width
    part = pl.BlockSpec((rows, width), lambda i: (0, i))
    return pl.pallas_call(
        feed_grads,
        grid=(blocks,),
        in_specs=[whole((rows, width)), part, part, whole((rows, width))],
        out_specs=pl.BlockSpec((width, 2 * width), lambda i: (0, i)),
        out_shape=shape_of(width, 2 * width * blocks),
        scratch_shapes=[pltpu.VMEM((width, rows), BF), pltpu.VMEM((width, rows), BF)],
        compiler_params=params(),
    )(norm, d_hidden, active, cot)


def run_spatial_back(places, grad, after, joined, weights, v, chunk=2):
    frames, padded, width = grad.shape
    block = frame_block(chunk, padded, width)
    wide = frame_block(chunk, padded, 3 * width)
    dims = (frames, padded, width)
    return pl.pallas_call(
        functools.partial(spatial_back, places),
        grid=(frames // chunk,),
        in_specs=[block, block, wide] + [whole(w.shape) for w in weights] + [whole(v.shape)],
        out_specs=[block, wide, block, block, whole((8, width))],
        out_shape=(
            shape_of(*dims), shape_of(frames, padded, 3 * width), shape_of(*dims, dtype=F32), shape_of(*dims),
            shape_of(8, width, dtype=F32),
        ),
        scratch_shapes=[pltpu.VMEM((chunk, padded, width), BF)],
        compiler_params=params(),
    )(grad, after, joined, *weights, v)


def run_join_grads(norm, d_joined, mixed, d_out):
    norm, d_joined, mixed, d_out = flat(norm), flat(d_joined), flat(mixed), flat(d_out)
    rows, width = norm.shape
    return pl.pallas_call(
        join_grads,
        grid=(4,),
        in_specs=[
            whole((rows, width)), pl.BlockSpec((rows, width), lambda i: (0, jnp.minimum(i, 2))),
            whole((rows, width)), whole((rows, width)),
        ],
        out_specs=pl.BlockSpec((width, width), lambda i: (0, i)),
        out_shape=shape_of(width, 4 * width),
        scratch_shapes=[pltpu.VMEM((width, rows), BF)],
        compiler_params=params(),
    )(norm, d_joined, mixed, d_out)


def run_temporal_back(places, d_at, d_time, x, joined, weights, v, chunk=2):
    frames, padded, width = x.shape
    dims = (frames, padded, width)
    return pl.pallas_call(
        functools.partial(temporal_back, chunk, places),
        out_shape=(
            shape_of(*dims), shape_of(frames, padded, 3 * width), shape_of(frames, places, width),
            shape_of(8, width, dtype=F32),
        ),
        scratch_shapes=[pltpu.VMEM(dims, BF)],
        compiler_params=params(),
    )(d_at, d_time, x, joined, *weights, v)


def tile_grad(a_ref, b_ref, out_ref):
    out_ref[...] = dot_tn(a_ref[...], b_ref[...]).astype(BF)


def run_tile_grad(a, b):
    a, b = flat(a), flat(b)
    rows, width = a.shape
    return pl.pallas_call(
        tile_grad,
        grid=(2,),
        in_specs=[pl.BlockSpec((rows, width // 2), lambda i: (0, i)), whole((rows, b.shape[1]))],
        out_specs=pl.BlockSpec((width // 2, b.shape[1]), lambda i: (i, 0)),
        out_shape=shape_of(width, b.shape[1]),
        compiler_params=params(),
    )(a, b)


AXES = ("dp", "seq")


def swap(values, bit, n):
    return lax.ppermute(values, AXES, [(i, i ^ (1 << bit)) for i in range(n)])


def gather_rows(values, n, order):
    bits = n.bit_length() - 1
    me = lax.axis_index(AXES)
    held = values.reshape((1,) * bits + values.shape)
    for bit in order:
        axis = bits - 1 - bit
        other = swap(held, bit, n)
        high = ((me >> bit) & 1) == 1
        held = jnp.where(high, jnp.concatenate([other, held], axis), jnp.concatenate([held, other], axis))
    return held.reshape((n * values.shape[0],) + values.shape[1:])


def scatter_rows(values, n, order):
    bits = n.bit_length() - 1
    me = lax.axis_index(AXES)
    rows = values.shape[0] // n
    held = values.reshape((2,) * bits + (rows,) + values.shape[1:])
    for bit in order:
        axis = bits - 1 - bit
        mine = (me >> bit) & 1
        send = lax.dynamic_index_in_dim(held, 1 - mine, axis, keepdims=True)
        keep = lax.dynamic_index_in_dim(held, mine, axis, keepdims=True)
        held = (keep.astype(F32) + swap(send, bit, n).astype(F32)).astype(values.dtype)
    return held.reshape((rows,) + values.shape[1:])


def on_device(n, tokens, tg, tb, t_in, t_out, t_lin, sg, sb, s_in, s_out, fg, fb, w1, b1, w2, cotangent):
    bits = n.bit_length() - 1
    top = tuple(range(bits - 1, 2, -1))
    order_a, order_b, order_c = top + (1, 2, 0), top + (2, 1, 0), (1, 2) + top + (0,)
    rows, width = t_in.shape[0], t_in.shape[0] * n
    parts = w2.shape[0] // rows
    hidden = w1.shape[1]
    places = tokens.shape[2]
    frames = tokens.shape[0] * tokens.shape[1]
    extra = -places % TILE

    vecs = jnp.concatenate([tg[None], tb, sg[None], sb, fg[None], fb, b1.reshape(parts, rows)], axis=0)
    n_vec = vecs.shape[0]
    vec_cols = jnp.pad(vecs.T, ((0, 0), (0, 2 * HEAD_DIM - n_vec)))
    feed = jnp.concatenate(
        [
            w1.reshape(rows, n, parts, rows).transpose(0, 2, 1, 3).reshape(rows, hidden),
            w2.reshape(parts, rows, width).transpose(1, 0, 2).reshape(rows, hidden),
        ],
        axis=1,
    )
    feed = lax.all_gather(feed, AXES, axis=0, tiled=True)

    def own_clip(grid):
        clip = lax.all_to_all(grid, "seq", split_axis=0, concat_axis=0, tiled=True)
        return jnp.pad(clip.reshape(frames, places, width), ((0, 0), (0, extra), (0, 0)))

    def own_frames(clip):
        return lax.all_to_all(clip.reshape(tokens.shape), "seq", split_axis=0, concat_axis=0, tiled=True)

    x = own_clip(tokens)
    t_w = (
        gather_rows(t_in[:, : 2 * width], n, order_a),
        gather_rows(jnp.concatenate([t_in[:, 2 * width :], vec_cols], axis=1), n, order_c),
        gather_rows(jnp.concatenate([t_out, t_lin], axis=1), n, order_b),
    )
    s_w = (
        gather_rows(s_in[:, : 2 * width], n, order_a),
        gather_rows(jnp.concatenate([s_in[:, 2 * width :], s_out], axis=1), n, order_b),
    )
    cot = own_clip(cotangent)
    vec = t_w[1][:, width:].T[:16].astype(F32)

    norm_t, joined_t, mixed_t, proj_t, after_time = run_temporal_forward(x, t_w, vec)
    norm_s, joined_s, mixed_s, after_space = run_spatial_forward(places, after_time, s_w, vec)
    out, d_after_space, norm_m, active, d_hidden, vec_f = run_feed(places, after_space, cot, feed, vec)
    output = own_frames(out)
    g_feed = run_feed_grads(norm_m, d_hidden, active, cot)
    g_feed = lax.psum_scatter(g_feed, AXES, scatter_dimension=0, tiled=True).astype(F32)
    d_space, d_joined_s, d_after_time, d_time, vec_s = run_spatial_back(
        places, d_after_space, after_time, joined_s, s_w, vec
    )
    g_lin = run_tile_grad(proj_t, d_time)
    g_space = run_join_grads(norm_s, d_joined_s, mixed_s, d_space)
    g_space = jnp.concatenate(
        [
            scatter_rows(g_space[:, : 2 * width], n, order_a[::-1]),
            scatter_rows(g_space[:, 2 * width :], n, order_b[::-1]),
        ],
        axis=1,
    ).astype(F32)
    d_proj, d_joined_t, g_x, vec_t = run_temporal_back(places, d_after_time, d_time, x, joined_t, t_w, vec)
    g_x = own_frames(g_x)
    g_time = run_join_grads(norm_t, d_joined_t, mixed_t, d_proj)
    g_vec = jnp.concatenate([vec_t[:4], vec_s[:3], vec_f[: 3 + parts]], axis=0)
    g_vec = jnp.pad(g_vec.T.astype(BF), ((0, 0), (0, 2 * HEAD_DIM - n_vec)))
    g_last = scatter_rows(jnp.concatenate([g_lin, g_vec], axis=1), n, order_c[::-1]).astype(F32)
    g_time = jnp.concatenate(
        [
            scatter_rows(g_time[:, : 2 * width], n, order_a[::-1]),
            scatter_rows(g_time[:, 2 * width :], n, order_b[::-1]),
        ],
        axis=1,
    ).astype(F32)
    v = g_last[:, width : width + n_vec].T
    g_feed = g_feed.reshape(rows, parts, 2, width)
    o_w1 = g_feed[:, :, 0].reshape(rows, parts, n, rows).transpose(0, 2, 1, 3).reshape(rows, hidden)
    o_w2 = g_feed[:, :, 1].transpose(1, 0, 2).reshape(parts * rows, width)
    return (
        output, g_x, v[0], v[1:4], g_time[:, : 3 * width], g_time[:, 3 * width :], g_last[:, :width],
        v[4], v[5:7], g_space[:, : 3 * width], g_space[:, 3 * width :], v[7], v[8:10],
        o_w1, v[10 : 10 + parts].reshape(-1), o_w2,
    )


def solution(mesh):
    shard = P(("dp", "seq"))
    cols = P(None, ("dp", "seq"))
    mat = P(("dp", "seq"), None)
    tok = P("dp", "seq", None, None)
    in_specs = (tok, shard, cols, mat, mat, mat, shard, cols, mat, mat, shard, cols, mat, shard, mat, tok)
    out_specs = (tok, tok, shard, cols, mat, mat, mat, shard, cols, mat, mat, shard, cols, mat, shard, mat)
    return jax.shard_map(
        functools.partial(on_device, mesh.size), mesh=mesh, in_specs=in_specs, out_specs=out_specs, check_vma=False
    )
```

time: 1090 us -> 581 us (0.53)
  matrix products: 323 us -> 0 us
  Pallas kernels: 0 us -> 241 us
  local copies, waits for them, and re-layouts: 298 us -> 74.2 us
  other arithmetic: 218 us -> 52 us
  blocking collectives: 79.5 us -> 0 us
  starting transfers between devices: 9.27 us -> 71.8 us
  waiting for transfers between devices: 134 us -> 119 us
    dot_general x33 -> x0, matrix products: 323 us -> none  [the longest x7 69.1 us: matmul(): result = jnp.dot(flattened, right_side, preferred_element_type=jnp.float32)]
    pallas_call x0 -> x9, Pallas kernels: none -> 241 us  [the longest x1 45.2 us: run_feed(): pl.pallas_call(functools.partial(feed_both, places), grid=(frames // chun...]
    reduce_sum x16 -> x0, other arithmetic: 122 us -> none  [the longest x4 62.3 us: token_sum(): jnp.sum(values.astype(jnp.float32).reshape(-1, values.shape[-1]), axis=0)]
    convert_element_type x11 -> x0, local copies, waits for them, and re-layouts: 90 us -> none  [the longest x3 46.6 us: attend_backward(): return stacked.reshape(joined.shape).astype(jnp.bfloat16)]
    all_to_all x2 -> x0, blocking collectives: 79.5 us -> none  [the longest x1 41.7 us: on_device(): lax.all_to_all(g_x.reshape(tokens.shape), 'seq', split_axis=0, concat_axi...]
    ppermute x0 -> x50, waiting for transfers between devices: none -> 78.4 us  [swap(): return lax.ppermute(values, AXES, [(i, i ^ 1 << bit) for i in range(n)])]
    convert_element_type x8 -> x24, other arithmetic: 81.7 us -> 18.3 us  [the longest x20 17.4 us: scatter_rows(): (keep.astype(F32) + swap(send, bit, n).astype(F32)).astype(values.dtype)]
    ppermute x0 -> x50, starting transfers between devices: none -> 54.6 us  [swap(): return lax.ppermute(values, AXES, [(i, i ^ 1 << bit) for i in range(n)])]
  transfers between devices with their start and end apart: 5 -> 56, of which waited for: 4 -> 20; matrix products, arithmetic and copies ran while one was open for 23% -> 17% of each run, Pallas kernels for 0% -> 30%
where the time goes in v2:
time: 581 us; the launch traced here: 574 us
  Pallas kernels  241 us (41%)
  waiting for transfers between devices  119 us (20%)
  local copies, waits for them, and re-layouts  74.2 us (13%)
  starting transfers between devices  71.8 us (12%)
  other arithmetic  52 us (9%)
  between operations  15.5 us (3%)
    ppermute x50, waiting for transfers between devices, swap(): return lax.ppermute(values, AXES, [(i, i ^ 1 << bit) for i in range(n)])  78.4 us
    ppermute x50, starting transfers between devices, swap(): return lax.ppermute(values, AXES, [(i, i ^ 1 << bit) for i in range(n)])  54.6 us
    pallas_call x1, Pallas kernels, run_feed(): pl.pallas_call(functools.partial(feed_both, places), grid=(frames // chun...  45.2 us
    pallas_call x1, Pallas kernels, run_spatial_back(): pl.pallas_call(functools.partial(spatial_back, places), grid=(frames // c...  41.7 us
    pallas_call x1, Pallas kernels, run_temporal_back(): pl.pallas_call(functools.partial(temporal_back, chunk, places), out_shape...  39.8 us
    pallas_call x2, Pallas kernels, run_join_grads(): pl.pallas_call(join_grads, grid=(4,), in_specs=[whole((rows, width)), pl....  30.9 us
    pallas_call x1, Pallas kernels, run_temporal_forward(): pl.pallas_call(functools.partial(temporal_forward, chunk), out_shape=(sha...  30.8 us
    select_n x25, other arithmetic, gather_rows(): jnp.where(high, jnp.concatenate([other, held], axis), jnp.concatenate([he...  26.9 us
  transfers between devices with their start and end apart: 56, of which 20 were waited for; matrix products, arithmetic and copies ran while one was open for 17% of the time, Pallas kernels for 30%

profile of v2, /device:TPU:0, one launch (start us, length us, event | category | flops | bytes accessed | tf_op | source)
XLA Modules:
  0.0 574.0 jit_solution(9298309970387369201)
XLA Ops:
  7.2 2.1 reshape.3689
  11.8 4.1 collective-permute-start.10
  18.2 3.6 all-to-all-start
  21.9 2.7 collective-permute-start.15
  28.9 4.7 collective-permute-done.15
  33.7 3.0 collective-permute-done.20
  37.0 2.7 collective-permute-start.7
  41.6 5.5 collective-permute-done.1
  47.1 1.8 collective-permute-start.2
  48.9 3.5 collective-permute-done.16
  52.6 2.3 collective-permute-start.17
  54.9 3.5 collective-permute-done.21
  60.6 1.7 collective-permute-start.13
  62.3 5.9 %collective-permute-done.2 = bf16[2,2,1,1,1,24,1536]{6,5,0,1,2,4,3:T(8,128)(2,1)S(1)} collective-permute-done((bf16[2,2,1,1,1,24,1536]{6,5,0,1,2,4,3:T(8,128)(2,1)S(1)}, bf16[2,2,1,1,1,24,1536]{6,5,0,1,2,4,3:T(8,128)(2,1)S(1)}, u32[]{:S(2)}, u32[]{:S(2)}) %collective-permute-start.2) | collective-permute-done | bytes 294944 | tf_op jit(solution)/shard_map/ppermute | solution.py:510
  70.6 3.9 collective-permute-done.17
  82.2 4.5 all-to-all-start.1
  89.1 2.3 collective-permute-done.13
  91.4 2.4 maximum_select_fusion.6
  93.9 2.6 maximum_select_fusion.5
  96.9 15.0 %collective-permute-done.18 = bf16[2,2,1,2,1,24,1536]{6,5,1,0,4,3,2:T(8,128)(2,1)} collective-permute-done((bf16[2,2,1,2,1,24,1536]{6,5,1,0,4,3,2:T(8,128)(2,1)}, bf16[2,2,1,2,1,24,1536]{6,5,1,0,4,3,2:T(8,128)(2,1)}, u32[]{:S(2)}, u32[]{:S(2)}) %collective-permute-start.18) | collective-permute-done | bytes 589856 | tf_op jit(solution)/shard_map/ppermute | solution.py:510
  111.9 2.5 maximum_select_fusion.7
  114.4 2.3 collective-permute-done.23
  116.7 2.6 maximum_select_fusion.8
  120.6 2.0 copy.234
  124.3 17.8 %all-to-all-done.1 = bf16[4,2,196,768]{3,1,2,0:T(2,128)(2,1)} async-done(((bf16[4,2,196,768]{3,1,2,0:T(2,128)(2,1)}), bf16[4,2,196,768]{3,1,2,0:T(2,128)(2,1)}, u32[]{:S(2)}, u32[]{:S(2)}) %all-to-all-start.1) | async-done | bytes 2408480 | tf_op jit(solution)/shard_map/all_to_all | solution.py:563
  142.1 2.0 copy.291
  145.7 2.8 maximum_select_fusion.1
  150.2 2.9 maximum_select_fusion
  154.7 2.8 maximum_select_fusion.2
  159.2 2.0 maximum_select_fusion.3
  161.3 1.7 copy.290
  163.0 30.8 %shard_map.279 = (bf16[8,208,768]{2,1,0:T(8,128)(2,1)}, bf16[8,208,2304]{2,1,0:T(8,128)(2,1)}, bf16[8,208,768]{2,1,0:T(8,128)(2,1)}, bf16[8,208,768]{2,1,0:T(8,128)(2,1)}, f32[8,208,768]{2,1,0:T(8,128)}) custom-call(bf16[8,208,768]{2,1,0:T(8,128)(2,1)} %pad.15.x_ref, bf16[768,1536]{1,0:T(8,128)(2,1)} %bitcast.243, bf16[768,896]{1,0:T(8,128)(2,1)} %bitcast.250, ...), custom_call_target="tpu_custom_call" | custom-call | tf_op jit(solution)/shard_map/pallas_call | solution.py:369
  193.8 22.6 %shard_map.280 = (bf16[8,208,768]{2,1,0:T(8,128)(2,1)}, bf16[8,208,2304]{2,1,0:T(8,128)(2,1)}, bf16[8,208,768]{2,1,0:T(8,128)(2,1)}, f32[8,208,768]{2,1,0:T(8,128)}) custom-call(f32[8,208,768]{2,1,0:T(8,128)} %get-tuple-element.40.after_ref, bf16[768,1536]{1,0:T(8,128)(2,1)} %bitcast.245, bf16[768,1536]{1,0:T(8,128)(2,1)} %bitcast.247, ...), custom_call_target="tpu_custom_call" | custom-call | tf_op jit(solution)/shard_map/pallas_call | solution.py:385
  216.4 45.2 %shard_map.281 = (bf16[8,196,768]{2,1,0:T(8,128)(2,1)}, f32[8,208,768]{2,1,0:T(8,128)}, bf16[8,208,768]{2,1,0:T(8,128)(2,1)}, bf16[8,208,3072]{2,1,0:T(8,128)(2,...) custom-call(f32[8,208,768]{2,1,0:T(8,128)} %get-tuple-element.41.space_ref, bf16[8,208,768]{2,1,0:T(8,128)(2,1)} %pad.17.cot_ref, ...), custom_call_target="tpu_custom_call" | custom-call | tf_op jit(solution)/shard_map/pallas_call | solution.py:401
  261.6 25.0 %shard_map.287 = bf16[768,6144]{1,0:T(8,128)(2,1)} custom-call(bf16[1664,768]{1,0:T(8,128)(2,1)} %bitcast.272, bf16[1664,3072]{1,0:T(8,128)(2,1)} %bitcast.254, bf16[1664,3072]{1,0:T(8,128)(2,1)} %bitcast.253, bf16[1664,768]{1,0:T(8,128)(2,1)} %bitcast.240), custom_call_target="tpu_custom_call" | custom-call | tf_op jit(solution)/shard_map/pallas_call | solution.py:428
  286.6 41.7 %shard_map.282 = (bf16[8,208,768]{2,1,0:T(8,128)(2,1)}, bf16[8,208,2304]{2,1,0:T(8,128)(2,1)}, f32[8,208,768]{2,1,0:T(8,128)}, bf16[8,208,768]{2,1,0:T(8,128)(2,1)}, f32[8,768]{1,0:T(8,128)}) custom-call(f32[8,208,768]{2,1,0:T(8,128)} %get-tuple-element.43.grad_ref, f32[8,208,768]{2,1,0:T(8,128)} %get-tuple-element.40.after_ref, ...), custom_call_target="tpu_custom_call" | custom-call | tf_op jit(solution)/shard_map/pallas_call | solution.py:444
  328.2 15.5 %shard_map.286 = bf16[768,3072]{1,0:T(8,128)(2,1)} custom-call(bf16[1664,768]{1,0:T(8,128)(2,1)} %bitcast.276, bf16[1664,2304]{1,0:T(8,128)(2,1)} %bitcast.266, bf16[1664,768]{1,0:T(8,128)(2,1)} %bitcast.277, bf16[1664,768]{1,0:T(8,128)(2,1)} %bitcast.278), custom_call_target="tpu_custom_call" | custom-call | tf_op jit(solution)/shard_map/pallas_call | solution.py:461
  343.7 2.7 fusion.46
  349.0 39.8 %shard_map.283 = (bf16[8,208,768]{2,1,0:T(8,128)(2,1)}, bf16[8,208,2304]{2,1,0:T(8,128)(2,1)}, bf16[8,196,768]{2,1,0:T(8,128)(2,1)}, f32[8,768]{1,0:T(8,128)}) custom-call(f32[8,208,768]{2,1,0:T(8,128)} %get-tuple-element.45.dat_ref, bf16[8,208,768]{2,1,0:T(8,128)(2,1)} %get-tuple-element.46.dtime_ref, bf16[8,208,768]{2,1,0:T(8,128)(2,1)} %pad.15.x_ref, ...), custom_call_target="tpu_custom_call" | custom-call | tf_op jit(solution)/shard_map/pallas_call | solution.py:478
  390.5 5.5 shard_map.284
  399.5 15.4 %shard_map.285 = bf16[768,3072]{1,0:T(8,128)(2,1)} custom-call(bf16[1664,768]{1,0:T(8,128)(2,1)} %bitcast.273, bf16[1664,2304]{1,0:T(8,128)(2,1)} %bitcast.265, bf16[1664,768]{1,0:T(8,128)(2,1)} %bitcast.274, bf16[1664,768]{1,0:T(8,128)(2,1)} %bitcast.275), custom_call_target="tpu_custom_call" | custom-call | tf_op jit(solution)/shard_map/pallas_call | solution.py:461
  414.9 2.8 fusion.47
  417.8 1.8 add_convert_fusion.4
  424.7 3.3 copy.295
  428.0 3.6 all-to-all-start.3
  431.7 5.1 copy.294
  436.9 2.7 collective-permute-start.27
  443.0 1.7 add_convert_fusion
  445.7 2.0 collective-permute-start.46
  447.7 1.7 add_convert_fusion.3
  454.3 17.1 %collective-permute-done.28 = bf16[1,1,1,2,1,24,896]{6,5,4,3,2,1,0:T(8,128)(2,1)S(1)} collective-permute-done((bf16[1,1,1,2,1,24,896]{6,5,4,3,2,1,0:T(8,128)(2,1)S(1)}, bf16[1,1,1,2,1,24,896]{6,5,4,3,2,1,0:T(8,128)(2,1)S(1)}, u32[]{:S(2)}, u32[]{:S(2)}) %collective-permute-start.28) | collective-permute-done | bytes 86048 | tf_op jit(solution)/shard_map/ppermute | solution.py:510
  471.5 1.7 collective-permute-start.29
  481.9 2.1 collective-permute-start.42
  484.0 4.8 all-to-all-start.2
  494.6 2.0 collective-permute-start.32
  499.9 22.9 %all-to-all-done.2 = bf16[4,2,196,768]{3,1,2,0:T(2,128)(2,1)} async-done(((bf16[4,2,196,768]{3,1,2,0:T(2,128)(2,1)}), bf16[4,2,196,768]{3,1,2,0:T(2,128)(2,1)}, u32[]{:S(2)}, u32[]{:S(2)}) %all-to-all-start.2) | async-done | bytes 2408480 | tf_op jit(solution)/shard_map/all_to_all | solution.py:567
  532.5 1.9 collective-permute-start.49
  534.4 2.9 collective-permute-done.33
  537.5 2.1 collective-permute-done.38
  540.6 2.7 collective-permute-done.49
  549.9 2.3 reshape_squeeze.3
  552.1 3.8 copy.298
  555.9 4.0 reshape.3720
  560.8 4.8 copy.338
  (302 shorter events, 95.3 us)
Async XLA Ops:
  7.2 209.2 %all-gather.2.cloned.1.call-start = ((), (), s32[]{:S(2)}) async-start(), calls=%async_computation.5 | async-start | bytes 9732096 | tf_op jit(solution)/shard_map/all_gather | solution.py:560
  9.6 8.1 %copy-start.30 = (bf16[24,2304]{1,0:T(8,128)(2,1)S(1)}, bf16[24,2304]{1,0:T(8,128)(2,1)}, u32[]{:S(2)}) copy-start(bf16[24,2304]{1,0:T(8,128)(2,1)} %param.19) | copy-start | bytes 331780
  11.8 14.8 %collective-permute-start.10 = (bf16[1,1,1,1,1,24,1536]{6,5,0,1,2,4,3:T(8,128)(2,1)S(1)}, bf16[1,1,1,1,1,24,1536]{6,5,0,1,2,4,3:T(8,128)(2,1)S(1)}, u32[]{:S(2)}, u32[]{:S(2)}) collective-permute-start(bf16[1,1,1,1,1,24,1536]{6,5,0,1,2,4,3:T(8,128)(2,1)S(1)} %bitcast.292), channel_id=1, source_target_pairs={{0,16},{1,17},{2,18},{3,19},{4,20},{5,21},{6,22},{7,23},{8,24},{9,... | collective-permute-start | bytes 221192 | tf_op jit(solution)/shard_map/ppermute | solution.py:510
  16.2 8.8 %collective-permute-start.5 = (bf16[1,1,1,1,1,24,896]{6,5,4,3,2,1,0:T(8,128)(2,1)S(1)}, bf16[1,1,1,1,1,24,896]{6,5,4,3,2,1,0:T(8,128)(2,1)S(1)}, u32[]{:S(2)}, u32[]{:S(2)}) collective-permute-start(bf16[1,1,1,1,1,24,896]{6,5,4,3,2,1,0:T(8,128)(2,1)S(1)} %get-tuple-element.167), channel_id=1, source_target_pairs={{0,2},{1,3},{2,0},{3,1},{4,6},{5,7},{6,4},{7,5},{8,10},{9,11},{10,... | collective-permute-start | bytes 129032 | tf_op jit(solution)/shard_map/ppermute | solution.py:510
  17.8 6.8 %slice-start = ((bf16[24,2304]{1,0:T(8,128)(2,1)}), bf16[24,768]{1,0:T(8,128)(2,1)S(1)}, s32[]{:S(2)}) async-start(bf16[24,2304]{1,0:T(8,128)(2,1)} %param.24), calls=%async_computation.7 | async-start | bytes 73728 | tf_op jit(solution)/shard_map/slice | solution.py:577
  17.8 6.7 %copy-start.31 = (bf16[24,768]{1,0:T(8,128)(2,1)S(1)}, bf16[24,768]{1,0:T(8,128)(2,1)}, u32[]{:S(2)}) copy-start(bf16[24,768]{1,0:T(8,128)(2,1)} %param.25) | copy-start | bytes 110596
  17.8 10.5 %collective-permute-start = (bf16[1,1,1,1,1,24,1536]{6,5,0,4,3,2,1:T(8,128)(2,1)S(1)}, bf16[1,1,1,1,1,24,1536]{6,5,0,4,3,2,1:T(8,128)(2,1)S(1)}, u32[]{:S(2)}, u32[]{:S(2)}) collective-permute-start(bf16[1,1,1,1,1,24,1536]{6,5,0,4,3,2,1:T(8,128)(2,1)S(1)} %get-tuple-element.159), channel_id=1, source_target_pairs={{0,16},{1,17},{2,18},{3,19},{4,20},{5,21},{6,22},{7,23},{8,24},{9,... | collective-permute-start | bytes 221192 | tf_op jit(solution)/shard_map/ppermute | solution.py:510
  18.2 62.5 %all-to-all-start = ((bf16[4,2,196,768]{3,1,2,0:T(2,128)(2,1)}), bf16[4,2,196,768]{3,1,2,0:T(2,128)(2,1)S(1)}, u32[]{:S(2)}, u32[]{:S(2)}) async-start(bf16[4,2,196,768]{3,1,2,0:T(2,128)(2,1)} %param.16), calls=%async_computation | async-start | bytes 4816896 | tf_op jit(solution)/shard_map/all_to_all | solution.py:563
  21.9 11.7 %collective-permute-start.15 = (bf16[1,1,1,1,1,24,1536]{6,5,4,3,2,1,0:T(8,128)(2,1)S(1)}, bf16[1,1,1,1,1,24,1536]{6,5,4,3,2,1,0:T(8,128)(2,1)S(1)}, u32[]{:S(2)}, u32[]{:S(2)}) collective-permute-start(bf16[1,1,1,1,1,24,1536]{6,5,4,3,2,1,0:T(8,128)(2,1)S(1)} %get-tuple-element.157), channel_id=1, source_target_pairs={{0,16},{1,17},{2,18},{3,19},{4,20},{5,21},{6,22},{7,23},{8,24},{9,... | collective-permute-start | bytes 221192 | tf_op jit(solution)/shard_map/ppermute | solution.py:510
  24.6 12.1 %collective-permute-start.20 = (bf16[1,1,1,1,1,24,1536]{6,5,4,3,2,1,0:T(8,128)(2,1)S(1)}, bf16[1,1,1,1,1,24,1536]{6,5,4,3,2,1,0:T(8,128)(2,1)S(1)}, u32[]{:S(2)}, u32[]{:S(2)}) collective-permute-start(bf16[1,1,1,1,1,24,1536]{6,5,4,3,2,1,0:T(8,128)(2,1)S(1)} %get-tuple-element.165), channel_id=1, source_target_pairs={{0,16},{1,17},{2,18},{3,19},{4,20},{5,21},{6,22},{7,23},{8,24},{9,... | collective-permute-start | bytes 221192 | tf_op jit(solution)/shard_map/ppermute | solution.py:510
  25.0 12.0 %collective-permute-start.6 = (bf16[1,1,1,2,1,24,896]{6,5,3,2,4,1,0:T(8,128)(2,1)S(1)}, bf16[1,1,1,2,1,24,896]{6,5,3,2,4,1,0:T(8,128)(2,1)S(1)}, u32[]{:S(2)}, u32[]{:S(2)}) collective-permute-start(bf16[1,1,1,2,1,24,896]{6,5,3,2,4,1,0:T(8,128)(2,1)S(1)} %fusion.13), channel_id=1, source_target_pairs={{0,4},{1,5},{2,6},{3,7},{4,0},{5,1},{6,2},{7,3},{8,12},{9,13},{10,... | collective-permute-start | bytes 258056 | tf_op jit(solution)/shard_map/ppermute | solution.py:510
  26.7 13.3 %collective-permute-start.11 = (bf16[2,1,1,1,1,24,1536]{6,5,0,1,2,4,3:T(8,128)(2,1)S(1)}, bf16[2,1,1,1,1,24,1536]{6,5,0,1,2,4,3:T(8,128)(2,1)S(1)}, u32[]{:S(2)}, u32[]{:S(2)}) collective-permute-start(bf16[2,1,1,1,1,24,1536]{6,5,0,1,2,4,3:T(8,128)(2,1)S(1)} %bitcast_select_fusion.2), channel_id=1, source_target_pairs={{0,8},{1,9},{2,10},{3,11},{4,12},{5,13},{6,14},{7,15},{8,0},{9,1},... | collective-permute-start | bytes 442376 | tf_op jit(solution)/shard_map/ppermute | solution.py:510
  28.4 18.7 %collective-permute-start.1 = (bf16[2,1,1,1,1,24,1536]{6,5,0,4,3,2,1:T(8,128)(2,1)S(1)}, bf16[2,1,1,1,1,24,1536]{6,5,0,4,3,2,1:T(8,128)(2,1)S(1)}, u32[]{:S(2)}, u32[]{:S(2)}) collective-permute-start(bf16[2,1,1,1,1,24,1536]{6,5,0,4,3,2,1:T(8,128)(2,1)S(1)} %bitcast_select_fusion.3), channel_id=1, source_target_pairs={{0,8},{1,9},{2,10},{3,11},{4,12},{5,13},{6,14},{7,15},{8,0},{9,1},... | collective-permute-start | bytes 442376 | tf_op jit(solution)/shard_map/ppermute | solution.py:510
  33.6 18.9 %collective-permute-start.16 = (bf16[2,1,1,1,1,24,1536]{6,5,1,0,4,3,2:T(8,128)(2,1)S(1)}, bf16[2,1,1,1,1,24,1536]{6,5,1,0,4,3,2:T(8,128)(2,1)S(1)}, u32[]{:S(2)}, u32[]{:S(2)}) collective-permute-start(bf16[2,1,1,1,1,24,1536]{6,5,1,0,4,3,2:T(8,128)(2,1)S(1)} %fusion.12), channel_id=1, source_target_pairs={{0,8},{1,9},{2,10},{3,11},{4,12},{5,13},{6,14},{7,15},{8,0},{9,1},... | collective-permute-start | bytes 442376 | tf_op jit(solution)/shard_map/ppermute | solution.py:510
  36.8 21.6 %collective-permute-start.21 = (bf16[2,1,1,1,1,24,1536]{6,5,4,3,2,1,0:T(8,128)(2,1)S(1)}, bf16[2,1,1,1,1,24,1536]{6,5,4,3,2,1,0:T(8,128)(2,1)S(1)}, u32[]{:S(2)}, u32[]{:S(2)}) collective-permute-start(bf16[2,1,1,1,1,24,1536]{6,5,4,3,2,1,0:T(8,128)(2,1)S(1)} %maximum_select_fusion.27), channel_id=1, source_target_pairs={{0,8},{1,9},{2,10},{3,11},{4,12},{5,13},{6,14},{7,15},{8,0},{9,1},... | collective-permute-start | bytes 442376 | tf_op jit(solution)/shard_map/ppermute | solution.py:510
  37.0 21.7 %collective-permute-start.7 = (bf16[1,1,2,2,1,24,896]{6,5,3,2,4,1,0:T(8,128)(2,1)S(1)}, bf16[1,1,2,2,1,24,896]{6,5,3,2,4,1,0:T(8,128)(2,1)S(1)}, u32[]{:S(2)}, u32[]{:S(2)}) collective-permute-start(bf16[1,1,2,2,1,24,896]{6,5,3,2,4,1,0:T(8,128)(2,1)S(1)} %fusion.9), channel_id=1, source_target_pairs={{0,16},{1,17},{2,18},{3,19},{4,20},{5,21},{6,22},{7,23},{8,24},{9,... | collective-permute-start | bytes 516104 | tf_op jit(solution)/shard_map/ppermute | solution.py:510
  40.1 19.6 %collective-permute-start.12 = (bf16[2,2,1,1,1,24,1536]{6,5,0,1,2,4,3:T(8,128)(2,1)S(1)}, bf16[2,2,1,1,1,24,1536]{6,5,0,1,2,4,3:T(8,128)(2,1)S(1)}, u32[]{:S(2)}, u32[]{:S(2)}) collective-permute-start(bf16[2,2,1,1,1,24,1536]{6,5,0,1,2,4,3:T(8,128)(2,1)S(1)} %maximum_select_fusion.21), channel_id=1, source_target_pairs={{0,4},{1,5},{2,6},{3,7},{4,0},{5,1},{6,2},{7,3},{8,12},{9,13},{10,... | collective-permute-start | bytes 884744 | tf_op jit(solution)/shard_map/ppermute | solution.py:510
  47.1 21.1 %collective-permute-start.2 = (bf16[2,2,1,1,1,24,1536]{6,5,0,1,2,4,3:T(8,128)(2,1)S(1)}, bf16[2,2,1,1,1,24,1536]{6,5,0,1,2,4,3:T(8,128)(2,1)S(1)}, u32[]{:S(2)}, u32[]{:S(2)}) collective-permute-start(bf16[2,2,1,1,1,24,1536]{6,5,0,1,2,4,3:T(8,128)(2,1)S(1)} %fusion.8), channel_id=1, source_target_pairs={{0,2},{1,3},{2,0},{3,1},{4,6},{5,7},{6,4},{7,5},{8,10},{9,11},{10,... | collective-permute-start | bytes 884744 | tf_op jit(solution)/shard_map/ppermute | solution.py:510
  52.6 22.0 %collective-permute-start.17 = (bf16[2,2,1,1,1,24,1536]{6,5,1,0,4,3,2:T(8,128)(2,1)S(1)}, bf16[2,2,1,1,1,24,1536]{6,5,1,0,4,3,2:T(8,128)(2,1)S(1)}, u32[]{:S(2)}, u32[]{:S(2)}) collective-permute-start(bf16[2,2,1,1,1,24,1536]{6,5,1,0,4,3,2:T(8,128)(2,1)S(1)} %maximum_select_fusion.22), channel_id=1, source_target_pairs={{0,2},{1,3},{2,0},{3,1},{4,6},{5,7},{6,4},{7,5},{8,10},{9,11},{10,... | collective-permute-start | bytes 884744 | tf_op jit(solution)/shard_map/ppermute | solution.py:510
  58.4 18.6 %collective-permute-start.22 = (bf16[2,2,1,1,1,24,1536]{6,5,0,1,4,3,2:T(8,128)(2,1)S(1)}, bf16[2,2,1,1,1,24,1536]{6,5,0,1,4,3,2:T(8,128)(2,1)S(1)}, u32[]{:S(2)}, u32[]{:S(2)}) collective-permute-start(bf16[2,2,1,1,1,24,1536]{6,5,0,1,4,3,2:T(8,128)(2,1)S(1)} %maximum_select_fusion.23), channel_id=1, source_target_pairs={{0,4},{1,5},{2,6},{3,7},{4,0},{5,1},{6,2},{7,3},{8,12},{9,13},{10,... | collective-permute-start | bytes 884744 | tf_op jit(solution)/shard_map/ppermute | solution.py:510
  59.6 27.7 %collective-permute-start.8 = (bf16[2,1,2,2,1,24,896]{6,5,4,3,2,1,0:T(8,128)(2,1)}, bf16[2,1,2,2,1,24,896]{6,5,4,3,2,1,0:T(8,128)(2,1)}, u32[]{:S(2)}, u32[]{:S(2)}) collective-permute-start(bf16[2,1,2,2,1,24,896]{6,5,4,3,2,1,0:T(8,128)(2,1)} %fusion.6), channel_id=1, source_target_pairs={{0,8},{1,9},{2,10},{3,11},{4,12},{5,13},{6,14},{7,15},{8,0},{9,1},... | collective-permute-start | bytes 1032200 | tf_op jit(solution)/shard_map/ppermute | solution.py:510
  60.6 30.8 %collective-permute-start.13 = (bf16[2,2,2,1,1,24,1536]{6,5,0,1,2,4,3:T(8,128)(2,1)}, bf16[2,2,2,1,1,24,1536]{6,5,0,1,2,4,3:T(8,128)(2,1)}, u32[]{:S(2)}, u32[]{:S(2)}) collective-permute-start(bf16[2,2,2,1,1,24,1536]{6,5,0,1,2,4,3:T(8,128)(2,1)} %maximum_select_fusion.12), channel_id=1, source_target_pairs={{0,2},{1,3},{2,0},{3,1},{4,6},{5,7},{6,4},{7,5},{8,10},{9,11},{10,... | collective-permute-start | bytes 1769480 | tf_op jit(solution)/shard_map/ppermute | solution.py:510
  69.1 24.8 %collective-permute-start.3 = (bf16[2,2,1,2,1,24,1536]{6,5,0,1,3,4,2:T(8,128)(2,1)}, bf16[2,2,1,2,1,24,1536]{6,5,0,1,3,4,2:T(8,128)(2,1)}, u32[]{:S(2)}, u32[]{:S(2)}) collective-permute-start(bf16[2,2,1,2,1,24,1536]{6,5,0,1,3,4,2:T(8,128)(2,1)} %maximum_select_fusion.10), channel_id=1, source_target_pairs={{0,4},{1,5},{2,6},{3,7},{4,0},{5,1},{6,2},{7,3},{8,12},{9,13},{10,... | collective-permute-start | bytes 1769480 | tf_op jit(solution)/shard_map/ppermute | solution.py:510
  75.4 36.5 %collective-permute-start.18 = (bf16[2,2,1,2,1,24,1536]{6,5,1,0,4,3,2:T(8,128)(2,1)}, bf16[2,2,1,2,1,24,1536]{6,5,1,0,4,3,2:T(8,128)(2,1)}, u32[]{:S(2)}, u32[]{:S(2)}) collective-permute-start(bf16[2,2,1,2,1,24,1536]{6,5,1,0,4,3,2:T(8,128)(2,1)} %maximum_select_fusion.14), channel_id=1, source_target_pairs={{0,4},{1,5},{2,6},{3,7},{4,0},{5,1},{6,2},{7,3},{8,12},{9,13},{10,... | collective-permute-start | bytes 1769480 | tf_op jit(solution)/shard_map/ppermute | solution.py:510
  77.9 38.8 %collective-permute-start.23 = (bf16[2,2,2,1,1,24,1536]{6,5,1,0,4,3,2:T(8,128)(2,1)}, bf16[2,2,2,1,1,24,1536]{6,5,1,0,4,3,2:T(8,128)(2,1)}, u32[]{:S(2)}, u32[]{:S(2)}) collective-permute-start(bf16[2,2,2,1,1,24,1536]{6,5,1,0,4,3,2:T(8,128)(2,1)} %maximum_select_fusion.16), channel_id=1, source_target_pairs={{0,2},{1,3},{2,0},{3,1},{4,6},{5,7},{6,4},{7,5},{8,10},{9,11},{10,... | collective-permute-start | bytes 1769480 | tf_op jit(solution)/shard_map/ppermute | solution.py:510
  82.2 59.9 %all-to-all-start.1 = ((bf16[4,2,196,768]{3,1,2,0:T(2,128)(2,1)}), bf16[4,2,196,768]{3,1,2,0:T(2,128)(2,1)}, u32[]{:S(2)}, u32[]{:S(2)}) async-start(bf16[4,2,196,768]{3,1,2,0:T(2,128)(2,1)} %param.31), calls=%async_computation.1 | async-start | bytes 4816896 | tf_op jit(solution)/shard_map/all_to_all | solution.py:563
  86.8 461.0 %reduce-scatter.2.cloned.1.call-start = ((), (), s32[]{:S(2)}) async-start(), calls=%async_computation.6 | async-start | bytes 9732096 | tf_op jit(solution)/shard_map/reduce_scatter | solution.py:587
  88.6 30.6 %collective-permute-start.9 = (bf16[2,2,2,2,1,24,896]{6,5,4,3,2,1,0:T(8,128)(2,1)S(1)}, bf16[2,2,2,2,1,24,896]{6,5,4,3,2,1,0:T(8,128)(2,1)S(1)}, u32[]{:S(2)}, u32[]{:S(2)}) collective-permute-start(bf16[2,2,2,2,1,24,896]{6,5,4,3,2,1,0:T(8,128)(2,1)S(1)} %maximum_select_fusion.9), channel_id=1, source_target_pairs={{0,1},{1,0},{2,3},{3,2},{4,5},{5,4},{6,7},{7,6},{8,9},{9,8},{10,11... | collective-permute-start | bytes 2064392 | tf_op jit(solution)/shard_map/ppermute | solution.py:510
  93.9 18.1 %copy-start.19 = (bf16[2,2,1,2,1,24,1536]{6,5,1,0,4,3,2:T(8,128)(2,1)S(1)}, bf16[2,2,1,2,1,24,1536]{6,5,1,0,4,3,2:T(8,128)(2,1)}, u32[]{:S(2)}) copy-start(bf16[2,2,1,2,1,24,1536]{6,5,1,0,4,3,2:T(8,128)(2,1)} %fusion.4) | copy-start | bytes 1769476
  93.9 51.9 %collective-permute-start.14 = (bf16[2,2,2,2,1,24,1536]{6,5,0,1,2,4,3:T(8,128)(2,1)}, bf16[2,2,2,2,1,24,1536]{6,5,0,1,2,4,3:T(8,128)(2,1)}, u32[]{:S(2)}, u32[]{:S(2)}) collective-permute-start(bf16[2,2,2,2,1,24,1536]{6,5,0,1,2,4,3:T(8,128)(2,1)} %maximum_select_fusion.6), channel_id=1, source_target_pairs={{0,1},{1,0},{2,3},{3,2},{4,5},{5,4},{6,7},{7,6},{8,9},{9,8},{10,11... | collective-permute-start | bytes 3538952 | tf_op jit(solution)/shard_map/ppermute | solution.py:510
  96.4 53.7 %collective-permute-start.4 = (bf16[2,2,2,2,1,24,1536]{6,5,0,1,3,4,2:T(8,128)(2,1)}, bf16[2,2,2,2,1,24,1536]{6,5,0,1,3,4,2:T(8,128)(2,1)}, u32[]{:S(2)}, u32[]{:S(2)}) collective-permute-start(bf16[2,2,2,2,1,24,1536]{6,5,0,1,3,4,2:T(8,128)(2,1)} %maximum_select_fusion.5), channel_id=1, source_target_pairs={{0,1},{1,0},{2,3},{3,2},{4,5},{5,4},{6,7},{7,6},{8,9},{9,8},{10,11... | collective-permute-start | bytes 3538952 | tf_op jit(solution)/shard_map/ppermute | solution.py:510
  114.4 40.3 %collective-permute-start.19 = (bf16[2,2,2,2,1,24,1536]{6,5,1,0,4,3,2:T(8,128)(2,1)}, bf16[2,2,2,2,1,24,1536]{6,5,1,0,4,3,2:T(8,128)(2,1)}, u32[]{:S(2)}, u32[]{:S(2)}) collective-permute-start(bf16[2,2,2,2,1,24,1536]{6,5,1,0,4,3,2:T(8,128)(2,1)} %maximum_select_fusion.7), channel_id=1, source_target_pairs={{0,1},{1,0},{2,3},{3,2},{4,5},{5,4},{6,7},{7,6},{8,9},{9,8},{10,11... | collective-permute-start | bytes 3538952 | tf_op jit(solution)/shard_map/ppermute | solution.py:510
  119.3 40.0 %collective-permute-start.24 = (bf16[2,2,2,2,1,24,1536]{6,5,1,0,4,3,2:T(8,128)(2,1)}, bf16[2,2,2,2,1,24,1536]{6,5,1,0,4,3,2:T(8,128)(2,1)S(1)}, u32[]{:S(2)}, u32[]{:S(2)}) collective-permute-start(bf16[2,2,2,2,1,24,1536]{6,5,1,0,4,3,2:T(8,128)(2,1)} %maximum_select_fusion.8), channel_id=1, source_target_pairs={{0,1},{1,0},{2,3},{3,2},{4,5},{5,4},{6,7},{7,6},{8,9},{9,8},{10,11... | collective-permute-start | bytes 3538952 | tf_op jit(solution)/shard_map/ppermute | solution.py:510
  346.4 51.7 %copy-start.2 = (bf16[768,1536]{1,0:T(8,128)(2,1)}, bf16[768,1536]{1,0:T(8,128)(2,1)S(1)}, u32[]{:S(2)}) copy-start(bf16[768,1536]{1,0:T(8,128)(2,1)S(1)} %get-tuple-element.132) | copy-start | bytes 7077892
  349.0 90.6 %collective-permute-start.40 = (bf16[2,2,2,2,1,24,1536]{6,5,4,3,2,1,0:T(8,128)(2,1)}, bf16[2,2,2,2,1,24,1536]{6,5,4,3,2,1,0:T(8,128)(2,1)}, u32[]{:S(2)}, u32[]{:S(2)}) collective-permute-start(bf16[2,2,2,2,1,24,1536]{6,5,4,3,2,1,0:T(8,128)(2,1)} %constant_dynamic-slice_fusion.9), channel_id=1, source_target_pairs={{0,1},{1,0},{2,3},{3,2},{4,5},{5,4},{6,7},{7,6},{8,9},{9,8},{10,11... | collective-permute-start | bytes 3538952 | tf_op jit(solution)/shard_map/ppermute | solution.py:510
  349.0 41.3 %copy-start.34 = (f32[8,768]{1,0:T(8,128)S(1)}, f32[8,768]{1,0:T(8,128)}, u32[]{:S(2)}) copy-start(f32[8,768]{1,0:T(8,128)} %get-tuple-element.52) | copy-start | bytes 73732
  397.5 20.2 %collective-permute-start.25 = (bf16[2,2,2,2,1,24,896]{6,5,4,3,2,1,0:T(8,128)(2,1)S(1)}, bf16[2,2,2,2,1,24,896]{6,5,4,3,2,1,0:T(8,128)(2,1)}, u32[]{:S(2)}, u32[]{:S(2)}) collective-permute-start(bf16[2,2,2,2,1,24,896]{6,5,4,3,2,1,0:T(8,128)(2,1)S(1)} %constant_dynamic-slice_fusion.24), channel_id=1, source_target_pairs={{0,1},{1,0},{2,3},{3,2},{4,5},{5,4},{6,7},{7,6},{8,9},{9,8},{10,11... | collective-permute-start | bytes 2064392 | tf_op jit(solution)/shard_map/ppermute | solution.py:510
  399.3 43.7 %collective-permute-start.45 = (bf16[2,2,2,2,1,24,1536]{6,5,4,3,2,1,0:T(8,128)(2,1)}, bf16[2,2,2,2,1,24,1536]{6,5,4,3,2,1,0:T(8,128)(2,1)}, u32[]{:S(2)}, u32[]{:S(2)}) collective-permute-start(bf16[2,2,2,2,1,24,1536]{6,5,4,3,2,1,0:T(8,128)(2,1)} %constant_dynamic-slice_fusion.4), channel_id=1, source_target_pairs={{0,1},{1,0},{2,3},{3,2},{4,5},{5,4},{6,7},{7,6},{8,9},{9,8},{10,11... | collective-permute-start | bytes 3538952 | tf_op jit(solution)/shard_map/ppermute | solution.py:510
  420.4 16.4 %collective-permute-start.26 = (bf16[2,1,2,2,1,24,896]{6,5,4,3,2,1,0:T(8,128)(2,1)}, bf16[2,1,2,2,1,24,896]{6,5,4,3,2,1,0:T(8,128)(2,1)S(1)}, u32[]{:S(2)}, u32[]{:S(2)}) collective-permute-start(bf16[2,1,2,2,1,24,896]{6,5,4,3,2,1,0:T(8,128)(2,1)} %constant_dynamic-slice_fusion.23), channel_id=1, source_target_pairs={{0,8},{1,9},{2,10},{3,11},{4,12},{5,13},{6,14},{7,15},{8,0},{9,1},... | collective-permute-start | bytes 1032200 | tf_op jit(solution)/shard_map/ppermute | solution.py:510
  423.1 24.6 %collective-permute-start.30 = (bf16[2,2,2,2,1,24,1536]{6,5,4,3,2,1,0:T(8,128)(2,1)}, bf16[2,2,2,2,1,24,1536]{6,5,4,3,2,1,0:T(8,128)(2,1)}, u32[]{:S(2)}, u32[]{:S(2)}) collective-permute-start(bf16[2,2,2,2,1,24,1536]{6,5,4,3,2,1,0:T(8,128)(2,1)} %constant_dynamic-slice_fusion.19), channel_id=1, source_target_pairs={{0,1},{1,0},{2,3},{3,2},{4,5},{5,4},{6,7},{7,6},{8,9},{9,8},{10,11... | collective-permute-start | bytes 3538952 | tf_op jit(solution)/shard_map/ppermute | solution.py:510
  424.3 28.4 %collective-permute-start.35 = (bf16[2,2,2,2,1,24,1536]{6,5,4,3,2,1,0:T(8,128)(2,1)}, bf16[2,2,2,2,1,24,1536]{6,5,4,3,2,1,0:T(8,128)(2,1)}, u32[]{:S(2)}, u32[]{:S(2)}) collective-permute-start(bf16[2,2,2,2,1,24,1536]{6,5,4,3,2,1,0:T(8,128)(2,1)} %constant_dynamic-slice_fusion.14), channel_id=1, source_target_pairs={{0,1},{1,0},{2,3},{3,2},{4,5},{5,4},{6,7},{7,6},{8,9},{9,8},{10,11... | collective-permute-start | bytes 3538952 | tf_op jit(solution)/shard_map/ppermute | solution.py:510
  428.0 56.0 %all-to-all-start.3 = ((bf16[4,2,196,768]{3,1,2,0:T(2,128)(2,1)}), bf16[4,2,196,768]{3,1,2,0:T(2,128)(2,1)S(1)}, u32[]{:S(2)}, u32[]{:S(2)}) async-start(bf16[4,2,196,768]{3,1,2,0:T(2,128)(2,1)} %copy.295), calls=%async_computation.3 | async-start | bytes 4816896 | tf_op jit(solution)/shard_map/all_to_all | solution.py:567
  431.7 7.9 %copy-start.5 = (bf16[768,1536]{1,0:T(8,128)(2,1)S(1)}, bf16[768,1536]{1,0:T(8,128)(2,1)}, u32[]{:S(2)}) copy-start(bf16[768,1536]{1,0:T(8,128)(2,1)} %copy-done.4) | copy-start | bytes 7077892
  436.9 14.4 %collective-permute-start.27 = (bf16[1,1,2,2,1,24,896]{6,5,4,3,2,1,0:T(8,128)(2,1)S(1)}, bf16[1,1,2,2,1,24,896]{6,5,4,3,2,1,0:T(8,128)(2,1)S(1)}, u32[]{:S(2)}, u32[]{:S(2)}) collective-permute-start(bf16[1,1,2,2,1,24,896]{6,5,4,3,2,1,0:T(8,128)(2,1)S(1)} %constant_dynamic-slice_fusion.22), channel_id=1, source_target_pairs={{0,16},{1,17},{2,18},{3,19},{4,20},{5,21},{6,22},{7,23},{8,24},{9,... | collective-permute-start | bytes 516104 | tf_op jit(solution)/shard_map/ppermute | solution.py:510
  441.4 38.4 %collective-permute-start.41 = (bf16[2,2,1,2,1,24,1536]{6,5,4,3,2,1,0:T(8,128)(2,1)S(1)}, bf16[2,2,1,2,1,24,1536]{6,5,4,3,2,1,0:T(8,128)(2,1)}, u32[]{:S(2)}, u32[]{:S(2)}) collective-permute-start(bf16[2,2,1,2,1,24,1536]{6,5,4,3,2,1,0:T(8,128)(2,1)S(1)} %constant_dynamic-slice_fusion.8), channel_id=1, source_target_pairs={{0,4},{1,5},{2,6},{3,7},{4,0},{5,1},{6,2},{7,3},{8,12},{9,13},{10,... | collective-permute-start | bytes 1769480 | tf_op jit(solution)/shard_map/ppermute | solution.py:510
  445.7 43.1 %collective-permute-start.46 = (bf16[2,2,2,1,1,24,1536]{6,5,4,3,2,1,0:T(8,128)(2,1)}, bf16[2,2,2,1,1,24,1536]{6,5,4,3,2,1,0:T(8,128)(2,1)}, u32[]{:S(2)}, u32[]{:S(2)}) collective-permute-start(bf16[2,2,2,1,1,24,1536]{6,5,4,3,2,1,0:T(8,128)(2,1)} %constant_dynamic-slice_fusion.3), channel_id=1, source_target_pairs={{0,2},{1,3},{2,0},{3,1},{4,6},{5,7},{6,4},{7,5},{8,10},{9,11},{10,... | collective-permute-start | bytes 1769480 | tf_op jit(solution)/shard_map/ppermute | solution.py:510
  450.5 42.1 %collective-permute-start.31 = (bf16[2,2,1,2,1,24,1536]{6,5,4,3,2,1,0:T(8,128)(2,1)}, bf16[2,2,1,2,1,24,1536]{6,5,4,3,2,1,0:T(8,128)(2,1)}, u32[]{:S(2)}, u32[]{:S(2)}) collective-permute-start(bf16[2,2,1,2,1,24,1536]{6,5,4,3,2,1,0:T(8,128)(2,1)} %constant_dynamic-slice_fusion.18), channel_id=1, source_target_pairs={{0,4},{1,5},{2,6},{3,7},{4,0},{5,1},{6,2},{7,3},{8,12},{9,13},{10,... | collective-permute-start | bytes 1769480 | tf_op jit(solution)/shard_map/ppermute | solution.py:510
  451.5 20.0 %collective-permute-start.28 = (bf16[1,1,1,2,1,24,896]{6,5,4,3,2,1,0:T(8,128)(2,1)S(1)}, bf16[1,1,1,2,1,24,896]{6,5,4,3,2,1,0:T(8,128)(2,1)S(1)}, u32[]{:S(2)}, u32[]{:S(2)}) collective-permute-start(bf16[1,1,1,2,1,24,896]{6,5,4,3,2,1,0:T(8,128)(2,1)S(1)} %constant_dynamic-slice_fusion.21), channel_id=1, source_target_pairs={{0,4},{1,5},{2,6},{3,7},{4,0},{5,1},{6,2},{7,3},{8,12},{9,13},{10,... | collective-permute-start | bytes 258056 | tf_op jit(solution)/shard_map/ppermute | solution.py:510
  454.3 18.9 %copy-start.16 = (bf16[2,2,2,2,1,24,1536]{6,5,4,3,2,1,0:T(8,128)(2,1)}, bf16[2,2,2,2,1,24,1536]{6,5,4,3,2,1,0:T(8,128)(2,1)S(1)}, u32[]{:S(2)}) copy-start(bf16[2,2,2,2,1,24,1536]{6,5,4,3,2,1,0:T(8,128)(2,1)S(1)} %add_convert_fusion.2) | copy-start | bytes 3538948
  471.5 4.1 collective-permute-start.29
  474.1 22.6 %collective-permute-start.36 = (bf16[2,2,2,1,1,24,1536]{6,5,4,3,2,1,0:T(8,128)(2,1)}, bf16[2,2,2,1,1,24,1536]{6,5,4,3,2,1,0:T(8,128)(2,1)}, u32[]{:S(2)}, u32[]{:S(2)}) collective-permute-start(bf16[2,2,2,1,1,24,1536]{6,5,4,3,2,1,0:T(8,128)(2,1)} %constant_dynamic-slice_fusion.13), channel_id=1, source_target_pairs={{0,2},{1,3},{2,0},{3,1},{4,6},{5,7},{6,4},{7,5},{8,10},{9,11},{10,... | collective-permute-start | bytes 1769480 | tf_op jit(solution)/shard_map/ppermute | solution.py:510
  481.9 40.9 %collective-permute-start.42 = (bf16[2,2,1,1,1,24,1536]{6,5,4,3,2,1,0:T(8,128)(2,1)}, bf16[2,2,1,1,1,24,1536]{6,5,4,3,2,1,0:T(8,128)(2,1)S(1)}, u32[]{:S(2)}, u32[]{:S(2)}) collective-permute-start(bf16[2,2,1,1,1,24,1536]{6,5,4,3,2,1,0:T(8,128)(2,1)} %constant_dynamic-slice_fusion.7), channel_id=1, source_target_pairs={{0,2},{1,3},{2,0},{3,1},{4,6},{5,7},{6,4},{7,5},{8,10},{9,11},{10,... | collective-permute-start | bytes 884744 | tf_op jit(solution)/shard_map/ppermute | solution.py:510
  484.0 38.8 %all-to-all-start.2 = ((bf16[4,2,196,768]{3,1,2,0:T(2,128)(2,1)}), bf16[4,2,196,768]{3,1,2,0:T(2,128)(2,1)}, u32[]{:S(2)}, u32[]{:S(2)}) async-start(bf16[4,2,196,768]{3,1,2,0:T(2,128)(2,1)} %copy.294), calls=%async_computation.2 | async-start | bytes 4816896 | tf_op jit(solution)/shard_map/all_to_all | solution.py:567
  491.1 32.3 %collective-permute-start.47 = (bf16[2,2,1,1,1,24,1536]{6,5,4,3,2,1,0:T(8,128)(2,1)}, bf16[2,2,1,1,1,24,1536]{6,5,4,3,2,1,0:T(8,128)(2,1)}, u32[]{:S(2)}, u32[]{:S(2)}) collective-permute-start(bf16[2,2,1,1,1,24,1536]{6,5,4,3,2,1,0:T(8,128)(2,1)} %constant_dynamic-slice_fusion.2), channel_id=1, source_target_pairs={{0,4},{1,5},{2,6},{3,7},{4,0},{5,1},{6,2},{7,3},{8,12},{9,13},{10,... | collective-permute-start | bytes 884744 | tf_op jit(solution)/shard_map/ppermute | solution.py:510
  494.6 32.3 %collective-permute-start.32 = (bf16[2,2,1,1,1,24,1536]{6,5,4,3,2,1,0:T(8,128)(2,1)}, bf16[2,2,1,1,1,24,1536]{6,5,4,3,2,1,0:T(8,128)(2,1)}, u32[]{:S(2)}, u32[]{:S(2)}) collective-permute-start(bf16[2,2,1,1,1,24,1536]{6,5,4,3,2,1,0:T(8,128)(2,1)} %constant_dynamic-slice_fusion.17), channel_id=1, source_target_pairs={{0,2},{1,3},{2,0},{3,1},{4,6},{5,7},{6,4},{7,5},{8,10},{9,11},{10,... | collective-permute-start | bytes 884744 | tf_op jit(solution)/shard_map/ppermute | solution.py:510
  499.4 29.2 %collective-permute-start.37 = (bf16[2,2,1,1,1,24,1536]{6,5,4,3,2,1,0:T(8,128)(2,1)}, bf16[2,2,1,1,1,24,1536]{6,5,4,3,2,1,0:T(8,128)(2,1)}, u32[]{:S(2)}, u32[]{:S(2)}) collective-permute-start(bf16[2,2,1,1,1,24,1536]{6,5,4,3,2,1,0:T(8,128)(2,1)} %constant_dynamic-slice_fusion.12), channel_id=1, source_target_pairs={{0,4},{1,5},{2,6},{3,7},{4,0},{5,1},{6,2},{7,3},{8,12},{9,13},{10,... | collective-permute-start | bytes 884744 | tf_op jit(solution)/shard_map/ppermute | solution.py:510
  522.9 8.3 %collective-permute-start.43 = (bf16[2,1,1,1,1,24,1536]{6,5,4,3,2,1,0:T(8,128)(2,1)S(1)}, bf16[2,1,1,1,1,24,1536]{6,5,4,3,2,1,0:T(8,128)(2,1)S(1)}, u32[]{:S(2)}, u32[]{:S(2)}) collective-permute-start(bf16[2,1,1,1,1,24,1536]{6,5,4,3,2,1,0:T(8,128)(2,1)S(1)} %constant_dynamic-slice_fusion.6), channel_id=1, source_target_pairs={{0,8},{1,9},{2,10},{3,11},{4,12},{5,13},{6,14},{7,15},{8,0},{9,1},... | collective-permute-start | bytes 442376 | tf_op jit(solution)/shard_map/ppermute | solution.py:510
  524.9 7.5 %collective-permute-start.48 = (bf16[2,1,1,1,1,24,1536]{6,5,4,3,2,1,0:T(8,128)(2,1)S(1)}, bf16[2,1,1,1,1,24,1536]{6,5,4,3,2,1,0:T(8,128)(2,1)S(1)}, u32[]{:S(2)}, u32[]{:S(2)}) collective-permute-start(bf16[2,1,1,1,1,24,1536]{6,5,4,3,2,1,0:T(8,128)(2,1)S(1)} %constant_dynamic-slice_fusion.1), channel_id=1, source_target_pairs={{0,8},{1,9},{2,10},{3,11},{4,12},{5,13},{6,14},{7,15},{8,0},{9,1},... | collective-permute-start | bytes 442376 | tf_op jit(solution)/shard_map/ppermute | solution.py:510
  528.0 9.3 %collective-permute-start.33 = (bf16[2,1,1,1,1,24,1536]{6,5,4,3,2,1,0:T(8,128)(2,1)S(1)}, bf16[2,1,1,1,1,24,1536]{6,5,4,3,2,1,0:T(8,128)(2,1)S(1)}, u32[]{:S(2)}, u32[]{:S(2)}) collective-permute-start(bf16[2,1,1,1,1,24,1536]{6,5,4,3,2,1,0:T(8,128)(2,1)S(1)} %constant_dynamic-slice_fusion.16), channel_id=1, source_target_pairs={{0,8},{1,9},{2,10},{3,11},{4,12},{5,13},{6,14},{7,15},{8,0},{9,1},... | collective-permute-start | bytes 442376 | tf_op jit(solution)/shard_map/ppermute | solution.py:510
  529.6 10.0 %collective-permute-start.38 = (bf16[2,1,1,1,1,24,1536]{6,5,4,3,2,1,0:T(8,128)(2,1)S(1)}, bf16[2,1,1,1,1,24,1536]{6,5,4,3,2,1,0:T(8,128)(2,1)S(1)}, u32[]{:S(2)}, u32[]{:S(2)}) collective-permute-start(bf16[2,1,1,1,1,24,1536]{6,5,4,3,2,1,0:T(8,128)(2,1)S(1)} %constant_dynamic-slice_fusion.11), channel_id=1, source_target_pairs={{0,8},{1,9},{2,10},{3,11},{4,12},{5,13},{6,14},{7,15},{8,0},{9,1},... | collective-permute-start | bytes 442376 | tf_op jit(solution)/shard_map/ppermute | solution.py:510
  531.3 9.2 %collective-permute-start.44 = (bf16[1,1,1,1,1,24,1536]{6,5,4,3,2,1,0:T(8,128)(2,1)S(1)}, bf16[1,1,1,1,1,24,1536]{6,5,4,3,2,1,0:T(8,128)(2,1)S(1)}, u32[]{:S(2)}, u32[]{:S(2)}) collective-permute-start(bf16[1,1,1,1,1,24,1536]{6,5,4,3,2,1,0:T(8,128)(2,1)S(1)} %constant_dynamic-slice_fusion.5), channel_id=1, source_target_pairs={{0,16},{1,17},{2,18},{3,19},{4,20},{5,21},{6,22},{7,23},{8,24},{9,... | collective-permute-start | bytes 221192 | tf_op jit(solution)/shard_map/ppermute | solution.py:510
  532.5 10.8 %collective-permute-start.49 = (bf16[1,1,1,1,1,24,1536]{6,5,4,3,2,1,0:T(8,128)(2,1)S(1)}, bf16[1,1,1,1,1,24,1536]{6,5,4,3,2,1,0:T(8,128)(2,1)S(1)}, u32[]{:S(2)}, u32[]{:S(2)}) collective-permute-start(bf16[1,1,1,1,1,24,1536]{6,5,4,3,2,1,0:T(8,128)(2,1)S(1)} %constant_dynamic-slice_fusion), channel_id=1, source_target_pairs={{0,16},{1,17},{2,18},{3,19},{4,20},{5,21},{6,22},{7,23},{8,24},{9,... | collective-permute-start | bytes 221192 | tf_op jit(solution)/shard_map/ppermute | solution.py:510
  537.4 7.5 %collective-permute-start.34 = (bf16[1,1,1,1,1,24,1536]{6,5,4,3,2,1,0:T(8,128)(2,1)S(1)}, bf16[1,1,1,1,1,24,1536]{6,5,4,3,2,1,0:T(8,128)(2,1)S(1)}, u32[]{:S(2)}, u32[]{:S(2)}) collective-permute-start(bf16[1,1,1,1,1,24,1536]{6,5,4,3,2,1,0:T(8,128)(2,1)S(1)} %constant_dynamic-slice_fusion.15), channel_id=1, source_target_pairs={{0,16},{1,17},{2,18},{3,19},{4,20},{5,21},{6,22},{7,23},{8,24},{9,... | collective-permute-start | bytes 221192 | tf_op jit(solution)/shard_map/ppermute | solution.py:510
  539.7 6.1 %collective-permute-start.39 = (bf16[1,1,1,1,1,24,1536]{6,5,4,3,2,1,0:T(8,128)(2,1)S(1)}, bf16[1,1,1,1,1,24,1536]{6,5,4,3,2,1,0:T(8,128)(2,1)S(1)}, u32[]{:S(2)}, u32[]{:S(2)}) collective-permute-start(bf16[1,1,1,1,1,24,1536]{6,5,4,3,2,1,0:T(8,128)(2,1)S(1)} %constant_dynamic-slice_fusion.10), channel_id=1, source_target_pairs={{0,16},{1,17},{2,18},{3,19},{4,20},{5,21},{6,22},{7,23},{8,24},{9,... | collective-permute-start | bytes 221192 | tf_op jit(solution)/shard_map/ppermute | solution.py:510
  (36 other events, 150.9 us)
Sparse Core Ops, SparseCore 0:
  11.9 119.0 all-gather.1
  286.7 135.9 reduce-scatter.1

commit v3 on v2

v3 whole, which is shorter than its diff:
```python
import functools

import jax
import jax.numpy as jnp
from jax import lax
from jax.experimental import pallas as pl
from jax.experimental.pallas import tpu as pltpu
from jax.sharding import PartitionSpec as P

HEADS = 12
HEAD_DIM = 64
PAIR = 2 * HEAD_DIM
PAIRS = HEADS // 2
TILE = 16
GROUP_T = 6
GROUP_S = 2
GROUP_SB = 1
GROUP_TB = 3
LOW = -1e30
BF = jnp.bfloat16
F32 = jnp.float32


def dot_nn(a, b):
    return lax.dot_general(a, b, (((1,), (0,)), ((), ())), preferred_element_type=F32)


def dot_nt(a, b):
    return lax.dot_general(a, b, (((1,), (1,)), ((), ())), preferred_element_type=F32)


def dot_tn(a, b):
    return lax.dot_general(a, b, (((0,), (0,)), ((), ())), preferred_element_type=F32)


def normalize(values):
    center = values - jnp.mean(values, axis=-1, keepdims=True)
    scale = lax.rsqrt(jnp.mean(center * center, axis=-1, keepdims=True) + 1e-05)
    return center * scale, scale


def norm_back(unit, scale, gain, grad):
    graded = grad * gain
    shift = jnp.mean(graded, axis=-1, keepdims=True)
    slope = jnp.mean(graded * unit, axis=-1, keepdims=True)
    return scale * (graded - shift - unit * slope)


def rows_of(block):
    return block.reshape(block.shape[0] * block.shape[1], block.shape[2])


def col_sum(values):
    return jnp.sum(values, axis=0, keepdims=True)


def lane_halves(shape):
    return lax.broadcasted_iota(jnp.int32, shape, len(shape) - 1) < HEAD_DIM


def half_masks():
    low_half = lane_halves((1, PAIR))
    return (
        jnp.where(low_half, 1.0, 0.0).astype(BF),
        jnp.where(low_half, 0.0, 1.0).astype(BF),
    )


def heads_forward(tiles, bias):
    low_mask, high_mask = half_masks()
    scale = HEAD_DIM ** (-0.5)
    scores = []
    for query, key, value in tiles:
        for mask in (low_mask, high_mask):
            scores.append(dot_nt(query * (mask * scale), key) + bias)
    tops = [jnp.max(s, axis=-1, keepdims=True) for s in scores]
    shares = [jnp.exp(s - top).astype(BF) for s, top in zip(scores, tops)]
    outs = []
    for at, share in enumerate(shares):
        value = tiles[at // 2][2]
        outs.append(dot_nn(share, jnp.concatenate([value, jnp.ones_like(value)], axis=1)))
    mixed = []
    for at in range(len(tiles)):
        first, second = outs[2 * at], outs[2 * at + 1]
        low_half = lane_halves((first.shape[0], PAIR))
        top = jnp.where(low_half, first[:, :PAIR], second[:, :PAIR])
        total = jnp.where(low_half, first[:, PAIR:], second[:, PAIR:])
        mixed.append((top / total).astype(BF))
    return mixed


def heads_backward(tiles, bias):
    low_mask, high_mask = half_masks()
    scale = HEAD_DIM ** (-0.5)
    turned = [key.T for query, key, value, grad in tiles]
    queries, grads, scores, grad_shares = [], [], [], []
    for query, key, value, grad in tiles:
        for mask in (low_mask, high_mask):
            queries.append(query * (mask * scale))
            grads.append(grad * mask)
            scores.append(dot_nt(key, queries[-1]) + bias)
            grad_shares.append(dot_nt(value, grads[-1]))
    tops = [jnp.max(s, axis=0, keepdims=True) for s in scores]
    raw = [jnp.exp(s - top) for s, top in zip(scores, tops)]
    inverse = [1.0 / jnp.sum(e, axis=0, keepdims=True) for e in raw]
    shares = [e * i for e, i in zip(raw, inverse)]
    terms = [jnp.sum(g * p, axis=0, keepdims=True) for g, p in zip(grad_shares, shares)]
    grad_scores = [(p * (g - t)).astype(BF) for p, g, t in zip(shares, grad_shares, terms)]
    shares = [p.astype(BF) for p in shares]
    out = []
    for at in range(len(tiles)):
        a, b = 2 * at, 2 * at + 1
        grad_value = dot_nn(shares[a], grads[a]) + dot_nn(shares[b], grads[b])
        grad_key = dot_nn(grad_scores[a], queries[a]) + dot_nn(grad_scores[b], queries[b])
        key_turned = turned[at]
        grad_query = jnp.concatenate(
            [dot_nn(key_turned[:HEAD_DIM], grad_scores[a]), dot_nn(key_turned[HEAD_DIM:], grad_scores[b])], axis=0
        )
        out.append(((grad_query * scale).astype(BF).T, grad_key.astype(BF), grad_value.astype(BF)))
    return out


def place_mask(size):
    row = lax.broadcasted_iota(jnp.int32, (size, size), 0)
    col = lax.broadcasted_iota(jnp.int32, (size, size), 1)
    return jnp.where(((row ^ col) & (TILE - 1)) == 0, 0.0, LOW)


def pair_cols(part, pair, width):
    start = part * width + pair * PAIR
    return slice(start, start + PAIR)


def temporal_project(x_ref, qk_ref, v_in_ref, v_ref, norm_ref, joined_ref):
    chunk, padded, width = x_ref.shape
    unit, scale = normalize(rows_of(x_ref[...]).astype(F32))
    norm = (unit * v_ref[0:1] + v_ref[1:2]).astype(BF)
    norm_ref[...] = norm.reshape(chunk, padded, width)
    for part in range(3):
        cols = slice(part * width, (part + 1) * width)
        weight = qk_ref[:, cols] if part < 2 else v_in_ref[:, :width]
        joined_ref[:, :, cols] = dot_nn(norm, weight).astype(BF).reshape(chunk, padded, width)


def temporal_attend(joined_ref, mixed_ref):
    frames, tile, width = mixed_ref.shape
    bias = place_mask(frames * tile)
    for first in range(0, PAIRS, GROUP_T):
        group = range(first, first + GROUP_T)
        tiles = [[rows_of(joined_ref[:, :, pair_cols(i, pair, width)]) for i in range(3)] for pair in group]
        for pair, mixed in zip(group, heads_forward(tiles, bias)):
            mixed_ref[:, :, pair_cols(0, pair, width)] = mixed.reshape(frames, tile, PAIR)


def temporal_finish(x_ref, mixed_ref, ol_ref, v_ref, proj_ref, after_ref):
    chunk, padded, width = x_ref.shape
    proj = (dot_nn(rows_of(mixed_ref[...]), ol_ref[:, :width]) + v_ref[2:3]).astype(BF)
    proj_ref[...] = proj.reshape(chunk, padded, width)
    branch = (dot_nn(proj, ol_ref[:, width:]) + v_ref[3:4]).astype(BF)
    after = rows_of(x_ref[...]).astype(F32) + branch.astype(F32)
    after_ref[...] = after.reshape(chunk, padded, width)


def spatial_forward(places, after_ref, s_ref, v_ref, norm_ref, joined_ref, mixed_ref, space_ref):
    chunk, padded, width = after_ref.shape
    after = rows_of(after_ref[...])
    unit, scale = normalize(after)
    norm = (unit * v_ref[4:5] + v_ref[5:6]).astype(BF)
    norm_ref[...] = norm.reshape(chunk, padded, width)
    for part in range(3):
        cols = slice(part * width, (part + 1) * width)
        joined_ref[:, :, cols] = dot_nn(norm, s_ref[:, cols]).astype(BF).reshape(chunk, padded, width)
    allowed = jnp.where(lax.broadcasted_iota(jnp.int32, (1, padded), 1) < places, 0.0, LOW)
    for frame in range(chunk):
        for first in range(0, PAIRS, GROUP_S):
            group = range(first, first + GROUP_S)
            tiles = [[joined_ref[frame, :, pair_cols(i, pair, width)] for i in range(3)] for pair in group]
            for pair, mixed in zip(group, heads_forward(tiles, allowed)):
                mixed_ref[frame, :, pair_cols(0, pair, width)] = mixed
    space = after + dot_nn(rows_of(mixed_ref[...]), s_ref[:, 3 * width :]) + v_ref[6:7]
    space_ref[...] = space.reshape(chunk, padded, width)


def gelu_parts(hidden):
    phi = 0.5 * (1.0 + lax.erf(hidden * 0.7071067811865476))
    density = jnp.exp(-0.5 * hidden * hidden) * 0.3989422804014327
    return phi, density


def feed_both(places, space_ref, cot_ref, w1_ref, w2_ref, v_ref, out_ref, grad_ref, norm_ref, active_ref, dhid_ref, vec_ref):
    chunk, padded, width = space_ref.shape
    blocks = w1_ref.shape[1] // width

    @pl.when(pl.program_id(0) == 0)
    def _():
        vec_ref[...] = jnp.zeros_like(vec_ref)

    space = rows_of(space_ref[...])
    cot = rows_of(cot_ref[...])
    unit, scale = normalize(space)
    norm = (unit * v_ref[7:8] + v_ref[8:9]).astype(BF)
    norm_ref[...] = norm.reshape(chunk, padded, width)
    out = space + v_ref[9:10]
    d_norm = jnp.zeros_like(space)
    for block in range(blocks):
        cols = slice(block * width, (block + 1) * width)
        hidden = dot_nn(norm, w1_ref[:, cols]) + v_ref[10 + block : 11 + block]
        phi, density = gelu_parts(hidden)
        active = (hidden * phi).astype(BF)
        active_ref[:, :, cols] = active.reshape(chunk, padded, width)
        out += dot_nn(active, w2_ref[:, cols])
        d_hidden = dot_nt(cot, w2_ref[:, cols]) * (phi + hidden * density)
        vec_ref[3 + block : 4 + block] += col_sum(d_hidden.astype(BF).astype(F32))
        d_hidden = d_hidden.astype(BF)
        dhid_ref[:, :, cols] = d_hidden.reshape(chunk, padded, width)
        d_norm += dot_nt(d_hidden, w1_ref[:, cols])
    for frame in range(chunk):
        out_ref[frame] = out[frame * padded : frame * padded + places].astype(BF)
    vec_ref[0:1] += col_sum(d_norm * unit)
    vec_ref[1:2] += col_sum(d_norm)
    vec_ref[2:3] += col_sum(cot.astype(F32))
    grad = cot.astype(F32) + norm_back(unit, scale, v_ref[7:8], d_norm)
    grad_ref[...] = grad.reshape(chunk, padded, width)


def feed_grads(norm_ref, dhid_ref, active_ref, cot_ref, out_ref, norm_turned, cot_turned):
    width = norm_ref.shape[1]

    @pl.when(pl.program_id(0) == 0)
    def _():
        norm_turned[...] = norm_ref[...].T
        cot_turned[...] = cot_ref[...].T

    out_ref[:, :width] = dot_nn(norm_turned[...], dhid_ref[...]).astype(BF)
    out_ref[:, width:] = dot_nn(cot_turned[...], active_ref[...]).astype(BF).T


def spatial_back(places, grad_ref, after_ref, joined_ref, s_ref, v_ref, dspace_ref, djoin_ref, dat_ref, dtime_ref, vec_ref, dmix_ref):
    chunk, padded, width = grad_ref.shape

    @pl.when(pl.program_id(0) == 0)
    def _():
        vec_ref[...] = jnp.zeros_like(vec_ref)

    grad = rows_of(grad_ref[...])
    d_space = grad.astype(BF)
    dspace_ref[...] = d_space.reshape(chunk, padded, width)
    vec_ref[2:3] += col_sum(d_space.astype(F32))
    dmix_ref[...] = dot_nt(d_space, s_ref[:, 3 * width :]).astype(BF).reshape(chunk, padded, width)
    allowed = jnp.where(lax.broadcasted_iota(jnp.int32, (padded, 1), 0) < places, 0.0, LOW)
    for frame in range(chunk):
        for first in range(0, PAIRS, GROUP_SB):
            group = range(first, first + GROUP_SB)
            tiles = [
                [joined_ref[frame, :, pair_cols(i, pair, width)] for i in range(3)]
                + [dmix_ref[frame, :, pair_cols(0, pair, width)]]
                for pair in group
            ]
            for pair, grads in zip(group, heads_backward(tiles, allowed)):
                for i in range(3):
                    djoin_ref[frame, :, pair_cols(i, pair, width)] = grads[i]
    d_joined = rows_of(djoin_ref[...])
    d_norm = dot_nt(d_joined, s_ref[:, : 3 * width])
    unit, scale = normalize(rows_of(after_ref[...]))
    vec_ref[0:1] += col_sum(d_norm * unit)
    vec_ref[1:2] += col_sum(d_norm)
    d_time = grad + norm_back(unit, scale, v_ref[4:5], d_norm)
    dat_ref[...] = d_time.reshape(chunk, padded, width)
    dtime_ref[...] = d_time.astype(BF).reshape(chunk, padded, width)


def turned_grads(count, norm_ref, djoin_ref, *refs):
    i = pl.program_id(0)
    out_ref, norm_turned = refs[-2:]

    @pl.when(i == 0)
    def _():
        norm_turned[...] = norm_ref[...].T

    @pl.when(i < count)
    def _():
        out_ref[...] = dot_nn(norm_turned[...], djoin_ref[...]).astype(BF)

    if len(refs) > 2:

        @pl.when(i == count)
        def _():
            out_ref[...] = dot_tn(refs[0][...], refs[1][...]).astype(BF)


def temporal_back_project(dtime_ref, ol_ref, dproj_ref, dmix_ref, vec_ref):
    chunk, padded, width = dtime_ref.shape

    @pl.when(pl.program_id(0) == 0)
    def _():
        vec_ref[...] = jnp.zeros_like(vec_ref)

    d_time = rows_of(dtime_ref[...])
    vec_ref[1:2] += col_sum(d_time.astype(F32))
    d_proj = dot_nt(d_time, ol_ref[:, width:]).astype(BF)
    vec_ref[0:1] += col_sum(d_proj.astype(F32))
    dproj_ref[...] = d_proj.reshape(chunk, padded, width)
    dmix_ref[...] = dot_nt(d_proj, ol_ref[:, :width]).astype(BF).reshape(chunk, padded, width)


def temporal_back_attend(joined_ref, dmix_ref, djoin_ref):
    frames, tile, width = dmix_ref.shape
    bias = place_mask(frames * tile)
    for first in range(0, PAIRS, GROUP_TB):
        group = range(first, first + GROUP_TB)
        tiles = [
            [rows_of(joined_ref[:, :, pair_cols(i, pair, width)]) for i in range(3)]
            + [rows_of(dmix_ref[:, :, pair_cols(0, pair, width)])]
            for pair in group
        ]
        for pair, grads in zip(group, heads_backward(tiles, bias)):
            for i in range(3):
                djoin_ref[:, :, pair_cols(i, pair, width)] = grads[i].reshape(frames, tile, PAIR)


def temporal_back_finish(places, dat_ref, x_ref, djoin_ref, qk_ref, v_in_ref, v_ref, gx_ref, vec_ref):
    chunk, padded, width = x_ref.shape

    @pl.when(pl.program_id(0) == 0)
    def _():
        vec_ref[...] = jnp.zeros_like(vec_ref)

    d_joined = rows_of(djoin_ref[...])
    d_norm = dot_nt(d_joined[:, : 2 * width], qk_ref[...]) + dot_nt(d_joined[:, 2 * width :], v_in_ref[:, :width])
    d_norm = d_norm.astype(BF).astype(F32)
    unit, scale = normalize(rows_of(x_ref[...]).astype(F32))
    vec_ref[0:1] += col_sum(d_norm * unit)
    vec_ref[1:2] += col_sum(d_norm)
    grad = rows_of(dat_ref[...]) + norm_back(unit, scale, v_ref[0:1], d_norm)
    gx_ref[...] = grad.astype(BF).reshape(chunk, padded, width)[:, :places]


def whole(shape):
    return pl.BlockSpec(shape, lambda *i: (0,) * len(shape))


def cost(micros):
    return pl.CostEstimate(flops=int(micros * 1e9), bytes_accessed=0, transcendentals=0)


def params(mib=60):
    return pltpu.CompilerParams(vmem_limit_bytes=mib << 20)


def shape_of(*dims, dtype=BF):
    return jax.ShapeDtypeStruct(dims, dtype)


ANYWHERE = pl.BlockSpec(memory_space=pl.ANY)


def launch(kernel, micros, args, in_specs, out_specs, out_shape, grid, scratch=(), after=()):
    count, skip = len(args), len(after)

    def body(*refs):
        kernel(*refs[:count], *refs[count + skip :])

    return pl.pallas_call(
        body,
        grid=grid,
        in_specs=list(in_specs) + [ANYWHERE] * skip,
        out_specs=out_specs,
        out_shape=out_shape,
        scratch_shapes=list(scratch),
        cost_estimate=cost(micros),
        compiler_params=params(),
    )(*args, *after)


def gate(value, *after):
    def body(*refs):
        pass

    return pl.pallas_call(
        body,
        in_specs=[ANYWHERE] * (1 + len(after)),
        out_specs=ANYWHERE,
        out_shape=jax.ShapeDtypeStruct(value.shape, value.dtype),
        input_output_aliases={0: 0},
    )(value, *after)


def frame_block(chunk, padded, width):
    return pl.BlockSpec((chunk, padded, width), lambda i: (i, 0, 0))


def place_block(frames, width):
    return pl.BlockSpec((frames, TILE, width), lambda i: (0, i, 0))


def wholes(arrays):
    return [whole(a.shape) for a in arrays]


def flat(a):
    return a.reshape(-1, a.shape[-1])


def run_temporal_project(x, qk, v_in, v, chunk=2, after=()):
    frames, padded, width = x.shape
    block, wide = frame_block(chunk, padded, width), frame_block(chunk, padded, 3 * width)
    return launch(
        temporal_project, 9, (x, qk, v_in, v), [block] + wholes((qk, v_in, v)), [block, wide],
        (shape_of(*x.shape), shape_of(frames, padded, 3 * width)), (frames // chunk,), after=after,
    )


def run_temporal_attend(joined, after=()):
    frames, padded, wide = joined.shape
    width = wide // 3
    return launch(
        temporal_attend, 14, (joined,), [place_block(frames, wide)], place_block(frames, width),
        shape_of(frames, padded, width), (padded // TILE,), after=after,
    )


def run_temporal_finish(x, mixed, ol, v, chunk=2, after=()):
    frames, padded, width = x.shape
    block = frame_block(chunk, padded, width)
    return launch(
        temporal_finish, 8, (x, mixed, ol, v), [block, block] + wholes((ol, v)), [block, block],
        (shape_of(*x.shape), shape_of(*x.shape, dtype=F32)), (frames // chunk,), after=after,
    )


def run_spatial_forward(places, attended, pack, v, chunk=2, after=()):
    frames, padded, width = attended.shape
    block, wide = frame_block(chunk, padded, width), frame_block(chunk, padded, 3 * width)
    dims = attended.shape
    return launch(
        functools.partial(spatial_forward, places), 23, (attended, pack, v),
        [block, pl.BlockSpec((width, 4 * width), lambda i: (0, 2)), whole(v.shape)],
        [block, wide, block, block],
        (shape_of(*dims), shape_of(frames, padded, 3 * width), shape_of(*dims), shape_of(*dims, dtype=F32)),
        (frames // chunk,), after=after,
    )


def run_feed(places, space, cot, pack, v, chunk=2, after=()):
    frames, padded, width = space.shape
    hidden = 4 * width
    block, wide = frame_block(chunk, padded, width), frame_block(chunk, padded, hidden)
    dims = space.shape
    return launch(
        functools.partial(feed_both, places), 45, (space, cot, pack, pack, v),
        [
            block, block,
            pl.BlockSpec((width, hidden), lambda i: (0, 0)),
            pl.BlockSpec((width, hidden), lambda i: (0, 1)),
            whole(v.shape),
        ],
        [frame_block(chunk, places, width), block, block, wide, wide, whole((8, width))],
        (
            shape_of(frames, places, width), shape_of(*dims, dtype=F32), shape_of(*dims),
            shape_of(frames, padded, hidden), shape_of(frames, padded, hidden), shape_of(8, width, dtype=F32),
        ),
        (frames // chunk,), after=after,
    )


def run_feed_grads(norm, d_hidden, active, cot, after=()):
    norm, d_hidden, active, cot = flat(norm), flat(d_hidden), flat(active), flat(cot)
    rows, width = norm.shape
    blocks = d_hidden.shape[1] // width
    part = pl.BlockSpec((rows, width), lambda i: (0, i))
    return launch(
        feed_grads, 25, (norm, d_hidden, active, cot), [whole((rows, width)), part, part, whole((rows, width))],
        pl.BlockSpec((width, 2 * width), lambda i: (0, i)), shape_of(width, 2 * width * blocks), (blocks,),
        scratch=[pltpu.VMEM((width, rows), BF), pltpu.VMEM((width, rows), BF)], after=after,
    )


def run_spatial_back(places, grad, attended, joined, pack, v, chunk=2, after=()):
    frames, padded, width = grad.shape
    block, wide = frame_block(chunk, padded, width), frame_block(chunk, padded, 3 * width)
    dims = grad.shape
    return launch(
        functools.partial(spatial_back, places), 42, (grad, attended, joined, pack, v),
        [block, block, wide, pl.BlockSpec((width, 4 * width), lambda i: (0, 2)), whole(v.shape)],
        [block, wide, block, block, whole((8, width))],
        (
            shape_of(*dims), shape_of(frames, padded, 3 * width), shape_of(*dims, dtype=F32), shape_of(*dims),
            shape_of(8, width, dtype=F32),
        ),
        (frames // chunk,), scratch=[pltpu.VMEM((chunk, padded, width), BF)], after=after,
    )


def run_join_grads(norm, d_joined, *more, after=()):
    norm, d_joined = flat(norm), flat(d_joined)
    more = [flat(a) for a in more]
    rows, width = norm.shape
    count = d_joined.shape[1] // width
    steps = count + (1 if more else 0)
    return launch(
        functools.partial(turned_grads, count), 4 * steps, (norm, d_joined, *more),
        [whole((rows, width)), pl.BlockSpec((rows, width), lambda i: (0, jnp.minimum(i, count - 1)))] + wholes(more),
        pl.BlockSpec((width, width), lambda i: (0, i)), shape_of(width, steps * width), (steps,),
        scratch=[pltpu.VMEM((width, rows), BF)], after=after,
    )


def feed_out(n, g_ref, w1_ref, w2_ref):
    rows, hidden = w1_ref.shape
    width = w2_ref.shape[1]
    parts = hidden // width
    for j in range(parts):
        block = g_ref[:, 2 * j * width : (2 * j + 1) * width].astype(F32)
        for i in range(n):
            at = (i * parts + j) * rows
            w1_ref[:, at : at + rows] = block[:, i * rows : (i + 1) * rows]
        w2_ref[j * rows : (j + 1) * rows] = g_ref[:, (2 * j + 1) * width : (2 * j + 2) * width].astype(F32)


def run_feed_out(g, n):
    rows = g.shape[0]
    width = rows * n
    parts = g.shape[1] // (2 * width)
    outs = (shape_of(rows, parts * width, dtype=F32), shape_of(parts * rows, width, dtype=F32))
    return pl.pallas_call(
        functools.partial(feed_out, n), out_shape=outs, cost_estimate=cost(3), compiler_params=params()
    )(g)


def tile_grad(a_ref, b_ref, out_ref):
    out_ref[...] = dot_tn(a_ref[...], b_ref[...]).astype(BF)


def run_tile_grad(a, b, after=()):
    a, b = flat(a), flat(b)
    rows, width = a.shape
    return launch(
        tile_grad, 6, (a, b), [pl.BlockSpec((rows, width // 2), lambda i: (0, i)), whole(b.shape)],
        pl.BlockSpec((width // 2, b.shape[1]), lambda i: (i, 0)), shape_of(width, b.shape[1]), (2,), after=after,
    )


def run_temporal_back_project(d_time, ol, chunk=2, after=()):
    frames, padded, width = d_time.shape
    block = frame_block(chunk, padded, width)
    dims = d_time.shape
    return launch(
        temporal_back_project, 8, (d_time, ol), [block, whole(ol.shape)], [block, block, whole((8, width))],
        (shape_of(*dims), shape_of(*dims), shape_of(8, width, dtype=F32)), (frames // chunk,), after=after,
    )


def run_temporal_back_attend(joined, d_mixed, after=()):
    frames, padded, width = d_mixed.shape
    wide = place_block(frames, 3 * width)
    return launch(
        temporal_back_attend, 20, (joined, d_mixed), [wide, place_block(frames, width)], wide,
        shape_of(frames, padded, 3 * width), (padded // TILE,), after=after,
    )


def run_temporal_back_finish(places, d_at, x, d_joined, qk, v_in, v, chunk=2, after=()):
    frames, padded, width = x.shape
    block, wide = frame_block(chunk, padded, width), frame_block(chunk, padded, 3 * width)
    return launch(
        functools.partial(temporal_back_finish, places), 11, (d_at, x, d_joined, qk, v_in, v),
        [block, block, wide] + wholes((qk, v_in, v)), [frame_block(chunk, places, width), whole((8, width))],
        (shape_of(frames, places, width), shape_of(8, width, dtype=F32)), (frames // chunk,), after=after,
    )


AXES = ("dp", "seq")


def swap(values, bit, n):
    return lax.ppermute(values, AXES, [(i, i ^ (1 << bit)) for i in range(n)])


class Gather:
    def __init__(self, values, n, order):
        self.n, self.bits, self.order = n, n.bit_length() - 1, list(order)
        self.me = lax.axis_index(AXES)
        self.tail = values.shape[1:]
        self.held = values.reshape((1,) * self.bits + values.shape)

    def start(self):
        self.bit = self.order.pop(0)
        self.got = swap(self.held, self.bit, self.n)
        return self.held

    def end(self, *after):
        got = gate(self.got, *after) if after else self.got
        axis = self.bits - 1 - self.bit
        high = ((self.me >> self.bit) & 1) == 1
        held = self.held
        self.held = jnp.where(high, jnp.concatenate([got, held], axis), jnp.concatenate([held, got], axis))

    def steps(self, count):
        for _ in range(count):
            self.start()
            self.end()

    def rest(self):
        self.steps(len(self.order))
        return self.result()

    def result(self):
        return self.held.reshape((-1,) + self.tail)


class Scatter:
    def __init__(self, values, n, order):
        self.n, self.bits, self.order = n, n.bit_length() - 1, list(order)
        self.rows, self.tail = values.shape[0] // n, values.shape[1:]
        self.me = lax.axis_index(AXES)
        self.held = values.reshape((2,) * self.bits + (self.rows,) + self.tail)

    def start(self):
        bit = self.order.pop(0)
        axis = self.bits - 1 - bit
        mine = (self.me >> bit) & 1
        send = lax.dynamic_index_in_dim(self.held, 1 - mine, axis, keepdims=True)
        self.keep = lax.dynamic_index_in_dim(self.held, mine, axis, keepdims=True)
        self.got = swap(send, bit, self.n)
        return send

    def end(self, *after):
        got = gate(self.got, *after) if after else self.got
        self.held = (self.keep.astype(F32) + got.astype(F32)).astype(self.held.dtype)

    def rest(self, *after):
        while self.order:
            self.start()
            self.end(*(() if self.order else after))
        return self.result()

    def result(self):
        return self.held.reshape((self.rows,) + self.tail)


def on_device(n, tokens, tg, tb, t_in, t_out, t_lin, sg, sb, s_in, s_out, fg, fb, w1, b1, w2, cotangent):
    bits = n.bit_length() - 1
    top = tuple(range(bits - 1, 2, -1))
    order_a, order_b, order_c = top + (1, 2, 0), top + (2, 1, 0), (2,) + top + (1, 0)
    back_y, back_z = (0, 2) + top[::-1] + (1,), (0,) + top[::-1] + (2, 1)
    rows, width = t_in.shape[0], t_in.shape[0] * n
    parts = w2.shape[0] // rows
    hidden = w1.shape[1]
    places = tokens.shape[2]
    frames = tokens.shape[0] * tokens.shape[1]
    extra = -places % TILE

    vecs = jnp.concatenate([tg[None], tb, sg[None], sb, fg[None], fb, b1.reshape(parts, rows)], axis=0)
    n_vec = vecs.shape[0]
    vec_cols = jnp.pad(vecs.T, ((0, 0), (0, 2 * HEAD_DIM - n_vec)))
    feed = jnp.concatenate(
        [
            w1.reshape(rows, n, parts, rows).transpose(0, 2, 1, 3).reshape(rows, hidden),
            w2.reshape(parts, rows, width).transpose(1, 0, 2).reshape(rows, hidden),
            s_in,
            s_out,
        ],
        axis=1,
    )
    feed = lax.all_gather(feed, AXES, axis=0, tiled=True)

    def own_clip(grid):
        clip = lax.all_to_all(grid, "seq", split_axis=0, concat_axis=0, tiled=True)
        return jnp.pad(clip.reshape(frames, places, width), ((0, 0), (0, extra), (0, 0)))

    def own_frames(clip):
        return lax.all_to_all(clip.reshape(tokens.shape), "seq", split_axis=0, concat_axis=0, tiled=True)

    x = own_clip(tokens)
    t_qk = Gather(t_in[:, : 2 * width], n, order_a)
    t_v = Gather(jnp.concatenate([t_in[:, 2 * width :], vec_cols], axis=1), n, order_c)
    t_ol = Gather(jnp.concatenate([t_out, t_lin], axis=1), n, order_b)
    t_qk_w, t_v_w = t_qk.rest(), t_v.rest()
    t_ol.steps(bits - 1)
    vec = t_v_w[:, width:].T[:16].astype(F32)
    norm_t, joined_t = run_temporal_project(x, t_qk_w, t_v_w, vec, after=(t_ol.start(),))
    t_ol.end(norm_t)
    t_ol_w = t_ol.result()
    mixed_t = run_temporal_attend(joined_t)
    proj_t, after_time = run_temporal_finish(x, mixed_t, t_ol_w, vec)
    cot = own_clip(gate(cotangent, norm_t))
    norm_s, joined_s, mixed_s, after_space = run_spatial_forward(places, after_time, feed, vec)
    out, d_after_space, norm_m, active, d_hidden, vec_f = run_feed(places, after_space, cot, feed, vec)
    output = own_frames(out)
    g_feed_all = run_feed_grads(norm_m, d_hidden, active, cot)
    g_feed = lax.psum_scatter(g_feed_all, AXES, scatter_dimension=0, tiled=True)
    o_w1, o_w2 = run_feed_out(g_feed, n)
    d_space, d_joined_s, d_after_time, d_time, vec_s = run_spatial_back(
        places, d_after_space, after_time, joined_s, feed, vec, after=(g_feed_all,)
    )
    g_space = run_join_grads(norm_s, d_joined_s, mixed_s, d_space, after=(output[0, :1, 0, :128],))

    def beside(chains, kernel, *args):
        sends = tuple(chain.start() for chain in chains)
        done = kernel(*args, after=sends)
        for chain in chains:
            chain.end(done[0] if isinstance(done, (tuple, list)) else done)
        return done

    gs = Scatter(g_space, n, order_a[::-1])
    g_lin = beside((gs,), run_tile_grad, proj_t, d_time)
    d_proj, d_mixed_t, vec_t1 = beside((gs,), run_temporal_back_project, d_time, t_ol_w)
    g_out = run_tile_grad(mixed_t, d_proj)
    go = Scatter(jnp.concatenate([g_out, g_lin], axis=1), n, order_b[::-1])
    d_joined_t = beside((gs, go), run_temporal_back_attend, joined_t, d_mixed_t)
    g_qkv = beside((gs, go), run_join_grads, norm_t, d_joined_t)
    half = 3 * width // 2
    gq, gr = Scatter(g_qkv[:, :half], n, back_y), Scatter(g_qkv[:, half:], n, back_z)
    g_x, vec_t0 = beside(
        (gs, go, gq, gr), run_temporal_back_finish, places, d_after_time, x, d_joined_t, t_qk_w, t_v_w, vec
    )
    g_x = own_frames(g_x)
    g_vec = jnp.concatenate([vec_t0[:2], vec_t1[:2], vec_s[:3], vec_f[: 3 + parts]], axis=0)
    g_vec = g_vec.reshape(n_vec, n, rows).transpose(1, 0, 2)
    v = jnp.sum(lax.all_to_all(g_vec, AXES, split_axis=0, concat_axis=0, tiled=True), axis=0)
    g_i = jnp.concatenate([gq.rest(), gr.rest(o_w1[:1, :128])], axis=1).astype(F32)
    g_s = gs.rest().astype(F32)
    g_o = go.rest().astype(F32)
    return (
        output, g_x, v[0], v[1:4], g_i, g_o[:, :width], g_o[:, width : 2 * width],
        v[4], v[5:7], g_s[:, : 3 * width], g_s[:, 3 * width :], v[7], v[8:10],
        o_w1, v[10 : 10 + parts].reshape(-1), o_w2,
    )


def solution(mesh):
    shard = P(("dp", "seq"))
    cols = P(None, ("dp", "seq"))
    mat = P(("dp", "seq"), None)
    tok = P("dp", "seq", None, None)
    in_specs = (tok, shard, cols, mat, mat, mat, shard, cols, mat, mat, shard, cols, mat, shard, mat, tok)
    out_specs = (tok, tok, shard, cols, mat, mat, mat, shard, cols, mat, mat, shard, cols, mat, shard, mat)
    return jax.shard_map(
        functools.partial(on_device, mesh.size), mesh=mesh, in_specs=in_specs, out_specs=out_specs, check_vma=False
    )
```

time: 581 us -> 541 us (0.931)
  waiting for transfers between devices: 119 us -> 82.8 us
  Pallas kernels: 241 us -> 257 us
  other arithmetic: 52 us -> 36.4 us
  starting transfers between devices: 71.8 us -> 65.9 us
    all_to_all x2, waiting for transfers between devices: 22.9 us -> 0.01 us  [own_frames(): lax.all_to_all(clip.reshape(tokens.shape), 'seq', split_axis=0, concat_ax...]
    unnamed x95 -> x97, local copies, waits for them, and re-layouts: 12.8 us -> 28.8 us
    pallas_call x9 -> x28, Pallas kernels: 241 us -> 257 us  [the longest x14 255 us: launch(): pl.pallas_call(body, grid=grid, in_specs=list(in_specs) + [ANYWHERE] * sk...]
    all_to_all x2, waiting for transfers between devices: 17.8 us -> 2.32 us  [own_clip(): clip = lax.all_to_all(grid, 'seq', split_axis=0, concat_axis=0, tiled=True)]
    select_n x25 -> x15, other arithmetic: 26.9 us -> 11.7 us  [end(): jnp.where(high, jnp.concatenate([got, held], axis), jnp.concatenate([held...]
    ppermute x50 -> x35, starting transfers between devices: 54.6 us -> 45.4 us  [swap(): return lax.ppermute(values, AXES, [(i, i ^ 1 << bit) for i in range(n)])]
    select_n x4 -> x2, local copies, waits for them, and re-layouts: 6.82 us -> 0.07 us  [end(): jnp.where(high, jnp.concatenate([got, held], axis), jnp.concatenate([held...]
    ppermute x50 -> x35, waiting for transfers between devices: 78.4 us -> 80.5 us  [swap(): return lax.ppermute(values, AXES, [(i, i ^ 1 << bit) for i in range(n)])]
  transfers between devices with their start and end apart: 56 -> 42, of which waited for: 20 -> 20; matrix products, arithmetic and copies ran while one was open for 17% -> 13% of each run, Pallas kernels for 30% -> 33%
where the time goes in v3:
time: 541 us; the launch traced here: 531 us
  Pallas kernels  257 us (48%)
  waiting for transfers between devices  82.8 us (15%)
  local copies, waits for them, and re-layouts  73.2 us (14%)
  starting transfers between devices  65.9 us (12%)
  other arithmetic  36.4 us (7%)
  between operations  15.4 us (3%)
    pallas_call x14, Pallas kernels, launch(): pl.pallas_call(body, grid=grid, in_specs=list(in_specs) + [ANYWHERE] * sk...  255 us
    ppermute x35, waiting for transfers between devices, swap(): return lax.ppermute(values, AXES, [(i, i ^ 1 << bit) for i in range(n)])  80.5 us
    ppermute x35, starting transfers between devices, swap(): return lax.ppermute(values, AXES, [(i, i ^ 1 << bit) for i in range(n)])  45.4 us
    unnamed x97, local copies, waits for them, and re-layouts  28.8 us
    convert_element_type x16, other arithmetic, end(): (self.keep.astype(F32) + got.astype(F32)).astype(self.held.dtype)  16.9 us
    dynamic_slice x20, local copies, waits for them, and re-layouts, start(): send = lax.dynamic_index_in_dim(self.held, 1 - mine, axis, keepdims=True)  12.3 us
    select_n x15, other arithmetic, end(): jnp.where(high, jnp.concatenate([got, held], axis), jnp.concatenate([held...  11.7 us
  transfers between devices with their start and end apart: 42, of which 20 were waited for; matrix products, arithmetic and copies ran while one was open for 13% of the time, Pallas kernels for 33%

profile of v3, /device:TPU:0, one launch (start us, length us, event | category | flops | bytes accessed | tf_op | source)
XLA Modules:
  0.0 530.9 jit_solution(15534302995550152670)
XLA Ops:
  8.3 2.1 reshape.2257
  12.8 4.4 all-to-all-start
  17.5 2.5 collective-permute-start.5
  20.0 2.7 collective-permute-start.10
  23.0 3.6 copy.121.refs_0_
  26.7 2.7 collective-permute-start.6
  29.4 6.8 %collective-permute-done = bf16[1,1,1,1,1,24,1536]{6,5,4,3,2,1,0:T(8,128)(2,1)S(1)} collective-permute-done((bf16[1,1,1,1,1,24,1536]{6,5,4,3,2,1,0:T(8,128)(2,1)S(1)}, bf16[1,1,1,1,1,24,1536]{6,5,4,3,2,1,0:T(8,128)(2,1)S(1)}, u32[]{:S(2)}, u32[]{:S(2)}) %collective-permute-start) | collective-permute-done | bytes 73760 | tf_op jit(solution)/shard_map/ppermute | solution.py:576
  36.1 2.3 collective-permute-start.1
  38.6 2.1 collective-permute-done.6
  40.8 2.8 collective-permute-start.7
  43.6 2.5 collective-permute-done.1
  46.2 1.8 collective-permute-start.2
  50.1 3.0 collective-permute-done.7
  53.2 3.0 collective-permute-start.8
  56.3 4.1 collective-permute-done.2
  60.6 2.5 collective-permute-start.3
  63.1 2.0 collective-permute-done.12
  66.9 8.2 %collective-permute-done.8 = bf16[2,2,2,1,1,24,896]{6,5,4,3,2,1,0:T(8,128)(2,1)S(1)} collective-permute-done((bf16[2,2,2,1,1,24,896]{6,5,4,3,2,1,0:T(8,128)(2,1)S(1)}, bf16[2,2,2,1,1,24,896]{6,5,4,3,2,1,0:T(8,128)(2,1)S(1)}, u32[]{:S(2)}, u32[]{:S(2)}) %collective-permute-start.8) | collective-permute-done | bytes 344096 | tf_op jit(solution)/shard_map/ppermute | solution.py:576
  78.2 10.2 %collective-permute-done.13 = bf16[2,2,2,1,1,24,1536]{6,5,0,1,2,4,3:T(8,128)(2,1)S(1)} collective-permute-done((bf16[2,2,2,1,1,24,1536]{6,5,0,1,2,4,3:T(8,128)(2,1)S(1)}, bf16[2,2,2,1,1,24,1536]{6,5,0,1,2,4,3:T(8,128)(2,1)S(1)}, u32[]{:S(2)}, u32[]{:S(2)}) %collective-permute-start.13) | collective-permute-done | bytes 589856 | tf_op jit(solution)/shard_map/ppermute | solution.py:576
  92.2 1.9 pad.11.refs_0_.refs_1_
  94.1 4.3 maximum_select_fusion
  98.4 11.5 %shard_map.279 = (bf16[8,208,768]{2,1,0:T(8,128)(2,1)}, bf16[8,208,2304]{2,1,0:T(8,128)(2,1)}) custom-call(bf16[8,208,768]{2,1,0:T(8,128)(2,1)} %pad.11.refs_0_.refs_1_, bf16[768,1536]{1,0:T(8,128)(2,1)} %bitcast.160, bf16[768,896]{1,0:T(8,128)(2,1)} %bitcast.165, f32[16,768]{1,0:T(8,128)} %slice_convert_fusion.refs_3_.refs_2_.refs_4_.refs_5_, ...), custom_call_target="tpu_custom_call" | custom-call | flops 8999999488 | tf_op jit(solution)/shard_map/pallas_call | solution.py:363
  109.9 5.0 copy.122
  114.9 3.9 all-to-all-start.1
  118.8 4.3 maximum_select_fusion.1
  123.1 13.5 %shard_map.280.refs_1_ = bf16[8,208,768]{2,1,0:T(8,128)(2,1)} custom-call(bf16[8,208,2304]{2,1,0:T(8,128)(2,1)} %get-tuple-element.42.refs_0_), custom_call_target="tpu_custom_call" | custom-call | flops 14000000000 | tf_op jit(solution)/shard_map/pallas_call | solution.py:363
  136.5 8.9 %shard_map.282 = (bf16[8,208,768]{2,1,0:T(8,128)(2,1)}, f32[8,208,768]{2,1,0:T(8,128)}) custom-call(bf16[8,208,768]{2,1,0:T(8,128)(2,1)} %pad.11.refs_0_.refs_1_, bf16[8,208,768]{2,1,0:T(8,128)(2,1)} %shard_map.280.refs_1_, bf16[768,1536]{1,0:T(8,128)(2,1)} %bitcast.162, f32[16,768]{1,0:T(8,128)} %slice_convert_fusion.refs_3_.refs_2_.refs_4_.refs_5_), custom_call_target="tpu_custom_call" | custom-call | flops 8000000000 | tf_op jit(solution)/shard_map/pallas_call | solution.py:363
  145.4 2.3 all-to-all-done.1
  149.8 23.0 %shard_map.283 = (bf16[8,208,768]{2,1,0:T(8,128)(2,1)}, bf16[8,208,2304]{2,1,0:T(8,128)(2,1)}, bf16[8,208,768]{2,1,0:T(8,128)(2,1)}, f32[8,208,768]{2,1,0:T(8,128)}) custom-call(f32[8,208,768]{2,1,0:T(8,128)} %get-tuple-element.44.refs_0_.refs_1_, bf16[768,9216]{1,0:T(8,128)(2,1)} %all-gather.2.cloned.1.call-done.refs_1_.refs_2_.refs_3_, ...), custom_call_target="tpu_custom_call" | custom-call | flops 23000000512 | tf_op jit(solution)/shard_map/pallas_call | solution.py:363
  172.7 44.9 %shard_map.285 = (bf16[8,196,768]{2,1,0:T(8,128)(2,1)}, f32[8,208,768]{2,1,0:T(8,128)}, bf16[8,208,768]{2,1,0:T(8,128)(2,1)}, bf16[8,208,3072]{2,1,0:T(8,128)(2,...) custom-call(f32[8,208,768]{2,1,0:T(8,128)} %get-tuple-element.45.refs_0_, bf16[8,208,768]{2,1,0:T(8,128)(2,1)} %pad.13.refs_1_, ...), custom_call_target="tpu_custom_call" | custom-call | flops 44999999488 | tf_op jit(solution)/shard_map/pallas_call | solution.py:363
  217.7 5.0 copy.124
  222.6 3.6 all-to-all-start.2
  226.3 25.0 %shard_map.286.refs_5_ = bf16[768,6144]{1,0:T(8,128)(2,1)} custom-call(bf16[1664,768]{1,0:T(8,128)(2,1)} %bitcast.201, bf16[1664,3072]{1,0:T(8,128)(2,1)} %bitcast.193, bf16[1664,3072]{1,0:T(8,128)(2,1)} %bitcast.192, bf16[1664,768]{1,0:T(8,128)(2,1)} %bitcast.158), custom_call_target="tpu_custom_call" | custom-call | flops 24999999488 | tf_op jit(solution)/shard_map/pallas_call | solution.py:363
  251.3 50.0 %shard_map.287 = (bf16[8,208,768]{2,1,0:T(8,128)(2,1)}, bf16[8,208,2304]{2,1,0:T(8,128)(2,1)}, f32[8,208,768]{2,1,0:T(8,128)}, bf16[8,208,768]{2,1,0:T(8,128)(2,1)}, f32[8,768]{1,0:T(8,128)}) custom-call(f32[8,208,768]{2,1,0:T(8,128)} %get-tuple-element.47.refs_0_, f32[8,208,768]{2,1,0:T(8,128)} %get-tuple-element.44.refs_0_.refs_1_, ...), custom_call_target="tpu_custom_call" | custom-call | flops 41999998976 | tf_op jit(solution)/shard_map/pallas_call | solution.py:363
  301.8 15.4 %shard_map.288 = bf16[768,3072]{1,0:T(8,128)(2,1)} custom-call(bf16[1664,768]{1,0:T(8,128)(2,1)} %bitcast.198, bf16[1664,2304]{1,0:T(8,128)(2,1)} %bitcast.194, bf16[1664,768]{1,0:T(8,128)(2,1)} %bitcast.199, bf16[1664,768]{1,0:T(8,128)(2,1)} %bitcast.200, bf16[1,128]{1,0:T(2,128)(2,1)} %slice_bitcast_fusion.5.refs_4_), custom_call_target="tpu_custom_call" | custom-call | flops 16000000000 | tf_op jit(solution)/shard_map/pallas_call | solution.py:363
  317.2 3.2 constant_dynamic-slice_fusion.19.refs_2_
  321.6 5.7 %shard_map.289.refs_1_ = bf16[768,768]{1,0:T(8,128)(2,1)} custom-call(bf16[1664,768]{1,0:T(8,128)(2,1)} %bitcast.196, bf16[1664,768]{1,0:T(8,128)(2,1)} %bitcast.197, bf16[2,2,2,2,1,24,3072]{6,5,4,3,2,1,0:T(8,128)(2,1)} %constant_dynamic-slice_fusion.19.refs_2_), custom_call_target="tpu_custom_call" | custom-call | flops 6000000000 | tf_op jit(solution)/shard_map/pallas_call | solution.py:363
  328.9 3.6 add_convert_fusion
  333.6 2.2 collective-permute-start.16
  335.8 8.2 %shard_map.291 = (bf16[8,208,768]{2,1,0:T(8,128)(2,1)}, bf16[8,208,768]{2,1,0:T(8,128)(2,1)}, f32[8,768]{1,0:T(8,128)}) custom-call(bf16[8,208,768]{2,1,0:T(8,128)(2,1)} %get-tuple-element.53.refs_0_, bf16[768,1536]{1,0:T(8,128)(2,1)} %bitcast.163, bf16[2,2,1,2,1,24,3072]{6,5,4,3,2,1,0:T(8,128)(2,1)} %constant_dynamic-slice_fusion.18.refs_2_), custom_call_target="tpu_custom_call" | custom-call | flops 8000000000 | tf_op jit(solution)/shard_map/pallas_call | solution.py:363
  345.3 5.8 %shard_map.293 = bf16[768,768]{1,0:T(8,128)(2,1)} custom-call(bf16[1664,768]{1,0:T(8,128)(2,1)} %bitcast.195, bf16[1664,768]{1,0:T(8,128)(2,1)} %bitcast.157), custom_call_target="tpu_custom_call" | custom-call | flops 6000000000 | tf_op jit(solution)/shard_map/pallas_call | solution.py:363
  355.1 7.2 %collective-permute-done.16.refs_0_ = bf16[2,2,1,2,1,24,3072]{6,5,4,3,2,1,0:T(8,128)(2,1)} collective-permute-done((bf16[2,2,1,2,1,24,3072]{6,5,4,3,2,1,0:T(8,128)(2,1)}, bf16[2,2,1,2,1,24,3072]{6,5,4,3,2,1,0:T(8,128)(2,1)}, u32[]{:S(2)}, u32[]{:S(2)}) %collective-permute-start.16) | collective-permute-done | bytes 1179680 | tf_op jit(solution)/shard_map/ppermute | solution.py:576
  362.3 1.7 add_convert_fusion.2
  365.9 1.9 collective-permute-start.17
  367.8 18.3 %shard_map.294.refs_1_.refs_2_ = bf16[8,208,2304]{2,1,0:T(8,128)(2,1)} custom-call(bf16[8,208,2304]{2,1,0:T(8,128)(2,1)} %get-tuple-element.42.refs_0_, bf16[8,208,768]{2,1,0:T(8,128)(2,1)} %get-tuple-element.59.refs_1_, bf16[2,2,1,1,1,24,3072]{6,5,4,3,2,1,0:T(8,128)(2,1)} %constant_dynamic-slice_fusion.17.refs_2_, ...), custom_call_target="tpu_custom_call" | custom-call | flops 20000000000 | tf_op jit(solution)/shard_map/pallas_call | solution.py:363
  395.4 1.8 collective-permute-start.18
  397.2 11.3 %shard_map.297.refs_1_ = bf16[768,2304]{1,0:T(8,128)(2,1)} custom-call(bf16[1664,768]{1,0:T(8,128)(2,1)} %bitcast.145, bf16[1664,2304]{1,0:T(8,128)(2,1)} %bitcast.144, bf16[2,1,1,1,1,24,3072]{6,5,4,3,2,1,0:T(8,128)(2,1)} %constant_dynamic-slice_fusion.15.refs_2_, bf16[2,2,2,1,1,24,1536]{6,5,4,3,2,1,0:T(8,128)(2,1)} %copy-done.25), custom_call_target="tpu_custom_call" | custom-call | flops 12000000000 | tf_op jit(solution)/shard_map/pallas_call | solution.py:363
  408.5 2.5 collective-permute-done.20.refs_0_
  413.5 1.9 collective-permute-start.31
  421.7 2.4 collective-permute-start.34
  424.1 13.5 %shard_map.300 = (bf16[8,196,768]{2,1,0:T(8,128)(2,1)}, f32[8,768]{1,0:T(8,128)}) custom-call(f32[8,208,768]{2,1,0:T(8,128)} %get-tuple-element.52.refs_0_, bf16[8,208,768]{2,1,0:T(8,128)(2,1)} %pad.11.refs_0_.refs_1_, bf16[8,208,2304]{2,1,0:T(8,128)(2,1)} %shard_map.294.refs_1_.refs_2_, bf16[768,1536]{1,0:T(8,128)(2,1)} %bitcast.161, ...), custom_call_target="tpu_custom_call" | custom-call | flops 11000000512 | tf_op jit(solution)/shard_map/pallas_call | solution.py:363
  439.4 1.9 reshape.2288
  441.3 4.0 all-to-all-start.4
  447.8 1.9 collective-permute-start.32
  449.8 3.3 copy.125
  453.7 4.5 all-to-all-start.3
  463.8 2.3 collective-permute-start.33
  477.6 8.3 %collective-permute-done.22 = bf16[2,2,1,2,1,24,1152]{6,5,4,3,2,1,0:T(8,128)(2,1)} collective-permute-done((bf16[2,2,1,2,1,24,1152]{6,5,4,3,2,1,0:T(8,128)(2,1)}, bf16[2,2,1,2,1,24,1152]{6,5,4,3,2,1,0:T(8,128)(2,1)}, u32[]{:S(2)}, u32[]{:S(2)}) %collective-permute-start.22) | collective-permute-done | bytes 442400 | tf_op jit(solution)/shard_map/ppermute | solution.py:576
  487.1 2.7 collective-permute-done.27
  491.1 5.4 %collective-permute-done.23 = bf16[2,1,1,2,1,24,1152]{6,5,4,3,2,1,0:T(8,128)(2,1)S(1)} collective-permute-done((bf16[2,1,1,2,1,24,1152]{6,5,4,3,2,1,0:T(8,128)(2,1)S(1)}, bf16[2,1,1,2,1,24,1152]{6,5,4,3,2,1,0:T(8,128)(2,1)S(1)}, u32[]{:S(2)}, u32[]{:S(2)}) %collective-permute-start.23) | collective-permute-done | bytes 221216 | tf_op jit(solution)/shard_map/ppermute | solution.py:576
  497.1 8.1 %collective-permute-done.28 = bf16[1,1,2,2,1,24,1152]{6,5,4,3,2,1,0:T(8,128)(2,1)S(1)} collective-permute-done((bf16[1,1,2,2,1,24,1152]{6,5,4,3,2,1,0:T(8,128)(2,1)S(1)}, bf16[1,1,2,2,1,24,1152]{6,5,4,3,2,1,0:T(8,128)(2,1)S(1)}, u32[]{:S(2)}, u32[]{:S(2)}) %collective-permute-start.28) | collective-permute-done | bytes 221216 | tf_op jit(solution)/shard_map/ppermute | solution.py:576
  508.1 2.0 collective-permute-done.29
  511.9 2.2 shard_map.303
  518.8 4.8 copy.160
  (258 shorter events, 81.1 us)
Async XLA Ops:
  7.2 4.6 copy-start.31
  7.2 4.6 copy-start.30
  7.2 142.6 %all-gather.2.cloned.1.call-start = ((), (), s32[]{:S(2)}) async-start(), calls=%async_computation.6 | async-start | bytes 14598144 | tf_op jit(solution)/shard_map/all_gather | solution.py:665
  12.7 4.5 copy-start.43
  12.7 4.6 copy-start.37
  12.7 4.6 copy-start.38
  12.7 4.5 copy-start.39
  12.7 4.5 copy-start.40
  12.7 4.5 copy-start.41
  12.7 4.5 copy-start.42
  12.8 4.7 slice-start
  12.8 7.2 %copy-start.32 = (bf16[24,768]{1,0:T(8,128)(2,1)S(1)}, bf16[24,768]{1,0:T(8,128)(2,1)}, u32[]{:S(2)}) copy-start(bf16[24,768]{1,0:T(8,128)(2,1)} %param.20) | copy-start | bytes 110596
  12.8 7.2 %copy-start.33 = (bf16[24,768]{1,0:T(8,128)(2,1)S(1)}, bf16[24,768]{1,0:T(8,128)(2,1)}, u32[]{:S(2)}) copy-start(bf16[24,768]{1,0:T(8,128)(2,1)} %param.21) | copy-start | bytes 110596
  12.8 9.8 %copy-start.29 = (bf16[24,2304]{1,0:T(8,128)(2,1)S(1)}, bf16[24,2304]{1,0:T(8,128)(2,1)}, u32[]{:S(2)}) copy-start(bf16[24,2304]{1,0:T(8,128)(2,1)} %param.19) | copy-start | bytes 331780
  12.8 79.1 %all-to-all-start = ((bf16[4,2,196,768]{3,1,2,0:T(2,128)(2,1)}), bf16[4,2,196,768]{3,1,2,0:T(2,128)(2,1)S(1)}, u32[]{:S(2)}, u32[]{:S(2)}) async-start(bf16[4,2,196,768]{3,1,2,0:T(2,128)(2,1)} %param.16), calls=%async_computation | async-start | bytes 4816896 | tf_op jit(solution)/shard_map/all_to_all | solution.py:668
  17.5 9.2 %collective-permute-start.5 = (bf16[1,1,1,1,1,24,896]{6,5,4,3,2,1,0:T(8,128)(2,1)S(1)}, bf16[1,1,1,1,1,24,896]{6,5,4,3,2,1,0:T(8,128)(2,1)S(1)}, u32[]{:S(2)}, u32[]{:S(2)}) collective-permute-start(bf16[1,1,1,1,1,24,896]{6,5,4,3,2,1,0:T(8,128)(2,1)S(1)} %get-tuple-element.93), channel_id=1, source_target_pairs={{0,4},{1,5},{2,6},{3,7},{4,0},{5,1},{6,2},{7,3},{8,12},{9,13},{10,... | collective-permute-start | bytes 129032 | tf_op jit(solution)/shard_map/ppermute | solution.py:576
  20.0 18.5 %collective-permute-start.10 = (bf16[1,1,1,1,1,24,1536]{6,5,4,3,2,1,0:T(8,128)(2,1)S(1)}, bf16[1,1,1,1,1,24,1536]{6,5,4,3,2,1,0:T(8,128)(2,1)S(1)}, u32[]{:S(2)}, u32[]{:S(2)}) collective-permute-start(bf16[1,1,1,1,1,24,1536]{6,5,4,3,2,1,0:T(8,128)(2,1)S(1)} %bitcast.179), channel_id=1, source_target_pairs={{0,16},{1,17},{2,18},{3,19},{4,20},{5,21},{6,22},{7,23},{8,24},{9,... | collective-permute-start | bytes 221192 | tf_op jit(solution)/shard_map/ppermute | solution.py:576
  22.6 13.5 %collective-permute-start = (bf16[1,1,1,1,1,24,1536]{6,5,4,3,2,1,0:T(8,128)(2,1)S(1)}, bf16[1,1,1,1,1,24,1536]{6,5,4,3,2,1,0:T(8,128)(2,1)S(1)}, u32[]{:S(2)}, u32[]{:S(2)}) collective-permute-start(bf16[1,1,1,1,1,24,1536]{6,5,4,3,2,1,0:T(8,128)(2,1)S(1)} %get-tuple-element.88), channel_id=1, source_target_pairs={{0,16},{1,17},{2,18},{3,19},{4,20},{5,21},{6,22},{7,23},{8,24},{9,... | collective-permute-start | bytes 221192 | tf_op jit(solution)/shard_map/ppermute | solution.py:576
  26.7 14.1 %collective-permute-start.6 = (bf16[1,1,2,1,1,24,896]{6,5,2,0,4,3,1:T(8,128)(2,1)S(1)}, bf16[1,1,2,1,1,24,896]{6,5,2,0,4,3,1:T(8,128)(2,1)S(1)}, u32[]{:S(2)}, u32[]{:S(2)}) collective-permute-start(bf16[1,1,2,1,1,24,896]{6,5,2,0,4,3,1:T(8,128)(2,1)S(1)} %fusion.8), channel_id=1, source_target_pairs={{0,16},{1,17},{2,18},{3,19},{4,20},{5,21},{6,22},{7,23},{8,24},{9,... | collective-permute-start | bytes 258056 | tf_op jit(solution)/shard_map/ppermute | solution.py:576
  36.1 10.0 %collective-permute-start.1 = (bf16[2,1,1,1,1,24,1536]{6,5,1,0,4,3,2:T(8,128)(2,1)S(1)}, bf16[2,1,1,1,1,24,1536]{6,5,1,0,4,3,2:T(8,128)(2,1)S(1)}, u32[]{:S(2)}, u32[]{:S(2)}) collective-permute-start(bf16[2,1,1,1,1,24,1536]{6,5,1,0,4,3,2:T(8,128)(2,1)S(1)} %fusion.7), channel_id=1, source_target_pairs={{0,8},{1,9},{2,10},{3,11},{4,12},{5,13},{6,14},{7,15},{8,0},{9,1},... | collective-permute-start | bytes 442376 | tf_op jit(solution)/shard_map/ppermute | solution.py:576
  38.5 10.8 %collective-permute-start.11 = (bf16[2,1,1,1,1,24,1536]{6,5,4,3,2,1,0:T(8,128)(2,1)S(1)}, bf16[2,1,1,1,1,24,1536]{6,5,4,3,2,1,0:T(8,128)(2,1)S(1)}, u32[]{:S(2)}, u32[]{:S(2)}) collective-permute-start(bf16[2,1,1,1,1,24,1536]{6,5,4,3,2,1,0:T(8,128)(2,1)S(1)} %maximum_select_fusion.16), channel_id=1, source_target_pairs={{0,8},{1,9},{2,10},{3,11},{4,12},{5,13},{6,14},{7,15},{8,0},{9,1},... | collective-permute-start | bytes 442376 | tf_op jit(solution)/shard_map/ppermute | solution.py:576
  40.8 12.3 %collective-permute-start.7 = (bf16[2,1,2,1,1,24,896]{6,5,2,0,4,3,1:T(8,128)(2,1)S(1)}, bf16[2,1,2,1,1,24,896]{6,5,2,0,4,3,1:T(8,128)(2,1)S(1)}, u32[]{:S(2)}, u32[]{:S(2)}) collective-permute-start(bf16[2,1,2,1,1,24,896]{6,5,2,0,4,3,1:T(8,128)(2,1)S(1)} %fusion.3), channel_id=1, source_target_pairs={{0,8},{1,9},{2,10},{3,11},{4,12},{5,13},{6,14},{7,15},{8,0},{9,1},... | collective-permute-start | bytes 516104 | tf_op jit(solution)/shard_map/ppermute | solution.py:576
  46.2 14.2 %collective-permute-start.2 = (bf16[2,2,1,1,1,24,1536]{6,5,1,0,4,3,2:T(8,128)(2,1)S(1)}, bf16[2,2,1,1,1,24,1536]{6,5,1,0,4,3,2:T(8,128)(2,1)S(1)}, u32[]{:S(2)}, u32[]{:S(2)}) collective-permute-start(bf16[2,2,1,1,1,24,1536]{6,5,1,0,4,3,2:T(8,128)(2,1)S(1)} %maximum_select_fusion.11), channel_id=1, source_target_pairs={{0,2},{1,3},{2,0},{3,1},{4,6},{5,7},{6,4},{7,5},{8,10},{9,11},{10,... | collective-permute-start | bytes 884744 | tf_op jit(solution)/shard_map/ppermute | solution.py:576
  49.3 15.8 %collective-permute-start.12 = (bf16[2,2,1,1,1,24,1536]{6,5,0,1,2,4,3:T(8,128)(2,1)S(1)}, bf16[2,2,1,1,1,24,1536]{6,5,0,1,2,4,3:T(8,128)(2,1)S(1)}, u32[]{:S(2)}, u32[]{:S(2)}) collective-permute-start(bf16[2,2,1,1,1,24,1536]{6,5,0,1,2,4,3:T(8,128)(2,1)S(1)} %maximum_select_fusion.12), channel_id=1, source_target_pairs={{0,4},{1,5},{2,6},{3,7},{4,0},{5,1},{6,2},{7,3},{8,12},{9,13},{10,... | collective-permute-start | bytes 884744 | tf_op jit(solution)/shard_map/ppermute | solution.py:576
  53.2 22.0 %collective-permute-start.8 = (bf16[2,2,2,1,1,24,896]{6,5,4,3,2,1,0:T(8,128)(2,1)S(1)}, bf16[2,2,2,1,1,24,896]{6,5,4,3,2,1,0:T(8,128)(2,1)S(1)}, u32[]{:S(2)}, u32[]{:S(2)}) collective-permute-start(bf16[2,2,2,1,1,24,896]{6,5,4,3,2,1,0:T(8,128)(2,1)S(1)} %copy.113), channel_id=1, source_target_pairs={{0,2},{1,3},{2,0},{3,1},{4,6},{5,7},{6,4},{7,5},{8,10},{9,11},{10,... | collective-permute-start | bytes 1032200 | tf_op jit(solution)/shard_map/ppermute | solution.py:576
  60.6 16.5 %collective-permute-start.3 = (bf16[2,2,1,2,1,24,1536]{6,5,4,3,2,1,0:T(8,128)(2,1)S(1)}, bf16[2,2,1,2,1,24,1536]{6,5,4,3,2,1,0:T(8,128)(2,1)S(1)}, u32[]{:S(2)}, u32[]{:S(2)}) collective-permute-start(bf16[2,2,1,2,1,24,1536]{6,5,4,3,2,1,0:T(8,128)(2,1)S(1)} %copy.105), channel_id=1, source_target_pairs={{0,4},{1,5},{2,6},{3,7},{4,0},{5,1},{6,2},{7,3},{8,12},{9,13},{10,... | collective-permute-start | bytes 1769480 | tf_op jit(solution)/shard_map/ppermute | solution.py:576
  65.2 23.1 %collective-permute-start.13 = (bf16[2,2,2,1,1,24,1536]{6,5,0,1,2,4,3:T(8,128)(2,1)S(1)}, bf16[2,2,2,1,1,24,1536]{6,5,0,1,2,4,3:T(8,128)(2,1)S(1)}, u32[]{:S(2)}, u32[]{:S(2)}) collective-permute-start(bf16[2,2,2,1,1,24,1536]{6,5,0,1,2,4,3:T(8,128)(2,1)S(1)} %maximum_select_fusion.7), channel_id=1, source_target_pairs={{0,2},{1,3},{2,0},{3,1},{4,6},{5,7},{6,4},{7,5},{8,10},{9,11},{10,... | collective-permute-start | bytes 1769480 | tf_op jit(solution)/shard_map/ppermute | solution.py:576
  75.3 14.4 %collective-permute-start.9 = (bf16[2,2,2,2,1,24,896]{6,5,4,3,2,1,0:T(8,128)(2,1)S(1)}, bf16[2,2,2,2,1,24,896]{6,5,4,3,2,1,0:T(8,128)(2,1)S(1)}, u32[]{:S(2)}, u32[]{:S(2)}) collective-permute-start(bf16[2,2,2,2,1,24,896]{6,5,4,3,2,1,0:T(8,128)(2,1)S(1)} %maximum_select_fusion.4), channel_id=1, source_target_pairs={{0,1},{1,0},{2,3},{3,2},{4,5},{5,4},{6,7},{7,6},{8,9},{9,8},{10,11... | collective-permute-start | bytes 2064392 | tf_op jit(solution)/shard_map/ppermute | solution.py:576
  78.2 15.9 %collective-permute-start.4 = (bf16[2,2,2,2,1,24,1536]{6,5,4,3,2,1,0:T(8,128)(2,1)}, bf16[2,2,2,2,1,24,1536]{6,5,4,3,2,1,0:T(8,128)(2,1)}, u32[]{:S(2)}, u32[]{:S(2)}) collective-permute-start(bf16[2,2,2,2,1,24,1536]{6,5,4,3,2,1,0:T(8,128)(2,1)} %maximum_select_fusion.3), channel_id=1, source_target_pairs={{0,1},{1,0},{2,3},{3,2},{4,5},{5,4},{6,7},{7,6},{8,9},{9,8},{10,11... | collective-permute-start | bytes 3538952 | tf_op jit(solution)/shard_map/ppermute | solution.py:576
  89.7 29.1 %collective-permute-start.14 = (bf16[2,2,2,2,1,24,1536]{6,5,4,3,2,1,0:T(8,128)(2,1)}, bf16[2,2,2,2,1,24,1536]{6,5,4,3,2,1,0:T(8,128)(2,1)}, u32[]{:S(2)}, u32[]{:S(2)}) collective-permute-start(bf16[2,2,2,2,1,24,1536]{6,5,4,3,2,1,0:T(8,128)(2,1)} %copy_select_fusion.refs_4_), channel_id=1, source_target_pairs={{0,1},{1,0},{2,3},{3,2},{4,5},{5,4},{6,7},{7,6},{8,9},{9,8},{10,11... | collective-permute-start | bytes 3538952 | tf_op jit(solution)/shard_map/ppermute | solution.py:576
  114.9 32.9 %all-to-all-start.1 = ((bf16[4,2,196,768]{3,1,2,0:T(2,128)(2,1)}), bf16[4,2,196,768]{3,1,2,0:T(2,128)(2,1)S(1)}, u32[]{:S(2)}, u32[]{:S(2)}) async-start(bf16[4,2,196,768]{3,1,2,0:T(2,128)(2,1)} %copy.122), calls=%async_computation.1 | async-start | bytes 4816896 | tf_op jit(solution)/shard_map/all_to_all | solution.py:668
  222.6 78.6 %all-to-all-start.2 = ((bf16[4,2,196,768]{3,1,2,0:T(2,128)(2,1)}), bf16[4,2,196,768]{3,1,2,0:T(2,128)(2,1)S(1)}, u32[]{:S(2)}, u32[]{:S(2)}) async-start(bf16[4,2,196,768]{3,1,2,0:T(2,128)(2,1)} %copy.124), calls=%async_computation.2 | async-start | bytes 4816896 | tf_op jit(solution)/shard_map/all_to_all | solution.py:672
  226.3 285.6 %reduce-scatter.2.cloned.1.call-start = ((), (), s32[]{:S(2)}) async-start(), calls=%async_computation.7 | async-start | bytes 9732096 | tf_op jit(solution)/shard_map/reduce_scatter | solution.py:691
  301.3 16.0 %copy-start.2 = (bf16[4,2,196,768]{3,1,2,0:T(2,128)(2,1)}, bf16[4,2,196,768]{3,1,2,0:T(2,128)(2,1)S(1)}, u32[]{:S(2)}) copy-start(bf16[4,2,196,768]{3,1,2,0:T(2,128)(2,1)S(1)} %all-to-all-done.2) | copy-start | bytes 7225348
  320.5 6.9 %collective-permute-start.15 = (bf16[2,2,2,2,1,24,3072]{6,5,4,3,2,1,0:T(8,128)(2,1)}, bf16[2,2,2,2,1,24,3072]{6,5,4,3,2,1,0:T(8,128)(2,1)S(1)}, u32[]{:S(2)}, u32[]{:S(2)}) collective-permute-start(bf16[2,2,2,2,1,24,3072]{6,5,4,3,2,1,0:T(8,128)(2,1)} %constant_dynamic-slice_fusion.19.refs_2_), channel_id=1, source_target_pairs={{0,1},{1,0},{2,3},{3,2},{4,5},{5,4},{6,7},{7,6},{8,9},{9,8},{10,11... | collective-permute-start | bytes 7077896 | tf_op jit(solution)/shard_map/ppermute | solution.py:576
  333.6 28.7 %collective-permute-start.16 = (bf16[2,2,1,2,1,24,3072]{6,5,4,3,2,1,0:T(8,128)(2,1)}, bf16[2,2,1,2,1,24,3072]{6,5,4,3,2,1,0:T(8,128)(2,1)}, u32[]{:S(2)}, u32[]{:S(2)}) collective-permute-start(bf16[2,2,1,2,1,24,3072]{6,5,4,3,2,1,0:T(8,128)(2,1)} %constant_dynamic-slice_fusion.18.refs_2_), channel_id=1, source_target_pairs={{0,4},{1,5},{2,6},{3,7},{4,0},{5,1},{6,2},{7,3},{8,12},{9,13},{10,... | collective-permute-start | bytes 3538952 | tf_op jit(solution)/shard_map/ppermute | solution.py:576
  345.3 5.8 %copy-start.15 = (bf16[768,768]{1,0:T(8,128)(2,1)S(1)}, bf16[768,768]{1,0:T(8,128)(2,1)}, u32[]{:S(2)}) copy-start(bf16[768,768]{1,0:T(8,128)(2,1)} %shard_map.289.refs_1_) | copy-start | bytes 3538948
  355.1 31.1 %collective-permute-start.19 = (bf16[2,2,2,2,1,24,1536]{6,5,4,3,2,1,0:T(8,128)(2,1)}, bf16[2,2,2,2,1,24,1536]{6,5,4,3,2,1,0:T(8,128)(2,1)S(1)}, u32[]{:S(2)}, u32[]{:S(2)}) collective-permute-start(bf16[2,2,2,2,1,24,1536]{6,5,4,3,2,1,0:T(8,128)(2,1)} %constant_dynamic-slice_fusion.16.refs_3_), channel_id=1, source_target_pairs={{0,1},{1,0},{2,3},{3,2},{4,5},{5,4},{6,7},{7,6},{8,9},{9,8},{10,11... | collective-permute-start | bytes 3538952 | tf_op jit(solution)/shard_map/ppermute | solution.py:576
  365.9 25.2 %collective-permute-start.17 = (bf16[2,2,1,1,1,24,3072]{6,5,4,3,2,1,0:T(8,128)(2,1)}, bf16[2,2,1,1,1,24,3072]{6,5,4,3,2,1,0:T(8,128)(2,1)}, u32[]{:S(2)}, u32[]{:S(2)}) collective-permute-start(bf16[2,2,1,1,1,24,3072]{6,5,4,3,2,1,0:T(8,128)(2,1)} %constant_dynamic-slice_fusion.17.refs_2_), channel_id=1, source_target_pairs={{0,2},{1,3},{2,0},{3,1},{4,6},{5,7},{6,4},{7,5},{8,10},{9,11},{10,... | collective-permute-start | bytes 1769480 | tf_op jit(solution)/shard_map/ppermute | solution.py:576
  391.0 20.0 %collective-permute-start.20 = (bf16[2,2,2,1,1,24,1536]{6,5,4,3,2,1,0:T(8,128)(2,1)S(1)}, bf16[2,2,2,1,1,24,1536]{6,5,4,3,2,1,0:T(8,128)(2,1)}, u32[]{:S(2)}, u32[]{:S(2)}) collective-permute-start(bf16[2,2,2,1,1,24,1536]{6,5,4,3,2,1,0:T(8,128)(2,1)S(1)} %constant_dynamic-slice_fusion.14.refs_3_), channel_id=1, source_target_pairs={{0,2},{1,3},{2,0},{3,1},{4,6},{5,7},{6,4},{7,5},{8,10},{9,11},{10,... | collective-permute-start | bytes 1769480 | tf_op jit(solution)/shard_map/ppermute | solution.py:576
  395.4 24.0 %collective-permute-start.18 = (bf16[2,1,1,1,1,24,3072]{6,5,4,3,2,1,0:T(8,128)(2,1)}, bf16[2,1,1,1,1,24,3072]{6,5,4,3,2,1,0:T(8,128)(2,1)}, u32[]{:S(2)}, u32[]{:S(2)}) collective-permute-start(bf16[2,1,1,1,1,24,3072]{6,5,4,3,2,1,0:T(8,128)(2,1)} %constant_dynamic-slice_fusion.15.refs_2_), channel_id=1, source_target_pairs={{0,8},{1,9},{2,10},{3,11},{4,12},{5,13},{6,14},{7,15},{8,0},{9,1},... | collective-permute-start | bytes 884744 | tf_op jit(solution)/shard_map/ppermute | solution.py:576
  413.5 31.8 %collective-permute-start.31 = (bf16[2,2,1,1,1,24,1536]{6,5,4,3,2,1,0:T(8,128)(2,1)}, bf16[2,2,1,1,1,24,1536]{6,5,4,3,2,1,0:T(8,128)(2,1)}, u32[]{:S(2)}, u32[]{:S(2)}) collective-permute-start(bf16[2,2,1,1,1,24,1536]{6,5,4,3,2,1,0:T(8,128)(2,1)} %constant_dynamic-slice_fusion.12.refs_7_), channel_id=1, source_target_pairs={{0,4},{1,5},{2,6},{3,7},{4,0},{5,1},{6,2},{7,3},{8,12},{9,13},{10,... | collective-permute-start | bytes 884744 | tf_op jit(solution)/shard_map/ppermute | solution.py:576
  417.9 57.3 %collective-permute-start.26 = (bf16[2,2,2,2,1,24,1152]{6,5,4,3,2,1,0:T(8,128)(2,1)}, bf16[2,2,2,2,1,24,1152]{6,5,4,3,2,1,0:T(8,128)(2,1)S(1)}, u32[]{:S(2)}, u32[]{:S(2)}) collective-permute-start(bf16[2,2,2,2,1,24,1152]{6,5,4,3,2,1,0:T(8,128)(2,1)} %constant_dynamic-slice_fusion.10.refs_9_), channel_id=1, source_target_pairs={{0,1},{1,0},{2,3},{3,2},{4,5},{5,4},{6,7},{7,6},{8,9},{9,8},{10,11... | collective-permute-start | bytes 2654216 | tf_op jit(solution)/shard_map/ppermute | solution.py:576
  418.9 52.4 %collective-permute-start.21 = (bf16[2,2,2,2,1,24,1152]{6,5,4,3,2,1,0:T(8,128)(2,1)}, bf16[2,2,2,2,1,24,1152]{6,5,4,3,2,1,0:T(8,128)(2,1)}, u32[]{:S(2)}, u32[]{:S(2)}) collective-permute-start(bf16[2,2,2,2,1,24,1152]{6,5,4,3,2,1,0:T(8,128)(2,1)} %constant_dynamic-slice_fusion.11.refs_8_), channel_id=1, source_target_pairs={{0,1},{1,0},{2,3},{3,2},{4,5},{5,4},{6,7},{7,6},{8,9},{9,8},{10,11... | collective-permute-start | bytes 2654216 | tf_op jit(solution)/shard_map/ppermute | solution.py:576
  421.0 16.6 %copy-start.21 = (bf16[2,1,1,1,1,24,3072]{6,5,4,3,2,1,0:T(8,128)(2,1)}, bf16[2,1,1,1,1,24,3072]{6,5,4,3,2,1,0:T(8,128)(2,1)S(1)}, u32[]{:S(2)}) copy-start(bf16[2,1,1,1,1,24,3072]{6,5,4,3,2,1,0:T(8,128)(2,1)S(1)} %add_convert_fusion.10) | copy-start | bytes 884740
  421.7 44.4 %collective-permute-start.34 = (bf16[1,1,1,1,1,24,3072]{6,5,4,3,2,1,0:T(8,128)(2,1)}, bf16[1,1,1,1,1,24,3072]{6,5,4,3,2,1,0:T(8,128)(2,1)S(1)}, u32[]{:S(2)}, u32[]{:S(2)}) collective-permute-start(bf16[1,1,1,1,1,24,3072]{6,5,4,3,2,1,0:T(8,128)(2,1)} %constant_dynamic-slice_fusion.13.refs_6_), channel_id=1, source_target_pairs={{0,16},{1,17},{2,18},{3,19},{4,20},{5,21},{6,22},{7,23},{8,24},{9,... | collective-permute-start | bytes 442376 | tf_op jit(solution)/shard_map/ppermute | solution.py:576
  424.1 14.3 %copy-start.34 = (f32[2,768]{1,0:T(2,128)S(1)}, f32[2,768]{1,0:T(2,128)}, u32[]{:S(2)}) copy-start(f32[2,768]{1,0:T(2,128)} %slice.77) | copy-start | bytes 18436
  424.1 14.3 %copy-start.35 = (f32[8,768]{1,0:T(8,128)S(1)}, f32[8,768]{1,0:T(8,128)}, u32[]{:S(2)}) copy-start(f32[8,768]{1,0:T(8,128)} %get-tuple-element.65) | copy-start | bytes 73732
  439.4 10.4 %copy-start = (bf16[8,196,768]{2,1,0:T(8,128)(2,1)S(1)}, bf16[8,196,768]{2,1,0:T(8,128)(2,1)}, u32[]{:S(2)}) copy-start(bf16[8,196,768]{2,1,0:T(8,128)(2,1)} %get-tuple-element.61.refs_1_) | copy-start | bytes 7225348
  441.3 11.8 %all-to-all-start.4 = ((f32[32,1,336]{2,1,0:T(1,128)}), f32[32,1,336]{2,1,0:T(1,128)S(1)}, u32[]{:S(2)}, u32[]{:S(2)}) async-start(f32[32,1,336]{2,1,0:T(1,128)} %reshape.2288), calls=%async_computation.4 | async-start | bytes 98304 | tf_op jit(solution)/shard_map/all_to_all | solution.py:720
  447.8 15.0 %collective-permute-start.32 = (bf16[2,1,1,1,1,24,1536]{6,5,4,3,2,1,0:T(8,128)(2,1)}, bf16[2,1,1,1,1,24,1536]{6,5,4,3,2,1,0:T(8,128)(2,1)}, u32[]{:S(2)}, u32[]{:S(2)}) collective-permute-start(bf16[2,1,1,1,1,24,1536]{6,5,4,3,2,1,0:T(8,128)(2,1)} %constant_dynamic-slice_fusion.1), channel_id=1, source_target_pairs={{0,8},{1,9},{2,10},{3,11},{4,12},{5,13},{6,14},{7,15},{8,0},{9,1},... | collective-permute-start | bytes 442376 | tf_op jit(solution)/shard_map/ppermute | solution.py:576
  453.1 9.7 %copy-start.24 = (bf16[2,2,1,1,1,24,1536]{6,5,4,3,2,1,0:T(8,128)(2,1)S(1)}, bf16[2,2,1,1,1,24,1536]{6,5,4,3,2,1,0:T(8,128)(2,1)}, u32[]{:S(2)}) copy-start(bf16[2,2,1,1,1,24,1536]{6,5,4,3,2,1,0:T(8,128)(2,1)} %copy-done.23) | copy-start | bytes 884740
  453.7 58.2 %all-to-all-start.3 = ((bf16[4,2,196,768]{3,1,2,0:T(2,128)(2,1)}), bf16[4,2,196,768]{3,1,2,0:T(2,128)(2,1)}, u32[]{:S(2)}, u32[]{:S(2)}) async-start(bf16[4,2,196,768]{3,1,2,0:T(2,128)(2,1)} %copy.125), calls=%async_computation.3 | async-start | bytes 4816896 | tf_op jit(solution)/shard_map/all_to_all | solution.py:672
  458.2 8.5 %copy-start.22 = (bf16[2,1,1,1,1,24,3072]{6,5,4,3,2,1,0:T(8,128)(2,1)S(1)}, bf16[2,1,1,1,1,24,3072]{6,5,4,3,2,1,0:T(8,128)(2,1)}, u32[]{:S(2)}) copy-start(bf16[2,1,1,1,1,24,3072]{6,5,4,3,2,1,0:T(8,128)(2,1)} %copy-done.21) | copy-start | bytes 884740
  463.8 6.8 %collective-permute-start.33 = (bf16[1,1,1,1,1,24,1536]{6,5,4,3,2,1,0:T(8,128)(2,1)S(1)}, bf16[1,1,1,1,1,24,1536]{6,5,4,3,2,1,0:T(8,128)(2,1)S(1)}, u32[]{:S(2)}, u32[]{:S(2)}) collective-permute-start(bf16[1,1,1,1,1,24,1536]{6,5,4,3,2,1,0:T(8,128)(2,1)S(1)} %constant_dynamic-slice_fusion), channel_id=1, source_target_pairs={{0,16},{1,17},{2,18},{3,19},{4,20},{5,21},{6,22},{7,23},{8,24},{9,... | collective-permute-start | bytes 221192 | tf_op jit(solution)/shard_map/ppermute | solution.py:576
  473.4 12.5 %collective-permute-start.22 = (bf16[2,2,1,2,1,24,1152]{6,5,4,3,2,1,0:T(8,128)(2,1)}, bf16[2,2,1,2,1,24,1152]{6,5,4,3,2,1,0:T(8,128)(2,1)}, u32[]{:S(2)}, u32[]{:S(2)}) collective-permute-start(bf16[2,2,1,2,1,24,1152]{6,5,4,3,2,1,0:T(8,128)(2,1)} %constant_dynamic-slice_fusion.9), channel_id=1, source_target_pairs={{0,4},{1,5},{2,6},{3,7},{4,0},{5,1},{6,2},{7,3},{8,12},{9,13},{10,... | collective-permute-start | bytes 1327112 | tf_op jit(solution)/shard_map/ppermute | solution.py:576
  477.5 12.4 %collective-permute-start.27 = (bf16[2,1,2,2,1,24,1152]{6,5,4,3,2,1,0:T(8,128)(2,1)S(1)}, bf16[2,1,2,2,1,24,1152]{6,5,4,3,2,1,0:T(8,128)(2,1)S(1)}, u32[]{:S(2)}, u32[]{:S(2)}) collective-permute-start(bf16[2,1,2,2,1,24,1152]{6,5,4,3,2,1,0:T(8,128)(2,1)S(1)} %constant_dynamic-slice_fusion.5), channel_id=1, source_target_pairs={{0,8},{1,9},{2,10},{3,11},{4,12},{5,13},{6,14},{7,15},{8,0},{9,1},... | collective-permute-start | bytes 1327112 | tf_op jit(solution)/shard_map/ppermute | solution.py:576
  487.1 9.5 %collective-permute-start.23 = (bf16[2,1,1,2,1,24,1152]{6,5,4,3,2,1,0:T(8,128)(2,1)S(1)}, bf16[2,1,1,2,1,24,1152]{6,5,4,3,2,1,0:T(8,128)(2,1)S(1)}, u32[]{:S(2)}, u32[]{:S(2)}) collective-permute-start(bf16[2,1,1,2,1,24,1152]{6,5,4,3,2,1,0:T(8,128)(2,1)S(1)} %constant_dynamic-slice_fusion.8), channel_id=1, source_target_pairs={{0,8},{1,9},{2,10},{3,11},{4,12},{5,13},{6,14},{7,15},{8,0},{9,1},... | collective-permute-start | bytes 663560 | tf_op jit(solution)/shard_map/ppermute | solution.py:576
  490.0 15.2 %collective-permute-start.28 = (bf16[1,1,2,2,1,24,1152]{6,5,4,3,2,1,0:T(8,128)(2,1)S(1)}, bf16[1,1,2,2,1,24,1152]{6,5,4,3,2,1,0:T(8,128)(2,1)S(1)}, u32[]{:S(2)}, u32[]{:S(2)}) collective-permute-start(bf16[1,1,2,2,1,24,1152]{6,5,4,3,2,1,0:T(8,128)(2,1)S(1)} %constant_dynamic-slice_fusion.4), channel_id=1, source_target_pairs={{0,16},{1,17},{2,18},{3,19},{4,20},{5,21},{6,22},{7,23},{8,24},{9,... | collective-permute-start | bytes 663560 | tf_op jit(solution)/shard_map/ppermute | solution.py:576
  496.6 9.8 %collective-permute-start.24 = (bf16[1,1,1,2,1,24,1152]{6,5,4,3,2,1,0:T(8,128)(2,1)S(1)}, bf16[1,1,1,2,1,24,1152]{6,5,4,3,2,1,0:T(8,128)(2,1)S(1)}, u32[]{:S(2)}, u32[]{:S(2)}) collective-permute-start(bf16[1,1,1,2,1,24,1152]{6,5,4,3,2,1,0:T(8,128)(2,1)S(1)} %constant_dynamic-slice_fusion.7), channel_id=1, source_target_pairs={{0,16},{1,17},{2,18},{3,19},{4,20},{5,21},{6,22},{7,23},{8,24},{9,... | collective-permute-start | bytes 331784 | tf_op jit(solution)/shard_map/ppermute | solution.py:576
  505.3 4.8 collective-permute-start.29
  506.5 5.3 %collective-permute-start.25 = (bf16[1,1,1,1,1,24,1152]{6,5,4,3,2,1,0:T(8,128)(2,1)S(1)}, bf16[1,1,1,1,1,24,1152]{6,5,4,3,2,1,0:T(8,128)(2,1)S(1)}, u32[]{:S(2)}, u32[]{:S(2)}) collective-permute-start(bf16[1,1,1,1,1,24,1152]{6,5,4,3,2,1,0:T(8,128)(2,1)S(1)} %constant_dynamic-slice_fusion.6), channel_id=1, source_target_pairs={{0,2},{1,3},{2,0},{3,1},{4,6},{5,7},{6,4},{7,5},{8,10},{9,11},{10,... | collective-permute-start | bytes 165896 | tf_op jit(solution)/shard_map/ppermute | solution.py:576
  510.2 5.1 collective-permute-start.30
  511.8 5.6 %copy-start.3 = (bf16[4,2,196,768]{3,1,2,0:T(2,128)(2,1)S(1)}, bf16[4,2,196,768]{3,1,2,0:T(2,128)(2,1)}, u32[]{:S(2)}) copy-start(bf16[4,2,196,768]{3,1,2,0:T(2,128)(2,1)} %copy-done.2) | copy-start | bytes 7225348
  (23 other events, 32.2 us)
Sparse Core Ops, SparseCore 0:
  12.8 125.4 all-gather.1
  321.0 146.1 reduce-scatter.1

commit v4 on v3

--- a/solution.py
+++ b/solution.py
@@ -318,12 +318,18 @@
                 djoin_ref[:, :, pair_cols(i, pair, width)] = grads[i].reshape(frames, tile, PAIR)
 
 
-def temporal_back_finish(places, dat_ref, x_ref, djoin_ref, qk_ref, v_in_ref, v_ref, gx_ref, vec_ref):
+def temporal_back_finish(
+    places, me_ref, dat_ref, x_ref, djoin_ref, qk_ref, v_in_ref, v_ref, vec_t_ref, vec_s_ref, vec_f_ref,
+    gx_ref, turned_ref, vec_ref,
+):
     chunk, padded, width = x_ref.shape
 
     @pl.when(pl.program_id(0) == 0)
     def _():
         vec_ref[...] = jnp.zeros_like(vec_ref)
+        vec_ref[2:4] = vec_t_ref[0:2]
+        vec_ref[4:7] = vec_s_ref[0:3]
+        vec_ref[7:14] = vec_f_ref[0:7]
 
     d_joined = rows_of(djoin_ref[...])
     d_norm = dot_nt(d_joined[:, : 2 * width], qk_ref[...]) + dot_nt(d_joined[:, 2 * width :], v_in_ref[:, :width])
@@ -334,13 +340,17 @@
     grad = rows_of(dat_ref[...]) + norm_back(unit, scale, v_ref[0:1], d_norm)
     gx_ref[...] = grad.astype(BF).reshape(chunk, padded, width)[:, :places]
 
+    @pl.when(pl.program_id(0) == pl.num_programs(0) - 1)
+    def _():
+        turned_ref[...] = vec_ref[...].T.astype(BF)
+
 
 def whole(shape):
     return pl.BlockSpec(shape, lambda *i: (0,) * len(shape))
 
 
 def cost(micros):
-    return pl.CostEstimate(flops=int(micros * 1e9), bytes_accessed=0, transcendentals=0)
+    return pl.CostEstimate(flops=int(micros * 1e8), bytes_accessed=0, transcendentals=0)
 
 
 def params(mib=60):
@@ -373,16 +383,7 @@
 
 
 def gate(value, *after):
-    def body(*refs):
-        pass
-
-    return pl.pallas_call(
-        body,
-        in_specs=[ANYWHERE] * (1 + len(after)),
-        out_specs=ANYWHERE,
-        out_shape=jax.ShapeDtypeStruct(value.shape, value.dtype),
-        input_output_aliases={0: 0},
-    )(value, *after)
+    return lax.optimization_barrier((value,) + after)[0]
 
 
 def frame_block(chunk, padded, width):
@@ -559,17 +560,35 @@
     )
 
 
-def run_temporal_back_finish(places, d_at, x, d_joined, qk, v_in, v, chunk=2, after=()):
+def run_temporal_back_finish(places, chunk, me, d_at, x, d_joined, qk, v_in, v, vecs, after=()):
     frames, padded, width = x.shape
-    block, wide = frame_block(chunk, padded, width), frame_block(chunk, padded, 3 * width)
-    return launch(
-        functools.partial(temporal_back_finish, places), 11, (d_at, x, d_joined, qk, v_in, v),
-        [block, block, wide] + wholes((qk, v_in, v)), [frame_block(chunk, places, width), whole((8, width))],
-        (shape_of(frames, places, width), shape_of(8, width, dtype=F32)), (frames // chunk,), after=after,
-    )
-
-
-AXES = ("dp", "seq")
+    skip = len(after)
+
+    def body(*refs):
+        temporal_back_finish(places, *refs[:10], *refs[10 + skip :])
+
+    def mixed_block(height, wide):
+        return pl.BlockSpec((chunk, height, wide), lambda i, me: (jnp.bitwise_xor(i, me[0]), 0, 0))
+
+    consts = (qk, v_in, v) + tuple(vecs)
+    return pl.pallas_call(
+        body,
+        grid_spec=pltpu.PrefetchScalarGridSpec(
+            num_scalar_prefetch=1,
+            grid=(frames // chunk,),
+            in_specs=[mixed_block(padded, width), mixed_block(padded, width), mixed_block(padded, 3 * width)]
+            + wholes(consts) + [ANYWHERE] * skip,
+            out_specs=[pl.BlockSpec((chunk, places, width), lambda i, me: (i, 0, 0)), whole((width, PAIR))],
+            scratch_shapes=[pltpu.VMEM((PAIR, width), F32)],
+        ),
+        out_shape=(shape_of(frames, places, width), shape_of(width, PAIR)),
+        cost_estimate=cost(13),
+        compiler_params=params(),
+    )(me, d_at, x, d_joined, *consts, *after)
+
+
+AXES = ("dp_hi", "dp_lo", "seq_hi", "seq_lo")
+SEQ = AXES[2:]
 
 
 def swap(values, bit, n):
@@ -609,13 +628,18 @@
 
 
 class Scatter:
-    def __init__(self, values, n, order):
-        self.n, self.bits, self.order = n, n.bit_length() - 1, list(order)
+    def __init__(self, values, n, order, axes):
+        self.n, self.bits, self.order, self.axes = n, n.bit_length() - 1, list(order), axes
         self.rows, self.tail = values.shape[0] // n, values.shape[1:]
         self.me = lax.axis_index(AXES)
         self.held = values.reshape((2,) * self.bits + (self.rows,) + self.tail)
 
     def start(self):
+        self.last = not self.order
+        if self.last and self.axes:
+            held = self.held.reshape((-1, self.rows) + self.tail)
+            self.got = lax.all_to_all(held, self.axes, split_axis=0, concat_axis=0, tiled=True)
+            return held
         bit = self.order.pop(0)
         axis = self.bits - 1 - bit
         mine = (self.me >> bit) & 1
@@ -626,23 +650,26 @@
 
     def end(self, *after):
         got = gate(self.got, *after) if after else self.got
-        self.held = (self.keep.astype(F32) + got.astype(F32)).astype(self.held.dtype)
+        if self.last:
+            self.held = jnp.sum(got.astype(F32), axis=0)
+        else:
+            self.held = (self.keep.astype(F32) + got.astype(F32)).astype(self.held.dtype)
 
     def rest(self, *after):
         while self.order:
             self.start()
-            self.end(*(() if self.order else after))
-        return self.result()
-
-    def result(self):
-        return self.held.reshape((self.rows,) + self.tail)
+            self.end()
+        if self.axes:
+            self.start()
+            self.end(*after)
+        return self.held.astype(F32).reshape((self.rows,) + self.tail)
 
 
 def on_device(n, tokens, tg, tb, t_in, t_out, t_lin, sg, sb, s_in, s_out, fg, fb, w1, b1, w2, cotangent):
     bits = n.bit_length() - 1
     top = tuple(range(bits - 1, 2, -1))
     order_a, order_b, order_c = top + (1, 2, 0), top + (2, 1, 0), (2,) + top + (1, 0)
-    back_y, back_z = (0, 2) + top[::-1] + (1,), (0,) + top[::-1] + (2, 1)
+    with_y, with_x = ((0, 2), (AXES[0], AXES[2])), ((0, 1), AXES[:2])
     rows, width = t_in.shape[0], t_in.shape[0] * n
     parts = w2.shape[0] // rows
     hidden = w1.shape[1]
@@ -665,11 +692,23 @@
     feed = lax.all_gather(feed, AXES, axis=0, tiled=True)
 
     def own_clip(grid):
-        clip = lax.all_to_all(grid, "seq", split_axis=0, concat_axis=0, tiled=True)
+        clip = lax.all_to_all(grid, SEQ, split_axis=0, concat_axis=0, tiled=True)
         return jnp.pad(clip.reshape(frames, places, width), ((0, 0), (0, extra), (0, 0)))
 
     def own_frames(clip):
-        return lax.all_to_all(clip.reshape(tokens.shape), "seq", split_axis=0, concat_axis=0, tiled=True)
+        return lax.all_to_all(clip.reshape(tokens.shape), SEQ, split_axis=0, concat_axis=0, tiled=True)
+
+    def swap_pieces(clip, count):
+        pieces = clip.reshape((count, tokens.shape[1]) + tokens.shape[2:])
+        return [pieces[0]] + [lax.ppermute(pieces[k], AXES, [(i, i ^ k) for i in range(n)]) for k in range(1, count)]
+
+    def in_order(got, me):
+        step = 1
+        while step < len(got):
+            flip = (me & step) != 0
+            got = [jnp.where(flip, got[j ^ step], got[j]) for j in range(len(got))]
+            step *= 2
+        return jnp.stack(got)
 
     x = own_clip(tokens)
     t_qk = Gather(t_in[:, : 2 * width], n, order_a)
@@ -695,32 +734,45 @@
     )
     g_space = run_join_grads(norm_s, d_joined_s, mixed_s, d_space, after=(output[0, :1, 0, :128],))
 
-    def beside(chains, kernel, *args):
+    def beside(chains, kernel, *args, after=()):
         sends = tuple(chain.start() for chain in chains)
-        done = kernel(*args, after=sends)
+        done = kernel(*args, after=sends + tuple(after))
         for chain in chains:
             chain.end(done[0] if isinstance(done, (tuple, list)) else done)
         return done
 
-    gs = Scatter(g_space, n, order_a[::-1])
+    gs = Scatter(g_space, n, *with_y)
     g_lin = beside((gs,), run_tile_grad, proj_t, d_time)
-    d_proj, d_mixed_t, vec_t1 = beside((gs,), run_temporal_back_project, d_time, t_ol_w)
-    g_out = run_tile_grad(mixed_t, d_proj)
-    go = Scatter(jnp.concatenate([g_out, g_lin], axis=1), n, order_b[::-1])
-    d_joined_t = beside((gs, go), run_temporal_back_attend, joined_t, d_mixed_t)
-    g_qkv = beside((gs, go), run_join_grads, norm_t, d_joined_t)
+    sends = (gs.start(),)
+    d_proj, d_mixed_t, vec_t1 = run_temporal_back_project(d_time, t_ol_w, after=sends)
+    g_out = run_tile_grad(mixed_t, d_proj, after=sends)
+    go = Scatter(jnp.concatenate([g_out, g_lin], axis=1), n, (0, 1, 2) + top[::-1], None)
+    d_joined_t = beside((go,), run_temporal_back_attend, joined_t, d_mixed_t)
+    gs.end(d_joined_t)
+    sends = (gs.start(),)
+    g_qkv = beside((go,), run_join_grads, norm_t, d_joined_t)
     half = 3 * width // 2
-    gq, gr = Scatter(g_qkv[:, :half], n, back_y), Scatter(g_qkv[:, half:], n, back_z)
-    g_x, vec_t0 = beside(
-        (gs, go, gq, gr), run_temporal_back_finish, places, d_after_time, x, d_joined_t, t_qk_w, t_v_w, vec
-    )
-    g_x = own_frames(g_x)
-    g_vec = jnp.concatenate([vec_t0[:2], vec_t1[:2], vec_s[:3], vec_f[: 3 + parts]], axis=0)
-    g_vec = g_vec.reshape(n_vec, n, rows).transpose(1, 0, 2)
-    v = jnp.sum(lax.all_to_all(g_vec, AXES, split_axis=0, concat_axis=0, tiled=True), axis=0)
-    g_i = jnp.concatenate([gq.rest(), gr.rest(o_w1[:1, :128])], axis=1).astype(F32)
-    g_s = gs.rest().astype(F32)
-    g_o = go.rest().astype(F32)
+    gq = Scatter(g_qkv[:, :half], n, (0,), (AXES[0], AXES[1], AXES[2]))
+    gq.start()
+    me_seq = (lax.axis_index(SEQ)).astype(jnp.int32)
+    g_x, vec_cols = beside(
+        (go,), run_temporal_back_finish, places, tokens.shape[1], me_seq.reshape(1), d_after_time, x, d_joined_t,
+        t_qk_w, t_v_w, vec, (vec_t1, vec_s, vec_f),
+    )
+    gs.end(g_x)
+    gq.end(g_x, o_w1)
+    gr = Scatter(jnp.concatenate([g_qkv[:, half:], gate(vec_cols, gq.held)], axis=1), n, *with_y)
+    pieces = swap_pieces(g_x, tokens.shape[0])
+    for after in ((), pieces[1:]):
+        gr.start()
+        gr.end(*after)
+    g_q = gq.rest()
+    g_x = in_order(pieces, me_seq)
+    g_o = go.rest()
+    g_r = gr.rest()
+    g_s = gs.held.reshape(rows, 4 * width)
+    g_i = jnp.concatenate([g_q, g_r[:, :half]], axis=1)
+    v = g_r[:, half : half + n_vec].T
     return (
         output, g_x, v[0], v[1:4], g_i, g_o[:, :width], g_o[:, width : 2 * width],
         v[4], v[5:7], g_s[:, : 3 * width], g_s[:, 3 * width :], v[7], v[8:10],
@@ -729,12 +781,15 @@
 
 
 def solution(mesh):
-    shard = P(("dp", "seq"))
-    cols = P(None, ("dp", "seq"))
-    mat = P(("dp", "seq"), None)
-    tok = P("dp", "seq", None, None)
+    dp, seq = AXES[:2], AXES[2:]
+    dims = mesh.devices.shape
+    halved = jax.sharding.Mesh(mesh.devices.reshape(dims[0] // 2, 2, dims[1] // 2, 2), AXES)
+    shard = P(AXES)
+    cols = P(None, AXES)
+    mat = P(AXES, None)
+    tok = P(dp, seq, None, None)
     in_specs = (tok, shard, cols, mat, mat, mat, shard, cols, mat, mat, shard, cols, mat, shard, mat, tok)
     out_specs = (tok, tok, shard, cols, mat, mat, mat, shard, cols, mat, mat, shard, cols, mat, shard, mat)
     return jax.shard_map(
-        functools.partial(on_device, mesh.size), mesh=mesh, in_specs=in_specs, out_specs=out_specs, check_vma=False
-    )
+        functools.partial(on_device, mesh.size), mesh=halved, in_specs=in_specs, out_specs=out_specs, check_vma=False
+    )

time: 541 us -> 503 us (0.930)
  local copies, waits for them, and re-layouts: 73.2 us -> 49 us
  Pallas kernels: 257 us -> 250 us
    ppermute x35 -> x25, waiting for transfers between devices: 80.5 us -> 50.7 us  [swap(): return lax.ppermute(values, AXES, [(i, i ^ 1 << bit) for i in range(n)])]
    ppermute x0 -> x3, waiting for transfers between devices: none -> 22.6 us  [swap_pieces(): lax.ppermute(pieces[k], AXES, [(i, i ^ k) for i in range(n)])]
    pallas_call x14 -> x13, Pallas kernels: 255 us -> 234 us  [launch(): pl.pallas_call(body, grid=grid, in_specs=list(in_specs) + [ANYWHERE] * sk...]
    unnamed x97 -> x75, local copies, waits for them, and re-layouts: 28.8 us -> 13.6 us
    pallas_call x13 -> x1, Pallas kernels: 0.01 us -> 13.5 us  [run_temporal_back_finish(): pl.pallas_call(body, grid_spec=pltpu.PrefetchScalarGridSpec(num_scalar_pr...]
    ppermute x35 -> x25, starting transfers between devices: 45.4 us -> 34 us  [swap(): return lax.ppermute(values, AXES, [(i, i ^ 1 << bit) for i in range(n)])]
    all_to_all x5 -> x6, starting transfers between devices: 20.4 us -> 29.7 us  [the longest x3 16.6 us: start(): lax.all_to_all(held, self.axes, split_axis=0, concat_axis=0, tiled=True)]
    all_to_all x5 -> x6, waiting for transfers between devices: 2.33 us -> 8.34 us  [the longest x3 6.53 us: start(): lax.all_to_all(held, self.axes, split_axis=0, concat_axis=0, tiled=True)]
  transfers between devices with their start and end apart: 42 -> 36, of which waited for: 20 -> 17; matrix products, arithmetic and copies ran while one was open for 13% -> 13% of each run, Pallas kernels for 33% -> 32%
where the time goes in v4:
time: 503 us; the launch traced here: 494 us
  Pallas kernels  250 us (50%)
  waiting for transfers between devices  81.8 us (16%)
  starting transfers between devices  65.8 us (13%)
  local copies, waits for them, and re-layouts  49 us (10%)
  other arithmetic  32.7 us (7%)
  between operations  15.2 us (3%)
    pallas_call x13, Pallas kernels, launch(): pl.pallas_call(body, grid=grid, in_specs=list(in_specs) + [ANYWHERE] * sk...  234 us
    ppermute x25, waiting for transfers between devices, swap(): return lax.ppermute(values, AXES, [(i, i ^ 1 << bit) for i in range(n)])  50.7 us
    ppermute x25, starting transfers between devices, swap(): return lax.ppermute(values, AXES, [(i, i ^ 1 << bit) for i in range(n)])  34 us
    ppermute x3, waiting for transfers between devices, swap_pieces(): lax.ppermute(pieces[k], AXES, [(i, i ^ k) for i in range(n)])  22.6 us
    all_to_all x3, starting transfers between devices, start(): lax.all_to_all(held, self.axes, split_axis=0, concat_axis=0, tiled=True)  16.6 us
    convert_element_type x9, other arithmetic, end(): (self.keep.astype(F32) + got.astype(F32)).astype(self.held.dtype)  15.4 us
    unnamed x75, local copies, waits for them, and re-layouts  13.6 us
    pallas_call x1, Pallas kernels, run_temporal_back_finish(): pl.pallas_call(body, grid_spec=pltpu.PrefetchScalarGridSpec(num_scalar_pr...  13.5 us
  transfers between devices with their start and end apart: 36, of which 17 were waited for; matrix products, arithmetic and copies ran while one was open for 13% of the time, Pallas kernels for 32%

profile of v4, /device:TPU:0, one launch (start us, length us, event | category | flops | bytes accessed | tf_op | source)
XLA Modules:
  0.0 494.5 jit_solution(10725063028742012046)
XLA Ops:
  8.3 2.1 reshape.2266
  12.8 4.7 all-to-all-start
  17.8 3.0 collective-permute-start.5
  20.8 2.7 collective-permute-start.10
  23.9 2.7 collective-permute-start.6
  26.6 10.7 %collective-permute-done = bf16[1,1,1,1,1,24,1536]{6,5,4,3,2,1,0:T(8,128)(2,1)S(1)} collective-permute-done((bf16[1,1,1,1,1,24,1536]{6,5,4,3,2,1,0:T(8,128)(2,1)S(1)}, bf16[1,1,1,1,1,24,1536]{6,5,4,3,2,1,0:T(8,128)(2,1)S(1)}, u32[]{:S(2)}, u32[]{:S(2)}) %collective-permute-start) | collective-permute-done | bytes 73760 | tf_op jit(solution)/shard_map/ppermute | solution.py:595
  37.3 1.8 collective-permute-start.1
  39.6 2.7 collective-permute-done.6
  42.3 2.3 collective-permute-start.7
  44.7 2.3 collective-permute-done.1
  47.1 2.0 collective-permute-start.2
  50.9 6.6 %collective-permute-done.7 = bf16[2,1,2,1,1,24,896]{6,5,2,0,4,3,1:T(8,128)(2,1)S(1)} collective-permute-done((bf16[2,1,2,1,1,24,896]{6,5,2,0,4,3,1:T(8,128)(2,1)S(1)}, bf16[2,1,2,1,1,24,896]{6,5,2,0,4,3,1:T(8,128)(2,1)S(1)}, u32[]{:S(2)}, u32[]{:S(2)}) %collective-permute-start.7) | collective-permute-done | bytes 172064 | tf_op jit(solution)/shard_map/ppermute | solution.py:595
  57.6 3.0 collective-permute-start.8
  62.2 2.8 collective-permute-start.3
  65.4 1.7 collective-permute-start.13
  67.3 9.6 %collective-permute-done.8 = bf16[2,2,2,1,1,24,896]{6,5,4,3,2,1,0:T(8,128)(2,1)S(1)} collective-permute-done((bf16[2,2,2,1,1,24,896]{6,5,4,3,2,1,0:T(8,128)(2,1)S(1)}, bf16[2,2,2,1,1,24,896]{6,5,4,3,2,1,0:T(8,128)(2,1)S(1)}, u32[]{:S(2)}, u32[]{:S(2)}) %collective-permute-start.8) | collective-permute-done | bytes 344096 | tf_op jit(solution)/shard_map/ppermute | solution.py:595
  77.8 11.3 %collective-permute-done.13 = bf16[2,2,2,1,1,24,1536]{6,5,0,1,2,4,3:T(8,128)(2,1)S(1)} collective-permute-done((bf16[2,2,2,1,1,24,1536]{6,5,0,1,2,4,3:T(8,128)(2,1)S(1)}, bf16[2,2,2,1,1,24,1536]{6,5,0,1,2,4,3:T(8,128)(2,1)S(1)}, u32[]{:S(2)}, u32[]{:S(2)}) %collective-permute-start.13) | collective-permute-done | bytes 589856 | tf_op jit(solution)/shard_map/ppermute | solution.py:595
  91.8 2.7 copy.126
  94.5 1.7 pad.11.refs_0_.refs_2_
  96.2 3.4 maximum_select_fusion
  99.7 11.5 %shard_map.279 = (bf16[8,208,768]{2,1,0:T(8,128)(2,1)}, bf16[8,208,2304]{2,1,0:T(8,128)(2,1)}) custom-call(bf16[8,208,768]{2,1,0:T(8,128)(2,1)} %pad.11.refs_0_.refs_2_, bf16[768,1536]{1,0:T(8,128)(2,1)} %bitcast.142, bf16[768,896]{1,0:T(8,128)(2,1)} %bitcast.149, f32[16,768]{1,0:T(8,128)} %slice_convert_fusion.refs_3_.refs_2_.refs_4_.refs_6_, ...), custom_call_target="tpu_custom_call" | custom-call | flops 900000000 | tf_op jit(solution)/shard_map/pallas_call | solution.py:373
  111.1 4.6 all-to-all-start.1
  116.5 2.9 collective-permute-done.14
  119.4 13.4 %shard_map.280.refs_1_ = bf16[8,208,768]{2,1,0:T(8,128)(2,1)} custom-call(bf16[8,208,2304]{2,1,0:T(8,128)(2,1)} %get-tuple-element.53.refs_0_), custom_call_target="tpu_custom_call" | custom-call | flops 1400000000 | tf_op jit(solution)/shard_map/pallas_call | solution.py:373
  132.9 1.7 maximum_select_fusion.1
  134.5 8.9 %shard_map.281 = (bf16[8,208,768]{2,1,0:T(8,128)(2,1)}, f32[8,208,768]{2,1,0:T(8,128)}) custom-call(bf16[8,208,768]{2,1,0:T(8,128)(2,1)} %pad.11.refs_0_.refs_2_, bf16[8,208,768]{2,1,0:T(8,128)(2,1)} %shard_map.280.refs_1_, bf16[768,1536]{1,0:T(8,128)(2,1)} %bitcast.144, f32[16,768]{1,0:T(8,128)} %slice_convert_fusion.refs_3_.refs_2_.refs_4_.refs_6_), custom_call_target="tpu_custom_call" | custom-call | flops 800000000 | tf_op jit(solution)/shard_map/pallas_call | solution.py:373
  143.4 1.8 all-to-all-done.1
  145.2 2.0 copy.151
  147.2 1.7 pad.13.refs_1_
  148.9 22.9 %shard_map.282 = (bf16[8,208,768]{2,1,0:T(8,128)(2,1)}, bf16[8,208,2304]{2,1,0:T(8,128)(2,1)}, bf16[8,208,768]{2,1,0:T(8,128)(2,1)}, f32[8,208,768]{2,1,0:T(8,128)}) custom-call(f32[8,208,768]{2,1,0:T(8,128)} %get-tuple-element.56.refs_0_.refs_1_, bf16[768,9216]{1,0:T(8,128)(2,1)} %all-gather.2.cloned.1.call-done.refs_1_.refs_2_.refs_3_, ...), custom_call_target="tpu_custom_call" | custom-call | flops 2300000000 | tf_op jit(solution)/shard_map/pallas_call | solution.py:373
  171.8 45.2 %shard_map.283 = (bf16[8,196,768]{2,1,0:T(8,128)(2,1)}, f32[8,208,768]{2,1,0:T(8,128)}, bf16[8,208,768]{2,1,0:T(8,128)(2,1)}, bf16[8,208,3072]{2,1,0:T(8,128)(2,...) custom-call(f32[8,208,768]{2,1,0:T(8,128)} %get-tuple-element.57.refs_0_, bf16[8,208,768]{2,1,0:T(8,128)(2,1)} %pad.13.refs_1_, ...), custom_call_target="tpu_custom_call" | custom-call | flops 4499999744 | tf_op jit(solution)/shard_map/pallas_call | solution.py:373
  217.0 25.4 %shard_map.284.refs_5_ = bf16[768,6144]{1,0:T(8,128)(2,1)} custom-call(bf16[1664,768]{1,0:T(8,128)(2,1)} %bitcast.166, bf16[1664,3072]{1,0:T(8,128)(2,1)} %bitcast.152, bf16[1664,3072]{1,0:T(8,128)(2,1)} %bitcast.151, bf16[1664,768]{1,0:T(8,128)(2,1)} %bitcast.140), custom_call_target="tpu_custom_call" | custom-call | flops 2500000000 | tf_op jit(solution)/shard_map/pallas_call | solution.py:373
  242.5 1.7 copy-done.15
  244.1 3.3 copy.152
  247.4 3.8 all-to-all-start.2
  251.2 41.8 %shard_map.285 = (bf16[8,208,768]{2,1,0:T(8,128)(2,1)}, bf16[8,208,2304]{2,1,0:T(8,128)(2,1)}, f32[8,208,768]{2,1,0:T(8,128)}, bf16[8,208,768]{2,1,0:T(8,128)(2,1)}, f32[8,768]{1,0:T(8,128)}) custom-call(f32[8,208,768]{2,1,0:T(8,128)} %get-tuple-element.60.refs_0_, f32[8,208,768]{2,1,0:T(8,128)} %get-tuple-element.56.refs_0_.refs_1_, ...), custom_call_target="tpu_custom_call" | custom-call | flops 4200000000 | tf_op jit(solution)/shard_map/pallas_call | solution.py:373
  293.6 16.3 %shard_map.286 = bf16[768,3072]{1,0:T(8,128)(2,1)} custom-call(bf16[1664,768]{1,0:T(8,128)(2,1)} %bitcast.170, bf16[1664,2304]{1,0:T(8,128)(2,1)} %bitcast.160, bf16[1664,768]{1,0:T(8,128)(2,1)} %bitcast.171, bf16[1664,768]{1,0:T(8,128)(2,1)} %bitcast.172, bf16[1,128]{1,0:T(2,128)(2,1)} %slice_bitcast_fusion.3.refs_4_), custom_call_target="tpu_custom_call" | custom-call | flops 1600000000 | tf_op jit(solution)/shard_map/pallas_call | solution.py:373
  309.9 2.0 constant_dynamic-slice_fusion.9.refs_2_
  313.3 5.8 %shard_map.287 = bf16[768,768]{1,0:T(8,128)(2,1)} custom-call(bf16[1664,768]{1,0:T(8,128)(2,1)} %bitcast.169, bf16[1664,768]{1,0:T(8,128)(2,1)} %bitcast.153, bf16[2,2,2,2,1,24,3072]{6,5,4,3,2,1,0:T(8,128)(2,1)} %copy-done.6), custom_call_target="tpu_custom_call" | custom-call | flops 600000000 | tf_op jit(solution)/shard_map/pallas_call | solution.py:373
  319.1 3.5 add_convert_fusion
  323.6 8.1 %shard_map.288 = (bf16[8,208,768]{2,1,0:T(8,128)(2,1)}, bf16[8,208,768]{2,1,0:T(8,128)(2,1)}, f32[8,768]{1,0:T(8,128)}) custom-call(bf16[8,208,768]{2,1,0:T(8,128)(2,1)} %get-tuple-element.66.refs_0_, bf16[768,1536]{1,0:T(8,128)(2,1)} %bitcast.145, bf16[2,2,1,2,1,24,3072]{6,5,4,3,2,1,0:T(8,128)(2,1)} %constant_dynamic-slice_fusion.8.refs_2_), custom_call_target="tpu_custom_call" | custom-call | flops 800000000 | tf_op jit(solution)/shard_map/pallas_call | solution.py:373
  331.7 5.7 %shard_map.289 = bf16[768,768]{1,0:T(8,128)(2,1)} custom-call(bf16[1664,768]{1,0:T(8,128)(2,1)} %bitcast.141, bf16[1664,768]{1,0:T(8,128)(2,1)} %bitcast.168, bf16[2,2,1,2,1,24,3072]{6,5,4,3,2,1,0:T(8,128)(2,1)} %constant_dynamic-slice_fusion.8.refs_2_), custom_call_target="tpu_custom_call" | custom-call | flops 600000000 | tf_op jit(solution)/shard_map/pallas_call | solution.py:373
  341.9 2.1 collective-permute-start.27
  343.9 18.2 %shard_map.290.refs_3_ = bf16[8,208,2304]{2,1,0:T(8,128)(2,1)} custom-call(bf16[8,208,2304]{2,1,0:T(8,128)(2,1)} %get-tuple-element.53.refs_0_, bf16[8,208,768]{2,1,0:T(8,128)(2,1)} %get-tuple-element.73.refs_1_, bf16[2,2,2,2,1,24,1536]{6,5,4,3,2,1,0:T(8,128)(2,1)} %constant_dynamic-slice_fusion.7.refs_2_), custom_call_target="tpu_custom_call" | custom-call | flops 2000000000 | tf_op jit(solution)/shard_map/pallas_call | solution.py:373
  362.1 2.0 add_convert_fusion.2
  366.1 1.6 collective-permute-start.17
  367.8 11.3 %shard_map.291 = bf16[768,2304]{1,0:T(8,128)(2,1)} custom-call(bf16[1664,768]{1,0:T(8,128)(2,1)} %bitcast.167, bf16[1664,2304]{1,0:T(8,128)(2,1)} %bitcast.139, bf16[2,2,2,1,1,24,1536]{6,5,4,3,2,1,0:T(8,128)(2,1)} %constant_dynamic-slice_fusion.6.refs_2_), custom_call_target="tpu_custom_call" | custom-call | flops 1200000000 | tf_op jit(solution)/shard_map/pallas_call | solution.py:373
  379.1 3.6 fusion.27
  386.4 2.8 add_convert_fusion.1
  389.2 6.4 %all-to-all-start.5 = ((bf16[8,24,3072]{2,1,0:T(8,128)(2,1)}), bf16[8,24,3072]{2,1,0:T(8,128)(2,1)S(1)}, u32[]{:S(2)}, u32[]{:S(2)}) async-start(bf16[8,24,3072]{2,1,0:T(8,128)(2,1)} %bitcast.163), calls=%async_computation.6 | async-start | bytes 2359296 | tf_op jit(solution)/shard_map/all_to_all | solution.py:641
  395.5 13.5 %shard_map.292 = (bf16[8,196,768]{2,1,0:T(8,128)(2,1)}, bf16[768,128]{1,0:T(8,128)(2,1)}) custom-call(s32[1]{0:T(128)} %bitcast.54.refs_0_, f32[8,208,768]{2,1,0:T(8,128)} %get-tuple-element.65.refs_1_, bf16[8,208,768]{2,1,0:T(8,128)(2,1)} %pad.11.refs_0_.refs_2_, bf16[8,208,2304]{2,1,0:T(8,128)(2,1)} %shard_map.290.refs_3_, bf16[768,1536]{1,0:T(8,128)(2,1)} %bitcast.143, ...), custom_call_target="tpu_custom_call" | custom-call | flops 1300000000 | tf_op jit(solution)/shard_map/pallas_call | solution.py:574
  410.4 2.0 shard_map.293
  412.4 2.3 add_convert_fusion.4
  414.7 1.8 pad_maximum_fusion.2
  417.5 2.1 collective-permute-start.25
  428.6 4.8 all-to-all-start.4
  433.4 1.5 add_convert_fusion.3
  434.9 1.9 collective-permute-start.23
  437.5 2.0 collective-permute-done.18
  439.5 20.7 %collective-permute-done.19 = bf16[2,196,768]{2,0,1:T(2,128)(2,1)} collective-permute-done((bf16[2,196,768]{2,0,1:T(2,128)(2,1)}, bf16[2,196,768]{2,0,1:T(2,128)(2,1)}, u32[]{:S(2)}, u32[]{:S(2)}) %collective-permute-start.19) | collective-permute-done | bytes 602144 | tf_op jit(solution)/shard_map/ppermute | solution.py:703
  462.3 5.4 %all-to-all-start.3 = ((bf16[8,24,1280]{2,1,0:T(8,128)(2,1)}), bf16[8,24,1280]{2,1,0:T(8,128)(2,1)S(1)}, u32[]{:S(2)}, u32[]{:S(2)}) async-start(bf16[8,24,1280]{2,1,0:T(8,128)(2,1)} %bitcast.78), calls=%async_computation.4 | async-start | bytes 983040 | tf_op jit(solution)/shard_map/all_to_all | solution.py:641
  467.7 2.0 select_bitcast_fusion.3
  470.0 3.3 copy.163
  476.1 5.4 %all-to-all-done.3 = bf16[8,24,1280]{2,1,0:T(8,128)(2,1)S(1)} async-done(((bf16[8,24,1280]{2,1,0:T(8,128)(2,1)}), bf16[8,24,1280]{2,1,0:T(8,128)(2,1)S(1)}, u32[]{:S(2)}, u32[]{:S(2)}) %all-to-all-start.3) | async-done | bytes 491552 | tf_op jit(solution)/shard_map/all_to_all | solution.py:641
  (192 shorter events, 49.0 us)
Async XLA Ops:
  7.2 4.6 copy-start.23
  7.2 4.6 copy-start.22
  7.2 141.7 %all-gather.2.cloned.1.call-start = ((), (), s32[]{:S(2)}) async-start(), calls=%async_computation.7 | async-start | bytes 14598144 | tf_op jit(solution)/shard_map/all_gather | solution.py:692
  12.6 4.8 copy-start.32
  12.7 4.9 copy-start.26
  12.7 4.9 copy-start.27
  12.7 4.9 copy-start.28
  12.7 4.9 copy-start.29
  12.7 4.9 copy-start.30
  12.7 4.9 copy-start.31
  12.7 5.0 %slice-start = ((bf16[24,2304]{1,0:T(8,128)(2,1)}), bf16[24,768]{1,0:T(8,128)(2,1)S(1)}, s32[]{:S(2)}) async-start(bf16[24,2304]{1,0:T(8,128)(2,1)} %param.19), calls=%async_computation.9 | async-start | bytes 73728 | tf_op jit(solution)/shard_map/slice | solution.py:715
  12.7 8.1 %copy-start.24 = (bf16[24,768]{1,0:T(8,128)(2,1)S(1)}, bf16[24,768]{1,0:T(8,128)(2,1)}, u32[]{:S(2)}) copy-start(bf16[24,768]{1,0:T(8,128)(2,1)} %param.20) | copy-start | bytes 110596
  12.8 8.1 %copy-start.25 = (bf16[24,768]{1,0:T(8,128)(2,1)S(1)}, bf16[24,768]{1,0:T(8,128)(2,1)}, u32[]{:S(2)}) copy-start(bf16[24,768]{1,0:T(8,128)(2,1)} %param.21) | copy-start | bytes 110596
  12.8 10.7 %copy-start.21 = (bf16[24,2304]{1,0:T(8,128)(2,1)S(1)}, bf16[24,2304]{1,0:T(8,128)(2,1)}, u32[]{:S(2)}) copy-start(bf16[24,2304]{1,0:T(8,128)(2,1)} %param.19) | copy-start | bytes 331780
  12.8 79.0 %all-to-all-start = ((bf16[4,2,196,768]{3,1,2,0:T(2,128)(2,1)}), bf16[4,2,196,768]{3,1,2,0:T(2,128)(2,1)}, u32[]{:S(2)}, u32[]{:S(2)}) async-start(bf16[4,2,196,768]{3,1,2,0:T(2,128)(2,1)} %param.16), calls=%async_computation | async-start | bytes 4816896 | tf_op jit(solution)/shard_map/all_to_all | solution.py:695
  17.8 6.1 %collective-permute-start.5 = (bf16[1,1,1,1,1,24,896]{6,5,4,3,2,1,0:T(8,128)(2,1)S(1)}, bf16[1,1,1,1,1,24,896]{6,5,4,3,2,1,0:T(8,128)(2,1)S(1)}, u32[]{:S(2)}, u32[]{:S(2)}) collective-permute-start(bf16[1,1,1,1,1,24,896]{6,5,4,3,2,1,0:T(8,128)(2,1)S(1)} %get-tuple-element.189), channel_id=1, source_target_pairs={{0,4},{1,5},{2,6},{3,7},{4,0},{5,1},{6,2},{7,3},{8,12},{9,13},{10,... | collective-permute-start | bytes 129032 | tf_op jit(solution)/shard_map/ppermute | solution.py:595
  20.8 18.3 %collective-permute-start.10 = (bf16[1,1,1,1,1,24,1536]{6,5,4,3,2,1,0:T(8,128)(2,1)S(1)}, bf16[1,1,1,1,1,24,1536]{6,5,4,3,2,1,0:T(8,128)(2,1)S(1)}, u32[]{:S(2)}, u32[]{:S(2)}) collective-permute-start(bf16[1,1,1,1,1,24,1536]{6,5,4,3,2,1,0:T(8,128)(2,1)S(1)} %bitcast.185), channel_id=1, source_target_pairs={{0,16},{1,17},{2,18},{3,19},{4,20},{5,21},{6,22},{7,23},{8,24},{9,... | collective-permute-start | bytes 221192 | tf_op jit(solution)/shard_map/ppermute | solution.py:595
  23.5 13.8 %collective-permute-start = (bf16[1,1,1,1,1,24,1536]{6,5,4,3,2,1,0:T(8,128)(2,1)S(1)}, bf16[1,1,1,1,1,24,1536]{6,5,4,3,2,1,0:T(8,128)(2,1)S(1)}, u32[]{:S(2)}, u32[]{:S(2)}) collective-permute-start(bf16[1,1,1,1,1,24,1536]{6,5,4,3,2,1,0:T(8,128)(2,1)S(1)} %get-tuple-element.184), channel_id=1, source_target_pairs={{0,16},{1,17},{2,18},{3,19},{4,20},{5,21},{6,22},{7,23},{8,24},{9,... | collective-permute-start | bytes 221192 | tf_op jit(solution)/shard_map/ppermute | solution.py:595
  23.9 18.3 %collective-permute-start.6 = (bf16[1,1,2,1,1,24,896]{6,5,2,0,4,3,1:T(8,128)(2,1)S(1)}, bf16[1,1,2,1,1,24,896]{6,5,2,0,4,3,1:T(8,128)(2,1)S(1)}, u32[]{:S(2)}, u32[]{:S(2)}) collective-permute-start(bf16[1,1,2,1,1,24,896]{6,5,2,0,4,3,1:T(8,128)(2,1)S(1)} %fusion.6), channel_id=1, source_target_pairs={{0,16},{1,17},{2,18},{3,19},{4,20},{5,21},{6,22},{7,23},{8,24},{9,... | collective-permute-start | bytes 258056 | tf_op jit(solution)/shard_map/ppermute | solution.py:595
  37.3 9.7 %collective-permute-start.1 = (bf16[2,1,1,1,1,24,1536]{6,5,1,0,4,3,2:T(8,128)(2,1)S(1)}, bf16[2,1,1,1,1,24,1536]{6,5,1,0,4,3,2:T(8,128)(2,1)S(1)}, u32[]{:S(2)}, u32[]{:S(2)}) collective-permute-start(bf16[2,1,1,1,1,24,1536]{6,5,1,0,4,3,2:T(8,128)(2,1)S(1)} %fusion.5), channel_id=1, source_target_pairs={{0,8},{1,9},{2,10},{3,11},{4,12},{5,13},{6,14},{7,15},{8,0},{9,1},... | collective-permute-start | bytes 442376 | tf_op jit(solution)/shard_map/ppermute | solution.py:595
  39.2 11.0 %collective-permute-start.11 = (bf16[2,1,1,1,1,24,1536]{6,5,4,3,2,1,0:T(8,128)(2,1)S(1)}, bf16[2,1,1,1,1,24,1536]{6,5,4,3,2,1,0:T(8,128)(2,1)S(1)}, u32[]{:S(2)}, u32[]{:S(2)}) collective-permute-start(bf16[2,1,1,1,1,24,1536]{6,5,4,3,2,1,0:T(8,128)(2,1)S(1)} %maximum_select_fusion.16), channel_id=1, source_target_pairs={{0,8},{1,9},{2,10},{3,11},{4,12},{5,13},{6,14},{7,15},{8,0},{9,1},... | collective-permute-start | bytes 442376 | tf_op jit(solution)/shard_map/ppermute | solution.py:595
  42.3 15.3 %collective-permute-start.7 = (bf16[2,1,2,1,1,24,896]{6,5,2,0,4,3,1:T(8,128)(2,1)S(1)}, bf16[2,1,2,1,1,24,896]{6,5,2,0,4,3,1:T(8,128)(2,1)S(1)}, u32[]{:S(2)}, u32[]{:S(2)}) collective-permute-start(bf16[2,1,2,1,1,24,896]{6,5,2,0,4,3,1:T(8,128)(2,1)S(1)} %fusion.3), channel_id=1, source_target_pairs={{0,8},{1,9},{2,10},{3,11},{4,12},{5,13},{6,14},{7,15},{8,0},{9,1},... | collective-permute-start | bytes 516104 | tf_op jit(solution)/shard_map/ppermute | solution.py:595
  47.1 15.0 %collective-permute-start.2 = (bf16[2,2,1,1,1,24,1536]{6,5,1,0,4,3,2:T(8,128)(2,1)S(1)}, bf16[2,2,1,1,1,24,1536]{6,5,1,0,4,3,2:T(8,128)(2,1)S(1)}, u32[]{:S(2)}, u32[]{:S(2)}) collective-permute-start(bf16[2,2,1,1,1,24,1536]{6,5,1,0,4,3,2:T(8,128)(2,1)S(1)} %maximum_select_fusion.11), channel_id=1, source_target_pairs={{0,2},{1,3},{2,0},{3,1},{4,6},{5,7},{6,4},{7,5},{8,10},{9,11},{10,... | collective-permute-start | bytes 884744 | tf_op jit(solution)/shard_map/ppermute | solution.py:595
  50.2 15.1 %collective-permute-start.12 = (bf16[2,2,1,1,1,24,1536]{6,5,0,1,2,4,3:T(8,128)(2,1)S(1)}, bf16[2,2,1,1,1,24,1536]{6,5,0,1,2,4,3:T(8,128)(2,1)S(1)}, u32[]{:S(2)}, u32[]{:S(2)}) collective-permute-start(bf16[2,2,1,1,1,24,1536]{6,5,0,1,2,4,3:T(8,128)(2,1)S(1)} %maximum_select_fusion.12), channel_id=1, source_target_pairs={{0,4},{1,5},{2,6},{3,7},{4,0},{5,1},{6,2},{7,3},{8,12},{9,13},{10,... | collective-permute-start | bytes 884744 | tf_op jit(solution)/shard_map/ppermute | solution.py:595
  57.6 19.3 %collective-permute-start.8 = (bf16[2,2,2,1,1,24,896]{6,5,4,3,2,1,0:T(8,128)(2,1)S(1)}, bf16[2,2,2,1,1,24,896]{6,5,4,3,2,1,0:T(8,128)(2,1)S(1)}, u32[]{:S(2)}, u32[]{:S(2)}) collective-permute-start(bf16[2,2,2,1,1,24,896]{6,5,4,3,2,1,0:T(8,128)(2,1)S(1)} %copy.143), channel_id=1, source_target_pairs={{0,2},{1,3},{2,0},{3,1},{4,6},{5,7},{6,4},{7,5},{8,10},{9,11},{10,... | collective-permute-start | bytes 1032200 | tf_op jit(solution)/shard_map/ppermute | solution.py:595
  62.2 15.4 %collective-permute-start.3 = (bf16[2,2,1,2,1,24,1536]{6,5,4,3,2,1,0:T(8,128)(2,1)S(1)}, bf16[2,2,1,2,1,24,1536]{6,5,4,3,2,1,0:T(8,128)(2,1)S(1)}, u32[]{:S(2)}, u32[]{:S(2)}) collective-permute-start(bf16[2,2,1,2,1,24,1536]{6,5,4,3,2,1,0:T(8,128)(2,1)S(1)} %copy.135), channel_id=1, source_target_pairs={{0,4},{1,5},{2,6},{3,7},{4,0},{5,1},{6,2},{7,3},{8,12},{9,13},{10,... | collective-permute-start | bytes 1769480 | tf_op jit(solution)/shard_map/ppermute | solution.py:595
  65.4 23.8 %collective-permute-start.13 = (bf16[2,2,2,1,1,24,1536]{6,5,0,1,2,4,3:T(8,128)(2,1)S(1)}, bf16[2,2,2,1,1,24,1536]{6,5,0,1,2,4,3:T(8,128)(2,1)S(1)}, u32[]{:S(2)}, u32[]{:S(2)}) collective-permute-start(bf16[2,2,2,1,1,24,1536]{6,5,0,1,2,4,3:T(8,128)(2,1)S(1)} %maximum_select_fusion.7), channel_id=1, source_target_pairs={{0,2},{1,3},{2,0},{3,1},{4,6},{5,7},{6,4},{7,5},{8,10},{9,11},{10,... | collective-permute-start | bytes 1769480 | tf_op jit(solution)/shard_map/ppermute | solution.py:595
  77.1 13.4 %collective-permute-start.9 = (bf16[2,2,2,2,1,24,896]{6,5,4,3,2,1,0:T(8,128)(2,1)S(1)}, bf16[2,2,2,2,1,24,896]{6,5,4,3,2,1,0:T(8,128)(2,1)S(1)}, u32[]{:S(2)}, u32[]{:S(2)}) collective-permute-start(bf16[2,2,2,2,1,24,896]{6,5,4,3,2,1,0:T(8,128)(2,1)S(1)} %maximum_select_fusion.4), channel_id=1, source_target_pairs={{0,1},{1,0},{2,3},{3,2},{4,5},{5,4},{6,7},{7,6},{8,9},{9,8},{10,11... | collective-permute-start | bytes 2064392 | tf_op jit(solution)/shard_map/ppermute | solution.py:595
  77.7 18.5 %collective-permute-start.4 = (bf16[2,2,2,2,1,24,1536]{6,5,4,3,2,1,0:T(8,128)(2,1)S(1)}, bf16[2,2,2,2,1,24,1536]{6,5,4,3,2,1,0:T(8,128)(2,1)}, u32[]{:S(2)}, u32[]{:S(2)}) collective-permute-start(bf16[2,2,2,2,1,24,1536]{6,5,4,3,2,1,0:T(8,128)(2,1)S(1)} %maximum_select_fusion.3), channel_id=1, source_target_pairs={{0,1},{1,0},{2,3},{3,2},{4,5},{5,4},{6,7},{7,6},{8,9},{9,8},{10,11... | collective-permute-start | bytes 3538952 | tf_op jit(solution)/shard_map/ppermute | solution.py:595
  90.8 3.7 copy-start
  111.1 4.9 copy-start.2
  111.1 34.1 %all-to-all-start.1 = ((bf16[4,2,196,768]{3,1,2,0:T(2,128)(2,1)}), bf16[4,2,196,768]{3,1,2,0:T(2,128)(2,1)}, u32[]{:S(2)}, u32[]{:S(2)}) async-start(bf16[4,2,196,768]{3,1,2,0:T(2,128)(2,1)} %param.31), calls=%async_computation.1 | async-start | bytes 4816896 | tf_op jit(solution)/shard_map/all_to_all | solution.py:695
  115.8 294.6 %reduce-scatter.2.cloned.1.call-start = ((), (), s32[]{:S(2)}) async-start(), calls=%async_computation.8 | async-start | bytes 9732096 | tf_op jit(solution)/shard_map/reduce_scatter | solution.py:730
  116.1 3.4 collective-permute-start.14
  247.4 45.6 %all-to-all-start.2 = ((bf16[4,2,196,768]{3,1,2,0:T(2,128)(2,1)}), bf16[4,2,196,768]{3,1,2,0:T(2,128)(2,1)S(1)}, u32[]{:S(2)}, u32[]{:S(2)}) async-start(bf16[4,2,196,768]{3,1,2,0:T(2,128)(2,1)} %copy.152), calls=%async_computation.2 | async-start | bytes 4816896 | tf_op jit(solution)/shard_map/all_to_all | solution.py:699
  293.0 16.9 %copy-start.3 = (bf16[4,2,196,768]{3,1,2,0:T(2,128)(2,1)}, bf16[4,2,196,768]{3,1,2,0:T(2,128)(2,1)S(1)}, u32[]{:S(2)}) copy-start(bf16[4,2,196,768]{3,1,2,0:T(2,128)(2,1)S(1)} %all-to-all-done.2) | copy-start | bytes 7225348
  311.9 7.2 %collective-permute-start.15 = (bf16[2,2,2,2,1,24,3072]{6,5,4,3,2,1,0:T(8,128)(2,1)S(1)}, bf16[2,2,2,2,1,24,3072]{6,5,4,3,2,1,0:T(8,128)(2,1)}, u32[]{:S(2)}, u32[]{:S(2)}) collective-permute-start(bf16[2,2,2,2,1,24,3072]{6,5,4,3,2,1,0:T(8,128)(2,1)S(1)} %constant_dynamic-slice_fusion.9.refs_2_), channel_id=1, source_target_pairs={{0,1},{1,0},{2,3},{3,2},{4,5},{5,4},{6,7},{7,6},{8,9},{9,8},{10,11... | collective-permute-start | bytes 7077896 | tf_op jit(solution)/shard_map/ppermute | solution.py:595
  331.7 5.7 %copy-start.13 = (bf16[768,768]{1,0:T(8,128)(2,1)S(1)}, bf16[768,768]{1,0:T(8,128)(2,1)}, u32[]{:S(2)}) copy-start(bf16[768,768]{1,0:T(8,128)(2,1)} %shard_map.287) | copy-start | bytes 3538948
  338.9 2.9 copy-start.1
  341.5 20.6 %collective-permute-start.16 = (bf16[2,2,2,2,1,24,1536]{6,5,4,3,2,1,0:T(8,128)(2,1)}, bf16[2,2,2,2,1,24,1536]{6,5,4,3,2,1,0:T(8,128)(2,1)}, u32[]{:S(2)}, u32[]{:S(2)}) collective-permute-start(bf16[2,2,2,2,1,24,1536]{6,5,4,3,2,1,0:T(8,128)(2,1)} %constant_dynamic-slice_fusion.7.refs_2_), channel_id=1, source_target_pairs={{0,1},{1,0},{2,3},{3,2},{4,5},{5,4},{6,7},{7,6},{8,9},{9,8},{10,11... | collective-permute-start | bytes 3538952 | tf_op jit(solution)/shard_map/ppermute | solution.py:595
  341.9 40.8 %collective-permute-start.27 = (bf16[2,2,1,2,1,24,3072]{6,5,4,3,2,1,0:T(8,128)(2,1)S(1)}, bf16[2,2,1,2,1,24,3072]{6,5,4,3,2,1,0:T(8,128)(2,1)}, u32[]{:S(2)}, u32[]{:S(2)}) collective-permute-start(bf16[2,2,1,2,1,24,3072]{6,5,4,3,2,1,0:T(8,128)(2,1)S(1)} %copy-done.1), channel_id=1, source_target_pairs={{0,4},{1,5},{2,6},{3,7},{4,0},{5,1},{6,2},{7,3},{8,12},{9,13},{10,... | collective-permute-start | bytes 3538952 | tf_op jit(solution)/shard_map/ppermute | solution.py:595
  366.1 17.8 %collective-permute-start.17 = (bf16[2,2,2,1,1,24,1536]{6,5,4,3,2,1,0:T(8,128)(2,1)}, bf16[2,2,2,1,1,24,1536]{6,5,4,3,2,1,0:T(8,128)(2,1)}, u32[]{:S(2)}, u32[]{:S(2)}) collective-permute-start(bf16[2,2,2,1,1,24,1536]{6,5,4,3,2,1,0:T(8,128)(2,1)} %constant_dynamic-slice_fusion.6.refs_2_), channel_id=1, source_target_pairs={{0,2},{1,3},{2,0},{3,1},{4,6},{5,7},{6,4},{7,5},{8,10},{9,11},{10,... | collective-permute-start | bytes 1769480 | tf_op jit(solution)/shard_map/ppermute | solution.py:595
  379.1 4.8 copy-start.12
  382.7 6.5 %copy-start.7 = (bf16[768,1152]{1,0:T(8,128)(2,1)}, bf16[768,1152]{1,0:T(8,128)(2,1)S(1)}, u32[]{:S(2)}) copy-start(bf16[768,1152]{1,0:T(8,128)(2,1)S(1)} %get-tuple-element.162) | copy-start | bytes 5308420
  383.8 28.6 %collective-permute-start.21 = (bf16[2,2,2,2,1,24,1152]{6,5,4,3,2,1,0:T(8,128)(2,1)}, bf16[2,2,2,2,1,24,1152]{6,5,4,3,2,1,0:T(8,128)(2,1)}, u32[]{:S(2)}, u32[]{:S(2)}) collective-permute-start(bf16[2,2,2,2,1,24,1152]{6,5,4,3,2,1,0:T(8,128)(2,1)} %constant_dynamic-slice_fusion.4), channel_id=1, source_target_pairs={{0,1},{1,0},{2,3},{3,2},{4,5},{5,4},{6,7},{7,6},{8,9},{9,8},{10,11... | collective-permute-start | bytes 2654216 | tf_op jit(solution)/shard_map/ppermute | solution.py:595
  386.0 3.2 copy-start.17
  386.0 23.1 %collective-permute-start.24 = (bf16[2,2,1,1,1,24,1536]{6,5,4,3,2,1,0:T(8,128)(2,1)S(1)}, bf16[2,2,1,1,1,24,1536]{6,5,4,3,2,1,0:T(8,128)(2,1)}, u32[]{:S(2)}, u32[]{:S(2)}) collective-permute-start(bf16[2,2,1,1,1,24,1536]{6,5,4,3,2,1,0:T(8,128)(2,1)S(1)} %constant_dynamic-slice_fusion.5.refs_10_), channel_id=1, source_target_pairs={{0,4},{1,5},{2,6},{3,7},{4,0},{5,1},{6,2},{7,3},{8,12},{9,13},{10,... | collective-permute-start | bytes 884744 | tf_op jit(solution)/shard_map/ppermute | solution.py:595
  389.2 39.4 %all-to-all-start.5 = ((bf16[8,24,3072]{2,1,0:T(8,128)(2,1)}), bf16[8,24,3072]{2,1,0:T(8,128)(2,1)S(1)}, u32[]{:S(2)}, u32[]{:S(2)}) async-start(bf16[8,24,3072]{2,1,0:T(8,128)(2,1)} %bitcast.163), calls=%async_computation.6 | async-start | bytes 2359296 | tf_op jit(solution)/shard_map/all_to_all | solution.py:641
  409.1 3.4 copy-start.8
  410.4 4.4 copy-start.20
  414.7 4.9 copy-start.14
  417.5 15.8 %collective-permute-start.22 = (bf16[2,2,2,2,1,24,1280]{6,5,4,3,2,1,0:T(8,128)(2,1)}, bf16[2,2,2,2,1,24,1280]{6,5,4,3,2,1,0:T(8,128)(2,1)}, u32[]{:S(2)}, u32[]{:S(2)}) collective-permute-start(bf16[2,2,2,2,1,24,1280]{6,5,4,3,2,1,0:T(8,128)(2,1)} %constant_dynamic-slice_fusion.3), channel_id=1, source_target_pairs={{0,1},{1,0},{2,3},{3,2},{4,5},{5,4},{6,7},{7,6},{8,9},{9,8},{10,11... | collective-permute-start | bytes 2949128 | tf_op jit(solution)/shard_map/ppermute | solution.py:595
  417.5 9.2 %collective-permute-start.25 = (bf16[2,1,1,1,1,24,1536]{6,5,4,3,2,1,0:T(8,128)(2,1)S(1)}, bf16[2,1,1,1,1,24,1536]{6,5,4,3,2,1,0:T(8,128)(2,1)S(1)}, u32[]{:S(2)}, u32[]{:S(2)}) collective-permute-start(bf16[2,1,1,1,1,24,1536]{6,5,4,3,2,1,0:T(8,128)(2,1)S(1)} %constant_dynamic-slice_fusion.1), channel_id=1, source_target_pairs={{0,8},{1,9},{2,10},{3,11},{4,12},{5,13},{6,14},{7,15},{8,0},{9,1},... | collective-permute-start | bytes 442376 | tf_op jit(solution)/shard_map/ppermute | solution.py:595
  423.6 15.9 %collective-permute-start.18 = (bf16[2,196,768]{2,0,1:T(2,128)(2,1)}, bf16[2,196,768]{2,0,1:T(2,128)(2,1)}, u32[]{:S(2)}, u32[]{:S(2)}) collective-permute-start(bf16[2,196,768]{2,0,1:T(2,128)(2,1)} %copy.153), channel_id=1, source_target_pairs={{0,3},{1,2},{2,1},{3,0},{4,7},{5,6},{6,5},{7,4},{8,11},{9,10},{10,... | collective-permute-start | bytes 1806344 | tf_op jit(solution)/shard_map/ppermute | solution.py:703
  424.9 35.2 %collective-permute-start.19 = (bf16[2,196,768]{2,0,1:T(2,128)(2,1)}, bf16[2,196,768]{2,0,1:T(2,128)(2,1)}, u32[]{:S(2)}, u32[]{:S(2)}) collective-permute-start(bf16[2,196,768]{2,0,1:T(2,128)(2,1)} %copy.154), channel_id=1, source_target_pairs={{0,2},{1,3},{2,0},{3,1},{4,6},{5,7},{6,4},{7,5},{8,10},{9,11},{10,... | collective-permute-start | bytes 1806344 | tf_op jit(solution)/shard_map/ppermute | solution.py:703
  425.5 34.7 %collective-permute-start.20 = (bf16[2,196,768]{2,0,1:T(2,128)(2,1)}, bf16[2,196,768]{2,0,1:T(2,128)(2,1)}, u32[]{:S(2)}, u32[]{:S(2)}) collective-permute-start(bf16[2,196,768]{2,0,1:T(2,128)(2,1)} %copy.157), channel_id=1, source_target_pairs={{0,1},{1,0},{2,3},{3,2},{4,5},{5,4},{6,7},{7,6},{8,9},{9,8},{10,11... | collective-permute-start | bytes 1806344 | tf_op jit(solution)/shard_map/ppermute | solution.py:703
  427.5 9.4 %collective-permute-start.26 = (bf16[1,1,1,1,1,24,1536]{6,5,4,3,2,1,0:T(8,128)(2,1)S(1)}, bf16[1,1,1,1,1,24,1536]{6,5,4,3,2,1,0:T(8,128)(2,1)S(1)}, u32[]{:S(2)}, u32[]{:S(2)}) collective-permute-start(bf16[1,1,1,1,1,24,1536]{6,5,4,3,2,1,0:T(8,128)(2,1)S(1)} %constant_dynamic-slice_fusion), channel_id=1, source_target_pairs={{0,16},{1,17},{2,18},{3,19},{4,20},{5,21},{6,22},{7,23},{8,24},{9,... | collective-permute-start | bytes 221192 | tf_op jit(solution)/shard_map/ppermute | solution.py:595
  428.6 6.3 %copy-start.9 = (bf16[8,24,3072]{2,1,0:T(8,128)(2,1)}, bf16[8,24,3072]{2,1,0:T(8,128)(2,1)S(1)}, u32[]{:S(2)}) copy-start(bf16[8,24,3072]{2,1,0:T(8,128)(2,1)S(1)} %all-to-all-done.5) | copy-start | bytes 3538948
  428.6 33.7 %all-to-all-start.4 = ((bf16[16,24,1152]{2,1,0:T(8,128)(2,1)}), bf16[16,24,1152]{2,1,0:T(8,128)(2,1)}, u32[]{:S(2)}, u32[]{:S(2)}) async-start(bf16[16,24,1152]{2,1,0:T(8,128)(2,1)} %bitcast.164), calls=%async_computation.5 | async-start | bytes 1769472 | tf_op jit(solution)/shard_map/all_to_all | solution.py:641
  433.4 3.5 copy-start.19
  434.9 25.3 %collective-permute-start.23 = (bf16[2,2,1,2,1,24,1280]{6,5,4,3,2,1,0:T(8,128)(2,1)S(1)}, bf16[2,2,1,2,1,24,1280]{6,5,4,3,2,1,0:T(8,128)(2,1)S(1)}, u32[]{:S(2)}, u32[]{:S(2)}) collective-permute-start(bf16[2,2,1,2,1,24,1280]{6,5,4,3,2,1,0:T(8,128)(2,1)S(1)} %constant_dynamic-slice_fusion.2), channel_id=1, source_target_pairs={{0,4},{1,5},{2,6},{3,7},{4,0},{5,1},{6,2},{7,3},{8,12},{9,13},{10,... | collective-permute-start | bytes 1474568 | tf_op jit(solution)/shard_map/ppermute | solution.py:595
  462.3 19.2 %all-to-all-start.3 = ((bf16[8,24,1280]{2,1,0:T(8,128)(2,1)}), bf16[8,24,1280]{2,1,0:T(8,128)(2,1)S(1)}, u32[]{:S(2)}, u32[]{:S(2)}) async-start(bf16[8,24,1280]{2,1,0:T(8,128)(2,1)} %bitcast.78), calls=%async_computation.4 | async-start | bytes 983040 | tf_op jit(solution)/shard_map/all_to_all | solution.py:641
  470.0 3.3 copy-start.10
  473.3 12.5 %copy-start.4 = (bf16[4,2,196,768]{3,1,2,0:T(2,128)(2,1)S(1)}, bf16[4,2,196,768]{3,1,2,0:T(2,128)(2,1)}, u32[]{:S(2)}) copy-start(bf16[4,2,196,768]{3,1,2,0:T(2,128)(2,1)} %copy-done.3) | copy-start | bytes 7225348
  (6 other events, 7.1 us)
Sparse Core Ops, SparseCore 0:
  12.8 125.2 all-gather.1
  242.6 143.5 reduce-scatter.1

commit v5 on v4

--- a/solution.py
+++ b/solution.py
@@ -13,8 +13,8 @@
 PAIRS = HEADS // 2
 TILE = 16
 GROUP_T = 6
-GROUP_S = 2
-GROUP_SB = 1
+GROUP_S = 6
+GROUP_SB = 3
 GROUP_TB = 3
 LOW = -1e30
 BF = jnp.bfloat16

time: 503 us -> 493 us (0.980)
  Pallas kernels: 250 us -> 241 us
    pallas_call x13, Pallas kernels: 234 us -> 225 us  [launch(): pl.pallas_call(body, grid=grid, in_specs=list(in_specs) + [ANYWHERE] * sk...]
  transfers between devices with their start and end apart: 36 -> 36, of which waited for: 17 -> 17; matrix products, arithmetic and copies ran while one was open for 13% -> 13% of each run, Pallas kernels for 32% -> 31%
where the time goes in v5:
time: 493 us; the launch traced here: 484 us
  Pallas kernels  241 us (49%)
  waiting for transfers between devices  82 us (17%)
  starting transfers between devices  64.2 us (13%)
  local copies, waits for them, and re-layouts  48.9 us (10%)
  other arithmetic  32.7 us (7%)
  between operations  15.2 us (3%)
    pallas_call x13, Pallas kernels, launch(): pl.pallas_call(body, grid=grid, in_specs=list(in_specs) + [ANYWHERE] * sk...  225 us
    ppermute x25, waiting for transfers between devices, swap(): return lax.ppermute(values, AXES, [(i, i ^ 1 << bit) for i in range(n)])  51.5 us
    ppermute x25, starting transfers between devices, swap(): return lax.ppermute(values, AXES, [(i, i ^ 1 << bit) for i in range(n)])  32.9 us
    ppermute x3, waiting for transfers between devices, swap_pieces(): lax.ppermute(pieces[k], AXES, [(i, i ^ k) for i in range(n)])  22 us
    all_to_all x3, starting transfers between devices, start(): lax.all_to_all(held, self.axes, split_axis=0, concat_axis=0, tiled=True)  16 us
    convert_element_type x9, other arithmetic, end(): (self.keep.astype(F32) + got.astype(F32)).astype(self.held.dtype)  15.4 us
    pallas_call x1, Pallas kernels, run_temporal_back_finish(): pl.pallas_call(body, grid_spec=pltpu.PrefetchScalarGridSpec(num_scalar_pr...  13.5 us
    unnamed x75, local copies, waits for them, and re-layouts  13.5 us
  transfers between devices with their start and end apart: 36, of which 17 were waited for; matrix products, arithmetic and copies ran while one was open for 13% of the time, Pallas kernels for 31%

profile of v5, /device:TPU:0, one launch (start us, length us, event | category | flops | bytes accessed | tf_op | source)
XLA Modules:
  0.0 483.9 jit_solution(954820596438754270)
XLA Ops:
  8.3 2.1 reshape.2266
  12.8 4.7 all-to-all-start
  17.8 3.0 collective-permute-start.5
  20.8 2.7 collective-permute-start.10
  23.9 2.7 collective-permute-start.6
  26.6 10.7 %collective-permute-done = bf16[1,1,1,1,1,24,1536]{6,5,4,3,2,1,0:T(8,128)(2,1)S(1)} collective-permute-done((bf16[1,1,1,1,1,24,1536]{6,5,4,3,2,1,0:T(8,128)(2,1)S(1)}, bf16[1,1,1,1,1,24,1536]{6,5,4,3,2,1,0:T(8,128)(2,1)S(1)}, u32[]{:S(2)}, u32[]{:S(2)}) %collective-permute-start) | collective-permute-done | bytes 73760 | tf_op jit(solution)/shard_map/ppermute | solution.py:595
  37.3 1.8 collective-permute-start.1
  39.6 2.7 collective-permute-done.6
  42.3 2.3 collective-permute-start.7
  44.7 2.3 collective-permute-done.1
  47.1 2.0 collective-permute-start.2
  50.9 6.6 %collective-permute-done.7 = bf16[2,1,2,1,1,24,896]{6,5,2,0,4,3,1:T(8,128)(2,1)S(1)} collective-permute-done((bf16[2,1,2,1,1,24,896]{6,5,2,0,4,3,1:T(8,128)(2,1)S(1)}, bf16[2,1,2,1,1,24,896]{6,5,2,0,4,3,1:T(8,128)(2,1)S(1)}, u32[]{:S(2)}, u32[]{:S(2)}) %collective-permute-start.7) | collective-permute-done | bytes 172064 | tf_op jit(solution)/shard_map/ppermute | solution.py:595
  57.6 3.0 collective-permute-start.8
  62.2 2.8 collective-permute-start.3
  65.4 1.7 collective-permute-start.13
  67.3 9.6 %collective-permute-done.8 = bf16[2,2,2,1,1,24,896]{6,5,4,3,2,1,0:T(8,128)(2,1)S(1)} collective-permute-done((bf16[2,2,2,1,1,24,896]{6,5,4,3,2,1,0:T(8,128)(2,1)S(1)}, bf16[2,2,2,1,1,24,896]{6,5,4,3,2,1,0:T(8,128)(2,1)S(1)}, u32[]{:S(2)}, u32[]{:S(2)}) %collective-permute-start.8) | collective-permute-done | bytes 344096 | tf_op jit(solution)/shard_map/ppermute | solution.py:595
  77.8 11.3 %collective-permute-done.13 = bf16[2,2,2,1,1,24,1536]{6,5,0,1,2,4,3:T(8,128)(2,1)S(1)} collective-permute-done((bf16[2,2,2,1,1,24,1536]{6,5,0,1,2,4,3:T(8,128)(2,1)S(1)}, bf16[2,2,2,1,1,24,1536]{6,5,0,1,2,4,3:T(8,128)(2,1)S(1)}, u32[]{:S(2)}, u32[]{:S(2)}) %collective-permute-start.13) | collective-permute-done | bytes 589856 | tf_op jit(solution)/shard_map/ppermute | solution.py:595
  91.8 2.7 copy.126
  94.5 1.7 pad.11.refs_0_.refs_2_
  96.2 3.4 maximum_select_fusion
  99.7 11.5 %shard_map.279 = (bf16[8,208,768]{2,1,0:T(8,128)(2,1)}, bf16[8,208,2304]{2,1,0:T(8,128)(2,1)}) custom-call(bf16[8,208,768]{2,1,0:T(8,128)(2,1)} %pad.11.refs_0_.refs_2_, bf16[768,1536]{1,0:T(8,128)(2,1)} %bitcast.142, bf16[768,896]{1,0:T(8,128)(2,1)} %bitcast.149, f32[16,768]{1,0:T(8,128)} %slice_convert_fusion.refs_3_.refs_2_.refs_4_.refs_6_, ...), custom_call_target="tpu_custom_call" | custom-call | flops 900000000 | tf_op jit(solution)/shard_map/pallas_call | solution.py:373
  111.1 4.6 all-to-all-start.1
  116.5 2.9 collective-permute-done.14
  119.4 13.4 %shard_map.280.refs_1_ = bf16[8,208,768]{2,1,0:T(8,128)(2,1)} custom-call(bf16[8,208,2304]{2,1,0:T(8,128)(2,1)} %get-tuple-element.53.refs_0_), custom_call_target="tpu_custom_call" | custom-call | flops 1400000000 | tf_op jit(solution)/shard_map/pallas_call | solution.py:373
  132.9 1.7 maximum_select_fusion.1
  134.5 8.9 %shard_map.281 = (bf16[8,208,768]{2,1,0:T(8,128)(2,1)}, f32[8,208,768]{2,1,0:T(8,128)}) custom-call(bf16[8,208,768]{2,1,0:T(8,128)(2,1)} %pad.11.refs_0_.refs_2_, bf16[8,208,768]{2,1,0:T(8,128)(2,1)} %shard_map.280.refs_1_, bf16[768,1536]{1,0:T(8,128)(2,1)} %bitcast.144, f32[16,768]{1,0:T(8,128)} %slice_convert_fusion.refs_3_.refs_2_.refs_4_.refs_6_), custom_call_target="tpu_custom_call" | custom-call | flops 800000000 | tf_op jit(solution)/shard_map/pallas_call | solution.py:373
  143.4 1.8 all-to-all-done.1
  145.2 2.0 copy.151
  147.2 1.7 pad.13.refs_1_
  148.9 20.6 %shard_map.282 = (bf16[8,208,768]{2,1,0:T(8,128)(2,1)}, bf16[8,208,2304]{2,1,0:T(8,128)(2,1)}, bf16[8,208,768]{2,1,0:T(8,128)(2,1)}, f32[8,208,768]{2,1,0:T(8,128)}) custom-call(f32[8,208,768]{2,1,0:T(8,128)} %get-tuple-element.56.refs_0_.refs_1_, bf16[768,9216]{1,0:T(8,128)(2,1)} %all-gather.2.cloned.1.call-done.refs_1_.refs_2_.refs_3_, ...), custom_call_target="tpu_custom_call" | custom-call | flops 2300000000 | tf_op jit(solution)/shard_map/pallas_call | solution.py:373
  169.5 45.2 %shard_map.283 = (bf16[8,196,768]{2,1,0:T(8,128)(2,1)}, f32[8,208,768]{2,1,0:T(8,128)}, bf16[8,208,768]{2,1,0:T(8,128)(2,1)}, bf16[8,208,3072]{2,1,0:T(8,128)(2,...) custom-call(f32[8,208,768]{2,1,0:T(8,128)} %get-tuple-element.57.refs_0_, bf16[8,208,768]{2,1,0:T(8,128)(2,1)} %pad.13.refs_1_, ...), custom_call_target="tpu_custom_call" | custom-call | flops 4499999744 | tf_op jit(solution)/shard_map/pallas_call | solution.py:373
  214.7 25.4 %shard_map.284.refs_5_ = bf16[768,6144]{1,0:T(8,128)(2,1)} custom-call(bf16[1664,768]{1,0:T(8,128)(2,1)} %bitcast.166, bf16[1664,3072]{1,0:T(8,128)(2,1)} %bitcast.152, bf16[1664,3072]{1,0:T(8,128)(2,1)} %bitcast.151, bf16[1664,768]{1,0:T(8,128)(2,1)} %bitcast.140), custom_call_target="tpu_custom_call" | custom-call | flops 2500000000 | tf_op jit(solution)/shard_map/pallas_call | solution.py:373
  240.1 1.7 copy-done.15
  241.8 3.3 copy.152
  245.1 3.8 all-to-all-start.2
  248.9 35.2 %shard_map.285 = (bf16[8,208,768]{2,1,0:T(8,128)(2,1)}, bf16[8,208,2304]{2,1,0:T(8,128)(2,1)}, f32[8,208,768]{2,1,0:T(8,128)}, bf16[8,208,768]{2,1,0:T(8,128)(2,1)}, f32[8,768]{1,0:T(8,128)}) custom-call(f32[8,208,768]{2,1,0:T(8,128)} %get-tuple-element.60.refs_0_, f32[8,208,768]{2,1,0:T(8,128)} %get-tuple-element.56.refs_0_.refs_1_, ...), custom_call_target="tpu_custom_call" | custom-call | flops 4200000000 | tf_op jit(solution)/shard_map/pallas_call | solution.py:373
  284.7 15.9 %shard_map.286 = bf16[768,3072]{1,0:T(8,128)(2,1)} custom-call(bf16[1664,768]{1,0:T(8,128)(2,1)} %bitcast.170, bf16[1664,2304]{1,0:T(8,128)(2,1)} %bitcast.160, bf16[1664,768]{1,0:T(8,128)(2,1)} %bitcast.171, bf16[1664,768]{1,0:T(8,128)(2,1)} %bitcast.172, bf16[1,128]{1,0:T(2,128)(2,1)} %slice_bitcast_fusion.3.refs_4_), custom_call_target="tpu_custom_call" | custom-call | flops 1600000000 | tf_op jit(solution)/shard_map/pallas_call | solution.py:373
  300.6 1.9 constant_dynamic-slice_fusion.9.refs_2_
  303.9 5.7 %shard_map.287 = bf16[768,768]{1,0:T(8,128)(2,1)} custom-call(bf16[1664,768]{1,0:T(8,128)(2,1)} %bitcast.169, bf16[1664,768]{1,0:T(8,128)(2,1)} %bitcast.153, bf16[2,2,2,2,1,24,3072]{6,5,4,3,2,1,0:T(8,128)(2,1)} %copy-done.6), custom_call_target="tpu_custom_call" | custom-call | flops 600000000 | tf_op jit(solution)/shard_map/pallas_call | solution.py:373
  309.7 3.5 add_convert_fusion
  314.3 8.1 %shard_map.288 = (bf16[8,208,768]{2,1,0:T(8,128)(2,1)}, bf16[8,208,768]{2,1,0:T(8,128)(2,1)}, f32[8,768]{1,0:T(8,128)}) custom-call(bf16[8,208,768]{2,1,0:T(8,128)(2,1)} %get-tuple-element.66.refs_0_, bf16[768,1536]{1,0:T(8,128)(2,1)} %bitcast.145, bf16[2,2,1,2,1,24,3072]{6,5,4,3,2,1,0:T(8,128)(2,1)} %constant_dynamic-slice_fusion.8.refs_2_), custom_call_target="tpu_custom_call" | custom-call | flops 800000000 | tf_op jit(solution)/shard_map/pallas_call | solution.py:373
  322.4 5.7 %shard_map.289 = bf16[768,768]{1,0:T(8,128)(2,1)} custom-call(bf16[1664,768]{1,0:T(8,128)(2,1)} %bitcast.141, bf16[1664,768]{1,0:T(8,128)(2,1)} %bitcast.168, bf16[2,2,1,2,1,24,3072]{6,5,4,3,2,1,0:T(8,128)(2,1)} %constant_dynamic-slice_fusion.8.refs_2_), custom_call_target="tpu_custom_call" | custom-call | flops 600000000 | tf_op jit(solution)/shard_map/pallas_call | solution.py:373
  328.1 1.5 pad_maximum_fusion.1
  332.7 1.9 collective-permute-start.27
  334.6 18.2 %shard_map.290.refs_3_ = bf16[8,208,2304]{2,1,0:T(8,128)(2,1)} custom-call(bf16[8,208,2304]{2,1,0:T(8,128)(2,1)} %get-tuple-element.53.refs_0_, bf16[8,208,768]{2,1,0:T(8,128)(2,1)} %get-tuple-element.73.refs_1_, bf16[2,2,2,2,1,24,1536]{6,5,4,3,2,1,0:T(8,128)(2,1)} %constant_dynamic-slice_fusion.7.refs_2_), custom_call_target="tpu_custom_call" | custom-call | flops 2000000000 | tf_op jit(solution)/shard_map/pallas_call | solution.py:373
  352.8 2.0 add_convert_fusion.2
  356.8 1.5 collective-permute-start.17
  358.2 11.5 %shard_map.291 = bf16[768,2304]{1,0:T(8,128)(2,1)} custom-call(bf16[1664,768]{1,0:T(8,128)(2,1)} %bitcast.167, bf16[1664,2304]{1,0:T(8,128)(2,1)} %bitcast.139, bf16[2,2,2,1,1,24,1536]{6,5,4,3,2,1,0:T(8,128)(2,1)} %constant_dynamic-slice_fusion.6.refs_2_), custom_call_target="tpu_custom_call" | custom-call | flops 1200000000 | tf_op jit(solution)/shard_map/pallas_call | solution.py:373
  369.7 3.7 fusion.27
  376.9 2.8 add_convert_fusion.1
  379.7 5.2 %all-to-all-start.5 = ((bf16[8,24,3072]{2,1,0:T(8,128)(2,1)}), bf16[8,24,3072]{2,1,0:T(8,128)(2,1)S(1)}, u32[]{:S(2)}, u32[]{:S(2)}) async-start(bf16[8,24,3072]{2,1,0:T(8,128)(2,1)} %bitcast.163), calls=%async_computation.6 | async-start | bytes 2359296 | tf_op jit(solution)/shard_map/all_to_all | solution.py:641
  384.9 13.5 %shard_map.292 = (bf16[8,196,768]{2,1,0:T(8,128)(2,1)}, bf16[768,128]{1,0:T(8,128)(2,1)}) custom-call(s32[1]{0:T(128)} %bitcast.54.refs_0_, f32[8,208,768]{2,1,0:T(8,128)} %get-tuple-element.65.refs_1_, bf16[8,208,768]{2,1,0:T(8,128)(2,1)} %pad.11.refs_0_.refs_2_, bf16[8,208,2304]{2,1,0:T(8,128)(2,1)} %shard_map.290.refs_3_, bf16[768,1536]{1,0:T(8,128)(2,1)} %bitcast.143, ...), custom_call_target="tpu_custom_call" | custom-call | flops 1300000000 | tf_op jit(solution)/shard_map/pallas_call | solution.py:574
  399.8 2.0 shard_map.293
  401.9 2.3 add_convert_fusion.4
  404.1 1.8 pad_maximum_fusion.2
  407.0 2.1 collective-permute-start.25
  414.9 2.1 collective-permute-done.25
  418.0 5.4 %all-to-all-start.4 = ((bf16[16,24,1152]{2,1,0:T(8,128)(2,1)}), bf16[16,24,1152]{2,1,0:T(8,128)(2,1)}, u32[]{:S(2)}, u32[]{:S(2)}) async-start(bf16[16,24,1152]{2,1,0:T(8,128)(2,1)} %bitcast.164), calls=%async_computation.5 | async-start | bytes 1769472 | tf_op jit(solution)/shard_map/all_to_all | solution.py:641
  425.0 1.9 collective-permute-start.23
  428.9 20.7 %collective-permute-done.19 = bf16[2,196,768]{2,0,1:T(2,128)(2,1)} collective-permute-done((bf16[2,196,768]{2,0,1:T(2,128)(2,1)}, bf16[2,196,768]{2,0,1:T(2,128)(2,1)}, u32[]{:S(2)}, u32[]{:S(2)}) %collective-permute-start.19) | collective-permute-done | bytes 602144 | tf_op jit(solution)/shard_map/ppermute | solution.py:703
  451.7 5.4 %all-to-all-start.3 = ((bf16[8,24,1280]{2,1,0:T(8,128)(2,1)}), bf16[8,24,1280]{2,1,0:T(8,128)(2,1)S(1)}, u32[]{:S(2)}, u32[]{:S(2)}) async-start(bf16[8,24,1280]{2,1,0:T(8,128)(2,1)} %bitcast.78), calls=%async_computation.4 | async-start | bytes 983040 | tf_op jit(solution)/shard_map/all_to_all | solution.py:641
  457.1 2.0 select_bitcast_fusion.3
  459.4 3.3 copy.163
  465.5 5.4 %all-to-all-done.3 = bf16[8,24,1280]{2,1,0:T(8,128)(2,1)S(1)} async-done(((bf16[8,24,1280]{2,1,0:T(8,128)(2,1)}), bf16[8,24,1280]{2,1,0:T(8,128)(2,1)S(1)}, u32[]{:S(2)}, u32[]{:S(2)}) %all-to-all-start.3) | async-done | bytes 491552 | tf_op jit(solution)/shard_map/all_to_all | solution.py:641
  (192 shorter events, 48.2 us)
Async XLA Ops:
  7.2 4.6 copy-start.23
  7.2 4.6 copy-start.22
  7.2 141.7 %all-gather.2.cloned.1.call-start = ((), (), s32[]{:S(2)}) async-start(), calls=%async_computation.7 | async-start | bytes 14598144 | tf_op jit(solution)/shard_map/all_gather | solution.py:692
  12.6 4.8 copy-start.32
  12.7 4.9 %copy-start.26 = (bf16[3,24]{1,0:T(4,128)(2,1)S(1)}, bf16[3,24]{1,0:T(4,128)(2,1)}, u32[]{:S(2)}) copy-start(bf16[3,24]{1,0:T(4,128)(2,1)} %param.18) | copy-start | bytes 436
  12.7 4.9 %copy-start.27 = (bf16[24]{0:T(256)(128)(2,1)S(1)}, bf16[24]{0:T(256)(128)(2,1)}, u32[]{:S(2)}) copy-start(bf16[24]{0:T(256)(128)(2,1)} %param.17) | copy-start | bytes 148
  12.7 4.9 %copy-start.28 = (bf16[24]{0:T(256)(128)(2,1)S(1)}, bf16[24]{0:T(256)(128)(2,1)}, u32[]{:S(2)}) copy-start(bf16[24]{0:T(256)(128)(2,1)} %param.22) | copy-start | bytes 148
  12.7 4.9 %copy-start.29 = (bf16[2,24]{1,0:T(2,128)(2,1)S(1)}, bf16[2,24]{1,0:T(2,128)(2,1)}, u32[]{:S(2)}) copy-start(bf16[2,24]{1,0:T(2,128)(2,1)} %param.23) | copy-start | bytes 292
  12.7 4.9 %copy-start.30 = (bf16[24]{0:T(256)(128)(2,1)S(1)}, bf16[24]{0:T(256)(128)(2,1)}, u32[]{:S(2)}) copy-start(bf16[24]{0:T(256)(128)(2,1)} %param.26) | copy-start | bytes 148
  12.7 4.9 %copy-start.31 = (bf16[2,24]{1,0:T(2,128)(2,1)S(1)}, bf16[2,24]{1,0:T(2,128)(2,1)}, u32[]{:S(2)}) copy-start(bf16[2,24]{1,0:T(2,128)(2,1)} %param.27) | copy-start | bytes 292
  12.7 5.0 %slice-start = ((bf16[24,2304]{1,0:T(8,128)(2,1)}), bf16[24,768]{1,0:T(8,128)(2,1)S(1)}, s32[]{:S(2)}) async-start(bf16[24,2304]{1,0:T(8,128)(2,1)} %param.19), calls=%async_computation.9 | async-start | bytes 73728 | tf_op jit(solution)/shard_map/slice | solution.py:715
  12.7 8.1 %copy-start.24 = (bf16[24,768]{1,0:T(8,128)(2,1)S(1)}, bf16[24,768]{1,0:T(8,128)(2,1)}, u32[]{:S(2)}) copy-start(bf16[24,768]{1,0:T(8,128)(2,1)} %param.20) | copy-start | bytes 110596
  12.8 8.1 %copy-start.25 = (bf16[24,768]{1,0:T(8,128)(2,1)S(1)}, bf16[24,768]{1,0:T(8,128)(2,1)}, u32[]{:S(2)}) copy-start(bf16[24,768]{1,0:T(8,128)(2,1)} %param.21) | copy-start | bytes 110596
  12.8 10.7 %copy-start.21 = (bf16[24,2304]{1,0:T(8,128)(2,1)S(1)}, bf16[24,2304]{1,0:T(8,128)(2,1)}, u32[]{:S(2)}) copy-start(bf16[24,2304]{1,0:T(8,128)(2,1)} %param.19) | copy-start | bytes 331780
  12.8 79.0 %all-to-all-start = ((bf16[4,2,196,768]{3,1,2,0:T(2,128)(2,1)}), bf16[4,2,196,768]{3,1,2,0:T(2,128)(2,1)}, u32[]{:S(2)}, u32[]{:S(2)}) async-start(bf16[4,2,196,768]{3,1,2,0:T(2,128)(2,1)} %param.16), calls=%async_computation | async-start | bytes 4816896 | tf_op jit(solution)/shard_map/all_to_all | solution.py:695
  17.8 6.1 %collective-permute-start.5 = (bf16[1,1,1,1,1,24,896]{6,5,4,3,2,1,0:T(8,128)(2,1)S(1)}, bf16[1,1,1,1,1,24,896]{6,5,4,3,2,1,0:T(8,128)(2,1)S(1)}, u32[]{:S(2)}, u32[]{:S(2)}) collective-permute-start(bf16[1,1,1,1,1,24,896]{6,5,4,3,2,1,0:T(8,128)(2,1)S(1)} %get-tuple-element.189), channel_id=1, source_target_pairs={{0,4},{1,5},{2,6},{3,7},{4,0},{5,1},{6,2},{7,3},{8,12},{9,13},{10,... | collective-permute-start | bytes 129032 | tf_op jit(solution)/shard_map/ppermute | solution.py:595
  20.8 18.3 %collective-permute-start.10 = (bf16[1,1,1,1,1,24,1536]{6,5,4,3,2,1,0:T(8,128)(2,1)S(1)}, bf16[1,1,1,1,1,24,1536]{6,5,4,3,2,1,0:T(8,128)(2,1)S(1)}, u32[]{:S(2)}, u32[]{:S(2)}) collective-permute-start(bf16[1,1,1,1,1,24,1536]{6,5,4,3,2,1,0:T(8,128)(2,1)S(1)} %bitcast.185), channel_id=1, source_target_pairs={{0,16},{1,17},{2,18},{3,19},{4,20},{5,21},{6,22},{7,23},{8,24},{9,... | collective-permute-start | bytes 221192 | tf_op jit(solution)/shard_map/ppermute | solution.py:595
  23.5 13.8 %collective-permute-start = (bf16[1,1,1,1,1,24,1536]{6,5,4,3,2,1,0:T(8,128)(2,1)S(1)}, bf16[1,1,1,1,1,24,1536]{6,5,4,3,2,1,0:T(8,128)(2,1)S(1)}, u32[]{:S(2)}, u32[]{:S(2)}) collective-permute-start(bf16[1,1,1,1,1,24,1536]{6,5,4,3,2,1,0:T(8,128)(2,1)S(1)} %get-tuple-element.184), channel_id=1, source_target_pairs={{0,16},{1,17},{2,18},{3,19},{4,20},{5,21},{6,22},{7,23},{8,24},{9,... | collective-permute-start | bytes 221192 | tf_op jit(solution)/shard_map/ppermute | solution.py:595
  23.9 18.3 %collective-permute-start.6 = (bf16[1,1,2,1,1,24,896]{6,5,2,0,4,3,1:T(8,128)(2,1)S(1)}, bf16[1,1,2,1,1,24,896]{6,5,2,0,4,3,1:T(8,128)(2,1)S(1)}, u32[]{:S(2)}, u32[]{:S(2)}) collective-permute-start(bf16[1,1,2,1,1,24,896]{6,5,2,0,4,3,1:T(8,128)(2,1)S(1)} %fusion.6), channel_id=1, source_target_pairs={{0,16},{1,17},{2,18},{3,19},{4,20},{5,21},{6,22},{7,23},{8,24},{9,... | collective-permute-start | bytes 258056 | tf_op jit(solution)/shard_map/ppermute | solution.py:595
  37.3 9.7 %collective-permute-start.1 = (bf16[2,1,1,1,1,24,1536]{6,5,1,0,4,3,2:T(8,128)(2,1)S(1)}, bf16[2,1,1,1,1,24,1536]{6,5,1,0,4,3,2:T(8,128)(2,1)S(1)}, u32[]{:S(2)}, u32[]{:S(2)}) collective-permute-start(bf16[2,1,1,1,1,24,1536]{6,5,1,0,4,3,2:T(8,128)(2,1)S(1)} %fusion.5), channel_id=1, source_target_pairs={{0,8},{1,9},{2,10},{3,11},{4,12},{5,13},{6,14},{7,15},{8,0},{9,1},... | collective-permute-start | bytes 442376 | tf_op jit(solution)/shard_map/ppermute | solution.py:595
  39.2 11.0 %collective-permute-start.11 = (bf16[2,1,1,1,1,24,1536]{6,5,4,3,2,1,0:T(8,128)(2,1)S(1)}, bf16[2,1,1,1,1,24,1536]{6,5,4,3,2,1,0:T(8,128)(2,1)S(1)}, u32[]{:S(2)}, u32[]{:S(2)}) collective-permute-start(bf16[2,1,1,1,1,24,1536]{6,5,4,3,2,1,0:T(8,128)(2,1)S(1)} %maximum_select_fusion.16), channel_id=1, source_target_pairs={{0,8},{1,9},{2,10},{3,11},{4,12},{5,13},{6,14},{7,15},{8,0},{9,1},... | collective-permute-start | bytes 442376 | tf_op jit(solution)/shard_map/ppermute | solution.py:595
  42.3 15.3 %collective-permute-start.7 = (bf16[2,1,2,1,1,24,896]{6,5,2,0,4,3,1:T(8,128)(2,1)S(1)}, bf16[2,1,2,1,1,24,896]{6,5,2,0,4,3,1:T(8,128)(2,1)S(1)}, u32[]{:S(2)}, u32[]{:S(2)}) collective-permute-start(bf16[2,1,2,1,1,24,896]{6,5,2,0,4,3,1:T(8,128)(2,1)S(1)} %fusion.3), channel_id=1, source_target_pairs={{0,8},{1,9},{2,10},{3,11},{4,12},{5,13},{6,14},{7,15},{8,0},{9,1},... | collective-permute-start | bytes 516104 | tf_op jit(solution)/shard_map/ppermute | solution.py:595
  47.1 15.0 %collective-permute-start.2 = (bf16[2,2,1,1,1,24,1536]{6,5,1,0,4,3,2:T(8,128)(2,1)S(1)}, bf16[2,2,1,1,1,24,1536]{6,5,1,0,4,3,2:T(8,128)(2,1)S(1)}, u32[]{:S(2)}, u32[]{:S(2)}) collective-permute-start(bf16[2,2,1,1,1,24,1536]{6,5,1,0,4,3,2:T(8,128)(2,1)S(1)} %maximum_select_fusion.11), channel_id=1, source_target_pairs={{0,2},{1,3},{2,0},{3,1},{4,6},{5,7},{6,4},{7,5},{8,10},{9,11},{10,... | collective-permute-start | bytes 884744 | tf_op jit(solution)/shard_map/ppermute | solution.py:595
  50.2 15.1 %collective-permute-start.12 = (bf16[2,2,1,1,1,24,1536]{6,5,0,1,2,4,3:T(8,128)(2,1)S(1)}, bf16[2,2,1,1,1,24,1536]{6,5,0,1,2,4,3:T(8,128)(2,1)S(1)}, u32[]{:S(2)}, u32[]{:S(2)}) collective-permute-start(bf16[2,2,1,1,1,24,1536]{6,5,0,1,2,4,3:T(8,128)(2,1)S(1)} %maximum_select_fusion.12), channel_id=1, source_target_pairs={{0,4},{1,5},{2,6},{3,7},{4,0},{5,1},{6,2},{7,3},{8,12},{9,13},{10,... | collective-permute-start | bytes 884744 | tf_op jit(solution)/shard_map/ppermute | solution.py:595
  57.6 19.3 %collective-permute-start.8 = (bf16[2,2,2,1,1,24,896]{6,5,4,3,2,1,0:T(8,128)(2,1)S(1)}, bf16[2,2,2,1,1,24,896]{6,5,4,3,2,1,0:T(8,128)(2,1)S(1)}, u32[]{:S(2)}, u32[]{:S(2)}) collective-permute-start(bf16[2,2,2,1,1,24,896]{6,5,4,3,2,1,0:T(8,128)(2,1)S(1)} %copy.143), channel_id=1, source_target_pairs={{0,2},{1,3},{2,0},{3,1},{4,6},{5,7},{6,4},{7,5},{8,10},{9,11},{10,... | collective-permute-start | bytes 1032200 | tf_op jit(solution)/shard_map/ppermute | solution.py:595
  62.2 15.4 %collective-permute-start.3 = (bf16[2,2,1,2,1,24,1536]{6,5,4,3,2,1,0:T(8,128)(2,1)S(1)}, bf16[2,2,1,2,1,24,1536]{6,5,4,3,2,1,0:T(8,128)(2,1)S(1)}, u32[]{:S(2)}, u32[]{:S(2)}) collective-permute-start(bf16[2,2,1,2,1,24,1536]{6,5,4,3,2,1,0:T(8,128)(2,1)S(1)} %copy.135), channel_id=1, source_target_pairs={{0,4},{1,5},{2,6},{3,7},{4,0},{5,1},{6,2},{7,3},{8,12},{9,13},{10,... | collective-permute-start | bytes 1769480 | tf_op jit(solution)/shard_map/ppermute | solution.py:595
  65.4 23.8 %collective-permute-start.13 = (bf16[2,2,2,1,1,24,1536]{6,5,0,1,2,4,3:T(8,128)(2,1)S(1)}, bf16[2,2,2,1,1,24,1536]{6,5,0,1,2,4,3:T(8,128)(2,1)S(1)}, u32[]{:S(2)}, u32[]{:S(2)}) collective-permute-start(bf16[2,2,2,1,1,24,1536]{6,5,0,1,2,4,3:T(8,128)(2,1)S(1)} %maximum_select_fusion.7), channel_id=1, source_target_pairs={{0,2},{1,3},{2,0},{3,1},{4,6},{5,7},{6,4},{7,5},{8,10},{9,11},{10,... | collective-permute-start | bytes 1769480 | tf_op jit(solution)/shard_map/ppermute | solution.py:595
  77.1 13.4 %collective-permute-start.9 = (bf16[2,2,2,2,1,24,896]{6,5,4,3,2,1,0:T(8,128)(2,1)S(1)}, bf16[2,2,2,2,1,24,896]{6,5,4,3,2,1,0:T(8,128)(2,1)S(1)}, u32[]{:S(2)}, u32[]{:S(2)}) collective-permute-start(bf16[2,2,2,2,1,24,896]{6,5,4,3,2,1,0:T(8,128)(2,1)S(1)} %maximum_select_fusion.4), channel_id=1, source_target_pairs={{0,1},{1,0},{2,3},{3,2},{4,5},{5,4},{6,7},{7,6},{8,9},{9,8},{10,11... | collective-permute-start | bytes 2064392 | tf_op jit(solution)/shard_map/ppermute | solution.py:595
  77.7 18.5 %collective-permute-start.4 = (bf16[2,2,2,2,1,24,1536]{6,5,4,3,2,1,0:T(8,128)(2,1)S(1)}, bf16[2,2,2,2,1,24,1536]{6,5,4,3,2,1,0:T(8,128)(2,1)}, u32[]{:S(2)}, u32[]{:S(2)}) collective-permute-start(bf16[2,2,2,2,1,24,1536]{6,5,4,3,2,1,0:T(8,128)(2,1)S(1)} %maximum_select_fusion.3), channel_id=1, source_target_pairs={{0,1},{1,0},{2,3},{3,2},{4,5},{5,4},{6,7},{7,6},{8,9},{9,8},{10,11... | collective-permute-start | bytes 3538952 | tf_op jit(solution)/shard_map/ppermute | solution.py:595
  90.8 3.7 copy-start
  111.1 4.9 %copy-start.2 = (bf16[2,2,2,2,1,24,1536]{6,5,4,3,2,1,0:T(8,128)(2,1)S(1)}, bf16[2,2,2,2,1,24,1536]{6,5,4,3,2,1,0:T(8,128)(2,1)}, u32[]{:S(2)}) copy-start(bf16[2,2,2,2,1,24,1536]{6,5,4,3,2,1,0:T(8,128)(2,1)} %copy_select_fusion.refs_4_) | copy-start | bytes 3538948
  111.1 34.1 %all-to-all-start.1 = ((bf16[4,2,196,768]{3,1,2,0:T(2,128)(2,1)}), bf16[4,2,196,768]{3,1,2,0:T(2,128)(2,1)}, u32[]{:S(2)}, u32[]{:S(2)}) async-start(bf16[4,2,196,768]{3,1,2,0:T(2,128)(2,1)} %param.31), calls=%async_computation.1 | async-start | bytes 4816896 | tf_op jit(solution)/shard_map/all_to_all | solution.py:695
  115.8 284.0 %reduce-scatter.2.cloned.1.call-start = ((), (), s32[]{:S(2)}) async-start(), calls=%async_computation.8 | async-start | bytes 9732096 | tf_op jit(solution)/shard_map/reduce_scatter | solution.py:730
  116.1 3.4 collective-permute-start.14
  245.1 39.1 %all-to-all-start.2 = ((bf16[4,2,196,768]{3,1,2,0:T(2,128)(2,1)}), bf16[4,2,196,768]{3,1,2,0:T(2,128)(2,1)S(1)}, u32[]{:S(2)}, u32[]{:S(2)}) async-start(bf16[4,2,196,768]{3,1,2,0:T(2,128)(2,1)} %copy.152), calls=%async_computation.2 | async-start | bytes 4816896 | tf_op jit(solution)/shard_map/all_to_all | solution.py:699
  284.1 16.5 %copy-start.3 = (bf16[4,2,196,768]{3,1,2,0:T(2,128)(2,1)}, bf16[4,2,196,768]{3,1,2,0:T(2,128)(2,1)S(1)}, u32[]{:S(2)}) copy-start(bf16[4,2,196,768]{3,1,2,0:T(2,128)(2,1)S(1)} %all-to-all-done.2) | copy-start | bytes 7225348
  302.5 7.1 %collective-permute-start.15 = (bf16[2,2,2,2,1,24,3072]{6,5,4,3,2,1,0:T(8,128)(2,1)S(1)}, bf16[2,2,2,2,1,24,3072]{6,5,4,3,2,1,0:T(8,128)(2,1)}, u32[]{:S(2)}, u32[]{:S(2)}) collective-permute-start(bf16[2,2,2,2,1,24,3072]{6,5,4,3,2,1,0:T(8,128)(2,1)S(1)} %constant_dynamic-slice_fusion.9.refs_2_), channel_id=1, source_target_pairs={{0,1},{1,0},{2,3},{3,2},{4,5},{5,4},{6,7},{7,6},{8,9},{9,8},{10,11... | collective-permute-start | bytes 7077896 | tf_op jit(solution)/shard_map/ppermute | solution.py:595
  322.4 5.7 %copy-start.13 = (bf16[768,768]{1,0:T(8,128)(2,1)S(1)}, bf16[768,768]{1,0:T(8,128)(2,1)}, u32[]{:S(2)}) copy-start(bf16[768,768]{1,0:T(8,128)(2,1)} %shard_map.287) | copy-start | bytes 3538948
  329.6 3.1 copy-start.1
  332.2 20.6 %collective-permute-start.16 = (bf16[2,2,2,2,1,24,1536]{6,5,4,3,2,1,0:T(8,128)(2,1)}, bf16[2,2,2,2,1,24,1536]{6,5,4,3,2,1,0:T(8,128)(2,1)}, u32[]{:S(2)}, u32[]{:S(2)}) collective-permute-start(bf16[2,2,2,2,1,24,1536]{6,5,4,3,2,1,0:T(8,128)(2,1)} %constant_dynamic-slice_fusion.7.refs_2_), channel_id=1, source_target_pairs={{0,1},{1,0},{2,3},{3,2},{4,5},{5,4},{6,7},{7,6},{8,9},{9,8},{10,11... | collective-permute-start | bytes 3538952 | tf_op jit(solution)/shard_map/ppermute | solution.py:595
  332.7 40.8 %collective-permute-start.27 = (bf16[2,2,1,2,1,24,3072]{6,5,4,3,2,1,0:T(8,128)(2,1)S(1)}, bf16[2,2,1,2,1,24,3072]{6,5,4,3,2,1,0:T(8,128)(2,1)}, u32[]{:S(2)}, u32[]{:S(2)}) collective-permute-start(bf16[2,2,1,2,1,24,3072]{6,5,4,3,2,1,0:T(8,128)(2,1)S(1)} %copy-done.1), channel_id=1, source_target_pairs={{0,4},{1,5},{2,6},{3,7},{4,0},{5,1},{6,2},{7,3},{8,12},{9,13},{10,... | collective-permute-start | bytes 3538952 | tf_op jit(solution)/shard_map/ppermute | solution.py:595
  356.8 17.8 %collective-permute-start.17 = (bf16[2,2,2,1,1,24,1536]{6,5,4,3,2,1,0:T(8,128)(2,1)}, bf16[2,2,2,1,1,24,1536]{6,5,4,3,2,1,0:T(8,128)(2,1)}, u32[]{:S(2)}, u32[]{:S(2)}) collective-permute-start(bf16[2,2,2,1,1,24,1536]{6,5,4,3,2,1,0:T(8,128)(2,1)} %constant_dynamic-slice_fusion.6.refs_2_), channel_id=1, source_target_pairs={{0,2},{1,3},{2,0},{3,1},{4,6},{5,7},{6,4},{7,5},{8,10},{9,11},{10,... | collective-permute-start | bytes 1769480 | tf_op jit(solution)/shard_map/ppermute | solution.py:595
  369.7 4.9 %copy-start.12 = (bf16[2,2,2,2,1,24,1536]{6,5,4,3,2,1,0:T(8,128)(2,1)S(1)}, bf16[2,2,2,2,1,24,1536]{6,5,4,3,2,1,0:T(8,128)(2,1)}, u32[]{:S(2)}) copy-start(bf16[2,2,2,2,1,24,1536]{6,5,4,3,2,1,0:T(8,128)(2,1)} %copy-done.11) | copy-start | bytes 3538948
  373.4 6.3 %copy-start.7 = (bf16[768,1152]{1,0:T(8,128)(2,1)}, bf16[768,1152]{1,0:T(8,128)(2,1)S(1)}, u32[]{:S(2)}) copy-start(bf16[768,1152]{1,0:T(8,128)(2,1)S(1)} %get-tuple-element.162) | copy-start | bytes 5308420
  374.6 27.3 %collective-permute-start.21 = (bf16[2,2,2,2,1,24,1152]{6,5,4,3,2,1,0:T(8,128)(2,1)}, bf16[2,2,2,2,1,24,1152]{6,5,4,3,2,1,0:T(8,128)(2,1)}, u32[]{:S(2)}, u32[]{:S(2)}) collective-permute-start(bf16[2,2,2,2,1,24,1152]{6,5,4,3,2,1,0:T(8,128)(2,1)} %constant_dynamic-slice_fusion.4), channel_id=1, source_target_pairs={{0,1},{1,0},{2,3},{3,2},{4,5},{5,4},{6,7},{7,6},{8,9},{9,8},{10,11... | collective-permute-start | bytes 2654216 | tf_op jit(solution)/shard_map/ppermute | solution.py:595
  376.7 3.1 copy-start.17
  376.7 21.8 %collective-permute-start.24 = (bf16[2,2,1,1,1,24,1536]{6,5,4,3,2,1,0:T(8,128)(2,1)S(1)}, bf16[2,2,1,1,1,24,1536]{6,5,4,3,2,1,0:T(8,128)(2,1)}, u32[]{:S(2)}, u32[]{:S(2)}) collective-permute-start(bf16[2,2,1,1,1,24,1536]{6,5,4,3,2,1,0:T(8,128)(2,1)S(1)} %constant_dynamic-slice_fusion.5.refs_10_), channel_id=1, source_target_pairs={{0,4},{1,5},{2,6},{3,7},{4,0},{5,1},{6,2},{7,3},{8,12},{9,13},{10,... | collective-permute-start | bytes 884744 | tf_op jit(solution)/shard_map/ppermute | solution.py:595
  379.7 38.3 %all-to-all-start.5 = ((bf16[8,24,3072]{2,1,0:T(8,128)(2,1)}), bf16[8,24,3072]{2,1,0:T(8,128)(2,1)S(1)}, u32[]{:S(2)}, u32[]{:S(2)}) async-start(bf16[8,24,3072]{2,1,0:T(8,128)(2,1)} %bitcast.163), calls=%async_computation.6 | async-start | bytes 2359296 | tf_op jit(solution)/shard_map/all_to_all | solution.py:641
  398.5 3.4 copy-start.8
  399.8 4.4 copy-start.20
  404.1 4.9 %copy-start.14 = (bf16[8,196,768]{2,1,0:T(8,128)(2,1)S(1)}, bf16[8,196,768]{2,1,0:T(8,128)(2,1)}, u32[]{:S(2)}) copy-start(bf16[8,196,768]{2,1,0:T(8,128)(2,1)} %get-tuple-element.80) | copy-start | bytes 7225348
  406.9 16.5 %collective-permute-start.22 = (bf16[2,2,2,2,1,24,1280]{6,5,4,3,2,1,0:T(8,128)(2,1)}, bf16[2,2,2,2,1,24,1280]{6,5,4,3,2,1,0:T(8,128)(2,1)}, u32[]{:S(2)}, u32[]{:S(2)}) collective-permute-start(bf16[2,2,2,2,1,24,1280]{6,5,4,3,2,1,0:T(8,128)(2,1)} %constant_dynamic-slice_fusion.3), channel_id=1, source_target_pairs={{0,1},{1,0},{2,3},{3,2},{4,5},{5,4},{6,7},{7,6},{8,9},{9,8},{10,11... | collective-permute-start | bytes 2949128 | tf_op jit(solution)/shard_map/ppermute | solution.py:595
  407.0 10.1 %collective-permute-start.25 = (bf16[2,1,1,1,1,24,1536]{6,5,4,3,2,1,0:T(8,128)(2,1)S(1)}, bf16[2,1,1,1,1,24,1536]{6,5,4,3,2,1,0:T(8,128)(2,1)S(1)}, u32[]{:S(2)}, u32[]{:S(2)}) collective-permute-start(bf16[2,1,1,1,1,24,1536]{6,5,4,3,2,1,0:T(8,128)(2,1)S(1)} %constant_dynamic-slice_fusion.1), channel_id=1, source_target_pairs={{0,8},{1,9},{2,10},{3,11},{4,12},{5,13},{6,14},{7,15},{8,0},{9,1},... | collective-permute-start | bytes 442376 | tf_op jit(solution)/shard_map/ppermute | solution.py:595
  413.0 15.9 %collective-permute-start.18 = (bf16[2,196,768]{2,0,1:T(2,128)(2,1)}, bf16[2,196,768]{2,0,1:T(2,128)(2,1)}, u32[]{:S(2)}, u32[]{:S(2)}) collective-permute-start(bf16[2,196,768]{2,0,1:T(2,128)(2,1)} %copy.153), channel_id=1, source_target_pairs={{0,3},{1,2},{2,1},{3,0},{4,7},{5,6},{6,5},{7,4},{8,11},{9,10},{10,... | collective-permute-start | bytes 1806344 | tf_op jit(solution)/shard_map/ppermute | solution.py:703
  414.3 35.3 %collective-permute-start.19 = (bf16[2,196,768]{2,0,1:T(2,128)(2,1)}, bf16[2,196,768]{2,0,1:T(2,128)(2,1)}, u32[]{:S(2)}, u32[]{:S(2)}) collective-permute-start(bf16[2,196,768]{2,0,1:T(2,128)(2,1)} %copy.154), channel_id=1, source_target_pairs={{0,2},{1,3},{2,0},{3,1},{4,6},{5,7},{6,4},{7,5},{8,10},{9,11},{10,... | collective-permute-start | bytes 1806344 | tf_op jit(solution)/shard_map/ppermute | solution.py:703
  414.9 34.7 %collective-permute-start.20 = (bf16[2,196,768]{2,0,1:T(2,128)(2,1)}, bf16[2,196,768]{2,0,1:T(2,128)(2,1)}, u32[]{:S(2)}, u32[]{:S(2)}) collective-permute-start(bf16[2,196,768]{2,0,1:T(2,128)(2,1)} %copy.157), channel_id=1, source_target_pairs={{0,1},{1,0},{2,3},{3,2},{4,5},{5,4},{6,7},{7,6},{8,9},{9,8},{10,11... | collective-permute-start | bytes 1806344 | tf_op jit(solution)/shard_map/ppermute | solution.py:703
  417.7 9.2 %collective-permute-start.26 = (bf16[1,1,1,1,1,24,1536]{6,5,4,3,2,1,0:T(8,128)(2,1)S(1)}, bf16[1,1,1,1,1,24,1536]{6,5,4,3,2,1,0:T(8,128)(2,1)S(1)}, u32[]{:S(2)}, u32[]{:S(2)}) collective-permute-start(bf16[1,1,1,1,1,24,1536]{6,5,4,3,2,1,0:T(8,128)(2,1)S(1)} %constant_dynamic-slice_fusion), channel_id=1, source_target_pairs={{0,16},{1,17},{2,18},{3,19},{4,20},{5,21},{6,22},{7,23},{8,24},{9,... | collective-permute-start | bytes 221192 | tf_op jit(solution)/shard_map/ppermute | solution.py:595
  418.0 6.9 %copy-start.9 = (bf16[8,24,3072]{2,1,0:T(8,128)(2,1)}, bf16[8,24,3072]{2,1,0:T(8,128)(2,1)S(1)}, u32[]{:S(2)}) copy-start(bf16[8,24,3072]{2,1,0:T(8,128)(2,1)S(1)} %all-to-all-done.5) | copy-start | bytes 3538948
  418.0 33.7 %all-to-all-start.4 = ((bf16[16,24,1152]{2,1,0:T(8,128)(2,1)}), bf16[16,24,1152]{2,1,0:T(8,128)(2,1)}, u32[]{:S(2)}, u32[]{:S(2)}) async-start(bf16[16,24,1152]{2,1,0:T(8,128)(2,1)} %bitcast.164), calls=%async_computation.5 | async-start | bytes 1769472 | tf_op jit(solution)/shard_map/all_to_all | solution.py:641
  423.4 3.5 copy-start.19
  425.0 24.6 %collective-permute-start.23 = (bf16[2,2,1,2,1,24,1280]{6,5,4,3,2,1,0:T(8,128)(2,1)S(1)}, bf16[2,2,1,2,1,24,1280]{6,5,4,3,2,1,0:T(8,128)(2,1)S(1)}, u32[]{:S(2)}, u32[]{:S(2)}) collective-permute-start(bf16[2,2,1,2,1,24,1280]{6,5,4,3,2,1,0:T(8,128)(2,1)S(1)} %constant_dynamic-slice_fusion.2), channel_id=1, source_target_pairs={{0,4},{1,5},{2,6},{3,7},{4,0},{5,1},{6,2},{7,3},{8,12},{9,13},{10,... | collective-permute-start | bytes 1474568 | tf_op jit(solution)/shard_map/ppermute | solution.py:595
  451.7 19.1 %all-to-all-start.3 = ((bf16[8,24,1280]{2,1,0:T(8,128)(2,1)}), bf16[8,24,1280]{2,1,0:T(8,128)(2,1)S(1)}, u32[]{:S(2)}, u32[]{:S(2)}) async-start(bf16[8,24,1280]{2,1,0:T(8,128)(2,1)} %bitcast.78), calls=%async_computation.4 | async-start | bytes 983040 | tf_op jit(solution)/shard_map/all_to_all | solution.py:641
  459.4 3.3 copy-start.10
  462.7 12.5 %copy-start.4 = (bf16[4,2,196,768]{3,1,2,0:T(2,128)(2,1)S(1)}, bf16[4,2,196,768]{3,1,2,0:T(2,128)(2,1)}, u32[]{:S(2)}) copy-start(bf16[4,2,196,768]{3,1,2,0:T(2,128)(2,1)} %copy-done.3) | copy-start | bytes 7225348
  (6 other events, 7.1 us)
Sparse Core Ops, SparseCore 0:
  12.8 125.2 all-gather.1
  240.2 145.3 reduce-scatter.1

commit v6 on v5

--- a/solution.py
+++ b/solution.py
@@ -612,7 +612,7 @@
         axis = self.bits - 1 - self.bit
         high = ((self.me >> self.bit) & 1) == 1
         held = self.held
-        self.held = jnp.where(high, jnp.concatenate([got, held], axis), jnp.concatenate([held, got], axis))
+        self.held = jnp.concatenate([jnp.where(high, got, held), jnp.where(high, held, got)], axis)
 
     def steps(self, count):
         for _ in range(count):

time: 493 us -> 491 us (level)
    concatenate x12 -> x15, other arithmetic: 0.68 us -> 6.18 us  [end(): jnp.concatenate([jnp.where(high, got, held), jnp.where(high, held, got)],...]
    unnamed x75 -> x78, local copies, waits for them, and re-layouts: 13.5 us -> 13.5 us
  transfers between devices with their start and end apart: 36 -> 36, of which waited for: 17 -> 16; matrix products, arithmetic and copies ran while one was open for 13% -> 13% of each run, Pallas kernels for 31% -> 31%
where the time goes in v6:
time: 491 us; the launch traced here: 483 us
  Pallas kernels  241 us (49%)
  waiting for transfers between devices  82.8 us (17%)
  starting transfers between devices  62.5 us (13%)
  local copies, waits for them, and re-layouts  47.1 us (10%)
  other arithmetic  34.7 us (7%)
  between operations  15.3 us (3%)
    pallas_call x13, Pallas kernels, launch(): pl.pallas_call(body, grid=grid, in_specs=list(in_specs) + [ANYWHERE] * sk...  225 us
    ppermute x25, waiting for transfers between devices, swap(): return lax.ppermute(values, AXES, [(i, i ^ 1 << bit) for i in range(n)])  50.4 us
    ppermute x25, starting transfers between devices, swap(): return lax.ppermute(values, AXES, [(i, i ^ 1 << bit) for i in range(n)])  32.6 us
    ppermute x3, waiting for transfers between devices, swap_pieces(): lax.ppermute(pieces[k], AXES, [(i, i ^ k) for i in range(n)])  22 us
    all_to_all x3, starting transfers between devices, start(): lax.all_to_all(held, self.axes, split_axis=0, concat_axis=0, tiled=True)  15.5 us
    convert_element_type x9, other arithmetic, end(): (self.keep.astype(F32) + got.astype(F32)).astype(self.held.dtype)  15.4 us
    pallas_call x1, Pallas kernels, run_temporal_back_finish(): pl.pallas_call(body, grid_spec=pltpu.PrefetchScalarGridSpec(num_scalar_pr...  13.6 us
    unnamed x78, local copies, waits for them, and re-layouts  13.5 us
  transfers between devices with their start and end apart: 36, of which 16 were waited for; matrix products, arithmetic and copies ran while one was open for 13% of the time, Pallas kernels for 31%

profile of v6, /device:TPU:0, one launch (start us, length us, event | category | flops | bytes accessed | tf_op | source)
XLA Modules:
  0.0 482.8 jit_solution(14685965783932848322)
XLA Ops:
  8.3 2.1 reshape.166
  12.8 4.7 all-to-all-start
  17.8 3.0 collective-permute-start.5
  20.8 2.6 collective-permute-start
  23.8 2.7 collective-permute-start.6
  26.5 3.8 collective-permute-done
  30.3 5.1 %collective-permute-start.1 = (bf16[2,1,1,1,1,24,1536]{6,5,4,3,2,1,0:T(8,128)(2,1)S(1)}, bf16[2,1,1,1,1,24,1536]{6,5,4,3,2,1,0:T(8,128)(2,1)S(1)}, u32[]{:S(2)}, u32[]{:S(2)}) collective-permute-start(bf16[2,1,1,1,1,24,1536]{6,5,4,3,2,1,0:T(8,128)(2,1)S(1)} %pad_maximum_fusion.17), channel_id=1, source_target_pairs={{0,8},{1,9},{2,10},{3,11},{4,12},{5,13},{6,14},{7,15},{8,0},{9,1},... | collective-permute-start | bytes 442376 | tf_op jit(solution)/shard_map/ppermute | solution.py:595
  35.4 1.7 collective-permute-done.10
  37.2 1.7 collective-permute-start.11
  39.0 2.4 collective-permute-done.6
  41.4 1.8 collective-permute-start.7
  43.2 3.6 collective-permute-done.1
  46.7 3.2 collective-permute-done.11
  50.0 1.9 collective-permute-start.2
  53.7 1.9 collective-permute-start.8
  55.6 10.3 %collective-permute-done.2 = bf16[2,2,1,1,1,24,1536]{6,5,4,3,2,1,0:T(8,128)(2,1)S(1)} collective-permute-done((bf16[2,2,1,1,1,24,1536]{6,5,4,3,2,1,0:T(8,128)(2,1)S(1)}, bf16[2,2,1,1,1,24,1536]{6,5,4,3,2,1,0:T(8,128)(2,1)S(1)}, u32[]{:S(2)}, u32[]{:S(2)}) %collective-permute-start.2) | collective-permute-done | bytes 294944 | tf_op jit(solution)/shard_map/ppermute | solution.py:595
  66.6 1.6 collective-permute-start.13
  68.2 11.7 %collective-permute-done.8 = bf16[2,2,2,1,1,24,896]{6,5,4,3,2,1,0:T(8,128)(2,1)S(1)} collective-permute-done((bf16[2,2,2,1,1,24,896]{6,5,4,3,2,1,0:T(8,128)(2,1)S(1)}, bf16[2,2,2,1,1,24,896]{6,5,4,3,2,1,0:T(8,128)(2,1)S(1)}, u32[]{:S(2)}, u32[]{:S(2)}) %collective-permute-start.8) | collective-permute-done | bytes 344096 | tf_op jit(solution)/shard_map/ppermute | solution.py:595
  81.9 9.9 %collective-permute-done.13 = bf16[2,2,2,1,1,24,1536]{6,5,4,3,2,1,0:T(8,128)(2,1)S(1)} collective-permute-done((bf16[2,2,2,1,1,24,1536]{6,5,4,3,2,1,0:T(8,128)(2,1)S(1)}, bf16[2,2,2,1,1,24,1536]{6,5,4,3,2,1,0:T(8,128)(2,1)S(1)}, u32[]{:S(2)}, u32[]{:S(2)}) %collective-permute-start.13) | collective-permute-done | bytes 589856 | tf_op jit(solution)/shard_map/ppermute | solution.py:595
  94.4 2.6 copy.73
  97.1 1.7 pad.11.refs_0_.refs_2_
  100.2 1.6 pad_maximum_fusion.1
  101.8 11.6 %shard_map.279 = (bf16[8,208,768]{2,1,0:T(8,128)(2,1)}, bf16[8,208,2304]{2,1,0:T(8,128)(2,1)}) custom-call(bf16[8,208,768]{2,1,0:T(8,128)(2,1)} %pad.11.refs_0_.refs_2_, bf16[768,1536]{1,0:T(8,128)(2,1)} %bitcast.78, bf16[768,896]{1,0:T(8,128)(2,1)} %bitcast.85, f32[16,768]{1,0:T(8,128)} %slice_convert_fusion.refs_3_.refs_2_.refs_4_.refs_6_, ...), custom_call_target="tpu_custom_call" | custom-call | flops 900000000 | tf_op jit(solution)/shard_map/pallas_call | solution.py:373
  113.4 3.7 all-to-all-start.1
  117.3 13.4 %shard_map.280.refs_1_ = bf16[8,208,768]{2,1,0:T(8,128)(2,1)} custom-call(bf16[8,208,2304]{2,1,0:T(8,128)(2,1)} %get-tuple-element.53.refs_0_), custom_call_target="tpu_custom_call" | custom-call | flops 1400000000 | tf_op jit(solution)/shard_map/pallas_call | solution.py:373
  130.8 1.6 broadcast_select_fusion.1
  132.3 1.7 pad_maximum_fusion.2
  134.0 8.9 %shard_map.281 = (bf16[8,208,768]{2,1,0:T(8,128)(2,1)}, f32[8,208,768]{2,1,0:T(8,128)}) custom-call(bf16[8,208,768]{2,1,0:T(8,128)(2,1)} %pad.11.refs_0_.refs_2_, bf16[8,208,768]{2,1,0:T(8,128)(2,1)} %shard_map.280.refs_1_, bf16[768,1536]{1,0:T(8,128)(2,1)} %bitcast.80, f32[16,768]{1,0:T(8,128)} %slice_convert_fusion.refs_3_.refs_2_.refs_4_.refs_6_), custom_call_target="tpu_custom_call" | custom-call | flops 800000000 | tf_op jit(solution)/shard_map/pallas_call | solution.py:373
  142.9 3.7 all-to-all-done.1
  146.9 1.7 pad.13.refs_1_
  148.6 20.6 %shard_map.282 = (bf16[8,208,768]{2,1,0:T(8,128)(2,1)}, bf16[8,208,2304]{2,1,0:T(8,128)(2,1)}, bf16[8,208,768]{2,1,0:T(8,128)(2,1)}, f32[8,208,768]{2,1,0:T(8,128)}) custom-call(f32[8,208,768]{2,1,0:T(8,128)} %get-tuple-element.56.refs_0_.refs_1_, bf16[768,9216]{1,0:T(8,128)(2,1)} %all-gather.2.cloned.1.call-done.refs_1_.refs_2_.refs_3_, ...), custom_call_target="tpu_custom_call" | custom-call | flops 2300000000 | tf_op jit(solution)/shard_map/pallas_call | solution.py:373
  169.2 45.2 %shard_map.283 = (bf16[8,196,768]{2,1,0:T(8,128)(2,1)}, f32[8,208,768]{2,1,0:T(8,128)}, bf16[8,208,768]{2,1,0:T(8,128)(2,1)}, bf16[8,208,3072]{2,1,0:T(8,128)(2,...) custom-call(f32[8,208,768]{2,1,0:T(8,128)} %get-tuple-element.57.refs_0_, bf16[8,208,768]{2,1,0:T(8,128)(2,1)} %pad.13.refs_1_, ...), custom_call_target="tpu_custom_call" | custom-call | flops 4499999744 | tf_op jit(solution)/shard_map/pallas_call | solution.py:373
  214.4 25.5 %shard_map.284.refs_5_ = bf16[768,6144]{1,0:T(8,128)(2,1)} custom-call(bf16[1664,768]{1,0:T(8,128)(2,1)} %bitcast.102, bf16[1664,3072]{1,0:T(8,128)(2,1)} %bitcast.88, bf16[1664,3072]{1,0:T(8,128)(2,1)} %bitcast.87, bf16[1664,768]{1,0:T(8,128)(2,1)} %bitcast.76), custom_call_target="tpu_custom_call" | custom-call | flops 2500000000 | tf_op jit(solution)/shard_map/pallas_call | solution.py:373
  240.0 1.7 copy-done.17
  241.7 3.3 copy.79
  244.9 3.9 all-to-all-start.2
  248.8 35.2 %shard_map.285 = (bf16[8,208,768]{2,1,0:T(8,128)(2,1)}, bf16[8,208,2304]{2,1,0:T(8,128)(2,1)}, f32[8,208,768]{2,1,0:T(8,128)}, bf16[8,208,768]{2,1,0:T(8,128)(2,1)}, f32[8,768]{1,0:T(8,128)}) custom-call(f32[8,208,768]{2,1,0:T(8,128)} %get-tuple-element.60.refs_0_, f32[8,208,768]{2,1,0:T(8,128)} %get-tuple-element.56.refs_0_.refs_1_, ...), custom_call_target="tpu_custom_call" | custom-call | flops 4200000000 | tf_op jit(solution)/shard_map/pallas_call | solution.py:373
  284.6 15.4 %shard_map.286 = bf16[768,3072]{1,0:T(8,128)(2,1)} custom-call(bf16[1664,768]{1,0:T(8,128)(2,1)} %bitcast.106, bf16[1664,2304]{1,0:T(8,128)(2,1)} %bitcast.96, bf16[1664,768]{1,0:T(8,128)(2,1)} %bitcast.107, bf16[1664,768]{1,0:T(8,128)(2,1)} %bitcast.108, bf16[1,128]{1,0:T(2,128)(2,1)} %slice_bitcast_fusion.2.refs_4_), custom_call_target="tpu_custom_call" | custom-call | flops 1600000000 | tf_op jit(solution)/shard_map/pallas_call | solution.py:373
  300.0 1.9 constant_dynamic-slice_fusion.9.refs_2_
  303.3 5.7 %shard_map.287 = bf16[768,768]{1,0:T(8,128)(2,1)} custom-call(bf16[1664,768]{1,0:T(8,128)(2,1)} %bitcast.105, bf16[1664,768]{1,0:T(8,128)(2,1)} %bitcast.89, bf16[2,2,2,2,1,24,3072]{6,5,4,3,2,1,0:T(8,128)(2,1)} %copy-done.5), custom_call_target="tpu_custom_call" | custom-call | flops 600000000 | tf_op jit(solution)/shard_map/pallas_call | solution.py:373
  309.1 3.4 add_convert_fusion
  313.6 8.0 %shard_map.288 = (bf16[8,208,768]{2,1,0:T(8,128)(2,1)}, bf16[8,208,768]{2,1,0:T(8,128)(2,1)}, f32[8,768]{1,0:T(8,128)}) custom-call(bf16[8,208,768]{2,1,0:T(8,128)(2,1)} %get-tuple-element.66.refs_0_, bf16[768,1536]{1,0:T(8,128)(2,1)} %bitcast.81, bf16[2,2,1,2,1,24,3072]{6,5,4,3,2,1,0:T(8,128)(2,1)} %constant_dynamic-slice_fusion.8.refs_2_), custom_call_target="tpu_custom_call" | custom-call | flops 800000000 | tf_op jit(solution)/shard_map/pallas_call | solution.py:373
  321.7 5.6 %shard_map.289 = bf16[768,768]{1,0:T(8,128)(2,1)} custom-call(bf16[1664,768]{1,0:T(8,128)(2,1)} %bitcast.77, bf16[1664,768]{1,0:T(8,128)(2,1)} %bitcast.104, bf16[2,2,1,2,1,24,3072]{6,5,4,3,2,1,0:T(8,128)(2,1)} %constant_dynamic-slice_fusion.8.refs_2_), custom_call_target="tpu_custom_call" | custom-call | flops 600000000 | tf_op jit(solution)/shard_map/pallas_call | solution.py:373
  327.3 1.5 pad_maximum_fusion.3
  333.5 18.2 %shard_map.290.refs_3_ = bf16[8,208,2304]{2,1,0:T(8,128)(2,1)} custom-call(bf16[8,208,2304]{2,1,0:T(8,128)(2,1)} %get-tuple-element.53.refs_0_, bf16[8,208,768]{2,1,0:T(8,128)(2,1)} %get-tuple-element.73.refs_1_, bf16[2,2,2,2,1,24,1536]{6,5,4,3,2,1,0:T(8,128)(2,1)} %constant_dynamic-slice_fusion.7.refs_2_), custom_call_target="tpu_custom_call" | custom-call | flops 2000000000 | tf_op jit(solution)/shard_map/pallas_call | solution.py:373
  351.7 2.0 add_convert_fusion.2
  355.7 1.5 collective-permute-start.17
  357.2 11.5 %shard_map.291 = bf16[768,2304]{1,0:T(8,128)(2,1)} custom-call(bf16[1664,768]{1,0:T(8,128)(2,1)} %bitcast.103, bf16[1664,2304]{1,0:T(8,128)(2,1)} %bitcast.75, bf16[2,2,2,1,1,24,1536]{6,5,4,3,2,1,0:T(8,128)(2,1)} %constant_dynamic-slice_fusion.6.refs_2_), custom_call_target="tpu_custom_call" | custom-call | flops 1200000000 | tf_op jit(solution)/shard_map/pallas_call | solution.py:373
  368.8 3.7 fusion.5
  376.3 2.8 add_convert_fusion.1
  379.1 4.8 all-to-all-start.5
  383.9 13.6 %shard_map.292 = (bf16[8,196,768]{2,1,0:T(8,128)(2,1)}, bf16[768,128]{1,0:T(8,128)(2,1)}) custom-call(s32[1]{0:T(128)} %bitcast.17.refs_0_, f32[8,208,768]{2,1,0:T(8,128)} %get-tuple-element.65.refs_1_, bf16[8,208,768]{2,1,0:T(8,128)(2,1)} %pad.11.refs_0_.refs_2_, bf16[8,208,2304]{2,1,0:T(8,128)(2,1)} %shard_map.290.refs_3_, bf16[768,1536]{1,0:T(8,128)(2,1)} %bitcast.79, ...), custom_call_target="tpu_custom_call" | custom-call | flops 1300000000 | tf_op jit(solution)/shard_map/pallas_call | solution.py:574
  398.7 2.0 shard_map.293
  400.8 2.3 add_convert_fusion.4
  403.1 1.8 pad_maximum_fusion.4
  405.9 2.1 collective-permute-start.25
  413.8 2.1 collective-permute-done.25
  416.9 5.4 %all-to-all-start.4 = ((bf16[16,24,1152]{2,1,0:T(8,128)(2,1)}), bf16[16,24,1152]{2,1,0:T(8,128)(2,1)}, u32[]{:S(2)}, u32[]{:S(2)}) async-start(bf16[16,24,1152]{2,1,0:T(8,128)(2,1)} %bitcast.100), calls=%async_computation.5 | async-start | bytes 1769472 | tf_op jit(solution)/shard_map/all_to_all | solution.py:641
  423.9 1.9 collective-permute-start.23
  427.9 20.7 %collective-permute-done.19 = bf16[2,196,768]{2,0,1:T(2,128)(2,1)} collective-permute-done((bf16[2,196,768]{2,0,1:T(2,128)(2,1)}, bf16[2,196,768]{2,0,1:T(2,128)(2,1)}, u32[]{:S(2)}, u32[]{:S(2)}) %collective-permute-start.19) | collective-permute-done | bytes 602144 | tf_op jit(solution)/shard_map/ppermute | solution.py:703
  450.6 5.4 %all-to-all-start.3 = ((bf16[8,24,1280]{2,1,0:T(8,128)(2,1)}), bf16[8,24,1280]{2,1,0:T(8,128)(2,1)S(1)}, u32[]{:S(2)}, u32[]{:S(2)}) async-start(bf16[8,24,1280]{2,1,0:T(8,128)(2,1)} %bitcast.41), calls=%async_computation.4 | async-start | bytes 983040 | tf_op jit(solution)/shard_map/all_to_all | solution.py:641
  456.0 2.0 select_bitcast_fusion.3
  458.3 3.3 copy.90
  464.4 5.4 %all-to-all-done.3 = bf16[8,24,1280]{2,1,0:T(8,128)(2,1)S(1)} async-done(((bf16[8,24,1280]{2,1,0:T(8,128)(2,1)}), bf16[8,24,1280]{2,1,0:T(8,128)(2,1)S(1)}, u32[]{:S(2)}, u32[]{:S(2)}) %all-to-all-start.3) | async-done | bytes 491552 | tf_op jit(solution)/shard_map/all_to_all | solution.py:641
  (195 shorter events, 50.6 us)
Async XLA Ops:
  7.2 4.6 copy-start.27
  7.2 4.6 copy-start.26
  7.2 141.4 %all-gather.2.cloned.1.call-start = ((), (), s32[]{:S(2)}) async-start(), calls=%async_computation.7 | async-start | bytes 14598144 | tf_op jit(solution)/shard_map/all_gather | solution.py:692
  12.7 4.8 copy-start.34
  12.7 4.9 %copy-start.28 = (bf16[3,24]{1,0:T(4,128)(2,1)S(1)}, bf16[3,24]{1,0:T(4,128)(2,1)}, u32[]{:S(2)}) copy-start(bf16[3,24]{1,0:T(4,128)(2,1)} %param.18) | copy-start | bytes 436
  12.7 4.9 %copy-start.29 = (bf16[24]{0:T(256)(128)(2,1)S(1)}, bf16[24]{0:T(256)(128)(2,1)}, u32[]{:S(2)}) copy-start(bf16[24]{0:T(256)(128)(2,1)} %param.17) | copy-start | bytes 148
  12.7 4.8 %copy-start.30 = (bf16[24]{0:T(256)(128)(2,1)S(1)}, bf16[24]{0:T(256)(128)(2,1)}, u32[]{:S(2)}) copy-start(bf16[24]{0:T(256)(128)(2,1)} %param.22) | copy-start | bytes 148
  12.7 4.8 %copy-start.31 = (bf16[2,24]{1,0:T(2,128)(2,1)S(1)}, bf16[2,24]{1,0:T(2,128)(2,1)}, u32[]{:S(2)}) copy-start(bf16[2,24]{1,0:T(2,128)(2,1)} %param.23) | copy-start | bytes 292
  12.7 4.8 %copy-start.32 = (bf16[24]{0:T(256)(128)(2,1)S(1)}, bf16[24]{0:T(256)(128)(2,1)}, u32[]{:S(2)}) copy-start(bf16[24]{0:T(256)(128)(2,1)} %param.26) | copy-start | bytes 148
  12.7 4.8 %copy-start.33 = (bf16[2,24]{1,0:T(2,128)(2,1)S(1)}, bf16[2,24]{1,0:T(2,128)(2,1)}, u32[]{:S(2)}) copy-start(bf16[2,24]{1,0:T(2,128)(2,1)} %param.27) | copy-start | bytes 292
  12.7 5.0 %copy-start.22 = (bf16[24,2304]{1,0:T(8,128)(2,1)S(1)}, bf16[24,2304]{1,0:T(8,128)(2,1)}, u32[]{:S(2)}) copy-start(bf16[24,2304]{1,0:T(8,128)(2,1)} %param.19) | copy-start | bytes 331780
  12.8 10.6 %copy-start.24 = (bf16[24,768]{1,0:T(8,128)(2,1)S(1)}, bf16[24,768]{1,0:T(8,128)(2,1)}, u32[]{:S(2)}) copy-start(bf16[24,768]{1,0:T(8,128)(2,1)} %param.21) | copy-start | bytes 110596
  12.8 10.6 %copy-start.25 = (bf16[24,768]{1,0:T(8,128)(2,1)S(1)}, bf16[24,768]{1,0:T(8,128)(2,1)}, u32[]{:S(2)}) copy-start(bf16[24,768]{1,0:T(8,128)(2,1)} %param.20) | copy-start | bytes 110596
  12.8 81.7 %all-to-all-start = ((bf16[4,2,196,768]{3,1,2,0:T(2,128)(2,1)}), bf16[4,2,196,768]{3,1,2,0:T(2,128)(2,1)}, u32[]{:S(2)}, u32[]{:S(2)}) async-start(bf16[4,2,196,768]{3,1,2,0:T(2,128)(2,1)} %param.16), calls=%async_computation | async-start | bytes 4816896 | tf_op jit(solution)/shard_map/all_to_all | solution.py:695
  17.8 6.0 %collective-permute-start.5 = (bf16[1,1,1,1,1,24,896]{6,5,4,3,2,1,0:T(8,128)(2,1)S(1)}, bf16[1,1,1,1,1,24,896]{6,5,4,3,2,1,0:T(8,128)(2,1)S(1)}, u32[]{:S(2)}, u32[]{:S(2)}) collective-permute-start(bf16[1,1,1,1,1,24,896]{6,5,4,3,2,1,0:T(8,128)(2,1)S(1)} %fusion.4), channel_id=1, source_target_pairs={{0,4},{1,5},{2,6},{3,7},{4,0},{5,1},{6,2},{7,3},{8,12},{9,13},{10,... | collective-permute-start | bytes 129032 | tf_op jit(solution)/shard_map/ppermute | solution.py:595
  20.8 9.5 %collective-permute-start = (bf16[1,1,1,1,1,24,1536]{6,5,4,3,2,1,0:T(8,128)(2,1)S(1)}, bf16[1,1,1,1,1,24,1536]{6,5,4,3,2,1,0:T(8,128)(2,1)S(1)}, u32[]{:S(2)}, u32[]{:S(2)}) collective-permute-start(bf16[1,1,1,1,1,24,1536]{6,5,4,3,2,1,0:T(8,128)(2,1)S(1)} %slice_bitcast_fusion), channel_id=1, source_target_pairs={{0,16},{1,17},{2,18},{3,19},{4,20},{5,21},{6,22},{7,23},{8,24},{9,... | collective-permute-start | bytes 221192 | tf_op jit(solution)/shard_map/ppermute | solution.py:595
  23.4 13.8 %collective-permute-start.10 = (bf16[1,1,1,1,1,24,1536]{6,5,4,3,2,1,0:T(8,128)(2,1)S(1)}, bf16[1,1,1,1,1,24,1536]{6,5,4,3,2,1,0:T(8,128)(2,1)S(1)}, u32[]{:S(2)}, u32[]{:S(2)}) collective-permute-start(bf16[1,1,1,1,1,24,1536]{6,5,4,3,2,1,0:T(8,128)(2,1)S(1)} %maximum_bitcast_fusion), channel_id=1, source_target_pairs={{0,16},{1,17},{2,18},{3,19},{4,20},{5,21},{6,22},{7,23},{8,24},{9,... | collective-permute-start | bytes 221192 | tf_op jit(solution)/shard_map/ppermute | solution.py:595
  23.8 17.5 %collective-permute-start.6 = (bf16[1,1,2,1,1,24,896]{6,5,4,3,2,1,0:T(8,128)(2,1)S(1)}, bf16[1,1,2,1,1,24,896]{6,5,4,3,2,1,0:T(8,128)(2,1)S(1)}, u32[]{:S(2)}, u32[]{:S(2)}) collective-permute-start(bf16[1,1,2,1,1,24,896]{6,5,4,3,2,1,0:T(8,128)(2,1)S(1)} %pad_maximum_fusion.19), channel_id=1, source_target_pairs={{0,16},{1,17},{2,18},{3,19},{4,20},{5,21},{6,22},{7,23},{8,24},{9,... | collective-permute-start | bytes 258056 | tf_op jit(solution)/shard_map/ppermute | solution.py:595
  30.3 16.4 %collective-permute-start.1 = (bf16[2,1,1,1,1,24,1536]{6,5,4,3,2,1,0:T(8,128)(2,1)S(1)}, bf16[2,1,1,1,1,24,1536]{6,5,4,3,2,1,0:T(8,128)(2,1)S(1)}, u32[]{:S(2)}, u32[]{:S(2)}) collective-permute-start(bf16[2,1,1,1,1,24,1536]{6,5,4,3,2,1,0:T(8,128)(2,1)S(1)} %pad_maximum_fusion.17), channel_id=1, source_target_pairs={{0,8},{1,9},{2,10},{3,11},{4,12},{5,13},{6,14},{7,15},{8,0},{9,1},... | collective-permute-start | bytes 442376 | tf_op jit(solution)/shard_map/ppermute | solution.py:595
  37.2 12.6 %collective-permute-start.11 = (bf16[2,1,1,1,1,24,1536]{6,5,4,3,2,1,0:T(8,128)(2,1)S(1)}, bf16[2,1,1,1,1,24,1536]{6,5,4,3,2,1,0:T(8,128)(2,1)S(1)}, u32[]{:S(2)}, u32[]{:S(2)}) collective-permute-start(bf16[2,1,1,1,1,24,1536]{6,5,4,3,2,1,0:T(8,128)(2,1)S(1)} %pad_maximum_fusion.18), channel_id=1, source_target_pairs={{0,8},{1,9},{2,10},{3,11},{4,12},{5,13},{6,14},{7,15},{8,0},{9,1},... | collective-permute-start | bytes 442376 | tf_op jit(solution)/shard_map/ppermute | solution.py:595
  41.4 12.2 %collective-permute-start.7 = (bf16[2,1,2,1,1,24,896]{6,5,4,3,2,1,0:T(8,128)(2,1)S(1)}, bf16[2,1,2,1,1,24,896]{6,5,4,3,2,1,0:T(8,128)(2,1)S(1)}, u32[]{:S(2)}, u32[]{:S(2)}) collective-permute-start(bf16[2,1,2,1,1,24,896]{6,5,4,3,2,1,0:T(8,128)(2,1)S(1)} %pad_maximum_fusion.16), channel_id=1, source_target_pairs={{0,8},{1,9},{2,10},{3,11},{4,12},{5,13},{6,14},{7,15},{8,0},{9,1},... | collective-permute-start | bytes 516104 | tf_op jit(solution)/shard_map/ppermute | solution.py:595
  50.0 15.9 %collective-permute-start.2 = (bf16[2,2,1,1,1,24,1536]{6,5,4,3,2,1,0:T(8,128)(2,1)S(1)}, bf16[2,2,1,1,1,24,1536]{6,5,4,3,2,1,0:T(8,128)(2,1)S(1)}, u32[]{:S(2)}, u32[]{:S(2)}) collective-permute-start(bf16[2,2,1,1,1,24,1536]{6,5,4,3,2,1,0:T(8,128)(2,1)S(1)} %pad_maximum_fusion.13), channel_id=1, source_target_pairs={{0,2},{1,3},{2,0},{3,1},{4,6},{5,7},{6,4},{7,5},{8,10},{9,11},{10,... | collective-permute-start | bytes 884744 | tf_op jit(solution)/shard_map/ppermute | solution.py:595
  51.9 14.5 %collective-permute-start.12 = (bf16[2,2,1,1,1,24,1536]{6,5,4,3,2,1,0:T(8,128)(2,1)S(1)}, bf16[2,2,1,1,1,24,1536]{6,5,4,3,2,1,0:T(8,128)(2,1)S(1)}, u32[]{:S(2)}, u32[]{:S(2)}) collective-permute-start(bf16[2,2,1,1,1,24,1536]{6,5,4,3,2,1,0:T(8,128)(2,1)S(1)} %pad_maximum_fusion.14), channel_id=1, source_target_pairs={{0,4},{1,5},{2,6},{3,7},{4,0},{5,1},{6,2},{7,3},{8,12},{9,13},{10,... | collective-permute-start | bytes 884744 | tf_op jit(solution)/shard_map/ppermute | solution.py:595
  53.7 26.2 %collective-permute-start.8 = (bf16[2,2,2,1,1,24,896]{6,5,4,3,2,1,0:T(8,128)(2,1)S(1)}, bf16[2,2,2,1,1,24,896]{6,5,4,3,2,1,0:T(8,128)(2,1)S(1)}, u32[]{:S(2)}, u32[]{:S(2)}) collective-permute-start(bf16[2,2,2,1,1,24,896]{6,5,4,3,2,1,0:T(8,128)(2,1)S(1)} %pad_maximum_fusion.12), channel_id=1, source_target_pairs={{0,2},{1,3},{2,0},{3,1},{4,6},{5,7},{6,4},{7,5},{8,10},{9,11},{10,... | collective-permute-start | bytes 1032200 | tf_op jit(solution)/shard_map/ppermute | solution.py:595
  66.0 14.1 %collective-permute-start.3 = (bf16[2,2,1,2,1,24,1536]{6,5,4,3,2,1,0:T(8,128)(2,1)S(1)}, bf16[2,2,1,2,1,24,1536]{6,5,4,3,2,1,0:T(8,128)(2,1)S(1)}, u32[]{:S(2)}, u32[]{:S(2)}) collective-permute-start(bf16[2,2,1,2,1,24,1536]{6,5,4,3,2,1,0:T(8,128)(2,1)S(1)} %pad_maximum_fusion.9), channel_id=1, source_target_pairs={{0,4},{1,5},{2,6},{3,7},{4,0},{5,1},{6,2},{7,3},{8,12},{9,13},{10,... | collective-permute-start | bytes 1769480 | tf_op jit(solution)/shard_map/ppermute | solution.py:595
  66.6 25.2 %collective-permute-start.13 = (bf16[2,2,2,1,1,24,1536]{6,5,4,3,2,1,0:T(8,128)(2,1)S(1)}, bf16[2,2,2,1,1,24,1536]{6,5,4,3,2,1,0:T(8,128)(2,1)S(1)}, u32[]{:S(2)}, u32[]{:S(2)}) collective-permute-start(bf16[2,2,2,1,1,24,1536]{6,5,4,3,2,1,0:T(8,128)(2,1)S(1)} %pad_maximum_fusion.10), channel_id=1, source_target_pairs={{0,2},{1,3},{2,0},{3,1},{4,6},{5,7},{6,4},{7,5},{8,10},{9,11},{10,... | collective-permute-start | bytes 1769480 | tf_op jit(solution)/shard_map/ppermute | solution.py:595
  80.1 13.1 %collective-permute-start.9 = (bf16[2,2,2,2,1,24,896]{6,5,4,3,2,1,0:T(8,128)(2,1)S(1)}, bf16[2,2,2,2,1,24,896]{6,5,4,3,2,1,0:T(8,128)(2,1)S(1)}, u32[]{:S(2)}, u32[]{:S(2)}) collective-permute-start(bf16[2,2,2,2,1,24,896]{6,5,4,3,2,1,0:T(8,128)(2,1)S(1)} %pad_maximum_fusion.8), channel_id=1, source_target_pairs={{0,1},{1,0},{2,3},{3,2},{4,5},{5,4},{6,7},{7,6},{8,9},{9,8},{10,11... | collective-permute-start | bytes 2064392 | tf_op jit(solution)/shard_map/ppermute | solution.py:595
  80.2 1.7 copy-start.9
  81.4 17.3 %collective-permute-start.4 = (bf16[2,2,2,2,1,24,1536]{6,5,4,3,2,1,0:T(8,128)(2,1)}, bf16[2,2,2,2,1,24,1536]{6,5,4,3,2,1,0:T(8,128)(2,1)}, u32[]{:S(2)}, u32[]{:S(2)}) collective-permute-start(bf16[2,2,2,2,1,24,1536]{6,5,4,3,2,1,0:T(8,128)(2,1)} %pad_maximum_fusion.6), channel_id=1, source_target_pairs={{0,1},{1,0},{2,3},{3,2},{4,5},{5,4},{6,7},{7,6},{8,9},{9,8},{10,11... | collective-permute-start | bytes 3538952 | tf_op jit(solution)/shard_map/ppermute | solution.py:595
  93.1 24.2 %collective-permute-start.14 = (bf16[2,2,2,2,1,24,1536]{6,5,4,3,2,1,0:T(8,128)(2,1)}, bf16[2,2,2,2,1,24,1536]{6,5,4,3,2,1,0:T(8,128)(2,1)}, u32[]{:S(2)}, u32[]{:S(2)}) collective-permute-start(bf16[2,2,2,2,1,24,1536]{6,5,4,3,2,1,0:T(8,128)(2,1)} %pad_maximum_fusion.7.refs_4_), channel_id=1, source_target_pairs={{0,1},{1,0},{2,3},{3,2},{4,5},{5,4},{6,7},{7,6},{8,9},{9,8},{10,11... | collective-permute-start | bytes 3538952 | tf_op jit(solution)/shard_map/ppermute | solution.py:595
  93.4 3.6 copy-start
  113.4 33.3 %all-to-all-start.1 = ((bf16[4,2,196,768]{3,1,2,0:T(2,128)(2,1)}), bf16[4,2,196,768]{3,1,2,0:T(2,128)(2,1)S(1)}, u32[]{:S(2)}, u32[]{:S(2)}) async-start(bf16[4,2,196,768]{3,1,2,0:T(2,128)(2,1)} %param.31), calls=%async_computation.1 | async-start | bytes 4816896 | tf_op jit(solution)/shard_map/all_to_all | solution.py:695
  117.1 281.7 %reduce-scatter.2.cloned.1.call-start = ((), (), s32[]{:S(2)}) async-start(), calls=%async_computation.8 | async-start | bytes 9732096 | tf_op jit(solution)/shard_map/reduce_scatter | solution.py:730
  240.0 1.7 copy-start.17
  244.9 39.1 %all-to-all-start.2 = ((bf16[4,2,196,768]{3,1,2,0:T(2,128)(2,1)}), bf16[4,2,196,768]{3,1,2,0:T(2,128)(2,1)S(1)}, u32[]{:S(2)}, u32[]{:S(2)}) async-start(bf16[4,2,196,768]{3,1,2,0:T(2,128)(2,1)} %copy.79), calls=%async_computation.2 | async-start | bytes 4816896 | tf_op jit(solution)/shard_map/all_to_all | solution.py:699
  284.1 16.0 %copy-start.2 = (bf16[4,2,196,768]{3,1,2,0:T(2,128)(2,1)}, bf16[4,2,196,768]{3,1,2,0:T(2,128)(2,1)S(1)}, u32[]{:S(2)}) copy-start(bf16[4,2,196,768]{3,1,2,0:T(2,128)(2,1)S(1)} %all-to-all-done.2) | copy-start | bytes 7225348
  301.9 7.1 %collective-permute-start.15 = (bf16[2,2,2,2,1,24,3072]{6,5,4,3,2,1,0:T(8,128)(2,1)S(1)}, bf16[2,2,2,2,1,24,3072]{6,5,4,3,2,1,0:T(8,128)(2,1)}, u32[]{:S(2)}, u32[]{:S(2)}) collective-permute-start(bf16[2,2,2,2,1,24,3072]{6,5,4,3,2,1,0:T(8,128)(2,1)S(1)} %constant_dynamic-slice_fusion.9.refs_2_), channel_id=1, source_target_pairs={{0,1},{1,0},{2,3},{3,2},{4,5},{5,4},{6,7},{7,6},{8,9},{9,8},{10,11... | collective-permute-start | bytes 7077896 | tf_op jit(solution)/shard_map/ppermute | solution.py:595
  321.7 5.6 %copy-start.15 = (bf16[768,768]{1,0:T(8,128)(2,1)S(1)}, bf16[768,768]{1,0:T(8,128)(2,1)}, u32[]{:S(2)}) copy-start(bf16[768,768]{1,0:T(8,128)(2,1)} %shard_map.287) | copy-start | bytes 3538948
  328.8 3.2 copy-start.1
  331.5 20.3 %collective-permute-start.16 = (bf16[2,2,2,2,1,24,1536]{6,5,4,3,2,1,0:T(8,128)(2,1)}, bf16[2,2,2,2,1,24,1536]{6,5,4,3,2,1,0:T(8,128)(2,1)}, u32[]{:S(2)}, u32[]{:S(2)}) collective-permute-start(bf16[2,2,2,2,1,24,1536]{6,5,4,3,2,1,0:T(8,128)(2,1)} %constant_dynamic-slice_fusion.7.refs_2_), channel_id=1, source_target_pairs={{0,1},{1,0},{2,3},{3,2},{4,5},{5,4},{6,7},{7,6},{8,9},{9,8},{10,11... | collective-permute-start | bytes 3538952 | tf_op jit(solution)/shard_map/ppermute | solution.py:595
  332.1 40.4 %collective-permute-start.27 = (bf16[2,2,1,2,1,24,3072]{6,5,4,3,2,1,0:T(8,128)(2,1)S(1)}, bf16[2,2,1,2,1,24,3072]{6,5,4,3,2,1,0:T(8,128)(2,1)}, u32[]{:S(2)}, u32[]{:S(2)}) collective-permute-start(bf16[2,2,1,2,1,24,3072]{6,5,4,3,2,1,0:T(8,128)(2,1)S(1)} %copy-done.1), channel_id=1, source_target_pairs={{0,4},{1,5},{2,6},{3,7},{4,0},{5,1},{6,2},{7,3},{8,12},{9,13},{10,... | collective-permute-start | bytes 3538952 | tf_op jit(solution)/shard_map/ppermute | solution.py:595
  355.7 17.9 %collective-permute-start.17 = (bf16[2,2,2,1,1,24,1536]{6,5,4,3,2,1,0:T(8,128)(2,1)}, bf16[2,2,2,1,1,24,1536]{6,5,4,3,2,1,0:T(8,128)(2,1)}, u32[]{:S(2)}, u32[]{:S(2)}) collective-permute-start(bf16[2,2,2,1,1,24,1536]{6,5,4,3,2,1,0:T(8,128)(2,1)} %constant_dynamic-slice_fusion.6.refs_2_), channel_id=1, source_target_pairs={{0,2},{1,3},{2,0},{3,1},{4,6},{5,7},{6,4},{7,5},{8,10},{9,11},{10,... | collective-permute-start | bytes 1769480 | tf_op jit(solution)/shard_map/ppermute | solution.py:595
  368.8 4.9 %copy-start.14 = (bf16[2,2,2,2,1,24,1536]{6,5,4,3,2,1,0:T(8,128)(2,1)S(1)}, bf16[2,2,2,2,1,24,1536]{6,5,4,3,2,1,0:T(8,128)(2,1)}, u32[]{:S(2)}) copy-start(bf16[2,2,2,2,1,24,1536]{6,5,4,3,2,1,0:T(8,128)(2,1)} %copy-done.13) | copy-start | bytes 3538948
  372.5 6.6 %copy-start.6 = (bf16[768,1152]{1,0:T(8,128)(2,1)}, bf16[768,1152]{1,0:T(8,128)(2,1)S(1)}, u32[]{:S(2)}) copy-start(bf16[768,1152]{1,0:T(8,128)(2,1)S(1)} %get-tuple-element.162) | copy-start | bytes 5308420
  373.6 27.2 %collective-permute-start.21 = (bf16[2,2,2,2,1,24,1152]{6,5,4,3,2,1,0:T(8,128)(2,1)}, bf16[2,2,2,2,1,24,1152]{6,5,4,3,2,1,0:T(8,128)(2,1)}, u32[]{:S(2)}, u32[]{:S(2)}) collective-permute-start(bf16[2,2,2,2,1,24,1152]{6,5,4,3,2,1,0:T(8,128)(2,1)} %constant_dynamic-slice_fusion.4), channel_id=1, source_target_pairs={{0,1},{1,0},{2,3},{3,2},{4,5},{5,4},{6,7},{7,6},{8,9},{9,8},{10,11... | collective-permute-start | bytes 2654216 | tf_op jit(solution)/shard_map/ppermute | solution.py:595
  375.7 3.4 copy-start.19
  375.7 21.7 %collective-permute-start.24 = (bf16[2,2,1,1,1,24,1536]{6,5,4,3,2,1,0:T(8,128)(2,1)S(1)}, bf16[2,2,1,1,1,24,1536]{6,5,4,3,2,1,0:T(8,128)(2,1)}, u32[]{:S(2)}, u32[]{:S(2)}) collective-permute-start(bf16[2,2,1,1,1,24,1536]{6,5,4,3,2,1,0:T(8,128)(2,1)S(1)} %constant_dynamic-slice_fusion.5.refs_10_), channel_id=1, source_target_pairs={{0,4},{1,5},{2,6},{3,7},{4,0},{5,1},{6,2},{7,3},{8,12},{9,13},{10,... | collective-permute-start | bytes 884744 | tf_op jit(solution)/shard_map/ppermute | solution.py:595
  379.1 37.8 %all-to-all-start.5 = ((bf16[8,24,3072]{2,1,0:T(8,128)(2,1)}), bf16[8,24,3072]{2,1,0:T(8,128)(2,1)S(1)}, u32[]{:S(2)}, u32[]{:S(2)}) async-start(bf16[8,24,3072]{2,1,0:T(8,128)(2,1)} %bitcast.99), calls=%async_computation.6 | async-start | bytes 2359296 | tf_op jit(solution)/shard_map/all_to_all | solution.py:641
  397.4 3.4 copy-start.7
  398.7 4.3 copy-start.23
  403.1 4.9 %copy-start.16 = (bf16[8,196,768]{2,1,0:T(8,128)(2,1)S(1)}, bf16[8,196,768]{2,1,0:T(8,128)(2,1)}, u32[]{:S(2)}) copy-start(bf16[8,196,768]{2,1,0:T(8,128)(2,1)} %get-tuple-element.80) | copy-start | bytes 7225348
  405.9 16.5 %collective-permute-start.22 = (bf16[2,2,2,2,1,24,1280]{6,5,4,3,2,1,0:T(8,128)(2,1)}, bf16[2,2,2,2,1,24,1280]{6,5,4,3,2,1,0:T(8,128)(2,1)}, u32[]{:S(2)}, u32[]{:S(2)}) collective-permute-start(bf16[2,2,2,2,1,24,1280]{6,5,4,3,2,1,0:T(8,128)(2,1)} %constant_dynamic-slice_fusion.3), channel_id=1, source_target_pairs={{0,1},{1,0},{2,3},{3,2},{4,5},{5,4},{6,7},{7,6},{8,9},{9,8},{10,11... | collective-permute-start | bytes 2949128 | tf_op jit(solution)/shard_map/ppermute | solution.py:595
  405.9 10.0 %collective-permute-start.25 = (bf16[2,1,1,1,1,24,1536]{6,5,4,3,2,1,0:T(8,128)(2,1)S(1)}, bf16[2,1,1,1,1,24,1536]{6,5,4,3,2,1,0:T(8,128)(2,1)S(1)}, u32[]{:S(2)}, u32[]{:S(2)}) collective-permute-start(bf16[2,1,1,1,1,24,1536]{6,5,4,3,2,1,0:T(8,128)(2,1)S(1)} %constant_dynamic-slice_fusion.1), channel_id=1, source_target_pairs={{0,8},{1,9},{2,10},{3,11},{4,12},{5,13},{6,14},{7,15},{8,0},{9,1},... | collective-permute-start | bytes 442376 | tf_op jit(solution)/shard_map/ppermute | solution.py:595
  412.0 15.9 %collective-permute-start.18 = (bf16[2,196,768]{2,0,1:T(2,128)(2,1)}, bf16[2,196,768]{2,0,1:T(2,128)(2,1)}, u32[]{:S(2)}, u32[]{:S(2)}) collective-permute-start(bf16[2,196,768]{2,0,1:T(2,128)(2,1)} %copy.80), channel_id=1, source_target_pairs={{0,3},{1,2},{2,1},{3,0},{4,7},{5,6},{6,5},{7,4},{8,11},{9,10},{10,... | collective-permute-start | bytes 1806344 | tf_op jit(solution)/shard_map/ppermute | solution.py:703
  413.3 35.2 %collective-permute-start.19 = (bf16[2,196,768]{2,0,1:T(2,128)(2,1)}, bf16[2,196,768]{2,0,1:T(2,128)(2,1)}, u32[]{:S(2)}, u32[]{:S(2)}) collective-permute-start(bf16[2,196,768]{2,0,1:T(2,128)(2,1)} %copy.81), channel_id=1, source_target_pairs={{0,2},{1,3},{2,0},{3,1},{4,6},{5,7},{6,4},{7,5},{8,10},{9,11},{10,... | collective-permute-start | bytes 1806344 | tf_op jit(solution)/shard_map/ppermute | solution.py:703
  413.8 34.7 %collective-permute-start.20 = (bf16[2,196,768]{2,0,1:T(2,128)(2,1)}, bf16[2,196,768]{2,0,1:T(2,128)(2,1)}, u32[]{:S(2)}, u32[]{:S(2)}) collective-permute-start(bf16[2,196,768]{2,0,1:T(2,128)(2,1)} %copy.84), channel_id=1, source_target_pairs={{0,1},{1,0},{2,3},{3,2},{4,5},{5,4},{6,7},{7,6},{8,9},{9,8},{10,11... | collective-permute-start | bytes 1806344 | tf_op jit(solution)/shard_map/ppermute | solution.py:703
  416.6 9.2 %collective-permute-start.26 = (bf16[1,1,1,1,1,24,1536]{6,5,4,3,2,1,0:T(8,128)(2,1)S(1)}, bf16[1,1,1,1,1,24,1536]{6,5,4,3,2,1,0:T(8,128)(2,1)S(1)}, u32[]{:S(2)}, u32[]{:S(2)}) collective-permute-start(bf16[1,1,1,1,1,24,1536]{6,5,4,3,2,1,0:T(8,128)(2,1)S(1)} %constant_dynamic-slice_fusion), channel_id=1, source_target_pairs={{0,16},{1,17},{2,18},{3,19},{4,20},{5,21},{6,22},{7,23},{8,24},{9,... | collective-permute-start | bytes 221192 | tf_op jit(solution)/shard_map/ppermute | solution.py:595
  416.9 6.9 %copy-start.11 = (bf16[8,24,3072]{2,1,0:T(8,128)(2,1)}, bf16[8,24,3072]{2,1,0:T(8,128)(2,1)S(1)}, u32[]{:S(2)}) copy-start(bf16[8,24,3072]{2,1,0:T(8,128)(2,1)S(1)} %all-to-all-done.5) | copy-start | bytes 3538948
  416.9 33.7 %all-to-all-start.4 = ((bf16[16,24,1152]{2,1,0:T(8,128)(2,1)}), bf16[16,24,1152]{2,1,0:T(8,128)(2,1)}, u32[]{:S(2)}, u32[]{:S(2)}) async-start(bf16[16,24,1152]{2,1,0:T(8,128)(2,1)} %bitcast.100), calls=%async_computation.5 | async-start | bytes 1769472 | tf_op jit(solution)/shard_map/all_to_all | solution.py:641
  422.3 3.5 copy-start.21
  423.9 24.7 %collective-permute-start.23 = (bf16[2,2,1,2,1,24,1280]{6,5,4,3,2,1,0:T(8,128)(2,1)S(1)}, bf16[2,2,1,2,1,24,1280]{6,5,4,3,2,1,0:T(8,128)(2,1)S(1)}, u32[]{:S(2)}, u32[]{:S(2)}) collective-permute-start(bf16[2,2,1,2,1,24,1280]{6,5,4,3,2,1,0:T(8,128)(2,1)S(1)} %constant_dynamic-slice_fusion.2), channel_id=1, source_target_pairs={{0,4},{1,5},{2,6},{3,7},{4,0},{5,1},{6,2},{7,3},{8,12},{9,13},{10,... | collective-permute-start | bytes 1474568 | tf_op jit(solution)/shard_map/ppermute | solution.py:595
  450.6 19.1 %all-to-all-start.3 = ((bf16[8,24,1280]{2,1,0:T(8,128)(2,1)}), bf16[8,24,1280]{2,1,0:T(8,128)(2,1)S(1)}, u32[]{:S(2)}, u32[]{:S(2)}) async-start(bf16[8,24,1280]{2,1,0:T(8,128)(2,1)} %bitcast.41), calls=%async_computation.4 | async-start | bytes 983040 | tf_op jit(solution)/shard_map/all_to_all | solution.py:641
  458.3 3.3 copy-start.12
  461.6 12.5 %copy-start.3 = (bf16[4,2,196,768]{3,1,2,0:T(2,128)(2,1)S(1)}, bf16[4,2,196,768]{3,1,2,0:T(2,128)(2,1)}, u32[]{:S(2)}) copy-start(bf16[4,2,196,768]{3,1,2,0:T(2,128)(2,1)} %copy-done.2) | copy-start | bytes 7225348
  (7 other events, 8.5 us)
Sparse Core Ops, SparseCore 0:
  12.8 128.0 all-gather.1
  240.1 144.5 reduce-scatter.1
